TPU v7x, 32 devices: a whole 2x2x4 slice. The times are simulated.
32 devices in a mesh: groups: 2 (over x), seq: 16 (over z, y, core).
Axes of the slice: x: 2, y: 2, z: 4, core: 2. Of those that a mesh axis runs over, the one named last changes fastest.
Arguments:
- tokens: bfloat16 [8192, 256], P(('groups', 'seq')), parts along dimension 0, may hold values from -6 to 6
- norm_gain: float32 [256], replicated, may hold values from 0.1 to 1.9
- w_in: bfloat16 [256, 768], replicated, may hold values from -0.375 to 0.375
- short_filter: float32 [3, 768], replicated, may hold values from -0.8 to 0.8
- long_filter: float32 [4096, 256], P('seq'), may hold values from -0.09375 to 0.09375
- medium_filter: float32 [128, 256], replicated, may hold values from -0.5 to 0.5
- skip_gain: float32 [256], replicated, may hold values from -1 to 1
- w_out: bfloat16 [256, 256], replicated, may hold values from -0.375 to 0.375
Outputs:
- result: bfloat16 [8192, 256], P(('groups', 'seq')), parts along dimension 0
There are 2 independent parts, one for each index of `groups`. A program takes and returns all parts, laid end to end along the dimension named above; an argument that names none is the same for every part. Nothing has to cross between parts.
All inputs are finite; a program needn't handle non-finite values.
Results may differ from a plain program's by a relative error of at most 0.015.
Values may be sent and summed in bfloat16 or wider, within the bound.
No kernel may reach another device: no remote copies, remote signals or barrier semaphores. Data moves between devices by JAX's collectives and lax.ppermute only.
A program may use at most 64 MiB of HBM per device.

v0:
```python
import functools
import math

import jax
import jax.numpy as jnp
import numpy as np
from jax import lax
from jax.experimental import pallas as pl
from jax.experimental.pallas import tpu as pltpu
from jax.sharding import PartitionSpec as P

epsilon = 1e-06
edge = 8
rim_step = 32
vmem_bytes = 32 * 2**20


def whole(space):
    return pl.BlockSpec(memory_space=space)


def call(body, outs, args, spaces, scratch=(), flops=0, moved=0):
    return pl.pallas_call(
        body,
        out_shape=outs,
        in_specs=[whole(space) for space in spaces],
        out_specs=jax.tree.map(lambda _: whole(pltpu.VMEM), outs),
        scratch_shapes=list(scratch),
        compiler_params=pltpu.CompilerParams(vmem_limit_bytes=vmem_bytes),
        cost_estimate=pl.CostEstimate(flops=flops, bytes_accessed=moved, transcendentals=0),
    )(*args)


def spectral_tables(devices, rows, chans):
    span = 2 * devices
    full_len = span * rows
    freq_count = devices + 1
    height = -(-freq_count * chans // 16) * 16
    freqs = np.arange(freq_count)
    blocks = np.arange(devices)
    offsets = np.arange(rows)
    eye = np.eye(chans)

    def grown(table):
        out = np.zeros((height, table.shape[1]))
        out[: table.shape[0]] = table
        return out

    angle = 2.0 * math.pi / span * (freqs[:, None] * blocks[None, :] % span)
    first = np.concatenate([grown(np.kron(np.cos(angle), eye)), grown(np.kron(-np.sin(angle), eye))])
    weight = np.where((freqs == 0) | (freqs == devices), 1.0, 2.0)[:, None] / full_len
    last = np.concatenate(
        [grown(np.kron(weight * np.cos(angle), eye)), grown(np.kron(-weight * np.sin(angle), eye))]
    ).T
    twist = 2.0 * math.pi / full_len * (freqs[:, None] * offsets[None, :] % full_len)
    tw_cos = grown(np.repeat(np.cos(twist), chans, axis=0))
    tw_sin = grown(np.repeat(np.sin(twist), chans, axis=0))
    turn = 2.0 * math.pi / rows * (offsets[:, None] * offsets[None, :] % rows)
    inner = np.concatenate([np.cos(turn), np.sin(turn)], axis=1)
    return (
        jnp.asarray(first, jnp.bfloat16),
        jnp.asarray(np.concatenate([tw_cos, tw_sin]), jnp.float32),
        jnp.asarray(inner, jnp.bfloat16),
        jnp.asarray(last, jnp.bfloat16),
    )


def prepare_body(*refs):
    hbm, (packed_ref, query_ref), held, proj_ref, sems = refs[:7], refs[7:9], refs[9:16], *refs[16:]
    copies = [pltpu.make_async_copy(h, v, sems.at[i]) for i, (h, v) in enumerate(zip(hbm, held))]
    for copy in copies:
        copy.start()
    tokens_ref, gain_ref, w_ref, short_ref, long_ref, medium_ref, skip_ref = held
    rows, width = tokens_ref.shape
    proj_ref[0:edge, :] = jnp.zeros((edge, proj_ref.shape[1]), jnp.float32)
    proj_ref[edge + rows :, :] = jnp.zeros((edge, proj_ref.shape[1]), jnp.float32)
    copies[0].wait()
    copies[1].wait()
    inputs = tokens_ref[...].astype(jnp.float32)
    mean_sq = jnp.mean(inputs * inputs, axis=-1, keepdims=True)
    normed = (inputs * lax.rsqrt(mean_sq + epsilon) * gain_ref[...]).astype(jnp.bfloat16)
    copies[2].wait()
    projected = jnp.dot(normed, w_ref[...], preferred_element_type=jnp.float32)
    proj_ref[edge : edge + rows, :] = projected.astype(jnp.bfloat16).astype(jnp.float32)
    copies[3].wait()
    taps_count = short_ref.shape[0]

    def mixed(part):
        cols = slice(part * width, (part + 1) * width)
        acc = short_ref[0:1, cols] * proj_ref[edge : 2 * edge + rows, cols]
        for tap_num in range(1, taps_count):
            begin = edge - tap_num
            acc = acc + short_ref[tap_num : tap_num + 1, cols] * proj_ref[begin : begin + rows + edge, cols]
        return acc

    query, key, value = mixed(0), mixed(1), mixed(2)
    row = lax.broadcasted_iota(jnp.int32, (rows, width), 0)
    query_ref[...] = jnp.where(row < taps_count - 1, 1.0, query[0:rows])
    packed_ref[:, 0:rows] = (key[0:rows] * value[0:rows]).T.astype(jnp.bfloat16)
    rims = []
    for part in (key, value, query):
        rims += [part[0:edge], part[rows:], jnp.zeros((rim_step - 2 * edge, width), jnp.float32)]
    rims.append(jnp.zeros((128 - 3 * rim_step, width), jnp.float32))
    packed_ref[:, 2 * rows :] = jnp.concatenate(rims).T.astype(jnp.bfloat16)
    for copy in copies[4:]:
        copy.wait()
    med_len = medium_ref.shape[0]
    is_first = jnp.where(lax.axis_index("seq") == 0, 1.0, 0.0)
    head = long_ref[0:med_len, :] + is_first * medium_ref[...]
    head_row = lax.broadcasted_iota(jnp.int32, head.shape, 0)
    head = head + jnp.where(head_row == 0, is_first * skip_ref[...], 0.0)
    packed_ref[:, rows : rows + med_len] = head.T.astype(jnp.bfloat16)
    packed_ref[:, rows + med_len : 2 * rows] = long_ref[med_len:, :].T.astype(jnp.bfloat16)


def convolve_body(chans, rim_count, packed_ref, first_ref, twist_ref, inner_ref, last_ref, out_ref):
    half = twist_ref.shape[0] // 2
    rows = twist_ref.shape[1]
    rim = packed_ref[:, 2 * rows :].astype(jnp.float32)
    before = jnp.concatenate([jnp.zeros((chans, 128), jnp.float32), rim[:-chans]])
    rim = rim + pltpu.roll(before, 128 - edge, 1)
    in_rim = lax.broadcasted_iota(jnp.int32, rim.shape, 1) < rim_count
    rim_signal = (rim * pltpu.roll(rim, 128 - rim_step, 1)).astype(jnp.bfloat16)
    rim_query = jnp.where(in_rim, pltpu.roll(rim, 128 - 2 * rim_step, 1), 1.0)
    values = jnp.concatenate(
        [jnp.where(in_rim, rim_signal, packed_ref[:, 0:128]), packed_ref[:, 128 : 2 * rows]], axis=1
    )
    spread = jnp.dot(first_ref[...], values, preferred_element_type=jnp.float32)
    tw_cos, tw_sin = twist_ref[0:half, :], twist_ref[half:, :]
    spectra = []
    for begin in (0, rows):
        real, imag = spread[0:half, begin : begin + rows], spread[half:, begin : begin + rows]
        turned = jnp.concatenate([real * tw_cos + imag * tw_sin, imag * tw_cos - real * tw_sin])
        both = jnp.dot(turned.astype(jnp.bfloat16), inner_ref[...], preferred_element_type=jnp.float32)
        spectra.append(both[0:half, 0:rows] + both[half:, rows:])
        spectra.append(both[half:, 0:rows] - both[0:half, rows:])
    real, imag, fil_re, fil_im = spectra
    product = jnp.concatenate([real * fil_re - imag * fil_im, real * fil_im + imag * fil_re])
    both = jnp.dot(product.astype(jnp.bfloat16), inner_ref[...], preferred_element_type=jnp.float32)
    real = both[0:half, 0:rows] - both[half:, rows:]
    imag = both[half:, 0:rows] + both[0:half, rows:]
    turned = jnp.concatenate([real * tw_cos - imag * tw_sin, imag * tw_cos + real * tw_sin])
    conv = jnp.dot(last_ref[...], turned.astype(jnp.bfloat16), preferred_element_type=jnp.float32)
    out_ref[:, 0:128] = (conv[:, 0:128] * rim_query).astype(jnp.bfloat16)
    out_ref[:, 128:] = conv[:, 128:].astype(jnp.bfloat16)


def output_body(conv_ref, query_ref, w_ref, out_ref):
    conv = conv_ref[...].astype(jnp.float32).T
    mixed_out = (query_ref[...] * conv).astype(jnp.bfloat16)
    out_ref[...] = jnp.dot(mixed_out, w_ref[...], preferred_element_type=jnp.float32).astype(
        jnp.bfloat16
    )


def local(tokens, norm_gain, w_in, short_filter, long_filter, medium_filter, skip_gain, w_out):
    rows, width = tokens.shape
    devices = lax.axis_size("seq")
    chans = width // devices
    first, twist, inner, last = spectral_tables(devices, rows, chans)

    def swap(array):
        pieces = array.reshape(devices, chans, array.shape[1])
        return lax.all_to_all(pieces, "seq", split_axis=0, concat_axis=0).reshape(array.shape)

    args = (tokens, norm_gain[None, :], w_in, short_filter, long_filter, medium_filter, skip_gain[None, :])
    args = tuple(pltpu.with_memory_space_constraint(arg, pltpu.HBM) for arg in args)
    packed, query = call(
        prepare_body,
        (
            jax.ShapeDtypeStruct((width, 2 * rows + 128), jnp.bfloat16),
            jax.ShapeDtypeStruct((rows, width), jnp.float32),
        ),
        args,
        [pltpu.HBM] * len(args),
        [pltpu.VMEM(arg.shape, arg.dtype) for arg in args]
        + [
            pltpu.VMEM((rows + 2 * edge, 3 * width), jnp.float32),
            pltpu.SemaphoreType.DMA((len(args),)),
        ],
        flops=2 * rows * width * 3 * width,
        moved=1_500_000,
    )
    conv = call(
        functools.partial(convolve_body, chans, short_filter.shape[0] - 1),
        jax.ShapeDtypeStruct((width, rows), jnp.bfloat16),
        (swap(packed), first, twist, inner, last),
        [pltpu.VMEM] * 5,
        flops=18 * first.shape[0] * width * rows,
        moved=2_000_000,
    )
    return call(
        output_body,
        jax.ShapeDtypeStruct((rows, width), jnp.bfloat16),
        (swap(conv), query, w_out),
        [pltpu.VMEM] * 3,
        flops=2 * rows * width * width,
        moved=600_000,
    )


def solution(mesh):
    placed = (P(("groups", "seq"), None), P(), P(), P(), P("seq", None), P(), P(), P())
    return jax.shard_map(
        local, mesh=mesh, in_specs=placed, out_specs=P(("groups", "seq"), None), check_vma=False
    )
```

profile of v0, /device:TPU:0, one launch (start us, length us, event | category | flops | bytes accessed | tf_op | source)
XLA Modules:
  0.0 34.0 jit_solution(4592560064597951527)
XLA Ops:
  0.0 0.0 copy-start.2
  0.0 0.0 copy-start.3
  0.0 0.0 copy-start.4
  0.0 2.0 %shard_map.118 = (bf16[256,640]{1,0:T(8,128)(2,1)S(1)}, f32[256,256]{1,0:T(8,128)S(1)}) custom-call(bf16[256,256]{1,0:T(8,128)(2,1)} %refs_0_.1, f32[1,256]{1,0:T(1,128)} %bitcast.10, bf16[256,768]{1,0:T(8,128)(2,1)} %refs_2_.1, f32[3,768]{1,0:T(4,128)} %refs_3_.1, f32[256,256]{1,0:T(8,128)} %refs_4_.1, f32[128,256]{1,0:T(8,128)} %refs_5_.1, f32[1,256]{1,0:T(1,128)} %bitcast.11), custom_call_target="tpu_custom_call" | custom-call | flops 100663296 | bytes 1500000 | tf_op jit(solution)/shard_map/pallas_call | solution.py:23
  2.0 0.0 copy-start.1
  2.0 18.4 %all_to_all.10 = bf16[16,16,640]{2,1,0:T(8,128)(2,1)S(1)} all-to-all(bf16[16,16,640]{2,1,0:T(8,128)(2,1)S(1)} %bitcast.8), channel_id=1, replica_groups=mesh['groups'=2,'seq'=16] {'seq'}, dimensions={0} | all-to-all | bytes 655360 | tf_op jit(solution)/shard_map/all_to_all | solution.py:164
  20.4 0.0 copy-done.2
  20.4 0.0 copy-done.3
  20.4 0.0 copy-done.4
  20.4 0.0 copy-done.1
  20.4 1.5 %shard_map.119 = bf16[256,256]{1,0:T(8,128)(2,1)S(1)} custom-call(bf16[256,640]{1,0:T(8,128)(2,1)S(1)} %bitcast.7, bf16[544,256]{1,0:T(8,128)(2,1)S(1)} %copy-done.3, f32[544,256]{1,0:T(8,128)S(1)} %copy-done.1, bf16[256,512]{1,0:T(8,128)(2,1)S(1)} %copy-done.4, bf16[256,544]{1,0:T(8,128)(2,1)S(1)} %copy-done.2), custom_call_target="tpu_custom_call" | custom-call | flops 641728512 | bytes 2000000 | tf_op jit(solution)/shard_map/pallas_call | solution.py:23
  21.9 0.0 copy-start
  22.0 11.1 %all_to_all.11 = bf16[16,16,256]{2,1,0:T(8,128)(2,1)S(1)} all-to-all(bf16[16,16,256]{2,1,0:T(8,128)(2,1)S(1)} %bitcast.9), channel_id=1, replica_groups=mesh['groups'=2,'seq'=16] {'seq'}, dimensions={0} | all-to-all | bytes 262144 | tf_op jit(solution)/shard_map/all_to_all | solution.py:164
  33.1 0.0 copy-done
  33.1 0.9 %shard_map.120 = bf16[256,256]{1,0:T(8,128)(2,1)} custom-call(bf16[256,256]{1,0:T(8,128)(2,1)S(1)} %bitcast.6, f32[256,256]{1,0:T(8,128)S(1)} %get-tuple-element.8.query_ref, bf16[256,256]{1,0:T(8,128)(2,1)S(1)} %copy-done), custom_call_target="tpu_custom_call" | custom-call | flops 33554432 | bytes 600000 | tf_op jit(solution)/shard_map/pallas_call | solution.py:23
Async XLA Ops:
  0.0 20.4 %copy-start.2 = (bf16[256,544]{1,0:T(8,128)(2,1)S(1)}, bf16[256,544]{1,0:T(8,128)(2,1)}, u32[]{:S(2)}) copy-start(bf16[256,544]{1,0:T(8,128)(2,1)} %constant.11.clone.last_ref) | copy-start | bytes 835588
  0.0 20.4 %copy-start.3 = (bf16[544,256]{1,0:T(8,128)(2,1)S(1)}, bf16[544,256]{1,0:T(8,128)(2,1)}, u32[]{:S(2)}) copy-start(bf16[544,256]{1,0:T(8,128)(2,1)} %constant.8.clone.first_ref) | copy-start | bytes 835588
  0.0 20.4 %copy-start.4 = (bf16[256,512]{1,0:T(8,128)(2,1)S(1)}, bf16[256,512]{1,0:T(8,128)(2,1)}, u32[]{:S(2)}) copy-start(bf16[256,512]{1,0:T(8,128)(2,1)} %constant.10.clone.inner_ref) | copy-start | bytes 786436
  2.0 18.4 %copy-start.1 = (f32[544,256]{1,0:T(8,128)S(1)}, f32[544,256]{1,0:T(8,128)}, u32[]{:S(2)}) copy-start(f32[544,256]{1,0:T(8,128)} %constant.9.clone.twist_ref) | copy-start | bytes 1671172
  21.9 11.1 %copy-start = (bf16[256,256]{1,0:T(8,128)(2,1)S(1)}, bf16[256,256]{1,0:T(8,128)(2,1)}, u32[]{:S(2)}) copy-start(bf16[256,256]{1,0:T(8,128)(2,1)} %w_ref.1) | copy-start | bytes 393220
where the time goes:
time: 34.2 us; the launch traced here: 34 us
  blocking collectives  29.5 us (86%)
  Pallas kernels  4.36 us (13%)
    all_to_all x2, blocking collectives, swap(): lax.all_to_all(pieces, 'seq', split_axis=0, concat_axis=0)  29.5 us
    pallas_call x3, Pallas kernels, call(): pl.pallas_call(body, out_shape=outs, in_specs=[whole(space) for space in...  4.36 us

commit v1 on v0

--- a/solution.py
+++ b/solution.py
@@ -31,13 +31,14 @@
     )(*args)
 
 
-def spectral_tables(devices, rows, chans):
+def spectral_tables(outer, inner_size, rows, chans):
+    devices = outer * inner_size
     span = 2 * devices
     full_len = span * rows
     freq_count = devices + 1
     height = -(-freq_count * chans // 16) * 16
     freqs = np.arange(freq_count)
-    blocks = np.arange(devices)
+    blocks = np.arange(devices).reshape(outer, inner_size).T.ravel()
     offsets = np.arange(rows)
     eye = np.eye(chans)
 
@@ -105,7 +106,7 @@
     for copy in copies[4:]:
         copy.wait()
     med_len = medium_ref.shape[0]
-    is_first = jnp.where(lax.axis_index("seq") == 0, 1.0, 0.0)
+    is_first = jnp.where(lax.axis_index(("outer", "inner")) == 0, 1.0, 0.0)
     head = long_ref[0:med_len, :] + is_first * medium_ref[...]
     head_row = lax.broadcasted_iota(jnp.int32, head.shape, 0)
     head = head + jnp.where(head_row == 0, is_first * skip_ref[...], 0.0)
@@ -113,11 +114,13 @@
     packed_ref[:, rows + med_len : 2 * rows] = long_ref[med_len:, :].T.astype(jnp.bfloat16)
 
 
-def convolve_body(chans, rim_count, packed_ref, first_ref, twist_ref, inner_ref, last_ref, out_ref):
+def convolve_body(chans, outer, rim_count, packed_ref, first_ref, twist_ref, inner_ref, last_ref, out_ref):
     half = twist_ref.shape[0] // 2
     rows = twist_ref.shape[1]
     rim = packed_ref[:, 2 * rows :].astype(jnp.float32)
-    before = jnp.concatenate([jnp.zeros((chans, 128), jnp.float32), rim[:-chans]])
+    turn = outer * chans
+    before = [jnp.zeros((chans, 128), jnp.float32), rim[-turn:-chans], rim[:-turn]]
+    before = jnp.concatenate(before)
     rim = rim + pltpu.roll(before, 128 - edge, 1)
     in_rim = lax.broadcasted_iota(jnp.int32, rim.shape, 1) < rim_count
     rim_signal = (rim * pltpu.roll(rim, 128 - rim_step, 1)).astype(jnp.bfloat16)
@@ -155,13 +158,20 @@
 
 def local(tokens, norm_gain, w_in, short_filter, long_filter, medium_filter, skip_gain, w_out):
     rows, width = tokens.shape
-    devices = lax.axis_size("seq")
+    devices = lax.axis_size(("outer", "inner"))
     chans = width // devices
-    first, twist, inner, last = spectral_tables(devices, rows, chans)
-
-    def swap(array):
-        pieces = array.reshape(devices, chans, array.shape[1])
-        return lax.all_to_all(pieces, "seq", split_axis=0, concat_axis=0).reshape(array.shape)
+    first, twist, inner, last = spectral_tables(
+        lax.axis_size("outer"), lax.axis_size("inner"), rows, chans
+    )
+
+
+    def swap(array, axes):
+        sizes = [lax.axis_size(axis) for axis in axes]
+        pieces = array.reshape(*sizes, chans, array.shape[1])
+        pieces = lax.all_to_all(pieces, axes[0], split_axis=0, concat_axis=0)
+        pieces = pieces.transpose(1, 0, 2, 3)
+        pieces = lax.all_to_all(pieces, axes[1], split_axis=0, concat_axis=0)
+        return pieces.reshape(array.shape)
 
     args = (tokens, norm_gain[None, :], w_in, short_filter, long_filter, medium_filter, skip_gain[None, :])
     args = tuple(pltpu.with_memory_space_constraint(arg, pltpu.HBM) for arg in args)
@@ -182,9 +192,9 @@
         moved=1_500_000,
     )
     conv = call(
-        functools.partial(convolve_body, chans, short_filter.shape[0] - 1),
+        functools.partial(convolve_body, chans, lax.axis_size("outer"), short_filter.shape[0] - 1),
         jax.ShapeDtypeStruct((width, rows), jnp.bfloat16),
-        (swap(packed), first, twist, inner, last),
+        (swap(packed, ("outer", "inner")), first, twist, inner, last),
         [pltpu.VMEM] * 5,
         flops=18 * first.shape[0] * width * rows,
         moved=2_000_000,
@@ -192,7 +202,7 @@
     return call(
         output_body,
         jax.ShapeDtypeStruct((rows, width), jnp.bfloat16),
-        (swap(conv), query, w_out),
+        (swap(conv, ("inner", "outer")), query, w_out),
         [pltpu.VMEM] * 3,
         flops=2 * rows * width * width,
         moved=600_000,
@@ -200,7 +210,11 @@
 
 
 def solution(mesh):
-    placed = (P(("groups", "seq"), None), P(), P(), P(), P("seq", None), P(), P(), P())
-    return jax.shard_map(
-        local, mesh=mesh, in_specs=placed, out_specs=P(("groups", "seq"), None), check_vma=False
-    )
+    groups, devices = mesh.devices.shape
+    outer = 2 ** (devices.bit_length() // 2)
+    split = jax.sharding.Mesh(
+        mesh.devices.reshape(groups, outer, devices // outer), ("groups", "outer", "inner")
+    )
+    rows = P(("groups", "outer", "inner"), None)
+    placed = (rows, P(), P(), P(), P(("outer", "inner"), None), P(), P(), P())
+    return jax.shard_map(local, mesh=split, in_specs=placed, out_specs=rows, check_vma=False)

time: 34.2 us -> 46.4 us (1.36)
  blocking collectives: 29.5 us -> 41.7 us
    all_to_all x2 -> x4, blocking collectives: 29.5 us -> 41.7 us  [the longest x2 23.5 us: swap(): pieces = lax.all_to_all(pieces, axes[0], split_axis=0, concat_axis=0)]
where the time goes in v1:
time: 46.4 us; the launch traced here: 46.1 us
  blocking collectives  41.7 us (90%)
  Pallas kernels  4.29 us (9%)
    all_to_all x2, blocking collectives, swap(): pieces = lax.all_to_all(pieces, axes[0], split_axis=0, concat_axis=0)  23.5 us
    all_to_all x2, blocking collectives, swap(): pieces = lax.all_to_all(pieces, axes[1], split_axis=0, concat_axis=0)  18.2 us
    pallas_call x3, Pallas kernels, call(): pl.pallas_call(body, out_shape=outs, in_specs=[whole(space) for space in...  4.29 us

profile of v1, /device:TPU:0, one launch (start us, length us, event | category | flops | bytes accessed | tf_op | source)
XLA Modules:
  0.0 46.1 jit_solution(17516276269715675285)
XLA Ops:
  0.0 1.9 %shard_map.118 = (bf16[256,640]{1,0:T(8,128)(2,1)S(1)}, f32[256,256]{1,0:T(8,128)S(1)}) custom-call(bf16[256,256]{1,0:T(8,128)(2,1)} %refs_0_.1, f32[1,256]{1,0:T(1,128)} %bitcast.14, bf16[256,768]{1,0:T(8,128)(2,1)} %refs_2_.1, f32[3,768]{1,0:T(4,128)} %refs_3_.1, f32[256,256]{1,0:T(8,128)} %refs_4_.1, f32[128,256]{1,0:T(8,128)} %refs_5_.1, f32[1,256]{1,0:T(1,128)} %bitcast.15), custom_call_target="tpu_custom_call" | custom-call | flops 100663296 | bytes 1500000 | tf_op jit(solution)/shard_map/pallas_call | solution.py:23
  1.9 0.0 copy-start.4
  1.9 16.5 %all_to_all.20 = bf16[4,4,16,640]{3,2,1,0:T(8,128)(2,1)S(1)} all-to-all(bf16[4,4,16,640]{3,2,1,0:T(8,128)(2,1)S(1)} %bitcast.10), channel_id=1, replica_groups=mesh['groups'=2,'outer'=4,'inner'=4] {'outer'}, dimensions={0} | all-to-all | bytes 655360 | tf_op jit(solution)/shard_map/all_to_all | solution.py:171
  18.5 0.0 copy-start.1
  18.5 0.0 copy-start.2
  18.5 0.0 copy-start.3
  18.5 9.5 %all_to_all.21 = bf16[4,4,16,640]{3,2,1,0:T(8,128)(2,1)S(1)} all-to-all(bf16[4,4,16,640]{3,2,1,0:T(8,128)(2,1)S(1)} %copy.17), channel_id=1, replica_groups=mesh['groups'=2,'outer'=4,'inner'=4] {'inner'}, dimensions={0} | all-to-all | bytes 655360 | tf_op jit(solution)/shard_map/all_to_all | solution.py:173
  28.0 0.0 copy-done.4
  28.0 0.0 copy-done.1
  28.0 0.0 copy-done.2
  28.0 0.0 copy-done.3
  28.0 1.5 %shard_map.119 = bf16[256,256]{1,0:T(8,128)(2,1)S(1)} custom-call(bf16[256,640]{1,0:T(8,128)(2,1)S(1)} %bitcast.9, bf16[544,256]{1,0:T(8,128)(2,1)S(1)} %copy-done.3, f32[544,256]{1,0:T(8,128)S(1)} %copy-done.1, bf16[256,512]{1,0:T(8,128)(2,1)S(1)} %copy-done.4, bf16[256,544]{1,0:T(8,128)(2,1)S(1)} %copy-done.2), custom_call_target="tpu_custom_call" | custom-call | flops 641728512 | bytes 2000000 | tf_op jit(solution)/shard_map/pallas_call | solution.py:23
  29.5 7.0 %all_to_all.22 = bf16[4,4,16,256]{3,2,1,0:T(8,128)(2,1)S(1)} all-to-all(bf16[4,4,16,256]{3,2,1,0:T(8,128)(2,1)S(1)} %bitcast.11), channel_id=1, replica_groups=mesh['groups'=2,'outer'=4,'inner'=4] {'inner'}, dimensions={0} | all-to-all | bytes 262144 | tf_op jit(solution)/shard_map/all_to_all | solution.py:171
  36.5 0.0 copy-start
  36.6 8.7 %all_to_all.23 = bf16[4,4,16,256]{3,2,1,0:T(8,128)(2,1)S(1)} all-to-all(bf16[4,4,16,256]{3,2,1,0:T(8,128)(2,1)S(1)} %copy.18), channel_id=1, replica_groups=mesh['groups'=2,'outer'=4,'inner'=4] {'outer'}, dimensions={0} | all-to-all | bytes 262144 | tf_op jit(solution)/shard_map/all_to_all | solution.py:173
  45.2 0.0 copy-done
  45.2 0.9 %shard_map.120 = bf16[256,256]{1,0:T(8,128)(2,1)} custom-call(bf16[256,256]{1,0:T(8,128)(2,1)S(1)} %bitcast.8, f32[256,256]{1,0:T(8,128)S(1)} %get-tuple-element.8.query_ref, bf16[256,256]{1,0:T(8,128)(2,1)S(1)} %copy-done), custom_call_target="tpu_custom_call" | custom-call | flops 33554432 | bytes 600000 | tf_op jit(solution)/shard_map/pallas_call | solution.py:23
  (2 shorter events, 0.0 us)
Async XLA Ops:
  1.9 26.1 %copy-start.4 = (bf16[256,512]{1,0:T(8,128)(2,1)S(1)}, bf16[256,512]{1,0:T(8,128)(2,1)}, u32[]{:S(2)}) copy-start(bf16[256,512]{1,0:T(8,128)(2,1)} %constant.10.clone.inner_ref) | copy-start | bytes 786436
  18.5 9.5 %copy-start.1 = (f32[544,256]{1,0:T(8,128)S(1)}, f32[544,256]{1,0:T(8,128)}, u32[]{:S(2)}) copy-start(f32[544,256]{1,0:T(8,128)} %constant.9.clone.twist_ref) | copy-start | bytes 1671172
  18.5 9.5 %copy-start.2 = (bf16[256,544]{1,0:T(8,128)(2,1)S(1)}, bf16[256,544]{1,0:T(8,128)(2,1)}, u32[]{:S(2)}) copy-start(bf16[256,544]{1,0:T(8,128)(2,1)} %constant.11.clone.last_ref) | copy-start | bytes 835588
  18.5 9.5 %copy-start.3 = (bf16[544,256]{1,0:T(8,128)(2,1)S(1)}, bf16[544,256]{1,0:T(8,128)(2,1)}, u32[]{:S(2)}) copy-start(bf16[544,256]{1,0:T(8,128)(2,1)} %constant.8.clone.first_ref) | copy-start | bytes 835588
  36.5 8.7 %copy-start = (bf16[256,256]{1,0:T(8,128)(2,1)S(1)}, bf16[256,256]{1,0:T(8,128)(2,1)}, u32[]{:S(2)}) copy-start(bf16[256,256]{1,0:T(8,128)(2,1)} %w_ref.1) | copy-start | bytes 393220

commit v2 on v0

--- a/solution.py
+++ b/solution.py
@@ -65,8 +65,40 @@
     )
 
 
-def prepare_body(*refs):
-    hbm, (packed_ref, query_ref), held, proj_ref, sems = refs[:7], refs[7:9], refs[9:16], *refs[16:]
+def put_pieces(source_ref, piece_refs):
+    if len(piece_refs) == 1:
+        piece_refs[0][...] = source_ref[...]
+        return
+    span = piece_refs[0].shape[0]
+    mine = lax.axis_index("outer")
+    for distance, piece_ref in enumerate(piece_refs):
+        piece_ref[...] = source_ref[pl.ds(pl.multiple_of((mine ^ distance) * span, span), span), :]
+
+
+def take_pieces(piece_refs, target_ref, chans):
+    if len(piece_refs) == 1:
+        target_ref[...] = piece_refs[0][...]
+        return
+    mine, mine_inner = lax.axis_index("outer"), lax.axis_index("inner")
+    for distance, piece_ref in enumerate(piece_refs):
+        for far in range(piece_ref.shape[0] // chans):
+            block = (mine ^ far) * len(piece_refs) + (mine_inner ^ distance)
+            target_ref[pl.ds(pl.multiple_of(block * chans, chans), chans), :] = piece_ref[
+                far * chans : (far + 1) * chans, :
+            ]
+
+
+def regroup_body(chans, outer, *refs):
+    mine = lax.axis_index("inner")
+    for distance, out_ref in enumerate(refs[outer:]):
+        begin = pl.multiple_of((mine ^ distance) * chans, chans)
+        for far in range(outer):
+            out_ref[far * chans : (far + 1) * chans, :] = refs[far][pl.ds(begin, chans), :]
+
+
+def prepare_body(outer, *refs):
+    hbm, query_ref, piece_refs, refs = refs[:7], refs[7], refs[8 : 8 + outer], refs[8 + outer :]
+    held, packed_ref, proj_ref, sems = refs[:7], *refs[7:]
     copies = [pltpu.make_async_copy(h, v, sems.at[i]) for i, (h, v) in enumerate(zip(hbm, held))]
     for copy in copies:
         copy.start()
@@ -105,15 +137,20 @@
     for copy in copies[4:]:
         copy.wait()
     med_len = medium_ref.shape[0]
-    is_first = jnp.where(lax.axis_index("seq") == 0, 1.0, 0.0)
+    is_first = jnp.where(lax.axis_index(("outer", "inner")) == 0, 1.0, 0.0)
     head = long_ref[0:med_len, :] + is_first * medium_ref[...]
     head_row = lax.broadcasted_iota(jnp.int32, head.shape, 0)
     head = head + jnp.where(head_row == 0, is_first * skip_ref[...], 0.0)
     packed_ref[:, rows : rows + med_len] = head.T.astype(jnp.bfloat16)
     packed_ref[:, rows + med_len : 2 * rows] = long_ref[med_len:, :].T.astype(jnp.bfloat16)
-
-
-def convolve_body(chans, rim_count, packed_ref, first_ref, twist_ref, inner_ref, last_ref, out_ref):
+    put_pieces(packed_ref, piece_refs)
+
+
+def convolve_body(chans, inner, outer, rim_count, *refs):
+    piece_refs, refs = refs[:inner], refs[inner:]
+    (first_ref, twist_ref, inner_ref, last_ref), refs = refs[:4], refs[4:]
+    out_refs, packed_ref, conv_ref = refs[:outer], *refs[outer:]
+    take_pieces(piece_refs, packed_ref, chans)
     half = twist_ref.shape[0] // 2
     rows = twist_ref.shape[1]
     rim = packed_ref[:, 2 * rows :].astype(jnp.float32)
@@ -141,11 +178,14 @@
     imag = both[half:, 0:rows] + both[0:half, rows:]
     turned = jnp.concatenate([real * tw_cos - imag * tw_sin, imag * tw_cos + real * tw_sin])
     conv = jnp.dot(last_ref[...], turned.astype(jnp.bfloat16), preferred_element_type=jnp.float32)
-    out_ref[:, 0:128] = (conv[:, 0:128] * rim_query).astype(jnp.bfloat16)
-    out_ref[:, 128:] = conv[:, 128:].astype(jnp.bfloat16)
-
-
-def output_body(conv_ref, query_ref, w_ref, out_ref):
+    conv_ref[:, 0:128] = (conv[:, 0:128] * rim_query).astype(jnp.bfloat16)
+    conv_ref[:, 128:] = conv[:, 128:].astype(jnp.bfloat16)
+    put_pieces(conv_ref, out_refs)
+
+
+def output_body(chans, inner, *refs):
+    piece_refs, (query_ref, w_ref, out_ref, conv_ref) = refs[:inner], refs[inner:]
+    take_pieces(piece_refs, conv_ref, chans)
     conv = conv_ref[...].astype(jnp.float32).T
     mixed_out = (query_ref[...] * conv).astype(jnp.bfloat16)
     out_ref[...] = jnp.dot(mixed_out, w_ref[...], preferred_element_type=jnp.float32).astype(
@@ -153,54 +193,86 @@
     )
 
 
+def away(array, axis, distance):
+    return lax.ppermute(array, axis, [(i, i ^ distance) for i in range(lax.axis_size(axis))])
+
+
+def exchange(pieces, axis):
+    order = sorted(range(1, len(pieces)), key=lambda d: -d.bit_length())
+    moved = {distance: away(pieces[distance], axis, distance) for distance in order}
+    return [moved.get(distance, pieces[distance]) for distance in range(len(pieces))]
+
+
 def local(tokens, norm_gain, w_in, short_filter, long_filter, medium_filter, skip_gain, w_out):
     rows, width = tokens.shape
-    devices = lax.axis_size("seq")
+    devices = lax.axis_size(("outer", "inner"))
     chans = width // devices
-    first, twist, inner, last = spectral_tables(devices, rows, chans)
-
-    def swap(array):
-        pieces = array.reshape(devices, chans, array.shape[1])
-        return lax.all_to_all(pieces, "seq", split_axis=0, concat_axis=0).reshape(array.shape)
+    first, twist, inner_table, last = spectral_tables(devices, rows, chans)
+    staged = chans % 16 == 0
+    outer, inner = (lax.axis_size("outer"), lax.axis_size("inner")) if staged else (1, 1)
+
+    def bf16(*shape):
+        return jax.ShapeDtypeStruct(shape, jnp.bfloat16)
+
+    def swap(pieces):
+        lanes = pieces[0].shape[1]
+        if not staged:
+            blocks = pieces[0].reshape(devices, chans, lanes)
+            blocks = lax.all_to_all(blocks, ("outer", "inner"), split_axis=0, concat_axis=0)
+            return [blocks.reshape(width, lanes)]
+        pieces = exchange(pieces, "outer")
+        pieces = call(
+            functools.partial(regroup_body, chans, outer),
+            (bf16(outer * chans, lanes),) * inner,
+            pieces,
+            [pltpu.VMEM] * outer,
+            moved=4 * width * lanes,
+        )
+        return exchange(pieces, "inner")
 
     args = (tokens, norm_gain[None, :], w_in, short_filter, long_filter, medium_filter, skip_gain[None, :])
     args = tuple(pltpu.with_memory_space_constraint(arg, pltpu.HBM) for arg in args)
-    packed, query = call(
-        prepare_body,
-        (
-            jax.ShapeDtypeStruct((width, 2 * rows + 128), jnp.bfloat16),
-            jax.ShapeDtypeStruct((rows, width), jnp.float32),
-        ),
+    lanes = 2 * rows + 128
+    query, *pieces = call(
+        functools.partial(prepare_body, outer),
+        (jax.ShapeDtypeStruct((rows, width), jnp.float32),) + (bf16(width // outer, lanes),) * outer,
         args,
         [pltpu.HBM] * len(args),
         [pltpu.VMEM(arg.shape, arg.dtype) for arg in args]
         + [
+            pltpu.VMEM((width, lanes), jnp.bfloat16),
             pltpu.VMEM((rows + 2 * edge, 3 * width), jnp.float32),
             pltpu.SemaphoreType.DMA((len(args),)),
         ],
         flops=2 * rows * width * 3 * width,
         moved=1_500_000,
     )
-    conv = call(
-        functools.partial(convolve_body, chans, short_filter.shape[0] - 1),
-        jax.ShapeDtypeStruct((width, rows), jnp.bfloat16),
-        (swap(packed), first, twist, inner, last),
-        [pltpu.VMEM] * 5,
+    pieces = call(
+        functools.partial(convolve_body, chans, inner, outer, short_filter.shape[0] - 1),
+        (bf16(width // outer, rows),) * outer,
+        (*swap(pieces), first, twist, inner_table, last),
+        [pltpu.VMEM] * (inner + 4),
+        [pltpu.VMEM((width, lanes), jnp.bfloat16), pltpu.VMEM((width, rows), jnp.bfloat16)],
         flops=18 * first.shape[0] * width * rows,
         moved=2_000_000,
     )
     return call(
-        output_body,
-        jax.ShapeDtypeStruct((rows, width), jnp.bfloat16),
-        (swap(conv), query, w_out),
-        [pltpu.VMEM] * 3,
+        functools.partial(output_body, chans, inner),
+        bf16(rows, width),
+        (*swap(pieces), query, w_out),
+        [pltpu.VMEM] * (inner + 2),
+        [pltpu.VMEM((width, rows), jnp.bfloat16)],
         flops=2 * rows * width * width,
         moved=600_000,
     )
 
 
 def solution(mesh):
-    placed = (P(("groups", "seq"), None), P(), P(), P(), P("seq", None), P(), P(), P())
-    return jax.shard_map(
-        local, mesh=mesh, in_specs=placed, out_specs=P(("groups", "seq"), None), check_vma=False
-    )
+    groups, devices = mesh.devices.shape
+    outer = 2 ** (devices.bit_length() // 2)
+    split = jax.sharding.Mesh(
+        mesh.devices.reshape(groups, outer, devices // outer), ("groups", "outer", "inner")
+    )
+    rows = P(("groups", "outer", "inner"), None)
+    placed = (rows, P(), P(), P(), P(("outer", "inner"), None), P(), P(), P())
+    return jax.shard_map(local, mesh=split, in_specs=placed, out_specs=rows, check_vma=False)

time: 34.2 us -> 38 us (1.11)
  blocking collectives: 29.5 us -> 0 us
  waiting for transfers between devices: 0 us -> 18.3 us
  starting transfers between devices: 0 us -> 14 us
  local copies, waits for them, and re-layouts: 0.02 us -> 0.97 us
    all_to_all x2 -> x0, blocking collectives: 29.5 us -> none  [swap(): lax.all_to_all(pieces, 'seq', split_axis=0, concat_axis=0)]
    ppermute x0 -> x12, waiting for transfers between devices: none -> 18.3 us  [away(): lax.ppermute(array, axis, [(i, i ^ distance) for i in range(lax.axis_size...]
    ppermute x0 -> x12, starting transfers between devices: none -> 14 us  [away(): lax.ppermute(array, axis, [(i, i ^ distance) for i in range(lax.axis_size...]
    unnamed x10, local copies, waits for them, and re-layouts: 0.02 us -> 0.97 us
    pallas_call x3 -> x5, Pallas kernels: 4.36 us -> 4.5 us  [call(): pl.pallas_call(body, out_shape=outs, in_specs=[whole(space) for space in...]
  transfers between devices with their start and end apart: 0 -> 12, of which waited for: 0 -> 7; matrix products, arithmetic and copies ran while one was open for 0% -> 0% of each run, Pallas kernels for 0% -> 0%
where the time goes in v2:
time: 38 us; the launch traced here: 37.9 us
  waiting for transfers between devices  18.3 us (48%)
  starting transfers between devices  14 us (37%)
  Pallas kernels  4.5 us (12%)
  local copies, waits for them, and re-layouts  0.97 us (3%)
    ppermute x12, waiting for transfers between devices, away(): lax.ppermute(array, axis, [(i, i ^ distance) for i in range(lax.axis_size...  18.3 us
    ppermute x12, starting transfers between devices, away(): lax.ppermute(array, axis, [(i, i ^ distance) for i in range(lax.axis_size...  14 us
    pallas_call x5, Pallas kernels, call(): pl.pallas_call(body, out_shape=outs, in_specs=[whole(space) for space in...  4.5 us
    unnamed x10, local copies, waits for them, and re-layouts  0.97 us
  transfers between devices with their start and end apart: 12, of which 7 were waited for; matrix products, arithmetic and copies ran while one was open for 0% of the time, Pallas kernels for 0%

profile of v2, /device:TPU:0, one launch (start us, length us, event | category | flops | bytes accessed | tf_op | source)
XLA Modules:
  0.0 37.9 jit_solution(7552519163416993480)
XLA Ops:
  0.0 0.0 copy-start.1
  0.0 0.0 copy-start.3
  0.0 2.0 %shard_map.118 = (f32[256,256]{1,0:T(8,128)S(1)}, bf16[64,640]{1,0:T(8,128)(2,1)S(1)}, bf16[64,640]{1,0:T(8,128)(2,1)S(1)}, bf16[64,640]{1,0:T(8,128)(2,1)S(1)}, bf16[64,640]{1,0:T(8,128)(2,1)S(1)}) custom-call(bf16[256,256]{1,0:T(8,128)(2,1)} %refs_0_.1, f32[1,256]{1,0:T(1,128)} %bitcast.2, bf16[256,768]{1,0:T(8,128)(2,1)} %refs_2_.1, f32[3,768]{1,0:T(4,128)} %refs_3_.1, ...), custom_call_target="tpu_custom_call" | custom-call | flops 100663296 | bytes 1500000 | tf_op jit(solution)/shard_map/pallas_call | solution.py:23
  2.0 0.0 copy-start.2
  2.0 3.1 %collective-permute-start = (bf16[64,640]{1,0:T(8,128)(2,1)S(1)}, bf16[64,640]{1,0:T(8,128)(2,1)S(1)}, u32[]{:S(2)}, u32[]{:S(2)}) collective-permute-start(bf16[64,640]{1,0:T(8,128)(2,1)S(1)} %get-tuple-element.23), channel_id=1, source_target_pairs={{0,4},{4,0},{8,12},{12,8},{1,5},{5,1},{9,13},{13,9},{2,6},{6,2},{1... | collective-permute-start | bytes 245768 | tf_op jit(solution)/shard_map/ppermute | solution.py:197
  5.1 2.6 %collective-permute-start.1 = (bf16[64,640]{1,0:T(8,128)(2,1)S(1)}, bf16[64,640]{1,0:T(8,128)(2,1)S(1)}, u32[]{:S(2)}, u32[]{:S(2)}) collective-permute-start(bf16[64,640]{1,0:T(8,128)(2,1)S(1)} %get-tuple-element.24), channel_id=1, source_target_pairs={{0,8},{4,12},{8,0},{12,4},{1,9},{5,13},{9,1},{13,5},{2,10},{6,14},... | collective-permute-start | bytes 245768 | tf_op jit(solution)/shard_map/ppermute | solution.py:197
  7.7 0.0 collective-permute-start.2
  7.7 0.0 collective-permute-done.refs_1_
  7.7 6.6 %collective-permute-done.1.refs_2_ = bf16[64,640]{1,0:T(8,128)(2,1)S(1)} collective-permute-done((bf16[64,640]{1,0:T(8,128)(2,1)S(1)}, bf16[64,640]{1,0:T(8,128)(2,1)S(1)}, u32[]{:S(2)}, u32[]{:S(2)}) %collective-permute-start.1) | collective-permute-done | bytes 81952 | tf_op jit(solution)/shard_map/ppermute | solution.py:197
  14.3 0.0 collective-permute-done.2.refs_3_
  14.4 0.1 collective-permute-start.3
  14.4 1.6 %collective-permute-start.4 = (bf16[64,640]{1,0:T(8,128)(2,1)S(1)}, bf16[64,640]{1,0:T(8,128)(2,1)S(1)}, u32[]{:S(2)}, u32[]{:S(2)}) collective-permute-start(bf16[64,640]{1,0:T(8,128)(2,1)S(1)} %get-tuple-element.28), channel_id=1, source_target_pairs={{0,2},{1,3},{2,0},{3,1},{4,6},{5,7},{6,4},{7,5},{8,10},{9,11},{10,... | collective-permute-start | bytes 245768 | tf_op jit(solution)/shard_map/ppermute | solution.py:197
  16.0 0.3 collective-permute-start.5
  16.3 0.0 collective-permute-done.3.refs_1_
  16.3 3.3 %collective-permute-done.4.refs_2_ = bf16[64,640]{1,0:T(8,128)(2,1)S(1)} collective-permute-done((bf16[64,640]{1,0:T(8,128)(2,1)S(1)}, bf16[64,640]{1,0:T(8,128)(2,1)S(1)}, u32[]{:S(2)}, u32[]{:S(2)}) %collective-permute-start.4) | collective-permute-done | bytes 81952 | tf_op jit(solution)/shard_map/ppermute | solution.py:197
  19.6 1.2 %collective-permute-done.5.refs_3_ = bf16[64,640]{1,0:T(8,128)(2,1)S(1)} collective-permute-done((bf16[64,640]{1,0:T(8,128)(2,1)S(1)}, bf16[64,640]{1,0:T(8,128)(2,1)S(1)}, u32[]{:S(2)}, u32[]{:S(2)}) %collective-permute-start.5) | collective-permute-done | bytes 81952 | tf_op jit(solution)/shard_map/ppermute | solution.py:197
  20.7 0.0 copy-done.1
  20.8 0.0 copy-done.3
  20.8 0.0 copy-done.2
  20.8 0.0 copy-start.4
  20.8 0.9 %copy-done.4 = bf16[256,512]{1,0:T(8,128)(2,1)S(1)} copy-done((bf16[256,512]{1,0:T(8,128)(2,1)S(1)}, bf16[256,512]{1,0:T(8,128)(2,1)}, u32[]{:S(2)}) %copy-start.4) | copy-done | bytes 262168
  21.7 1.5 %shard_map.120 = (bf16[64,256]{1,0:T(8,128)(2,1)S(1)}, bf16[64,256]{1,0:T(8,128)(2,1)S(1)}, bf16[64,256]{1,0:T(8,128)(2,1)S(1)}, bf16[64,256]{1,0:T(8,128)(2,1)S(1)}) custom-call(bf16[64,640]{1,0:T(8,128)(2,1)S(1)} %get-tuple-element.26.refs_0_, bf16[64,640]{1,0:T(8,128)(2,1)S(1)} %collective-permute-done.3.refs_1_, ...), custom_call_target="tpu_custom_call" | custom-call | flops 641728512 | bytes 2000000 | tf_op jit(solution)/shard_map/pallas_call | solution.py:23
  23.3 0.0 copy-start
  23.3 1.5 %collective-permute-start.6 = (bf16[64,256]{1,0:T(8,128)(2,1)S(1)}, bf16[64,256]{1,0:T(8,128)(2,1)S(1)}, u32[]{:S(2)}, u32[]{:S(2)}) collective-permute-start(bf16[64,256]{1,0:T(8,128)(2,1)S(1)} %get-tuple-element.31), channel_id=1, source_target_pairs={{0,4},{4,0},{8,12},{12,8},{1,5},{5,1},{9,13},{13,9},{2,6},{6,2},{1... | collective-permute-start | bytes 98312 | tf_op jit(solution)/shard_map/ppermute | solution.py:197
  24.8 1.6 %collective-permute-start.7 = (bf16[64,256]{1,0:T(8,128)(2,1)S(1)}, bf16[64,256]{1,0:T(8,128)(2,1)S(1)}, u32[]{:S(2)}, u32[]{:S(2)}) collective-permute-start(bf16[64,256]{1,0:T(8,128)(2,1)S(1)} %get-tuple-element.32), channel_id=1, source_target_pairs={{0,8},{4,12},{8,0},{12,4},{1,9},{5,13},{9,1},{13,5},{2,10},{6,14},... | collective-permute-start | bytes 98312 | tf_op jit(solution)/shard_map/ppermute | solution.py:197
  26.4 1.4 %collective-permute-start.8 = (bf16[64,256]{1,0:T(8,128)(2,1)S(1)}, bf16[64,256]{1,0:T(8,128)(2,1)S(1)}, u32[]{:S(2)}, u32[]{:S(2)}) collective-permute-start(bf16[64,256]{1,0:T(8,128)(2,1)S(1)} %get-tuple-element.33), channel_id=1, source_target_pairs={{0,12},{4,8},{8,4},{12,0},{1,13},{5,9},{9,5},{13,1},{2,14},{6,10},... | collective-permute-start | bytes 98312 | tf_op jit(solution)/shard_map/ppermute | solution.py:197
  27.7 0.0 collective-permute-done.6.refs_1_
  27.7 2.4 %collective-permute-done.7.refs_2_ = bf16[64,256]{1,0:T(8,128)(2,1)S(1)} collective-permute-done((bf16[64,256]{1,0:T(8,128)(2,1)S(1)}, bf16[64,256]{1,0:T(8,128)(2,1)S(1)}, u32[]{:S(2)}, u32[]{:S(2)}) %collective-permute-start.7) | collective-permute-done | bytes 32800 | tf_op jit(solution)/shard_map/ppermute | solution.py:197
  30.2 1.9 %collective-permute-done.8.refs_3_ = bf16[64,256]{1,0:T(8,128)(2,1)S(1)} collective-permute-done((bf16[64,256]{1,0:T(8,128)(2,1)S(1)}, bf16[64,256]{1,0:T(8,128)(2,1)S(1)}, u32[]{:S(2)}, u32[]{:S(2)}) %collective-permute-start.8) | collective-permute-done | bytes 32800 | tf_op jit(solution)/shard_map/ppermute | solution.py:197
  32.1 0.1 collective-permute-start.9
  32.2 1.4 %collective-permute-start.10 = (bf16[64,256]{1,0:T(8,128)(2,1)S(1)}, bf16[64,256]{1,0:T(8,128)(2,1)S(1)}, u32[]{:S(2)}, u32[]{:S(2)}) collective-permute-start(bf16[64,256]{1,0:T(8,128)(2,1)S(1)} %get-tuple-element.36), channel_id=1, source_target_pairs={{0,2},{1,3},{2,0},{3,1},{4,6},{5,7},{6,4},{7,5},{8,10},{9,11},{10,... | collective-permute-start | bytes 98312 | tf_op jit(solution)/shard_map/ppermute | solution.py:197
  33.6 0.4 %collective-permute-start.11 = (bf16[64,256]{1,0:T(8,128)(2,1)S(1)}, bf16[64,256]{1,0:T(8,128)(2,1)S(1)}, u32[]{:S(2)}, u32[]{:S(2)}) collective-permute-start(bf16[64,256]{1,0:T(8,128)(2,1)S(1)} %get-tuple-element.37), channel_id=1, source_target_pairs={{0,3},{1,2},{2,1},{3,0},{4,7},{5,6},{6,5},{7,4},{8,11},{9,10},{10,... | collective-permute-start | bytes 98312 | tf_op jit(solution)/shard_map/ppermute | solution.py:197
  34.0 0.0 collective-permute-done.9.refs_1_
  34.0 2.1 %collective-permute-done.10.refs_2_ = bf16[64,256]{1,0:T(8,128)(2,1)S(1)} collective-permute-done((bf16[64,256]{1,0:T(8,128)(2,1)S(1)}, bf16[64,256]{1,0:T(8,128)(2,1)S(1)}, u32[]{:S(2)}, u32[]{:S(2)}) %collective-permute-start.10) | collective-permute-done | bytes 32800 | tf_op jit(solution)/shard_map/ppermute | solution.py:197
  36.2 0.8 %collective-permute-done.11.refs_3_ = bf16[64,256]{1,0:T(8,128)(2,1)S(1)} collective-permute-done((bf16[64,256]{1,0:T(8,128)(2,1)S(1)}, bf16[64,256]{1,0:T(8,128)(2,1)S(1)}, u32[]{:S(2)}, u32[]{:S(2)}) %collective-permute-start.11) | collective-permute-done | bytes 32800 | tf_op jit(solution)/shard_map/ppermute | solution.py:197
  37.0 0.0 copy-done
  37.0 0.9 %shard_map.122 = bf16[256,256]{1,0:T(8,128)(2,1)} custom-call(bf16[64,256]{1,0:T(8,128)(2,1)S(1)} %get-tuple-element.34.refs_0_, bf16[64,256]{1,0:T(8,128)(2,1)S(1)} %collective-permute-done.9.refs_1_, bf16[64,256]{1,0:T(8,128)(2,1)S(1)} %collective-permute-done.10.refs_2_, bf16[64,256]{1,0:T(8,128)(2,1)S(1)} %collective-permute-done.11.refs_3_, ...), custom_call_target="tpu_custom_call" | custom-call | flops 33554432 | bytes 600000 | tf_op jit(solution)/shard_map/pallas_call | solution.py:23
  (2 shorter events, 0.0 us)
Async XLA Ops:
  0.0 20.8 %copy-start.1 = (f32[544,256]{1,0:T(8,128)S(1)}, f32[544,256]{1,0:T(8,128)}, u32[]{:S(2)}) copy-start(f32[544,256]{1,0:T(8,128)} %constant.9.clone.refs_5_) | copy-start | bytes 1671172
  0.0 20.8 %copy-start.3 = (bf16[544,256]{1,0:T(8,128)(2,1)S(1)}, bf16[544,256]{1,0:T(8,128)(2,1)}, u32[]{:S(2)}) copy-start(bf16[544,256]{1,0:T(8,128)(2,1)} %constant.8.clone.refs_4_) | copy-start | bytes 835588
  2.0 18.7 %copy-start.2 = (bf16[256,544]{1,0:T(8,128)(2,1)S(1)}, bf16[256,544]{1,0:T(8,128)(2,1)}, u32[]{:S(2)}) copy-start(bf16[256,544]{1,0:T(8,128)(2,1)} %constant.11.clone.refs_7_) | copy-start | bytes 835588
  2.0 5.7 %collective-permute-start = (bf16[64,640]{1,0:T(8,128)(2,1)S(1)}, bf16[64,640]{1,0:T(8,128)(2,1)S(1)}, u32[]{:S(2)}, u32[]{:S(2)}) collective-permute-start(bf16[64,640]{1,0:T(8,128)(2,1)S(1)} %get-tuple-element.23), channel_id=1, source_target_pairs={{0,4},{4,0},{8,12},{12,8},{1,5},{5,1},{9,13},{13,9},{2,6},{6,2},{1... | collective-permute-start | bytes 245768 | tf_op jit(solution)/shard_map/ppermute | solution.py:197
  5.1 9.2 %collective-permute-start.1 = (bf16[64,640]{1,0:T(8,128)(2,1)S(1)}, bf16[64,640]{1,0:T(8,128)(2,1)S(1)}, u32[]{:S(2)}, u32[]{:S(2)}) collective-permute-start(bf16[64,640]{1,0:T(8,128)(2,1)S(1)} %get-tuple-element.24), channel_id=1, source_target_pairs={{0,8},{4,12},{8,0},{12,4},{1,9},{5,13},{9,1},{13,5},{2,10},{6,14},... | collective-permute-start | bytes 245768 | tf_op jit(solution)/shard_map/ppermute | solution.py:197
  7.7 6.6 %collective-permute-start.2 = (bf16[64,640]{1,0:T(8,128)(2,1)S(1)}, bf16[64,640]{1,0:T(8,128)(2,1)S(1)}, u32[]{:S(2)}, u32[]{:S(2)}) collective-permute-start(bf16[64,640]{1,0:T(8,128)(2,1)S(1)} %get-tuple-element.25), channel_id=1, source_target_pairs={{0,12},{4,8},{8,4},{12,0},{1,13},{5,9},{9,5},{13,1},{2,14},{6,10},... | collective-permute-start | bytes 245768 | tf_op jit(solution)/shard_map/ppermute | solution.py:197
  14.4 1.9 %collective-permute-start.3 = (bf16[64,640]{1,0:T(8,128)(2,1)S(1)}, bf16[64,640]{1,0:T(8,128)(2,1)S(1)}, u32[]{:S(2)}, u32[]{:S(2)}) collective-permute-start(bf16[64,640]{1,0:T(8,128)(2,1)S(1)} %get-tuple-element.27), channel_id=1, source_target_pairs={{0,1},{1,0},{2,3},{3,2},{4,5},{5,4},{6,7},{7,6},{8,9},{9,8},{10,11... | collective-permute-start | bytes 245768 | tf_op jit(solution)/shard_map/ppermute | solution.py:197
  14.4 5.2 %collective-permute-start.4 = (bf16[64,640]{1,0:T(8,128)(2,1)S(1)}, bf16[64,640]{1,0:T(8,128)(2,1)S(1)}, u32[]{:S(2)}, u32[]{:S(2)}) collective-permute-start(bf16[64,640]{1,0:T(8,128)(2,1)S(1)} %get-tuple-element.28), channel_id=1, source_target_pairs={{0,2},{1,3},{2,0},{3,1},{4,6},{5,7},{6,4},{7,5},{8,10},{9,11},{10,... | collective-permute-start | bytes 245768 | tf_op jit(solution)/shard_map/ppermute | solution.py:197
  16.0 4.7 %collective-permute-start.5 = (bf16[64,640]{1,0:T(8,128)(2,1)S(1)}, bf16[64,640]{1,0:T(8,128)(2,1)S(1)}, u32[]{:S(2)}, u32[]{:S(2)}) collective-permute-start(bf16[64,640]{1,0:T(8,128)(2,1)S(1)} %get-tuple-element.29), channel_id=1, source_target_pairs={{0,3},{1,2},{2,1},{3,0},{4,7},{5,6},{6,5},{7,4},{8,11},{9,10},{10,... | collective-permute-start | bytes 245768 | tf_op jit(solution)/shard_map/ppermute | solution.py:197
  20.8 1.0 %copy-start.4 = (bf16[256,512]{1,0:T(8,128)(2,1)S(1)}, bf16[256,512]{1,0:T(8,128)(2,1)}, u32[]{:S(2)}) copy-start(bf16[256,512]{1,0:T(8,128)(2,1)} %constant.10.clone.refs_6_) | copy-start | bytes 786436
  23.3 13.7 %copy-start = (bf16[256,256]{1,0:T(8,128)(2,1)S(1)}, bf16[256,256]{1,0:T(8,128)(2,1)}, u32[]{:S(2)}) copy-start(bf16[256,256]{1,0:T(8,128)(2,1)} %refs_5_.4) | copy-start | bytes 393220
  23.3 4.5 %collective-permute-start.6 = (bf16[64,256]{1,0:T(8,128)(2,1)S(1)}, bf16[64,256]{1,0:T(8,128)(2,1)S(1)}, u32[]{:S(2)}, u32[]{:S(2)}) collective-permute-start(bf16[64,256]{1,0:T(8,128)(2,1)S(1)} %get-tuple-element.31), channel_id=1, source_target_pairs={{0,4},{4,0},{8,12},{12,8},{1,5},{5,1},{9,13},{13,9},{2,6},{6,2},{1... | collective-permute-start | bytes 98312 | tf_op jit(solution)/shard_map/ppermute | solution.py:197
  24.8 5.4 %collective-permute-start.7 = (bf16[64,256]{1,0:T(8,128)(2,1)S(1)}, bf16[64,256]{1,0:T(8,128)(2,1)S(1)}, u32[]{:S(2)}, u32[]{:S(2)}) collective-permute-start(bf16[64,256]{1,0:T(8,128)(2,1)S(1)} %get-tuple-element.32), channel_id=1, source_target_pairs={{0,8},{4,12},{8,0},{12,4},{1,9},{5,13},{9,1},{13,5},{2,10},{6,14},... | collective-permute-start | bytes 98312 | tf_op jit(solution)/shard_map/ppermute | solution.py:197
  26.4 5.7 %collective-permute-start.8 = (bf16[64,256]{1,0:T(8,128)(2,1)S(1)}, bf16[64,256]{1,0:T(8,128)(2,1)S(1)}, u32[]{:S(2)}, u32[]{:S(2)}) collective-permute-start(bf16[64,256]{1,0:T(8,128)(2,1)S(1)} %get-tuple-element.33), channel_id=1, source_target_pairs={{0,12},{4,8},{8,4},{12,0},{1,13},{5,9},{9,5},{13,1},{2,14},{6,10},... | collective-permute-start | bytes 98312 | tf_op jit(solution)/shard_map/ppermute | solution.py:197
  32.1 1.9 %collective-permute-start.9 = (bf16[64,256]{1,0:T(8,128)(2,1)S(1)}, bf16[64,256]{1,0:T(8,128)(2,1)S(1)}, u32[]{:S(2)}, u32[]{:S(2)}) collective-permute-start(bf16[64,256]{1,0:T(8,128)(2,1)S(1)} %get-tuple-element.35), channel_id=1, source_target_pairs={{0,1},{1,0},{2,3},{3,2},{4,5},{5,4},{6,7},{7,6},{8,9},{9,8},{10,11... | collective-permute-start | bytes 98312 | tf_op jit(solution)/shard_map/ppermute | solution.py:197
  32.2 4.0 %collective-permute-start.10 = (bf16[64,256]{1,0:T(8,128)(2,1)S(1)}, bf16[64,256]{1,0:T(8,128)(2,1)S(1)}, u32[]{:S(2)}, u32[]{:S(2)}) collective-permute-start(bf16[64,256]{1,0:T(8,128)(2,1)S(1)} %get-tuple-element.36), channel_id=1, source_target_pairs={{0,2},{1,3},{2,0},{3,1},{4,6},{5,7},{6,4},{7,5},{8,10},{9,11},{10,... | collective-permute-start | bytes 98312 | tf_op jit(solution)/shard_map/ppermute | solution.py:197
  33.6 3.3 %collective-permute-start.11 = (bf16[64,256]{1,0:T(8,128)(2,1)S(1)}, bf16[64,256]{1,0:T(8,128)(2,1)S(1)}, u32[]{:S(2)}, u32[]{:S(2)}) collective-permute-start(bf16[64,256]{1,0:T(8,128)(2,1)S(1)} %get-tuple-element.37), channel_id=1, source_target_pairs={{0,3},{1,2},{2,1},{3,0},{4,7},{5,6},{6,5},{7,4},{8,11},{9,10},{10,... | collective-permute-start | bytes 98312 | tf_op jit(solution)/shard_map/ppermute | solution.py:197

commit v3 on v0

--- a/solution.py
+++ b/solution.py
@@ -11,7 +11,8 @@
 
 epsilon = 1e-06
 edge = 8
-rim_step = 32
+lane = 128
+rim_step = 2 * edge
 vmem_bytes = 32 * 2**20
 
 
@@ -96,12 +97,12 @@
     query, key, value = mixed(0), mixed(1), mixed(2)
     row = lax.broadcasted_iota(jnp.int32, (rows, width), 0)
     query_ref[...] = jnp.where(row < taps_count - 1, 1.0, query[0:rows])
-    packed_ref[:, 0:rows] = (key[0:rows] * value[0:rows]).T.astype(jnp.bfloat16)
+    signal = (key[0:rows] * value[0:rows]).astype(jnp.bfloat16).T
     rims = []
     for part in (key, value, query):
-        rims += [part[0:edge], part[rows:], jnp.zeros((rim_step - 2 * edge, width), jnp.float32)]
-    rims.append(jnp.zeros((128 - 3 * rim_step, width), jnp.float32))
-    packed_ref[:, 2 * rows :] = jnp.concatenate(rims).T.astype(jnp.bfloat16)
+        rims += [part[0:edge], part[rows:]]
+    rims.append(jnp.zeros((lane - 3 * rim_step, width), jnp.float32))
+    rim = jnp.concatenate(rims).T
     for copy in copies[4:]:
         copy.wait()
     med_len = medium_ref.shape[0]
@@ -109,21 +110,51 @@
     head = long_ref[0:med_len, :] + is_first * medium_ref[...]
     head_row = lax.broadcasted_iota(jnp.int32, head.shape, 0)
     head = head + jnp.where(head_row == 0, is_first * skip_ref[...], 0.0)
-    packed_ref[:, rows : rows + med_len] = head.T.astype(jnp.bfloat16)
-    packed_ref[:, rows + med_len : 2 * rows] = long_ref[med_len:, :].T.astype(jnp.bfloat16)
+    taps = jnp.concatenate([head, long_ref[med_len:, :]]).astype(jnp.bfloat16).T
+    put_blocks(packed_ref, signal, taps, rim)
+
+
+def put_blocks(packed_ref, signal, taps, rim):
+    devices = packed_ref.shape[0]
+    chans = signal.shape[0] // devices
+    if chans % 16:
+        packed_ref[...] = jnp.concatenate([signal, taps, rim.astype(jnp.bfloat16)], axis=1)
+        return
+    begin = 0
+    for part in (signal, taps):
+        part = part.reshape(devices, chans, -1)
+        for column in range(part.shape[2] // lane):
+            packed_ref[:, begin : begin + chans, :] = part[:, :, column * lane : (column + 1) * lane]
+            begin += chans
+    rim = rim.reshape(devices, chans, lane)
+    both = rim[:, : chans // 2] + pltpu.roll(rim[:, chans // 2 :], lane // 2, 2)
+    packed_ref[:, begin:, :] = both.astype(jnp.bfloat16)
+
+
+def take_blocks(packed_ref, chans, rows):
+    if chans % 16:
+        return packed_ref[:, : 2 * rows], packed_ref[:, 2 * rows :].astype(jnp.float32)
+    width = packed_ref.shape[0] * chans
+    count = 2 * rows // lane
+    columns = [
+        packed_ref[:, i * chans : (i + 1) * chans, :].reshape(width, lane) for i in range(count)
+    ]
+    both = packed_ref[:, count * chans :, :].astype(jnp.float32)
+    rim = jnp.concatenate([both, pltpu.roll(both, lane // 2, 2)], axis=1).reshape(width, lane)
+    return jnp.concatenate(columns, axis=1), rim
 
 
 def convolve_body(chans, rim_count, packed_ref, first_ref, twist_ref, inner_ref, last_ref, out_ref):
     half = twist_ref.shape[0] // 2
     rows = twist_ref.shape[1]
-    rim = packed_ref[:, 2 * rows :].astype(jnp.float32)
-    before = jnp.concatenate([jnp.zeros((chans, 128), jnp.float32), rim[:-chans]])
-    rim = rim + pltpu.roll(before, 128 - edge, 1)
+    values, rim = take_blocks(packed_ref, chans, rows)
+    before = jnp.concatenate([jnp.zeros((chans, lane), jnp.float32), rim[:-chans]])
+    rim = rim + pltpu.roll(before, lane - edge, 1)
     in_rim = lax.broadcasted_iota(jnp.int32, rim.shape, 1) < rim_count
-    rim_signal = (rim * pltpu.roll(rim, 128 - rim_step, 1)).astype(jnp.bfloat16)
-    rim_query = jnp.where(in_rim, pltpu.roll(rim, 128 - 2 * rim_step, 1), 1.0)
+    rim_signal = (rim * pltpu.roll(rim, lane - rim_step, 1)).astype(jnp.bfloat16)
+    rim_query = jnp.where(in_rim, pltpu.roll(rim, lane - 2 * rim_step, 1), 1.0)
     values = jnp.concatenate(
-        [jnp.where(in_rim, rim_signal, packed_ref[:, 0:128]), packed_ref[:, 128 : 2 * rows]], axis=1
+        [jnp.where(in_rim, rim_signal, values[:, 0:lane]), values[:, lane:]], axis=1
     )
     spread = jnp.dot(first_ref[...], values, preferred_element_type=jnp.float32)
     tw_cos, tw_sin = twist_ref[0:half, :], twist_ref[half:, :]
@@ -141,8 +172,8 @@
     imag = both[half:, 0:rows] + both[0:half, rows:]
     turned = jnp.concatenate([real * tw_cos - imag * tw_sin, imag * tw_cos + real * tw_sin])
     conv = jnp.dot(last_ref[...], turned.astype(jnp.bfloat16), preferred_element_type=jnp.float32)
-    out_ref[:, 0:128] = (conv[:, 0:128] * rim_query).astype(jnp.bfloat16)
-    out_ref[:, 128:] = conv[:, 128:].astype(jnp.bfloat16)
+    out_ref[:, 0:lane] = (conv[:, 0:lane] * rim_query).astype(jnp.bfloat16)
+    out_ref[:, lane:] = conv[:, lane:].astype(jnp.bfloat16)
 
 
 def output_body(conv_ref, query_ref, w_ref, out_ref):
@@ -159,8 +190,13 @@
     chans = width // devices
     first, twist, inner, last = spectral_tables(devices, rows, chans)
 
+    if chans % 16:
+        packed_shape = (width, 2 * rows + lane)
+    else:
+        packed_shape = (devices, 2 * rows // lane * chans + chans // 2, lane)
+
     def swap(array):
-        pieces = array.reshape(devices, chans, array.shape[1])
+        pieces = array.reshape(devices, -1, array.shape[-1])
         return lax.all_to_all(pieces, "seq", split_axis=0, concat_axis=0).reshape(array.shape)
 
     args = (tokens, norm_gain[None, :], w_in, short_filter, long_filter, medium_filter, skip_gain[None, :])
@@ -168,7 +204,7 @@
     packed, query = call(
         prepare_body,
         (
-            jax.ShapeDtypeStruct((width, 2 * rows + 128), jnp.bfloat16),
+            jax.ShapeDtypeStruct(packed_shape, jnp.bfloat16),
             jax.ShapeDtypeStruct((rows, width), jnp.float32),
         ),
         args,

time: 34.2 us -> 33.6 us (0.982)
  blocking collectives: 29.5 us -> 28.9 us
    all_to_all x2, blocking collectives: 29.5 us -> 28.9 us  [swap(): lax.all_to_all(pieces, 'seq', split_axis=0, concat_axis=0)]
where the time goes in v3:
time: 33.6 us; the launch traced here: 33.3 us
  blocking collectives  28.9 us (86%)
  Pallas kernels  4.4 us (13%)
    all_to_all x2, blocking collectives, swap(): lax.all_to_all(pieces, 'seq', split_axis=0, concat_axis=0)  28.9 us
    pallas_call x3, Pallas kernels, call(): pl.pallas_call(body, out_shape=outs, in_specs=[whole(space) for space in...  4.4 us

profile of v3, /device:TPU:0, one launch (start us, length us, event | category | flops | bytes accessed | tf_op | source)
XLA Modules:
  0.0 33.3 jit_solution(635967381756028719)
XLA Ops:
  0.0 0.0 copy-start.1
  0.0 0.0 copy-start.3
  0.0 1.9 %shard_map.118 = (bf16[16,72,128]{2,1,0:T(8,128)(2,1)S(1)}, f32[256,256]{1,0:T(8,128)S(1)}) custom-call(bf16[256,256]{1,0:T(8,128)(2,1)} %refs_0_.1, f32[1,256]{1,0:T(1,128)} %bitcast.6, bf16[256,768]{1,0:T(8,128)(2,1)} %refs_2_.1, f32[3,768]{1,0:T(4,128)} %refs_3_.1, f32[256,256]{1,0:T(8,128)} %refs_4_.1, f32[128,256]{1,0:T(8,128)} %refs_5_.1, f32[1,256]{1,0:T(1,128)} %bitcast.7), custom_call_target="tpu_custom_call" | custom-call | flops 100663296 | bytes 1500000 | tf_op jit(solution)/shard_map/pallas_call | solution.py:24
  2.0 0.0 copy-start.2
  2.0 0.0 copy-start.4
  2.0 17.9 %all_to_all.10.packed_ref = bf16[16,72,128]{2,1,0:T(8,128)(2,1)S(1)} all-to-all(bf16[16,72,128]{2,1,0:T(8,128)(2,1)S(1)} %get-tuple-element.7), channel_id=1, replica_groups=mesh['groups'=2,'seq'=16] {'seq'}, dimensions={0} | all-to-all | bytes 589824 | tf_op jit(solution)/shard_map/all_to_all | solution.py:200
  19.9 0.0 copy-done.1
  19.9 0.0 copy-done.3
  19.9 0.0 copy-done.2
  19.9 0.0 copy-done.4
  19.9 1.6 %shard_map.119 = bf16[256,256]{1,0:T(8,128)(2,1)S(1)} custom-call(bf16[16,72,128]{2,1,0:T(8,128)(2,1)S(1)} %all_to_all.10.packed_ref, bf16[544,256]{1,0:T(8,128)(2,1)S(1)} %copy-done.3, f32[544,256]{1,0:T(8,128)S(1)} %copy-done.1, bf16[256,512]{1,0:T(8,128)(2,1)S(1)} %copy-done.4, bf16[256,544]{1,0:T(8,128)(2,1)S(1)} %copy-done.2), custom_call_target="tpu_custom_call" | custom-call | flops 641728512 | bytes 2000000 | tf_op jit(solution)/shard_map/pallas_call | solution.py:24
  21.5 0.0 copy-start
  21.5 11.0 %all_to_all.11 = bf16[16,16,256]{2,1,0:T(8,128)(2,1)S(1)} all-to-all(bf16[16,16,256]{2,1,0:T(8,128)(2,1)S(1)} %bitcast.5), channel_id=1, replica_groups=mesh['groups'=2,'seq'=16] {'seq'}, dimensions={0} | all-to-all | bytes 262144 | tf_op jit(solution)/shard_map/all_to_all | solution.py:200
  32.5 0.0 copy-done
  32.5 0.9 %shard_map.120 = bf16[256,256]{1,0:T(8,128)(2,1)} custom-call(bf16[256,256]{1,0:T(8,128)(2,1)S(1)} %bitcast.4, f32[256,256]{1,0:T(8,128)S(1)} %get-tuple-element.8.query_ref, bf16[256,256]{1,0:T(8,128)(2,1)S(1)} %copy-done), custom_call_target="tpu_custom_call" | custom-call | flops 33554432 | bytes 600000 | tf_op jit(solution)/shard_map/pallas_call | solution.py:24
Async XLA Ops:
  0.0 19.9 %copy-start.1 = (f32[544,256]{1,0:T(8,128)S(1)}, f32[544,256]{1,0:T(8,128)}, u32[]{:S(2)}) copy-start(f32[544,256]{1,0:T(8,128)} %constant.9.clone.twist_ref) | copy-start | bytes 1671172
  0.0 19.9 %copy-start.3 = (bf16[544,256]{1,0:T(8,128)(2,1)S(1)}, bf16[544,256]{1,0:T(8,128)(2,1)}, u32[]{:S(2)}) copy-start(bf16[544,256]{1,0:T(8,128)(2,1)} %constant.8.clone.first_ref) | copy-start | bytes 835588
  2.0 17.9 %copy-start.2 = (bf16[256,544]{1,0:T(8,128)(2,1)S(1)}, bf16[256,544]{1,0:T(8,128)(2,1)}, u32[]{:S(2)}) copy-start(bf16[256,544]{1,0:T(8,128)(2,1)} %constant.11.clone.last_ref) | copy-start | bytes 835588
  2.0 17.9 %copy-start.4 = (bf16[256,512]{1,0:T(8,128)(2,1)S(1)}, bf16[256,512]{1,0:T(8,128)(2,1)}, u32[]{:S(2)}) copy-start(bf16[256,512]{1,0:T(8,128)(2,1)} %constant.10.clone.inner_ref) | copy-start | bytes 786436
  21.5 11.0 %copy-start = (bf16[256,256]{1,0:T(8,128)(2,1)S(1)}, bf16[256,256]{1,0:T(8,128)(2,1)}, u32[]{:S(2)}) copy-start(bf16[256,256]{1,0:T(8,128)(2,1)} %w_ref.1) | copy-start | bytes 393220

commit v4 on v3

--- a/solution.py
+++ b/solution.py
@@ -33,48 +33,34 @@
 
 
 def spectral_tables(devices, rows, chans):
-    span = 2 * devices
-    full_len = span * rows
-    freq_count = devices + 1
-    height = -(-freq_count * chans // 16) * 16
-    freqs = np.arange(freq_count)
-    blocks = np.arange(devices)
+    full_len = devices * rows
+    freqs = 4 * np.arange(devices) + 1
+    eye = np.eye(chans)
+    angle = 2.0 * math.pi / (4 * devices) * (freqs[:, None] * np.arange(devices)[None, :] % (4 * devices))
+    cosine, sine = np.kron(np.cos(angle), eye), np.kron(np.sin(angle), eye)
+    first = np.concatenate([cosine, -sine])
+    last = np.concatenate([cosine, -sine]).T / full_len
     offsets = np.arange(rows)
-    eye = np.eye(chans)
-
-    def grown(table):
-        out = np.zeros((height, table.shape[1]))
-        out[: table.shape[0]] = table
-        return out
-
-    angle = 2.0 * math.pi / span * (freqs[:, None] * blocks[None, :] % span)
-    first = np.concatenate([grown(np.kron(np.cos(angle), eye)), grown(np.kron(-np.sin(angle), eye))])
-    weight = np.where((freqs == 0) | (freqs == devices), 1.0, 2.0)[:, None] / full_len
-    last = np.concatenate(
-        [grown(np.kron(weight * np.cos(angle), eye)), grown(np.kron(-weight * np.sin(angle), eye))]
-    ).T
-    twist = 2.0 * math.pi / full_len * (freqs[:, None] * offsets[None, :] % full_len)
-    tw_cos = grown(np.repeat(np.cos(twist), chans, axis=0))
-    tw_sin = grown(np.repeat(np.sin(twist), chans, axis=0))
+    twist = 2.0 * math.pi / (4 * full_len) * (freqs[:, None] * offsets[None, :] % (4 * full_len))
+    twist = np.repeat(np.concatenate([np.cos(twist), np.sin(twist)]), chans, axis=0)
     turn = 2.0 * math.pi / rows * (offsets[:, None] * offsets[None, :] % rows)
-    inner = np.concatenate([np.cos(turn), np.sin(turn)], axis=1)
+    cosine, sine = np.cos(turn), np.sin(turn)
+    inner = np.block([[cosine, -sine], [sine, cosine]])
     return (
         jnp.asarray(first, jnp.bfloat16),
-        jnp.asarray(np.concatenate([tw_cos, tw_sin]), jnp.float32),
+        jnp.asarray(twist, jnp.float32),
         jnp.asarray(inner, jnp.bfloat16),
         jnp.asarray(last, jnp.bfloat16),
     )
 
 
 def prepare_body(*refs):
-    hbm, (packed_ref, query_ref), held, proj_ref, sems = refs[:7], refs[7:9], refs[9:16], *refs[16:]
+    hbm, (packed_ref, query_ref), held, sems = refs[:7], refs[7:9], refs[9:16], refs[16]
     copies = [pltpu.make_async_copy(h, v, sems.at[i]) for i, (h, v) in enumerate(zip(hbm, held))]
     for copy in copies:
         copy.start()
     tokens_ref, gain_ref, w_ref, short_ref, long_ref, medium_ref, skip_ref = held
     rows, width = tokens_ref.shape
-    proj_ref[0:edge, :] = jnp.zeros((edge, proj_ref.shape[1]), jnp.float32)
-    proj_ref[edge + rows :, :] = jnp.zeros((edge, proj_ref.shape[1]), jnp.float32)
     copies[0].wait()
     copies[1].wait()
     inputs = tokens_ref[...].astype(jnp.float32)
@@ -82,16 +68,16 @@
     normed = (inputs * lax.rsqrt(mean_sq + epsilon) * gain_ref[...]).astype(jnp.bfloat16)
     copies[2].wait()
     projected = jnp.dot(normed, w_ref[...], preferred_element_type=jnp.float32)
-    proj_ref[edge : edge + rows, :] = projected.astype(jnp.bfloat16).astype(jnp.float32)
+    projected = projected.astype(jnp.bfloat16).astype(jnp.float32)
+    projected = jnp.concatenate([projected, jnp.zeros((edge, 3 * width), jnp.float32)])
     copies[3].wait()
     taps_count = short_ref.shape[0]
 
     def mixed(part):
         cols = slice(part * width, (part + 1) * width)
-        acc = short_ref[0:1, cols] * proj_ref[edge : 2 * edge + rows, cols]
+        acc = short_ref[0:1, cols] * projected[:, cols]
         for tap_num in range(1, taps_count):
-            begin = edge - tap_num
-            acc = acc + short_ref[tap_num : tap_num + 1, cols] * proj_ref[begin : begin + rows + edge, cols]
+            acc = acc + short_ref[tap_num : tap_num + 1, cols] * pltpu.roll(projected[:, cols], tap_num, 0)
         return acc
 
     query, key, value = mixed(0), mixed(1), mixed(2)
@@ -158,18 +144,18 @@
     )
     spread = jnp.dot(first_ref[...], values, preferred_element_type=jnp.float32)
     tw_cos, tw_sin = twist_ref[0:half, :], twist_ref[half:, :]
-    spectra = []
+    turned = []
     for begin in (0, rows):
         real, imag = spread[0:half, begin : begin + rows], spread[half:, begin : begin + rows]
-        turned = jnp.concatenate([real * tw_cos + imag * tw_sin, imag * tw_cos - real * tw_sin])
-        both = jnp.dot(turned.astype(jnp.bfloat16), inner_ref[...], preferred_element_type=jnp.float32)
-        spectra.append(both[0:half, 0:rows] + both[half:, rows:])
-        spectra.append(both[half:, 0:rows] - both[0:half, rows:])
-    real, imag, fil_re, fil_im = spectra
-    product = jnp.concatenate([real * fil_re - imag * fil_im, real * fil_im + imag * fil_re])
-    both = jnp.dot(product.astype(jnp.bfloat16), inner_ref[...], preferred_element_type=jnp.float32)
-    real = both[0:half, 0:rows] - both[half:, rows:]
-    imag = both[half:, 0:rows] + both[0:half, rows:]
+        turned.append([real * tw_cos + imag * tw_sin, imag * tw_cos - real * tw_sin])
+    turned = jnp.concatenate([jnp.concatenate(pair, axis=1).astype(jnp.bfloat16) for pair in turned])
+    spectra = jnp.dot(turned, inner_ref[...], preferred_element_type=jnp.float32)
+    real, imag = spectra[0:half, 0:rows], spectra[0:half, rows:]
+    fil_re, fil_im = spectra[half:, 0:rows], spectra[half:, rows:]
+    product = [real * fil_im + imag * fil_re, real * fil_re - imag * fil_im]
+    product = jnp.concatenate(product, axis=1).astype(jnp.bfloat16)
+    back = jnp.dot(product, inner_ref[...], preferred_element_type=jnp.float32)
+    imag, real = back[:, 0:rows], back[:, rows:]
     turned = jnp.concatenate([real * tw_cos - imag * tw_sin, imag * tw_cos + real * tw_sin])
     conv = jnp.dot(last_ref[...], turned.astype(jnp.bfloat16), preferred_element_type=jnp.float32)
     out_ref[:, 0:lane] = (conv[:, 0:lane] * rim_query).astype(jnp.bfloat16)
@@ -177,7 +163,7 @@
 
 
 def output_body(conv_ref, query_ref, w_ref, out_ref):
-    conv = conv_ref[...].astype(jnp.float32).T
+    conv = conv_ref[...].T.astype(jnp.float32)
     mixed_out = (query_ref[...] * conv).astype(jnp.bfloat16)
     out_ref[...] = jnp.dot(mixed_out, w_ref[...], preferred_element_type=jnp.float32).astype(
         jnp.bfloat16
@@ -210,10 +196,7 @@
         args,
         [pltpu.HBM] * len(args),
         [pltpu.VMEM(arg.shape, arg.dtype) for arg in args]
-        + [
-            pltpu.VMEM((rows + 2 * edge, 3 * width), jnp.float32),
-            pltpu.SemaphoreType.DMA((len(args),)),
-        ],
+        + [pltpu.SemaphoreType.DMA((len(args),))],
         flops=2 * rows * width * 3 * width,
         moved=1_500_000,
     )

time: 33.6 us -> 34.3 us (1.021)
  local copies, waits for them, and re-layouts: 0.03 us -> 0.97 us
    unnamed x10, local copies, waits for them, and re-layouts: 0.03 us -> 0.97 us
where the time goes in v4:
time: 34.3 us; the launch traced here: 34 us
  blocking collectives  28.9 us (84%)
  Pallas kernels  4.15 us (12%)
  local copies, waits for them, and re-layouts  0.97 us (3%)
    all_to_all x2, blocking collectives, swap(): lax.all_to_all(pieces, 'seq', split_axis=0, concat_axis=0)  28.9 us
    pallas_call x3, Pallas kernels, call(): pl.pallas_call(body, out_shape=outs, in_specs=[whole(space) for space in...  4.15 us
    unnamed x10, local copies, waits for them, and re-layouts  0.97 us

profile of v4, /device:TPU:0, one launch (start us, length us, event | category | flops | bytes accessed | tf_op | source)
XLA Modules:
  0.0 34.0 jit_solution(345443327775866841)
XLA Ops:
  0.0 0.0 copy-start.2
  0.0 0.0 copy-start.3
  0.0 1.9 %shard_map.118 = (bf16[16,72,128]{2,1,0:T(8,128)(2,1)S(1)}, f32[256,256]{1,0:T(8,128)S(1)}) custom-call(bf16[256,256]{1,0:T(8,128)(2,1)} %refs_0_.1, f32[1,256]{1,0:T(1,128)} %bitcast.6, bf16[256,768]{1,0:T(8,128)(2,1)} %refs_2_.1, f32[3,768]{1,0:T(4,128)} %refs_3_.1, f32[256,256]{1,0:T(8,128)} %refs_4_.1, f32[128,256]{1,0:T(8,128)} %refs_5_.1, f32[1,256]{1,0:T(1,128)} %bitcast.7), custom_call_target="tpu_custom_call" | custom-call | flops 100663296 | bytes 1500000 | tf_op jit(solution)/shard_map/pallas_call | solution.py:24
  2.0 0.0 copy-start.1
  2.0 17.9 %all_to_all.10.packed_ref = bf16[16,72,128]{2,1,0:T(8,128)(2,1)S(1)} all-to-all(bf16[16,72,128]{2,1,0:T(8,128)(2,1)S(1)} %get-tuple-element.7), channel_id=1, replica_groups=mesh['groups'=2,'seq'=16] {'seq'}, dimensions={0} | all-to-all | bytes 589824 | tf_op jit(solution)/shard_map/all_to_all | solution.py:186
  19.9 0.0 copy-done.2
  19.9 0.0 copy-done.3
  19.9 0.0 copy-done.1
  19.9 0.0 copy-start.4
  19.9 0.9 %copy-done.4 = bf16[512,256]{1,0:T(8,128)(2,1)S(1)} copy-done((bf16[512,256]{1,0:T(8,128)(2,1)S(1)}, bf16[512,256]{1,0:T(8,128)(2,1)}, u32[]{:S(2)}) %copy-start.4) | copy-done | bytes 262168
  20.8 1.3 %shard_map.119 = bf16[256,256]{1,0:T(8,128)(2,1)S(1)} custom-call(bf16[16,72,128]{2,1,0:T(8,128)(2,1)S(1)} %all_to_all.10.packed_ref, bf16[512,256]{1,0:T(8,128)(2,1)S(1)} %copy-done.4, f32[512,256]{1,0:T(8,128)S(1)} %copy-done.2, bf16[512,512]{1,0:T(8,128)(2,1)S(1)} %copy-done.1, bf16[256,512]{1,0:T(8,128)(2,1)S(1)} %copy-done.3), custom_call_target="tpu_custom_call" | custom-call | flops 603979776 | bytes 2000000 | tf_op jit(solution)/shard_map/pallas_call | solution.py:24
  22.2 0.0 copy-start
  22.2 11.0 %all_to_all.11 = bf16[16,16,256]{2,1,0:T(8,128)(2,1)S(1)} all-to-all(bf16[16,16,256]{2,1,0:T(8,128)(2,1)S(1)} %bitcast.5), channel_id=1, replica_groups=mesh['groups'=2,'seq'=16] {'seq'}, dimensions={0} | all-to-all | bytes 262144 | tf_op jit(solution)/shard_map/all_to_all | solution.py:186
  33.1 0.0 copy-done
  33.1 0.9 %shard_map.120 = bf16[256,256]{1,0:T(8,128)(2,1)} custom-call(bf16[256,256]{1,0:T(8,128)(2,1)S(1)} %bitcast.4, f32[256,256]{1,0:T(8,128)S(1)} %get-tuple-element.8.query_ref, bf16[256,256]{1,0:T(8,128)(2,1)S(1)} %copy-done), custom_call_target="tpu_custom_call" | custom-call | flops 33554432 | bytes 600000 | tf_op jit(solution)/shard_map/pallas_call | solution.py:24
Async XLA Ops:
  0.0 19.9 %copy-start.2 = (f32[512,256]{1,0:T(8,128)S(1)}, f32[512,256]{1,0:T(8,128)}, u32[]{:S(2)}) copy-start(f32[512,256]{1,0:T(8,128)} %constant.9.clone.twist_ref) | copy-start | bytes 1572868
  0.0 19.9 %copy-start.3 = (bf16[256,512]{1,0:T(8,128)(2,1)S(1)}, bf16[256,512]{1,0:T(8,128)(2,1)}, u32[]{:S(2)}) copy-start(bf16[256,512]{1,0:T(8,128)(2,1)} %constant.11.clone.last_ref) | copy-start | bytes 786436
  2.0 17.9 %copy-start.1 = (bf16[512,512]{1,0:T(8,128)(2,1)S(1)}, bf16[512,512]{1,0:T(8,128)(2,1)}, u32[]{:S(2)}) copy-start(bf16[512,512]{1,0:T(8,128)(2,1)} %constant.10.clone.inner_ref) | copy-start | bytes 1572868
  19.9 1.0 %copy-start.4 = (bf16[512,256]{1,0:T(8,128)(2,1)S(1)}, bf16[512,256]{1,0:T(8,128)(2,1)}, u32[]{:S(2)}) copy-start(bf16[512,256]{1,0:T(8,128)(2,1)} %constant.8.clone.first_ref) | copy-start | bytes 786436
  22.2 11.0 %copy-start = (bf16[256,256]{1,0:T(8,128)(2,1)S(1)}, bf16[256,256]{1,0:T(8,128)(2,1)}, u32[]{:S(2)}) copy-start(bf16[256,256]{1,0:T(8,128)(2,1)} %w_ref.1) | copy-start | bytes 393220

commit v5 on v4

--- a/solution.py
+++ b/solution.py
@@ -42,7 +42,9 @@
     last = np.concatenate([cosine, -sine]).T / full_len
     offsets = np.arange(rows)
     twist = 2.0 * math.pi / (4 * full_len) * (freqs[:, None] * offsets[None, :] % (4 * full_len))
-    twist = np.repeat(np.concatenate([np.cos(twist), np.sin(twist)]), chans, axis=0)
+    twist = np.concatenate([np.cos(twist), np.sin(twist)])
+    if chans % 8:
+        twist = np.repeat(twist, chans, axis=0)
     turn = 2.0 * math.pi / rows * (offsets[:, None] * offsets[None, :] % rows)
     cosine, sine = np.cos(turn), np.sin(turn)
     inner = np.block([[cosine, -sine], [sine, cosine]])
@@ -56,65 +58,91 @@
 
 def prepare_body(*refs):
     hbm, (packed_ref, query_ref), held, sems = refs[:7], refs[7:9], refs[9:16], refs[16]
-    copies = [pltpu.make_async_copy(h, v, sems.at[i]) for i, (h, v) in enumerate(zip(hbm, held))]
-    for copy in copies:
-        copy.start()
     tokens_ref, gain_ref, w_ref, short_ref, long_ref, medium_ref, skip_ref = held
     rows, width = tokens_ref.shape
-    copies[0].wait()
-    copies[1].wait()
+    is_first = lax.axis_index("seq") == 0
+    parts = [slice(part * width, (part + 1) * width) for part in range(3)]
+
+    def copy_of(index, cols=None, sem=None):
+        source, target = hbm[index], held[index]
+        if cols is not None:
+            source, target = source.at[:, cols], target.at[:, cols]
+        return pltpu.make_async_copy(source, target, sems.at[index if sem is None else sem])
+
+    tokens_copy, gain_copy, short_copy, long_copy = (copy_of(index) for index in (0, 1, 3, 4))
+    medium_copy, skip_copy = copy_of(5), copy_of(6)
+    w_copies = [copy_of(2, cols, 6 + part if part else 2) for part, cols in enumerate(parts)]
+    for copy in (tokens_copy, gain_copy, w_copies[1], w_copies[2], short_copy, long_copy, w_copies[0]):
+        copy.start()
+
+    @pl.when(is_first)
+    def _():
+        medium_copy.start()
+        skip_copy.start()
+
+    tokens_copy.wait()
+    gain_copy.wait()
     inputs = tokens_ref[...].astype(jnp.float32)
     mean_sq = jnp.mean(inputs * inputs, axis=-1, keepdims=True)
     normed = (inputs * lax.rsqrt(mean_sq + epsilon) * gain_ref[...]).astype(jnp.bfloat16)
-    copies[2].wait()
-    projected = jnp.dot(normed, w_ref[...], preferred_element_type=jnp.float32)
-    projected = projected.astype(jnp.bfloat16).astype(jnp.float32)
-    projected = jnp.concatenate([projected, jnp.zeros((edge, 3 * width), jnp.float32)])
-    copies[3].wait()
     taps_count = short_ref.shape[0]
 
     def mixed(part):
-        cols = slice(part * width, (part + 1) * width)
-        acc = short_ref[0:1, cols] * projected[:, cols]
+        w_copies[part].wait()
+        cols = parts[part]
+        projected = jnp.dot(normed, w_ref[:, cols], preferred_element_type=jnp.float32)
+        projected = projected.astype(jnp.bfloat16).astype(jnp.float32)
+        projected = jnp.concatenate([projected, jnp.zeros((edge, width), jnp.float32)])
+        acc = short_ref[0:1, cols] * projected
         for tap_num in range(1, taps_count):
-            acc = acc + short_ref[tap_num : tap_num + 1, cols] * pltpu.roll(projected[:, cols], tap_num, 0)
+            acc = acc + short_ref[tap_num : tap_num + 1, cols] * pltpu.roll(projected, tap_num, 0)
         return acc
 
-    query, key, value = mixed(0), mixed(1), mixed(2)
+    short_copy.wait()
+    key, value = mixed(1), mixed(2)
+    put_columns(packed_ref, 0, (key[0:rows] * value[0:rows]).astype(jnp.bfloat16).T)
+    long_copy.wait()
+
+    @pl.when(is_first)
+    def _():
+        medium_copy.wait()
+        skip_copy.wait()
+        med_len = medium_ref.shape[0]
+        head_row = lax.broadcasted_iota(jnp.int32, medium_ref.shape, 0)
+        direct = jnp.where(head_row == 0, skip_ref[...], 0.0)
+        long_ref[0:med_len, :] = long_ref[0:med_len, :] + medium_ref[...] + direct
+
+    put_columns(packed_ref, rows, long_ref[...].astype(jnp.bfloat16).T)
+    query = mixed(0)
     row = lax.broadcasted_iota(jnp.int32, (rows, width), 0)
     query_ref[...] = jnp.where(row < taps_count - 1, 1.0, query[0:rows])
-    signal = (key[0:rows] * value[0:rows]).astype(jnp.bfloat16).T
     rims = []
     for part in (key, value, query):
         rims += [part[0:edge], part[rows:]]
     rims.append(jnp.zeros((lane - 3 * rim_step, width), jnp.float32))
-    rim = jnp.concatenate(rims).T
-    for copy in copies[4:]:
-        copy.wait()
-    med_len = medium_ref.shape[0]
-    is_first = jnp.where(lax.axis_index("seq") == 0, 1.0, 0.0)
-    head = long_ref[0:med_len, :] + is_first * medium_ref[...]
-    head_row = lax.broadcasted_iota(jnp.int32, head.shape, 0)
-    head = head + jnp.where(head_row == 0, is_first * skip_ref[...], 0.0)
-    taps = jnp.concatenate([head, long_ref[med_len:, :]]).astype(jnp.bfloat16).T
-    put_blocks(packed_ref, signal, taps, rim)
-
-
-def put_blocks(packed_ref, signal, taps, rim):
+    put_rim(packed_ref, 2 * rows, jnp.concatenate(rims).T)
+
+
+def put_columns(packed_ref, begin, values):
+    if len(packed_ref.shape) == 2:
+        packed_ref[:, begin : begin + values.shape[1]] = values
+        return
     devices = packed_ref.shape[0]
-    chans = signal.shape[0] // devices
-    if chans % 16:
-        packed_ref[...] = jnp.concatenate([signal, taps, rim.astype(jnp.bfloat16)], axis=1)
+    values = values.reshape(devices, -1, values.shape[1])
+    chans = values.shape[1]
+    for column in range(values.shape[2] // lane):
+        place = (begin // lane + column) * chans
+        packed_ref[:, place : place + chans, :] = values[:, :, column * lane : (column + 1) * lane]
+
+
+def put_rim(packed_ref, begin, rim):
+    if len(packed_ref.shape) == 2:
+        packed_ref[:, begin:] = rim.astype(jnp.bfloat16)
         return
-    begin = 0
-    for part in (signal, taps):
-        part = part.reshape(devices, chans, -1)
-        for column in range(part.shape[2] // lane):
-            packed_ref[:, begin : begin + chans, :] = part[:, :, column * lane : (column + 1) * lane]
-            begin += chans
-    rim = rim.reshape(devices, chans, lane)
+    rim = rim.reshape(packed_ref.shape[0], -1, lane)
+    chans = rim.shape[1]
     both = rim[:, : chans // 2] + pltpu.roll(rim[:, chans // 2 :], lane // 2, 2)
-    packed_ref[:, begin:, :] = both.astype(jnp.bfloat16)
+    packed_ref[:, begin // lane * chans :, :] = both.astype(jnp.bfloat16)
 
 
 def take_blocks(packed_ref, chans, rows):
@@ -130,9 +158,20 @@
     return jnp.concatenate(columns, axis=1), rim
 
 
+def twist_rows(twist_ref, chans):
+    half, rows = twist_ref.shape[0] // 2, twist_ref.shape[1]
+    tables = twist_ref[0:half, :], twist_ref[half:, :]
+    if chans % 8:
+        return tables
+    return tuple(
+        jnp.broadcast_to(table[:, None, :], (half, chans, rows)).reshape(half * chans, rows)
+        for table in tables
+    )
+
+
 def convolve_body(chans, rim_count, packed_ref, first_ref, twist_ref, inner_ref, last_ref, out_ref):
-    half = twist_ref.shape[0] // 2
     rows = twist_ref.shape[1]
+    half = first_ref.shape[0] // 2
     values, rim = take_blocks(packed_ref, chans, rows)
     before = jnp.concatenate([jnp.zeros((chans, lane), jnp.float32), rim[:-chans]])
     rim = rim + pltpu.roll(before, lane - edge, 1)
@@ -143,7 +182,7 @@
         [jnp.where(in_rim, rim_signal, values[:, 0:lane]), values[:, lane:]], axis=1
     )
     spread = jnp.dot(first_ref[...], values, preferred_element_type=jnp.float32)
-    tw_cos, tw_sin = twist_ref[0:half, :], twist_ref[half:, :]
+    tw_cos, tw_sin = twist_rows(twist_ref, chans)
     turned = []
     for begin in (0, rows):
         real, imag = spread[0:half, begin : begin + rows], spread[half:, begin : begin + rows]
@@ -196,7 +235,7 @@
         args,
         [pltpu.HBM] * len(args),
         [pltpu.VMEM(arg.shape, arg.dtype) for arg in args]
-        + [pltpu.SemaphoreType.DMA((len(args),))],
+        + [pltpu.SemaphoreType.DMA((len(args) + 2,))],
         flops=2 * rows * width * 3 * width,
         moved=1_500_000,
     )

time: 34.3 us -> 33.6 us (0.980)
  local copies, waits for them, and re-layouts: 0.97 us -> 0.03 us
  Pallas kernels: 4.15 us -> 4.5 us
    unnamed x10, local copies, waits for them, and re-layouts: 0.97 us -> 0.03 us
    pallas_call x3, Pallas kernels: 4.15 us -> 4.5 us  [call(): pl.pallas_call(body, out_shape=outs, in_specs=[whole(space) for space in...]
where the time goes in v5:
time: 33.6 us; the launch traced here: 33.4 us
  blocking collectives  28.9 us (86%)
  Pallas kernels  4.5 us (13%)
    all_to_all x2, blocking collectives, swap(): lax.all_to_all(pieces, 'seq', split_axis=0, concat_axis=0)  28.9 us
    pallas_call x3, Pallas kernels, call(): pl.pallas_call(body, out_shape=outs, in_specs=[whole(space) for space in...  4.5 us

profile of v5, /device:TPU:0, one launch (start us, length us, event | category | flops | bytes accessed | tf_op | source)
XLA Modules:
  0.0 33.4 jit_solution(6730811654001249302)
XLA Ops:
  0.0 0.0 copy-start.2
  0.0 0.0 copy-start.3
  0.0 2.3 %shard_map.118 = (bf16[16,72,128]{2,1,0:T(8,128)(2,1)S(1)}, f32[256,256]{1,0:T(8,128)S(1)}) custom-call(bf16[256,256]{1,0:T(8,128)(2,1)} %refs_0_.1, f32[1,256]{1,0:T(1,128)} %bitcast.6, bf16[256,768]{1,0:T(8,128)(2,1)} %refs_2_.1, f32[3,768]{1,0:T(4,128)} %refs_3_.1, f32[256,256]{1,0:T(8,128)} %refs_4_.1, f32[128,256]{1,0:T(8,128)} %refs_5_.1, f32[1,256]{1,0:T(1,128)} %bitcast.7), custom_call_target="tpu_custom_call" | custom-call | flops 100663296 | bytes 1500000 | tf_op jit(solution)/shard_map/pallas_call | solution.py:24
  2.3 0.0 copy-start.1
  2.3 0.0 copy-start.4
  2.3 17.9 %all_to_all.10.packed_ref = bf16[16,72,128]{2,1,0:T(8,128)(2,1)S(1)} all-to-all(bf16[16,72,128]{2,1,0:T(8,128)(2,1)S(1)} %get-tuple-element.7), channel_id=1, replica_groups=mesh['groups'=2,'seq'=16] {'seq'}, dimensions={0} | all-to-all | bytes 589824 | tf_op jit(solution)/shard_map/all_to_all | solution.py:225
  20.2 0.0 copy-done.2
  20.2 0.0 copy-done.3
  20.2 0.0 copy-done.1
  20.2 0.0 copy-done.4
  20.2 1.3 %shard_map.119 = bf16[256,256]{1,0:T(8,128)(2,1)S(1)} custom-call(bf16[16,72,128]{2,1,0:T(8,128)(2,1)S(1)} %all_to_all.10.packed_ref, bf16[512,256]{1,0:T(8,128)(2,1)S(1)} %copy-done.3, f32[32,256]{1,0:T(8,128)S(1)} %copy-done.4, bf16[512,512]{1,0:T(8,128)(2,1)S(1)} %copy-done.1, bf16[256,512]{1,0:T(8,128)(2,1)S(1)} %copy-done.2), custom_call_target="tpu_custom_call" | custom-call | flops 603979776 | bytes 2000000 | tf_op jit(solution)/shard_map/pallas_call | solution.py:24
  21.6 0.0 copy-start
  21.6 11.0 %all_to_all.11 = bf16[16,16,256]{2,1,0:T(8,128)(2,1)S(1)} all-to-all(bf16[16,16,256]{2,1,0:T(8,128)(2,1)S(1)} %bitcast.5), channel_id=1, replica_groups=mesh['groups'=2,'seq'=16] {'seq'}, dimensions={0} | all-to-all | bytes 262144 | tf_op jit(solution)/shard_map/all_to_all | solution.py:225
  32.5 0.0 copy-done
  32.5 0.9 %shard_map.120 = bf16[256,256]{1,0:T(8,128)(2,1)} custom-call(bf16[256,256]{1,0:T(8,128)(2,1)S(1)} %bitcast.4, f32[256,256]{1,0:T(8,128)S(1)} %get-tuple-element.8.query_ref, bf16[256,256]{1,0:T(8,128)(2,1)S(1)} %copy-done), custom_call_target="tpu_custom_call" | custom-call | flops 33554432 | bytes 600000 | tf_op jit(solution)/shard_map/pallas_call | solution.py:24
Async XLA Ops:
  0.0 20.2 %copy-start.2 = (bf16[256,512]{1,0:T(8,128)(2,1)S(1)}, bf16[256,512]{1,0:T(8,128)(2,1)}, u32[]{:S(2)}) copy-start(bf16[256,512]{1,0:T(8,128)(2,1)} %constant.11.clone.last_ref) | copy-start | bytes 786436
  0.0 20.2 %copy-start.3 = (bf16[512,256]{1,0:T(8,128)(2,1)S(1)}, bf16[512,256]{1,0:T(8,128)(2,1)}, u32[]{:S(2)}) copy-start(bf16[512,256]{1,0:T(8,128)(2,1)} %constant.8.clone.first_ref) | copy-start | bytes 786436
  2.3 17.9 %copy-start.1 = (bf16[512,512]{1,0:T(8,128)(2,1)S(1)}, bf16[512,512]{1,0:T(8,128)(2,1)}, u32[]{:S(2)}) copy-start(bf16[512,512]{1,0:T(8,128)(2,1)} %constant.10.clone.inner_ref) | copy-start | bytes 1572868
  2.3 17.9 %copy-start.4 = (f32[32,256]{1,0:T(8,128)S(1)}, f32[32,256]{1,0:T(8,128)}, u32[]{:S(2)}) copy-start(f32[32,256]{1,0:T(8,128)} %constant.9.clone.twist_ref) | copy-start | bytes 98308
  21.6 11.0 %copy-start = (bf16[256,256]{1,0:T(8,128)(2,1)S(1)}, bf16[256,256]{1,0:T(8,128)(2,1)}, u32[]{:S(2)}) copy-start(bf16[256,256]{1,0:T(8,128)(2,1)} %w_ref.1) | copy-start | bytes 393220

commit v6 on v5

--- a/solution.py
+++ b/solution.py
@@ -60,62 +60,41 @@
     hbm, (packed_ref, query_ref), held, sems = refs[:7], refs[7:9], refs[9:16], refs[16]
     tokens_ref, gain_ref, w_ref, short_ref, long_ref, medium_ref, skip_ref = held
     rows, width = tokens_ref.shape
-    is_first = lax.axis_index("seq") == 0
-    parts = [slice(part * width, (part + 1) * width) for part in range(3)]
-
-    def copy_of(index, cols=None, sem=None):
-        source, target = hbm[index], held[index]
-        if cols is not None:
-            source, target = source.at[:, cols], target.at[:, cols]
-        return pltpu.make_async_copy(source, target, sems.at[index if sem is None else sem])
-
-    tokens_copy, gain_copy, short_copy, long_copy = (copy_of(index) for index in (0, 1, 3, 4))
-    medium_copy, skip_copy = copy_of(5), copy_of(6)
-    w_copies = [copy_of(2, cols, 6 + part if part else 2) for part, cols in enumerate(parts)]
-    for copy in (tokens_copy, gain_copy, w_copies[1], w_copies[2], short_copy, long_copy, w_copies[0]):
-        copy.start()
-
-    @pl.when(is_first)
-    def _():
-        medium_copy.start()
-        skip_copy.start()
-
-    tokens_copy.wait()
-    gain_copy.wait()
+    copies = [pltpu.make_async_copy(h, v, sems.at[i]) for i, (h, v) in enumerate(zip(hbm, held))]
+    for index in (4, 5, 6, 0, 1, 2, 3):
+        copies[index].start()
+    for copy in copies[4:]:
+        copy.wait()
+    med_len = medium_ref.shape[0]
+    is_first = jnp.where(lax.axis_index("seq") == 0, 1.0, 0.0)
+    head = long_ref[0:med_len, :] + is_first * medium_ref[...]
+    head_row = lax.broadcasted_iota(jnp.int32, head.shape, 0)
+    head = head + jnp.where(head_row == 0, is_first * skip_ref[...], 0.0)
+    taps = jnp.concatenate([head, long_ref[med_len:, :]]).astype(jnp.bfloat16)
+    put_columns(packed_ref, rows, taps.T)
+    copies[0].wait()
+    copies[1].wait()
     inputs = tokens_ref[...].astype(jnp.float32)
     mean_sq = jnp.mean(inputs * inputs, axis=-1, keepdims=True)
     normed = (inputs * lax.rsqrt(mean_sq + epsilon) * gain_ref[...]).astype(jnp.bfloat16)
+    copies[2].wait()
+    copies[3].wait()
+    projected = jnp.dot(normed, w_ref[...], preferred_element_type=jnp.float32)
+    projected = projected.astype(jnp.bfloat16).astype(jnp.float32)
+    projected = jnp.concatenate([projected, jnp.zeros((edge, 3 * width), jnp.float32)])
     taps_count = short_ref.shape[0]
 
     def mixed(part):
-        w_copies[part].wait()
-        cols = parts[part]
-        projected = jnp.dot(normed, w_ref[:, cols], preferred_element_type=jnp.float32)
-        projected = projected.astype(jnp.bfloat16).astype(jnp.float32)
-        projected = jnp.concatenate([projected, jnp.zeros((edge, width), jnp.float32)])
-        acc = short_ref[0:1, cols] * projected
+        cols = slice(part * width, (part + 1) * width)
+        acc = short_ref[0:1, cols] * projected[:, cols]
         for tap_num in range(1, taps_count):
-            acc = acc + short_ref[tap_num : tap_num + 1, cols] * pltpu.roll(projected, tap_num, 0)
+            acc = acc + short_ref[tap_num : tap_num + 1, cols] * pltpu.roll(projected[:, cols], tap_num, 0)
         return acc
 
-    short_copy.wait()
-    key, value = mixed(1), mixed(2)
-    put_columns(packed_ref, 0, (key[0:rows] * value[0:rows]).astype(jnp.bfloat16).T)
-    long_copy.wait()
-
-    @pl.when(is_first)
-    def _():
-        medium_copy.wait()
-        skip_copy.wait()
-        med_len = medium_ref.shape[0]
-        head_row = lax.broadcasted_iota(jnp.int32, medium_ref.shape, 0)
-        direct = jnp.where(head_row == 0, skip_ref[...], 0.0)
-        long_ref[0:med_len, :] = long_ref[0:med_len, :] + medium_ref[...] + direct
-
-    put_columns(packed_ref, rows, long_ref[...].astype(jnp.bfloat16).T)
-    query = mixed(0)
+    query, key, value = mixed(0), mixed(1), mixed(2)
     row = lax.broadcasted_iota(jnp.int32, (rows, width), 0)
     query_ref[...] = jnp.where(row < taps_count - 1, 1.0, query[0:rows])
+    put_columns(packed_ref, 0, (key[0:rows] * value[0:rows]).astype(jnp.bfloat16).T)
     rims = []
     for part in (key, value, query):
         rims += [part[0:edge], part[rows:]]
@@ -181,22 +160,31 @@
     values = jnp.concatenate(
         [jnp.where(in_rim, rim_signal, values[:, 0:lane]), values[:, lane:]], axis=1
     )
-    spread = jnp.dot(first_ref[...], values, preferred_element_type=jnp.float32)
     tw_cos, tw_sin = twist_rows(twist_ref, chans)
-    turned = []
-    for begin in (0, rows):
-        real, imag = spread[0:half, begin : begin + rows], spread[half:, begin : begin + rows]
-        turned.append([real * tw_cos + imag * tw_sin, imag * tw_cos - real * tw_sin])
-    turned = jnp.concatenate([jnp.concatenate(pair, axis=1).astype(jnp.bfloat16) for pair in turned])
-    spectra = jnp.dot(turned, inner_ref[...], preferred_element_type=jnp.float32)
-    real, imag = spectra[0:half, 0:rows], spectra[0:half, rows:]
-    fil_re, fil_im = spectra[half:, 0:rows], spectra[half:, rows:]
-    product = [real * fil_im + imag * fil_re, real * fil_re - imag * fil_im]
-    product = jnp.concatenate(product, axis=1).astype(jnp.bfloat16)
-    back = jnp.dot(product, inner_ref[...], preferred_element_type=jnp.float32)
-    imag, real = back[:, 0:rows], back[:, rows:]
-    turned = jnp.concatenate([real * tw_cos - imag * tw_sin, imag * tw_cos + real * tw_sin])
-    conv = jnp.dot(last_ref[...], turned.astype(jnp.bfloat16), preferred_element_type=jnp.float32)
+    span = half // 2
+    conv = 0.0
+    for begin in range(0, half, span):
+        own, other = slice(begin, begin + span), slice(half + begin, half + begin + span)
+        table = jnp.concatenate([first_ref[own, :], first_ref[other, :]])
+        spread = jnp.dot(table, values, preferred_element_type=jnp.float32)
+        cosine, sine = tw_cos[own], tw_sin[own]
+        turned = []
+        for cols in (slice(0, rows), slice(rows, 2 * rows)):
+            real, imag = spread[0:span, cols], spread[span:, cols]
+            pair = [real * cosine + imag * sine, imag * cosine - real * sine]
+            turned.append(jnp.concatenate(pair, axis=1).astype(jnp.bfloat16))
+        spectra = jnp.dot(
+            jnp.concatenate(turned), inner_ref[...], preferred_element_type=jnp.float32
+        )
+        real, imag = spectra[0:span, 0:rows], spectra[0:span, rows:]
+        fil_re, fil_im = spectra[span:, 0:rows], spectra[span:, rows:]
+        product = [real * fil_im + imag * fil_re, real * fil_re - imag * fil_im]
+        product = jnp.concatenate(product, axis=1).astype(jnp.bfloat16)
+        back = jnp.dot(product, inner_ref[...], preferred_element_type=jnp.float32)
+        imag, real = back[:, 0:rows], back[:, rows:]
+        turned = jnp.concatenate([real * cosine - imag * sine, imag * cosine + real * sine])
+        table = jnp.concatenate([last_ref[:, own], last_ref[:, other]], axis=1)
+        conv = conv + jnp.dot(table, turned.astype(jnp.bfloat16), preferred_element_type=jnp.float32)
     out_ref[:, 0:lane] = (conv[:, 0:lane] * rim_query).astype(jnp.bfloat16)
     out_ref[:, lane:] = conv[:, lane:].astype(jnp.bfloat16)
 
@@ -235,7 +223,7 @@
         args,
         [pltpu.HBM] * len(args),
         [pltpu.VMEM(arg.shape, arg.dtype) for arg in args]
-        + [pltpu.SemaphoreType.DMA((len(args) + 2,))],
+        + [pltpu.SemaphoreType.DMA((len(args),))],
         flops=2 * rows * width * 3 * width,
         moved=1_500_000,
     )

time: 33.6 us -> 33.8 us (level)
  no operation moved by 1% of the time
where the time goes in v6:
time: 33.8 us; the launch traced here: 33.5 us
  blocking collectives  28.9 us (86%)
  Pallas kernels  4.58 us (14%)
    all_to_all x2, blocking collectives, swap(): lax.all_to_all(pieces, 'seq', split_axis=0, concat_axis=0)  28.9 us
    pallas_call x3, Pallas kernels, call(): pl.pallas_call(body, out_shape=outs, in_specs=[whole(space) for space in...  4.58 us

profile of v6, /device:TPU:0, one launch (start us, length us, event | category | flops | bytes accessed | tf_op | source)
XLA Modules:
  0.0 33.5 jit_solution(1380289775947815509)
XLA Ops:
  0.0 0.0 copy-start.2
  0.0 0.0 copy-start.3
  0.0 2.0 %shard_map.118 = (bf16[16,72,128]{2,1,0:T(8,128)(2,1)S(1)}, f32[256,256]{1,0:T(8,128)S(1)}) custom-call(bf16[256,256]{1,0:T(8,128)(2,1)} %refs_0_.1, f32[1,256]{1,0:T(1,128)} %bitcast.6, bf16[256,768]{1,0:T(8,128)(2,1)} %refs_2_.1, f32[3,768]{1,0:T(4,128)} %refs_3_.1, f32[256,256]{1,0:T(8,128)} %refs_4_.1, f32[128,256]{1,0:T(8,128)} %refs_5_.1, f32[1,256]{1,0:T(1,128)} %bitcast.7), custom_call_target="tpu_custom_call" | custom-call | flops 100663296 | bytes 1500000 | tf_op jit(solution)/shard_map/pallas_call | solution.py:24
  2.0 0.0 copy-start.1
  2.1 0.0 copy-start.4
  2.1 17.9 %all_to_all.10.packed_ref = bf16[16,72,128]{2,1,0:T(8,128)(2,1)S(1)} all-to-all(bf16[16,72,128]{2,1,0:T(8,128)(2,1)S(1)} %get-tuple-element.7), channel_id=1, replica_groups=mesh['groups'=2,'seq'=16] {'seq'}, dimensions={0} | all-to-all | bytes 589824 | tf_op jit(solution)/shard_map/all_to_all | solution.py:213
  20.0 0.0 copy-done.2
  20.0 0.0 copy-done.3
  20.0 0.0 copy-done.1
  20.0 0.0 copy-done.4
  20.0 1.7 %shard_map.119 = bf16[256,256]{1,0:T(8,128)(2,1)S(1)} custom-call(bf16[16,72,128]{2,1,0:T(8,128)(2,1)S(1)} %all_to_all.10.packed_ref, bf16[512,256]{1,0:T(8,128)(2,1)S(1)} %copy-done.3, f32[32,256]{1,0:T(8,128)S(1)} %copy-done.4, bf16[512,512]{1,0:T(8,128)(2,1)S(1)} %copy-done.1, bf16[256,512]{1,0:T(8,128)(2,1)S(1)} %copy-done.2), custom_call_target="tpu_custom_call" | custom-call | flops 603979776 | bytes 2000000 | tf_op jit(solution)/shard_map/pallas_call | solution.py:24
  21.7 0.0 copy-start
  21.7 11.0 %all_to_all.11 = bf16[16,16,256]{2,1,0:T(8,128)(2,1)S(1)} all-to-all(bf16[16,16,256]{2,1,0:T(8,128)(2,1)S(1)} %bitcast.5), channel_id=1, replica_groups=mesh['groups'=2,'seq'=16] {'seq'}, dimensions={0} | all-to-all | bytes 262144 | tf_op jit(solution)/shard_map/all_to_all | solution.py:213
  32.7 0.0 copy-done
  32.7 0.9 %shard_map.120 = bf16[256,256]{1,0:T(8,128)(2,1)} custom-call(bf16[256,256]{1,0:T(8,128)(2,1)S(1)} %bitcast.4, f32[256,256]{1,0:T(8,128)S(1)} %get-tuple-element.8.query_ref, bf16[256,256]{1,0:T(8,128)(2,1)S(1)} %copy-done), custom_call_target="tpu_custom_call" | custom-call | flops 33554432 | bytes 600000 | tf_op jit(solution)/shard_map/pallas_call | solution.py:24
Async XLA Ops:
  0.0 20.0 %copy-start.2 = (bf16[256,512]{1,0:T(8,128)(2,1)S(1)}, bf16[256,512]{1,0:T(8,128)(2,1)}, u32[]{:S(2)}) copy-start(bf16[256,512]{1,0:T(8,128)(2,1)} %constant.11.clone.last_ref) | copy-start | bytes 786436
  0.0 20.0 %copy-start.3 = (bf16[512,256]{1,0:T(8,128)(2,1)S(1)}, bf16[512,256]{1,0:T(8,128)(2,1)}, u32[]{:S(2)}) copy-start(bf16[512,256]{1,0:T(8,128)(2,1)} %constant.8.clone.first_ref) | copy-start | bytes 786436
  2.0 17.9 %copy-start.1 = (bf16[512,512]{1,0:T(8,128)(2,1)S(1)}, bf16[512,512]{1,0:T(8,128)(2,1)}, u32[]{:S(2)}) copy-start(bf16[512,512]{1,0:T(8,128)(2,1)} %constant.10.clone.inner_ref) | copy-start | bytes 1572868
  2.1 17.9 %copy-start.4 = (f32[32,256]{1,0:T(8,128)S(1)}, f32[32,256]{1,0:T(8,128)}, u32[]{:S(2)}) copy-start(f32[32,256]{1,0:T(8,128)} %constant.9.clone.twist_ref) | copy-start | bytes 98308
  21.7 11.0 %copy-start = (bf16[256,256]{1,0:T(8,128)(2,1)S(1)}, bf16[256,256]{1,0:T(8,128)(2,1)}, u32[]{:S(2)}) copy-start(bf16[256,256]{1,0:T(8,128)(2,1)} %w_ref.1) | copy-start | bytes 393220

commit v7 on v4

--- a/solution.py
+++ b/solution.py
@@ -42,7 +42,9 @@
     last = np.concatenate([cosine, -sine]).T / full_len
     offsets = np.arange(rows)
     twist = 2.0 * math.pi / (4 * full_len) * (freqs[:, None] * offsets[None, :] % (4 * full_len))
-    twist = np.repeat(np.concatenate([np.cos(twist), np.sin(twist)]), chans, axis=0)
+    twist = np.concatenate([np.cos(twist), np.sin(twist)])
+    if chans % 8:
+        twist = np.repeat(twist, chans, axis=0)
     turn = 2.0 * math.pi / rows * (offsets[:, None] * offsets[None, :] % rows)
     cosine, sine = np.cos(turn), np.sin(turn)
     inner = np.block([[cosine, -sine], [sine, cosine]])
@@ -56,21 +58,21 @@
 
 def prepare_body(*refs):
     hbm, (packed_ref, query_ref), held, sems = refs[:7], refs[7:9], refs[9:16], refs[16]
+    tokens_ref, gain_ref, w_ref, short_ref, long_ref, medium_ref, skip_ref = held
+    rows, width = tokens_ref.shape
     copies = [pltpu.make_async_copy(h, v, sems.at[i]) for i, (h, v) in enumerate(zip(hbm, held))]
     for copy in copies:
         copy.start()
-    tokens_ref, gain_ref, w_ref, short_ref, long_ref, medium_ref, skip_ref = held
-    rows, width = tokens_ref.shape
     copies[0].wait()
     copies[1].wait()
     inputs = tokens_ref[...].astype(jnp.float32)
     mean_sq = jnp.mean(inputs * inputs, axis=-1, keepdims=True)
     normed = (inputs * lax.rsqrt(mean_sq + epsilon) * gain_ref[...]).astype(jnp.bfloat16)
     copies[2].wait()
+    copies[3].wait()
     projected = jnp.dot(normed, w_ref[...], preferred_element_type=jnp.float32)
     projected = projected.astype(jnp.bfloat16).astype(jnp.float32)
     projected = jnp.concatenate([projected, jnp.zeros((edge, 3 * width), jnp.float32)])
-    copies[3].wait()
     taps_count = short_ref.shape[0]
 
     def mixed(part):
@@ -83,12 +85,12 @@
     query, key, value = mixed(0), mixed(1), mixed(2)
     row = lax.broadcasted_iota(jnp.int32, (rows, width), 0)
     query_ref[...] = jnp.where(row < taps_count - 1, 1.0, query[0:rows])
-    signal = (key[0:rows] * value[0:rows]).astype(jnp.bfloat16).T
+    put_columns(packed_ref, 0, (key[0:rows] * value[0:rows]).astype(jnp.bfloat16).T)
     rims = []
     for part in (key, value, query):
         rims += [part[0:edge], part[rows:]]
     rims.append(jnp.zeros((lane - 3 * rim_step, width), jnp.float32))
-    rim = jnp.concatenate(rims).T
+    put_rim(packed_ref, 2 * rows, jnp.concatenate(rims).T)
     for copy in copies[4:]:
         copy.wait()
     med_len = medium_ref.shape[0]
@@ -96,25 +98,30 @@
     head = long_ref[0:med_len, :] + is_first * medium_ref[...]
     head_row = lax.broadcasted_iota(jnp.int32, head.shape, 0)
     head = head + jnp.where(head_row == 0, is_first * skip_ref[...], 0.0)
-    taps = jnp.concatenate([head, long_ref[med_len:, :]]).astype(jnp.bfloat16).T
-    put_blocks(packed_ref, signal, taps, rim)
-
-
-def put_blocks(packed_ref, signal, taps, rim):
+    taps = jnp.concatenate([head, long_ref[med_len:, :]]).astype(jnp.bfloat16)
+    put_columns(packed_ref, rows, taps.T)
+
+
+def put_columns(packed_ref, begin, values):
+    if len(packed_ref.shape) == 2:
+        packed_ref[:, begin : begin + values.shape[1]] = values
+        return
     devices = packed_ref.shape[0]
-    chans = signal.shape[0] // devices
-    if chans % 16:
-        packed_ref[...] = jnp.concatenate([signal, taps, rim.astype(jnp.bfloat16)], axis=1)
+    values = values.reshape(devices, -1, values.shape[1])
+    chans = values.shape[1]
+    for column in range(values.shape[2] // lane):
+        place = (begin // lane + column) * chans
+        packed_ref[:, place : place + chans, :] = values[:, :, column * lane : (column + 1) * lane]
+
+
+def put_rim(packed_ref, begin, rim):
+    if len(packed_ref.shape) == 2:
+        packed_ref[:, begin:] = rim.astype(jnp.bfloat16)
         return
-    begin = 0
-    for part in (signal, taps):
-        part = part.reshape(devices, chans, -1)
-        for column in range(part.shape[2] // lane):
-            packed_ref[:, begin : begin + chans, :] = part[:, :, column * lane : (column + 1) * lane]
-            begin += chans
-    rim = rim.reshape(devices, chans, lane)
+    rim = rim.reshape(packed_ref.shape[0], -1, lane)
+    chans = rim.shape[1]
     both = rim[:, : chans // 2] + pltpu.roll(rim[:, chans // 2 :], lane // 2, 2)
-    packed_ref[:, begin:, :] = both.astype(jnp.bfloat16)
+    packed_ref[:, begin // lane * chans :, :] = both.astype(jnp.bfloat16)
 
 
 def take_blocks(packed_ref, chans, rows):
@@ -130,9 +137,20 @@
     return jnp.concatenate(columns, axis=1), rim
 
 
+def twist_rows(twist_ref, chans):
+    half, rows = twist_ref.shape[0] // 2, twist_ref.shape[1]
+    tables = twist_ref[0:half, :], twist_ref[half:, :]
+    if chans % 8:
+        return tables
+    return tuple(
+        jnp.broadcast_to(table[:, None, :], (half, chans, rows)).reshape(half * chans, rows)
+        for table in tables
+    )
+
+
 def convolve_body(chans, rim_count, packed_ref, first_ref, twist_ref, inner_ref, last_ref, out_ref):
-    half = twist_ref.shape[0] // 2
     rows = twist_ref.shape[1]
+    half = first_ref.shape[0] // 2
     values, rim = take_blocks(packed_ref, chans, rows)
     before = jnp.concatenate([jnp.zeros((chans, lane), jnp.float32), rim[:-chans]])
     rim = rim + pltpu.roll(before, lane - edge, 1)
@@ -143,7 +161,7 @@
         [jnp.where(in_rim, rim_signal, values[:, 0:lane]), values[:, lane:]], axis=1
     )
     spread = jnp.dot(first_ref[...], values, preferred_element_type=jnp.float32)
-    tw_cos, tw_sin = twist_ref[0:half, :], twist_ref[half:, :]
+    tw_cos, tw_sin = twist_rows(twist_ref, chans)
     turned = []
     for begin in (0, rows):
         real, imag = spread[0:half, begin : begin + rows], spread[half:, begin : begin + rows]
@@ -200,10 +218,11 @@
         flops=2 * rows * width * 3 * width,
         moved=1_500_000,
     )
+    packed, tables = lax.optimization_barrier((packed, (first, twist, inner, last)))
     conv = call(
         functools.partial(convolve_body, chans, short_filter.shape[0] - 1),
         jax.ShapeDtypeStruct((width, rows), jnp.bfloat16),
-        (swap(packed), first, twist, inner, last),
+        (swap(packed), *tables),
         [pltpu.VMEM] * 5,
         flops=18 * first.shape[0] * width * rows,
         moved=2_000_000,

time: 34.3 us -> 33.4 us (0.974)
  local copies, waits for them, and re-layouts: 0.97 us -> 0.03 us
    unnamed x10, local copies, waits for them, and re-layouts: 0.97 us -> 0.03 us
where the time goes in v7:
time: 33.4 us; the launch traced here: 33.1 us
  blocking collectives  28.9 us (87%)
  Pallas kernels  4.2 us (13%)
    all_to_all x2, blocking collectives, swap(): lax.all_to_all(pieces, 'seq', split_axis=0, concat_axis=0)  28.9 us
    pallas_call x3, Pallas kernels, call(): pl.pallas_call(body, out_shape=outs, in_specs=[whole(space) for space in...  4.2 us

profile of v7, /device:TPU:0, one launch (start us, length us, event | category | flops | bytes accessed | tf_op | source)
XLA Modules:
  0.0 33.1 jit_solution(14288064405590367554)
XLA Ops:
  0.0 0.0 copy-start.2
  0.0 0.0 copy-start.3
  0.0 2.0 %shard_map.118 = (bf16[16,72,128]{2,1,0:T(8,128)(2,1)S(1)}, f32[256,256]{1,0:T(8,128)S(1)}) custom-call(bf16[256,256]{1,0:T(8,128)(2,1)} %refs_0_.1, f32[1,256]{1,0:T(1,128)} %bitcast.6, bf16[256,768]{1,0:T(8,128)(2,1)} %refs_2_.1, f32[3,768]{1,0:T(4,128)} %refs_3_.1, f32[256,256]{1,0:T(8,128)} %refs_4_.1, f32[128,256]{1,0:T(8,128)} %refs_5_.1, f32[1,256]{1,0:T(1,128)} %bitcast.7), custom_call_target="tpu_custom_call" | custom-call | flops 100663296 | bytes 1500000 | tf_op jit(solution)/shard_map/pallas_call | solution.py:24
  2.0 0.0 copy-start.1
  2.0 0.0 copy-start.4
  2.0 17.9 %all_to_all.10.packed_ref = bf16[16,72,128]{2,1,0:T(8,128)(2,1)S(1)} all-to-all(bf16[16,72,128]{2,1,0:T(8,128)(2,1)S(1)} %get-tuple-element.13), channel_id=1, replica_groups=mesh['groups'=2,'seq'=16] {'seq'}, dimensions={0} | all-to-all | bytes 589824 | tf_op jit(solution)/shard_map/all_to_all | solution.py:204
  19.9 0.0 copy-done.2
  19.9 0.0 copy-done.3
  19.9 0.0 copy-done.1
  19.9 0.0 copy-done.4
  19.9 1.3 %shard_map.119 = bf16[256,256]{1,0:T(8,128)(2,1)S(1)} custom-call(bf16[16,72,128]{2,1,0:T(8,128)(2,1)S(1)} %all_to_all.10.packed_ref, bf16[512,256]{1,0:T(8,128)(2,1)S(1)} %copy-done.3, f32[32,256]{1,0:T(8,128)S(1)} %copy-done.4, bf16[512,512]{1,0:T(8,128)(2,1)S(1)} %copy-done.1, bf16[256,512]{1,0:T(8,128)(2,1)S(1)} %copy-done.2), custom_call_target="tpu_custom_call" | custom-call | flops 603979776 | bytes 2000000 | tf_op jit(solution)/shard_map/pallas_call | solution.py:24
  21.3 0.0 copy-start
  21.3 11.0 %all_to_all.11 = bf16[16,16,256]{2,1,0:T(8,128)(2,1)S(1)} all-to-all(bf16[16,16,256]{2,1,0:T(8,128)(2,1)S(1)} %bitcast.5), channel_id=1, replica_groups=mesh['groups'=2,'seq'=16] {'seq'}, dimensions={0} | all-to-all | bytes 262144 | tf_op jit(solution)/shard_map/all_to_all | solution.py:204
  32.3 0.0 copy-done
  32.3 0.9 %shard_map.120 = bf16[256,256]{1,0:T(8,128)(2,1)} custom-call(bf16[256,256]{1,0:T(8,128)(2,1)S(1)} %bitcast.4, f32[256,256]{1,0:T(8,128)S(1)} %get-tuple-element.18.query_ref, bf16[256,256]{1,0:T(8,128)(2,1)S(1)} %copy-done), custom_call_target="tpu_custom_call" | custom-call | flops 33554432 | bytes 600000 | tf_op jit(solution)/shard_map/pallas_call | solution.py:24
Async XLA Ops:
  0.0 19.9 %copy-start.2 = (bf16[256,512]{1,0:T(8,128)(2,1)S(1)}, bf16[256,512]{1,0:T(8,128)(2,1)}, u32[]{:S(2)}) copy-start(bf16[256,512]{1,0:T(8,128)(2,1)} %constant.11.clone.last_ref) | copy-start | bytes 786436
  0.0 19.9 %copy-start.3 = (bf16[512,256]{1,0:T(8,128)(2,1)S(1)}, bf16[512,256]{1,0:T(8,128)(2,1)}, u32[]{:S(2)}) copy-start(bf16[512,256]{1,0:T(8,128)(2,1)} %constant.8.clone.first_ref) | copy-start | bytes 786436
  2.0 17.9 %copy-start.1 = (bf16[512,512]{1,0:T(8,128)(2,1)S(1)}, bf16[512,512]{1,0:T(8,128)(2,1)}, u32[]{:S(2)}) copy-start(bf16[512,512]{1,0:T(8,128)(2,1)} %constant.10.clone.inner_ref) | copy-start | bytes 1572868
  2.0 17.9 %copy-start.4 = (f32[32,256]{1,0:T(8,128)S(1)}, f32[32,256]{1,0:T(8,128)}, u32[]{:S(2)}) copy-start(f32[32,256]{1,0:T(8,128)} %constant.9.clone.twist_ref) | copy-start | bytes 98308
  21.3 11.0 %copy-start = (bf16[256,256]{1,0:T(8,128)(2,1)S(1)}, bf16[256,256]{1,0:T(8,128)(2,1)}, u32[]{:S(2)}) copy-start(bf16[256,256]{1,0:T(8,128)(2,1)} %w_ref.1) | copy-start | bytes 393220

commit v8 on v7

--- a/solution.py
+++ b/solution.py
@@ -39,20 +39,17 @@
     angle = 2.0 * math.pi / (4 * devices) * (freqs[:, None] * np.arange(devices)[None, :] % (4 * devices))
     cosine, sine = np.kron(np.cos(angle), eye), np.kron(np.sin(angle), eye)
     first = np.concatenate([cosine, -sine])
-    last = np.concatenate([cosine, -sine]).T / full_len
     offsets = np.arange(rows)
     twist = 2.0 * math.pi / (4 * full_len) * (freqs[:, None] * offsets[None, :] % (4 * full_len))
     twist = np.concatenate([np.cos(twist), np.sin(twist)])
     if chans % 8:
         twist = np.repeat(twist, chans, axis=0)
     turn = 2.0 * math.pi / rows * (offsets[:, None] * offsets[None, :] % rows)
-    cosine, sine = np.cos(turn), np.sin(turn)
-    inner = np.block([[cosine, -sine], [sine, cosine]])
+    inner = np.concatenate([np.cos(turn), np.sin(turn)], axis=1)
     return (
         jnp.asarray(first, jnp.bfloat16),
         jnp.asarray(twist, jnp.float32),
         jnp.asarray(inner, jnp.bfloat16),
-        jnp.asarray(last, jnp.bfloat16),
     )
 
 
@@ -83,8 +80,9 @@
         return acc
 
     query, key, value = mixed(0), mixed(1), mixed(2)
-    row = lax.broadcasted_iota(jnp.int32, (rows, width), 0)
-    query_ref[...] = jnp.where(row < taps_count - 1, 1.0, query[0:rows])
+    query_ref[...] = query[0:rows]
+    row = lax.broadcasted_iota(jnp.int32, (edge, width), 0)
+    query_ref[0:edge, :] = jnp.where(row < taps_count - 1, 1.0, query[0:edge])
     put_columns(packed_ref, 0, (key[0:rows] * value[0:rows]).astype(jnp.bfloat16).T)
     rims = []
     for part in (key, value, query):
@@ -148,17 +146,22 @@
     )
 
 
-def convolve_body(chans, rim_count, packed_ref, first_ref, twist_ref, inner_ref, last_ref, out_ref):
+def convolve_body(chans, rim_count, packed_ref, first_ref, twist_ref, inner_ref, out_ref):
     rows = twist_ref.shape[1]
     half = first_ref.shape[0] // 2
+    scale = chans / (half * rows)
     values, rim = take_blocks(packed_ref, chans, rows)
     before = jnp.concatenate([jnp.zeros((chans, lane), jnp.float32), rim[:-chans]])
     rim = rim + pltpu.roll(before, lane - edge, 1)
     in_rim = lax.broadcasted_iota(jnp.int32, rim.shape, 1) < rim_count
     rim_signal = (rim * pltpu.roll(rim, lane - rim_step, 1)).astype(jnp.bfloat16)
-    rim_query = jnp.where(in_rim, pltpu.roll(rim, lane - 2 * rim_step, 1), 1.0)
+    rim_query = scale * jnp.where(in_rim, pltpu.roll(rim, lane - 2 * rim_step, 1), 1.0)
     values = jnp.concatenate(
         [jnp.where(in_rim, rim_signal, values[:, 0:lane]), values[:, lane:]], axis=1
+    )
+    cosine, sine = inner_ref[:, 0:rows], inner_ref[:, rows:]
+    inner = jnp.concatenate(
+        [jnp.concatenate([cosine, -sine], axis=1), jnp.concatenate([sine, cosine], axis=1)]
     )
     spread = jnp.dot(first_ref[...], values, preferred_element_type=jnp.float32)
     tw_cos, tw_sin = twist_rows(twist_ref, chans)
@@ -167,17 +170,18 @@
         real, imag = spread[0:half, begin : begin + rows], spread[half:, begin : begin + rows]
         turned.append([real * tw_cos + imag * tw_sin, imag * tw_cos - real * tw_sin])
     turned = jnp.concatenate([jnp.concatenate(pair, axis=1).astype(jnp.bfloat16) for pair in turned])
-    spectra = jnp.dot(turned, inner_ref[...], preferred_element_type=jnp.float32)
+    spectra = jnp.dot(turned, inner, preferred_element_type=jnp.float32)
     real, imag = spectra[0:half, 0:rows], spectra[0:half, rows:]
     fil_re, fil_im = spectra[half:, 0:rows], spectra[half:, rows:]
     product = [real * fil_im + imag * fil_re, real * fil_re - imag * fil_im]
     product = jnp.concatenate(product, axis=1).astype(jnp.bfloat16)
-    back = jnp.dot(product, inner_ref[...], preferred_element_type=jnp.float32)
+    back = jnp.dot(product, inner, preferred_element_type=jnp.float32)
     imag, real = back[:, 0:rows], back[:, rows:]
     turned = jnp.concatenate([real * tw_cos - imag * tw_sin, imag * tw_cos + real * tw_sin])
-    conv = jnp.dot(last_ref[...], turned.astype(jnp.bfloat16), preferred_element_type=jnp.float32)
+    last = jnp.concatenate([first_ref[0:half, :].T, first_ref[half:, :].T], axis=1)
+    conv = jnp.dot(last, turned.astype(jnp.bfloat16), preferred_element_type=jnp.float32)
     out_ref[:, 0:lane] = (conv[:, 0:lane] * rim_query).astype(jnp.bfloat16)
-    out_ref[:, lane:] = conv[:, lane:].astype(jnp.bfloat16)
+    out_ref[:, lane:] = (conv[:, lane:] * scale).astype(jnp.bfloat16)
 
 
 def output_body(conv_ref, query_ref, w_ref, out_ref):
@@ -192,7 +196,7 @@
     rows, width = tokens.shape
     devices = lax.axis_size("seq")
     chans = width // devices
-    first, twist, inner, last = spectral_tables(devices, rows, chans)
+    first, twist, inner = spectral_tables(devices, rows, chans)
 
     if chans % 16:
         packed_shape = (width, 2 * rows + lane)
@@ -218,12 +222,11 @@
         flops=2 * rows * width * 3 * width,
         moved=1_500_000,
     )
-    packed, tables = lax.optimization_barrier((packed, (first, twist, inner, last)))
     conv = call(
         functools.partial(convolve_body, chans, short_filter.shape[0] - 1),
         jax.ShapeDtypeStruct((width, rows), jnp.bfloat16),
-        (swap(packed), *tables),
-        [pltpu.VMEM] * 5,
+        (swap(packed), first, twist, inner),
+        [pltpu.VMEM] * 4,
         flops=18 * first.shape[0] * width * rows,
         moved=2_000_000,
     )

time: 33.4 us -> 33.3 us (level)
  no operation moved by 1% of the time
where the time goes in v8:
time: 33.3 us; the launch traced here: 33.1 us
  blocking collectives  28.9 us (87%)
  Pallas kernels  4.15 us (12%)
    all_to_all x2, blocking collectives, swap(): lax.all_to_all(pieces, 'seq', split_axis=0, concat_axis=0)  28.9 us
    pallas_call x3, Pallas kernels, call(): pl.pallas_call(body, out_shape=outs, in_specs=[whole(space) for space in...  4.15 us

profile of v8, /device:TPU:0, one launch (start us, length us, event | category | flops | bytes accessed | tf_op | source)
XLA Modules:
  0.0 33.1 jit_solution(3923832681036819712)
XLA Ops:
  0.0 1.9 %shard_map.109 = (bf16[16,72,128]{2,1,0:T(8,128)(2,1)S(1)}, f32[256,256]{1,0:T(8,128)S(1)}) custom-call(bf16[256,256]{1,0:T(8,128)(2,1)} %refs_0_.1, f32[1,256]{1,0:T(1,128)} %bitcast.6, bf16[256,768]{1,0:T(8,128)(2,1)} %refs_2_.1, f32[3,768]{1,0:T(4,128)} %refs_3_.1, f32[256,256]{1,0:T(8,128)} %refs_4_.1, f32[128,256]{1,0:T(8,128)} %refs_5_.1, f32[1,256]{1,0:T(1,128)} %bitcast.7), custom_call_target="tpu_custom_call" | custom-call | flops 100663296 | bytes 1500000 | tf_op jit(solution)/shard_map/pallas_call | solution.py:24
  1.9 0.0 copy-start.1
  2.0 0.0 copy-start.2
  2.0 0.0 copy-start.3
  2.0 17.9 %all_to_all.10.packed_ref = bf16[16,72,128]{2,1,0:T(8,128)(2,1)S(1)} all-to-all(bf16[16,72,128]{2,1,0:T(8,128)(2,1)S(1)} %get-tuple-element.7), channel_id=1, replica_groups=mesh['groups'=2,'seq'=16] {'seq'}, dimensions={0} | all-to-all | bytes 589824 | tf_op jit(solution)/shard_map/all_to_all | solution.py:208
  19.9 0.0 copy-done.1
  19.9 0.0 copy-done.2
  19.9 0.0 copy-done.3
  19.9 1.3 %shard_map.110 = bf16[256,256]{1,0:T(8,128)(2,1)S(1)} custom-call(bf16[16,72,128]{2,1,0:T(8,128)(2,1)S(1)} %all_to_all.10.packed_ref, bf16[512,256]{1,0:T(8,128)(2,1)S(1)} %copy-done.2, f32[32,256]{1,0:T(8,128)S(1)} %copy-done.3, bf16[256,512]{1,0:T(8,128)(2,1)S(1)} %copy-done.1), custom_call_target="tpu_custom_call" | custom-call | flops 603979776 | bytes 2000000 | tf_op jit(solution)/shard_map/pallas_call | solution.py:24
  21.2 0.0 copy-start
  21.2 11.0 %all_to_all.11 = bf16[16,16,256]{2,1,0:T(8,128)(2,1)S(1)} all-to-all(bf16[16,16,256]{2,1,0:T(8,128)(2,1)S(1)} %bitcast.5), channel_id=1, replica_groups=mesh['groups'=2,'seq'=16] {'seq'}, dimensions={0} | all-to-all | bytes 262144 | tf_op jit(solution)/shard_map/all_to_all | solution.py:208
  32.2 0.0 copy-done
  32.2 0.9 %shard_map.111 = bf16[256,256]{1,0:T(8,128)(2,1)} custom-call(bf16[256,256]{1,0:T(8,128)(2,1)S(1)} %bitcast.4, f32[256,256]{1,0:T(8,128)S(1)} %get-tuple-element.8.query_ref, bf16[256,256]{1,0:T(8,128)(2,1)S(1)} %copy-done), custom_call_target="tpu_custom_call" | custom-call | flops 33554432 | bytes 600000 | tf_op jit(solution)/shard_map/pallas_call | solution.py:24
Async XLA Ops:
  1.9 17.9 %copy-start.1 = (bf16[256,512]{1,0:T(8,128)(2,1)S(1)}, bf16[256,512]{1,0:T(8,128)(2,1)}, u32[]{:S(2)}) copy-start(bf16[256,512]{1,0:T(8,128)(2,1)} %constant.8.clone.inner_ref) | copy-start | bytes 786436
  2.0 17.9 %copy-start.2 = (bf16[512,256]{1,0:T(8,128)(2,1)S(1)}, bf16[512,256]{1,0:T(8,128)(2,1)}, u32[]{:S(2)}) copy-start(bf16[512,256]{1,0:T(8,128)(2,1)} %constant.6.clone.first_ref) | copy-start | bytes 786436
  2.0 17.9 %copy-start.3 = (f32[32,256]{1,0:T(8,128)S(1)}, f32[32,256]{1,0:T(8,128)}, u32[]{:S(2)}) copy-start(f32[32,256]{1,0:T(8,128)} %constant.7.clone.twist_ref) | copy-start | bytes 98308
  21.2 11.0 %copy-start = (bf16[256,256]{1,0:T(8,128)(2,1)S(1)}, bf16[256,256]{1,0:T(8,128)(2,1)}, u32[]{:S(2)}) copy-start(bf16[256,256]{1,0:T(8,128)(2,1)} %w_ref.1) | copy-start | bytes 393220

commit v9 on v8

--- a/solution.py
+++ b/solution.py
@@ -12,6 +12,7 @@
 epsilon = 1e-06
 edge = 8
 lane = 128
+seq = ("chip", "core")
 rim_step = 2 * edge
 vmem_bytes = 32 * 2**20
 
@@ -53,8 +54,65 @@
     )
 
 
+def routes_of(chips):
+    far = sorted(range(2, chips, 2), key=lambda d: (-d.bit_length(), d))
+    return [(d + 1, d) if turn % 2 == 0 else (d, d + 1) for turn, d in enumerate(far)]
+
+
+def carried(route, core):
+    mine, others = route
+    return jnp.where(core == 0, mine, others), jnp.where(core == 0, others, mine)
+
+
+def put_routes(source_ref, keep_ref, give_ref, near_ref, home_ref):
+    chip, core = lax.axis_index("chip"), lax.axis_index("core")
+
+    def blocks(distance):
+        return source_ref[pl.ds((chip ^ distance) * 2, 2)]
+
+    for turn, route in enumerate(routes_of(source_ref.shape[0] // 2)):
+        own, other = carried(route, core)
+        keep_ref[turn] = blocks(own)
+        give_ref[turn] = blocks(other)
+    near_ref[...] = blocks(1)
+    home_ref[...] = blocks(0)
+
+
+def merge_body(keep_ref, got_ref, *out_refs):
+    for turn, out_ref in enumerate(out_refs):
+        out_ref[0] = keep_ref[turn]
+        out_ref[1] = got_ref[turn]
+
+
+def split_body(*refs):
+    far_refs, (near_ref, home_ref, keep_ref, give_ref) = refs[:-4], refs[-4:]
+    core = lax.axis_index("core")
+    for out_ref, target in ((keep_ref, core), (give_ref, 1 - core)):
+        for turn, far_ref in enumerate(far_refs):
+            for sender in range(2):
+                out_ref[2 * turn + sender] = far_ref[sender, target]
+        out_ref[2 * len(far_refs)] = near_ref[target]
+        out_ref[2 * len(far_refs) + 1] = home_ref[target]
+
+
+def take_routes(keep_ref, got_ref, target_ref):
+    chip, core = lax.axis_index("chip"), lax.axis_index("core")
+    routes = routes_of(target_ref.shape[0] // 2)
+    for turn, route in enumerate(routes):
+        own, other = carried(route, core)
+        target_ref[(chip ^ own) * 2 + core] = keep_ref[2 * turn]
+        target_ref[(chip ^ own) * 2 + 1 - core] = keep_ref[2 * turn + 1]
+        target_ref[(chip ^ other) * 2 + 1 - core] = got_ref[2 * turn]
+        target_ref[(chip ^ other) * 2 + core] = got_ref[2 * turn + 1]
+    for place, distance in ((2 * len(routes), 1), (2 * len(routes) + 1, 0)):
+        target_ref[(chip ^ distance) * 2 + core] = keep_ref[place]
+        target_ref[(chip ^ distance) * 2 + 1 - core] = got_ref[place]
+
+
 def prepare_body(*refs):
-    hbm, (packed_ref, query_ref), held, sems = refs[:7], refs[7:9], refs[9:16], refs[16]
+    hbm, query_ref, outs, held, sems = refs[:7], refs[7], refs[8:-8], refs[-8:-1], refs[-1]
+    staged = len(outs) > 1
+    outs, packed_ref = (outs[:-1], outs[-1]) if staged else (outs, outs[0])
     tokens_ref, gain_ref, w_ref, short_ref, long_ref, medium_ref, skip_ref = held
     rows, width = tokens_ref.shape
     copies = [pltpu.make_async_copy(h, v, sems.at[i]) for i, (h, v) in enumerate(zip(hbm, held))]
@@ -92,12 +150,14 @@
     for copy in copies[4:]:
         copy.wait()
     med_len = medium_ref.shape[0]
-    is_first = jnp.where(lax.axis_index("seq") == 0, 1.0, 0.0)
+    is_first = jnp.where(lax.axis_index(seq) == 0, 1.0, 0.0)
     head = long_ref[0:med_len, :] + is_first * medium_ref[...]
     head_row = lax.broadcasted_iota(jnp.int32, head.shape, 0)
     head = head + jnp.where(head_row == 0, is_first * skip_ref[...], 0.0)
     taps = jnp.concatenate([head, long_ref[med_len:, :]]).astype(jnp.bfloat16)
     put_columns(packed_ref, rows, taps.T)
+    if staged:
+        put_routes(packed_ref, *outs)
 
 
 def put_columns(packed_ref, begin, values):
@@ -146,7 +206,13 @@
     )
 
 
-def convolve_body(chans, rim_count, packed_ref, first_ref, twist_ref, inner_ref, out_ref):
+def convolve_body(chans, rim_count, first_ref, twist_ref, inner_ref, *refs):
+    staged = len(refs) > 2
+    if staged:
+        keep_ref, got_ref, *outs, packed_ref, out_ref = refs
+        take_routes(keep_ref, got_ref, packed_ref)
+    else:
+        packed_ref, out_ref = refs
     rows = twist_ref.shape[1]
     half = first_ref.shape[0] // 2
     scale = chans / (half * rows)
@@ -180,68 +246,115 @@
     turned = jnp.concatenate([real * tw_cos - imag * tw_sin, imag * tw_cos + real * tw_sin])
     last = jnp.concatenate([first_ref[0:half, :].T, first_ref[half:, :].T], axis=1)
     conv = jnp.dot(last, turned.astype(jnp.bfloat16), preferred_element_type=jnp.float32)
-    out_ref[:, 0:lane] = (conv[:, 0:lane] * rim_query).astype(jnp.bfloat16)
-    out_ref[:, lane:] = (conv[:, lane:] * scale).astype(jnp.bfloat16)
-
-
-def output_body(conv_ref, query_ref, w_ref, out_ref):
-    conv = conv_ref[...].T.astype(jnp.float32)
+    conv = jnp.concatenate([conv[:, 0:lane] * rim_query, conv[:, lane:] * scale], axis=1)
+    out_ref[...] = conv.astype(jnp.bfloat16).reshape(out_ref.shape)
+    if staged:
+        put_routes(out_ref, *outs)
+
+
+def output_body(query_ref, w_ref, *refs):
+    if len(refs) > 2:
+        keep_ref, got_ref, out_ref, conv_ref = refs
+        take_routes(keep_ref, got_ref, conv_ref)
+    else:
+        conv_ref, out_ref = refs
+    conv = conv_ref[...].reshape(w_ref.shape[0], query_ref.shape[0]).T.astype(jnp.float32)
     mixed_out = (query_ref[...] * conv).astype(jnp.bfloat16)
     out_ref[...] = jnp.dot(mixed_out, w_ref[...], preferred_element_type=jnp.float32).astype(
         jnp.bfloat16
     )
 
 
+def permute(array, partner):
+    return lax.ppermute(array, seq, [(i, partner(i)) for i in range(lax.axis_size(seq))])
+
+
+def bf16(*shape):
+    return jax.ShapeDtypeStruct(shape, jnp.bfloat16)
+
+
+def exchange(keep, give, near, home):
+    block, turns = keep.shape[2:], keep.shape[0]
+    got = permute(give, lambda i: i ^ 1)
+    near = permute(near, lambda i: i ^ 2)
+    far = call(
+        merge_body, (bf16(2, 2, *block),) * turns, (keep, got), [pltpu.VMEM] * 2, moved=4 * keep.size
+    )
+    routes = routes_of(lax.axis_size("chip"))
+    far = [permute(part, lambda i: i ^ 2 * route[i % 2]) for part, route in zip(far, routes)]
+    half = bf16(2 * turns + 2, *block)
+    keep, give = call(
+        split_body, (half, half), (*far, near, home), [pltpu.VMEM] * (turns + 2), moved=4 * keep.size
+    )
+    return keep, permute(give, lambda i: i ^ 1)
+
+
 def local(tokens, norm_gain, w_in, short_filter, long_filter, medium_filter, skip_gain, w_out):
     rows, width = tokens.shape
-    devices = lax.axis_size("seq")
+    devices, chips = lax.axis_size(seq), lax.axis_size("chip")
     chans = width // devices
     first, twist, inner = spectral_tables(devices, rows, chans)
-
+    staged = chans % 16 == 0 and chips >= 4
     if chans % 16:
-        packed_shape = (width, 2 * rows + lane)
+        packed_shape, conv_shape = (width, 2 * rows + lane), (width, rows)
     else:
         packed_shape = (devices, 2 * rows // lane * chans + chans // 2, lane)
-
-    def swap(array):
-        pieces = array.reshape(devices, -1, array.shape[-1])
-        return lax.all_to_all(pieces, "seq", split_axis=0, concat_axis=0).reshape(array.shape)
+        conv_shape = (devices, chans, rows)
+
+    def pieces(shape):
+        if not staged:
+            return (bf16(*shape),), []
+        block, turns = shape[1:], len(routes_of(chips))
+        outs = [bf16(turns, 2, *block)] * 2 + [bf16(2, *block)] * 2
+        return tuple(outs), [pltpu.VMEM(shape, jnp.bfloat16)]
+
+    def swap(parts):
+        if staged:
+            return exchange(*parts)
+        (array,) = parts
+        blocks = array.reshape(devices, -1, array.shape[-1])
+        return (lax.all_to_all(blocks, seq, split_axis=0, concat_axis=0).reshape(array.shape),)
 
     args = (tokens, norm_gain[None, :], w_in, short_filter, long_filter, medium_filter, skip_gain[None, :])
     args = tuple(pltpu.with_memory_space_constraint(arg, pltpu.HBM) for arg in args)
-    packed, query = call(
+    outs, packed_scratch = pieces(packed_shape)
+    query, *parts = call(
         prepare_body,
-        (
-            jax.ShapeDtypeStruct(packed_shape, jnp.bfloat16),
-            jax.ShapeDtypeStruct((rows, width), jnp.float32),
-        ),
+        (jax.ShapeDtypeStruct((rows, width), jnp.float32), *outs),
         args,
         [pltpu.HBM] * len(args),
-        [pltpu.VMEM(arg.shape, arg.dtype) for arg in args]
+        packed_scratch
+        + [pltpu.VMEM(arg.shape, arg.dtype) for arg in args]
         + [pltpu.SemaphoreType.DMA((len(args),))],
         flops=2 * rows * width * 3 * width,
         moved=1_500_000,
     )
-    conv = call(
+    outs, conv_scratch = pieces(conv_shape)
+    parts = swap(parts)
+    parts = call(
         functools.partial(convolve_body, chans, short_filter.shape[0] - 1),
-        jax.ShapeDtypeStruct((width, rows), jnp.bfloat16),
-        (swap(packed), first, twist, inner),
-        [pltpu.VMEM] * 4,
+        outs,
+        (first, twist, inner, *parts),
+        [pltpu.VMEM] * (3 + len(parts)),
+        packed_scratch + conv_scratch,
         flops=18 * first.shape[0] * width * rows,
         moved=2_000_000,
     )
+    parts = swap(parts)
     return call(
         output_body,
-        jax.ShapeDtypeStruct((rows, width), jnp.bfloat16),
-        (swap(conv), query, w_out),
-        [pltpu.VMEM] * 3,
+        bf16(rows, width),
+        (query, w_out, *parts),
+        [pltpu.VMEM] * (2 + len(parts)),
+        conv_scratch,
         flops=2 * rows * width * width,
         moved=600_000,
     )
 
 
 def solution(mesh):
-    placed = (P(("groups", "seq"), None), P(), P(), P(), P("seq", None), P(), P(), P())
-    return jax.shard_map(
-        local, mesh=mesh, in_specs=placed, out_specs=P(("groups", "seq"), None), check_vma=False
-    )
+    groups, devices = mesh.devices.shape
+    split = jax.sharding.Mesh(mesh.devices.reshape(groups, devices // 2, 2), ("groups", *seq))
+    rows = P(("groups", *seq), None)
+    placed = (rows, P(), P(), P(), P(seq, None), P(), P(), P())
+    return jax.shard_map(local, mesh=split, in_specs=placed, out_specs=rows, check_vma=False)

time: 33.3 us -> 31.4 us (0.943)
  blocking collectives: 28.9 us -> 0 us
  starting transfers between devices: 0 us -> 14.6 us
  waiting for transfers between devices: 0 us -> 12.3 us
    all_to_all x2 -> x0, blocking collectives: 28.9 us -> none  [swap(): lax.all_to_all(pieces, 'seq', split_axis=0, concat_axis=0)]
    ppermute x0 -> x12, starting transfers between devices: none -> 14.6 us  [permute(): lax.ppermute(array, seq, [(i, partner(i)) for i in range(lax.axis_size(se...]
    ppermute x0 -> x12, waiting for transfers between devices: none -> 12.3 us  [permute(): lax.ppermute(array, seq, [(i, partner(i)) for i in range(lax.axis_size(se...]
    pallas_call x3 -> x7, Pallas kernels: 4.15 us -> 4.32 us  [call(): pl.pallas_call(body, out_shape=outs, in_specs=[whole(space) for space in...]
  transfers between devices with their start and end apart: 0 -> 12, of which waited for: 0 -> 10; matrix products, arithmetic and copies ran while one was open for 0% -> 0% of each run, Pallas kernels for 0% -> 0%
where the time goes in v9:
time: 31.4 us; the launch traced here: 31.3 us
  starting transfers between devices  14.6 us (46%)
  waiting for transfers between devices  12.3 us (39%)
  Pallas kernels  4.32 us (14%)
    ppermute x12, starting transfers between devices, permute(): lax.ppermute(array, seq, [(i, partner(i)) for i in range(lax.axis_size(se...  14.6 us
    ppermute x12, waiting for transfers between devices, permute(): lax.ppermute(array, seq, [(i, partner(i)) for i in range(lax.axis_size(se...  12.3 us
    pallas_call x7, Pallas kernels, call(): pl.pallas_call(body, out_shape=outs, in_specs=[whole(space) for space in...  4.32 us
  transfers between devices with their start and end apart: 12, of which 10 were waited for; matrix products, arithmetic and copies ran while one was open for 0% of the time, Pallas kernels for 0%

profile of v9, /device:TPU:0, one launch (start us, length us, event | category | flops | bytes accessed | tf_op | source)
XLA Modules:
  0.0 31.3 jit_solution(8031815406283195164)
XLA Ops:
  0.0 0.0 copy-start.3
  0.0 2.0 %shard_map.109 = (f32[256,256]{1,0:T(8,128)S(1)}, bf16[3,2,72,128]{3,2,1,0:T(8,128)(2,1)S(1)}, bf16[3,2,72,128]{3,2,1,0:T(8,128)(2,1)S(1)}, bf16[2,72,128]{2,1,0:T(8,128)(2,1)S(1)}, bf16[2,72,128]{2,1,0:T(8,128)(2,1)S(1)}) custom-call(bf16[256,256]{1,0:T(8,128)(2,1)} %refs_0_.1, f32[1,256]{1,0:T(1,128)} %bitcast.2, bf16[256,768]{1,0:T(8,128)(2,1)} %refs_2_.1, ...), custom_call_target="tpu_custom_call" | custom-call | flops 100663296 | bytes 1500000 | tf_op jit(solution)/shard_map/pallas_call | solution.py:25
  2.0 0.5 %collective-permute-start = (bf16[3,2,72,128]{3,2,1,0:T(8,128)(2,1)S(1)}, bf16[3,2,72,128]{3,2,1,0:T(8,128)(2,1)S(1)}, u32[]{:S(2)}, u32[]{:S(2)}) collective-permute-start(bf16[3,2,72,128]{3,2,1,0:T(8,128)(2,1)S(1)} %get-tuple-element.26), channel_id=1, source_target_pairs={{0,1},{1,0},{2,3},{3,2},{4,5},{5,4},{6,7},{7,6},{8,9},{9,8},{10,11... | collective-permute-start | bytes 331784 | tf_op jit(solution)/shard_map/ppermute | solution.py:269
  2.5 1.0 %collective-permute-done.got_ref = bf16[3,2,72,128]{3,2,1,0:T(8,128)(2,1)S(1)} collective-permute-done((bf16[3,2,72,128]{3,2,1,0:T(8,128)(2,1)S(1)}, bf16[3,2,72,128]{3,2,1,0:T(8,128)(2,1)S(1)}, u32[]{:S(2)}, u32[]{:S(2)}) %collective-permute-start) | collective-permute-done | bytes 110624 | tf_op jit(solution)/shard_map/ppermute | solution.py:269
  3.4 0.0 copy-start.1
  3.4 0.0 copy-start.2
  3.5 5.0 %collective-permute-start.1 = (bf16[2,2,72,128]{3,2,1,0:T(8,128)(2,1)S(1)}, bf16[2,2,72,128]{3,2,1,0:T(8,128)(2,1)S(1)}, u32[]{:S(2)}, u32[]{:S(2)}) collective-permute-start(bf16[2,2,72,128]{3,2,1,0:T(8,128)(2,1)S(1)} %get-tuple-element.27), channel_id=1, source_target_pairs={{0,10},{1,9},{2,8},{3,11},{4,14},{5,13},{6,12},{7,15},{8,2},{9,1},... | collective-permute-start | bytes 221192 | tf_op jit(solution)/shard_map/ppermute | solution.py:269
  8.4 1.3 %collective-permute-start.2 = (bf16[2,2,72,128]{3,2,1,0:T(8,128)(2,1)S(1)}, bf16[2,2,72,128]{3,2,1,0:T(8,128)(2,1)S(1)}, u32[]{:S(2)}, u32[]{:S(2)}) collective-permute-start(bf16[2,2,72,128]{3,2,1,0:T(8,128)(2,1)S(1)} %get-tuple-element.28), channel_id=1, source_target_pairs={{0,12},{1,15},{2,14},{3,13},{4,8},{5,11},{6,10},{7,9},{8,4},{9,7},... | collective-permute-start | bytes 221192 | tf_op jit(solution)/shard_map/ppermute | solution.py:269
  9.8 0.2 collective-permute-start.3
  10.0 1.5 %collective-permute-start.4 = (bf16[2,72,128]{2,1,0:T(8,128)(2,1)S(1)}, bf16[2,72,128]{2,1,0:T(8,128)(2,1)S(1)}, u32[]{:S(2)}, u32[]{:S(2)}) collective-permute-start(bf16[2,72,128]{2,1,0:T(8,128)(2,1)S(1)} %get-tuple-element.30), channel_id=1, source_target_pairs={{0,2},{1,3},{2,0},{3,1},{4,6},{5,7},{6,4},{7,5},{8,10},{9,11},{10,... | collective-permute-start | bytes 110600 | tf_op jit(solution)/shard_map/ppermute | solution.py:269
  11.5 2.7 %collective-permute-done.4.refs_3_ = bf16[2,72,128]{2,1,0:T(8,128)(2,1)S(1)} collective-permute-done((bf16[2,72,128]{2,1,0:T(8,128)(2,1)S(1)}, bf16[2,72,128]{2,1,0:T(8,128)(2,1)S(1)}, u32[]{:S(2)}, u32[]{:S(2)}) %collective-permute-start.4) | collective-permute-done | bytes 36896 | tf_op jit(solution)/shard_map/ppermute | solution.py:269
  14.1 0.0 collective-permute-done.1.refs_0_
  14.1 1.0 %collective-permute-done.2.refs_1_ = bf16[2,2,72,128]{3,2,1,0:T(8,128)(2,1)S(1)} collective-permute-done((bf16[2,2,72,128]{3,2,1,0:T(8,128)(2,1)S(1)}, bf16[2,2,72,128]{3,2,1,0:T(8,128)(2,1)S(1)}, u32[]{:S(2)}, u32[]{:S(2)}) %collective-permute-start.2) | collective-permute-done | bytes 73760 | tf_op jit(solution)/shard_map/ppermute | solution.py:269
  15.1 0.5 %collective-permute-done.3.refs_2_ = bf16[2,2,72,128]{3,2,1,0:T(8,128)(2,1)S(1)} collective-permute-done((bf16[2,2,72,128]{3,2,1,0:T(8,128)(2,1)S(1)}, bf16[2,2,72,128]{3,2,1,0:T(8,128)(2,1)S(1)}, u32[]{:S(2)}, u32[]{:S(2)}) %collective-permute-start.3) | collective-permute-done | bytes 73760 | tf_op jit(solution)/shard_map/ppermute | solution.py:269
  15.6 0.1 collective-permute-start.5
  15.7 1.4 %collective-permute-done.5.refs_1_ = bf16[8,72,128]{2,1,0:T(8,128)(2,1)S(1)} collective-permute-done((bf16[8,72,128]{2,1,0:T(8,128)(2,1)S(1)}, bf16[8,72,128]{2,1,0:T(8,128)(2,1)S(1)}, u32[]{:S(2)}, u32[]{:S(2)}) %collective-permute-start.5) | collective-permute-done | bytes 147488 | tf_op jit(solution)/shard_map/ppermute | solution.py:269
  17.0 0.0 copy-done.3
  17.0 0.0 copy-done.1
  17.0 0.0 copy-done.2
  17.0 1.4 %shard_map.112 = (bf16[3,2,16,256]{3,2,1,0:T(8,128)(2,1)S(1)}, bf16[3,2,16,256]{3,2,1,0:T(8,128)(2,1)S(1)}, bf16[2,16,256]{2,1,0:T(8,128)(2,1)S(1)}, bf16[2,16,256]{2,1,0:T(8,128)(2,1)S(1)}) custom-call(bf16[512,256]{1,0:T(8,128)(2,1)S(1)} %copy-done.2, f32[32,256]{1,0:T(8,128)S(1)} %copy-done.3, bf16[256,512]{1,0:T(8,128)(2,1)S(1)} %copy-done.1, ...), custom_call_target="tpu_custom_call" | custom-call | flops 603979776 | bytes 2000000 | tf_op jit(solution)/shard_map/pallas_call | solution.py:25
  18.4 0.0 copy-start
  18.5 0.2 collective-permute-start.6
  18.7 1.1 %collective-permute-done.6.got_ref = bf16[3,2,16,256]{3,2,1,0:T(8,128)(2,1)S(1)} collective-permute-done((bf16[3,2,16,256]{3,2,1,0:T(8,128)(2,1)S(1)}, bf16[3,2,16,256]{3,2,1,0:T(8,128)(2,1)S(1)}, u32[]{:S(2)}, u32[]{:S(2)}) %collective-permute-start.6) | collective-permute-done | bytes 49184 | tf_op jit(solution)/shard_map/ppermute | solution.py:269
  19.8 2.9 %collective-permute-start.7 = (bf16[2,2,16,256]{3,2,1,0:T(8,128)(2,1)S(1)}, bf16[2,2,16,256]{3,2,1,0:T(8,128)(2,1)S(1)}, u32[]{:S(2)}, u32[]{:S(2)}) collective-permute-start(bf16[2,2,16,256]{3,2,1,0:T(8,128)(2,1)S(1)} %get-tuple-element.36), channel_id=1, source_target_pairs={{0,10},{1,9},{2,8},{3,11},{4,14},{5,13},{6,12},{7,15},{8,2},{9,1},... | collective-permute-start | bytes 98312 | tf_op jit(solution)/shard_map/ppermute | solution.py:269
  22.7 1.2 %collective-permute-start.8 = (bf16[2,2,16,256]{3,2,1,0:T(8,128)(2,1)S(1)}, bf16[2,2,16,256]{3,2,1,0:T(8,128)(2,1)S(1)}, u32[]{:S(2)}, u32[]{:S(2)}) collective-permute-start(bf16[2,2,16,256]{3,2,1,0:T(8,128)(2,1)S(1)} %get-tuple-element.37), channel_id=1, source_target_pairs={{0,12},{1,15},{2,14},{3,13},{4,8},{5,11},{6,10},{7,9},{8,4},{9,7},... | collective-permute-start | bytes 98312 | tf_op jit(solution)/shard_map/ppermute | solution.py:269
  23.9 0.7 %collective-permute-start.9 = (bf16[2,2,16,256]{3,2,1,0:T(8,128)(2,1)S(1)}, bf16[2,2,16,256]{3,2,1,0:T(8,128)(2,1)S(1)}, u32[]{:S(2)}, u32[]{:S(2)}) collective-permute-start(bf16[2,2,16,256]{3,2,1,0:T(8,128)(2,1)S(1)} %get-tuple-element.38), channel_id=1, source_target_pairs={{0,6},{1,5},{2,4},{3,7},{4,2},{5,1},{6,0},{7,3},{8,14},{9,13},{10,... | collective-permute-start | bytes 98312 | tf_op jit(solution)/shard_map/ppermute | solution.py:269
  24.6 0.9 %collective-permute-start.10 = (bf16[2,16,256]{2,1,0:T(8,128)(2,1)S(1)}, bf16[2,16,256]{2,1,0:T(8,128)(2,1)S(1)}, u32[]{:S(2)}, u32[]{:S(2)}) collective-permute-start(bf16[2,16,256]{2,1,0:T(8,128)(2,1)S(1)} %get-tuple-element.39), channel_id=1, source_target_pairs={{0,2},{1,3},{2,0},{3,1},{4,6},{5,7},{6,4},{7,5},{8,10},{9,11},{10,... | collective-permute-start | bytes 49160 | tf_op jit(solution)/shard_map/ppermute | solution.py:269
  25.5 2.9 %collective-permute-done.10.refs_3_ = bf16[2,16,256]{2,1,0:T(8,128)(2,1)S(1)} collective-permute-done((bf16[2,16,256]{2,1,0:T(8,128)(2,1)S(1)}, bf16[2,16,256]{2,1,0:T(8,128)(2,1)S(1)}, u32[]{:S(2)}, u32[]{:S(2)}) %collective-permute-start.10) | collective-permute-done | bytes 16416 | tf_op jit(solution)/shard_map/ppermute | solution.py:269
  28.4 0.0 collective-permute-done.7.refs_0_
  28.4 0.1 collective-permute-done.8.refs_1_
  28.4 0.6 %collective-permute-done.9.refs_2_ = bf16[2,2,16,256]{3,2,1,0:T(8,128)(2,1)S(1)} collective-permute-done((bf16[2,2,16,256]{3,2,1,0:T(8,128)(2,1)S(1)}, bf16[2,2,16,256]{3,2,1,0:T(8,128)(2,1)S(1)}, u32[]{:S(2)}, u32[]{:S(2)}) %collective-permute-start.9) | collective-permute-done | bytes 32800 | tf_op jit(solution)/shard_map/ppermute | solution.py:269
  29.1 0.1 collective-permute-start.11
  29.1 1.2 %collective-permute-done.11.refs_1_ = bf16[8,16,256]{2,1,0:T(8,128)(2,1)S(1)} collective-permute-done((bf16[8,16,256]{2,1,0:T(8,128)(2,1)S(1)}, bf16[8,16,256]{2,1,0:T(8,128)(2,1)S(1)}, u32[]{:S(2)}, u32[]{:S(2)}) %collective-permute-start.11) | collective-permute-done | bytes 65568 | tf_op jit(solution)/shard_map/ppermute | solution.py:269
  30.4 0.0 copy-done
  30.4 0.9 %shard_map.115 = bf16[256,256]{1,0:T(8,128)(2,1)} custom-call(f32[256,256]{1,0:T(8,128)S(1)} %get-tuple-element.24.query_ref, bf16[256,256]{1,0:T(8,128)(2,1)S(1)} %copy-done, bf16[8,16,256]{2,1,0:T(8,128)(2,1)S(1)} %get-tuple-element.41.refs_0_, bf16[8,16,256]{2,1,0:T(8,128)(2,1)S(1)} %collective-permute-done.11.refs_1_), custom_call_target="tpu_custom_call" | custom-call | flops 33554432 | bytes 600000 | tf_op jit(solution)/shard_map/pallas_call | solution.py:25
  (4 shorter events, 0.1 us)
Async XLA Ops:
  0.0 17.0 %copy-start.3 = (f32[32,256]{1,0:T(8,128)S(1)}, f32[32,256]{1,0:T(8,128)}, u32[]{:S(2)}) copy-start(f32[32,256]{1,0:T(8,128)} %constant.7.clone.twist_ref) | copy-start | bytes 98308
  2.0 1.5 %collective-permute-start = (bf16[3,2,72,128]{3,2,1,0:T(8,128)(2,1)S(1)}, bf16[3,2,72,128]{3,2,1,0:T(8,128)(2,1)S(1)}, u32[]{:S(2)}, u32[]{:S(2)}) collective-permute-start(bf16[3,2,72,128]{3,2,1,0:T(8,128)(2,1)S(1)} %get-tuple-element.26), channel_id=1, source_target_pairs={{0,1},{1,0},{2,3},{3,2},{4,5},{5,4},{6,7},{7,6},{8,9},{9,8},{10,11... | collective-permute-start | bytes 331784 | tf_op jit(solution)/shard_map/ppermute | solution.py:269
  3.4 13.6 %copy-start.1 = (bf16[256,512]{1,0:T(8,128)(2,1)S(1)}, bf16[256,512]{1,0:T(8,128)(2,1)}, u32[]{:S(2)}) copy-start(bf16[256,512]{1,0:T(8,128)(2,1)} %constant.8.clone.inner_ref) | copy-start | bytes 786436
  3.4 13.6 %copy-start.2 = (bf16[512,256]{1,0:T(8,128)(2,1)S(1)}, bf16[512,256]{1,0:T(8,128)(2,1)}, u32[]{:S(2)}) copy-start(bf16[512,256]{1,0:T(8,128)(2,1)} %constant.6.clone.first_ref) | copy-start | bytes 786436
  3.5 10.7 %collective-permute-start.1 = (bf16[2,2,72,128]{3,2,1,0:T(8,128)(2,1)S(1)}, bf16[2,2,72,128]{3,2,1,0:T(8,128)(2,1)S(1)}, u32[]{:S(2)}, u32[]{:S(2)}) collective-permute-start(bf16[2,2,72,128]{3,2,1,0:T(8,128)(2,1)S(1)} %get-tuple-element.27), channel_id=1, source_target_pairs={{0,10},{1,9},{2,8},{3,11},{4,14},{5,13},{6,12},{7,15},{8,2},{9,1},... | collective-permute-start | bytes 221192 | tf_op jit(solution)/shard_map/ppermute | solution.py:269
  8.4 6.7 %collective-permute-start.2 = (bf16[2,2,72,128]{3,2,1,0:T(8,128)(2,1)S(1)}, bf16[2,2,72,128]{3,2,1,0:T(8,128)(2,1)S(1)}, u32[]{:S(2)}, u32[]{:S(2)}) collective-permute-start(bf16[2,2,72,128]{3,2,1,0:T(8,128)(2,1)S(1)} %get-tuple-element.28), channel_id=1, source_target_pairs={{0,12},{1,15},{2,14},{3,13},{4,8},{5,11},{6,10},{7,9},{8,4},{9,7},... | collective-permute-start | bytes 221192 | tf_op jit(solution)/shard_map/ppermute | solution.py:269
  9.8 5.8 %collective-permute-start.3 = (bf16[2,2,72,128]{3,2,1,0:T(8,128)(2,1)S(1)}, bf16[2,2,72,128]{3,2,1,0:T(8,128)(2,1)S(1)}, u32[]{:S(2)}, u32[]{:S(2)}) collective-permute-start(bf16[2,2,72,128]{3,2,1,0:T(8,128)(2,1)S(1)} %get-tuple-element.29), channel_id=1, source_target_pairs={{0,6},{1,5},{2,4},{3,7},{4,2},{5,1},{6,0},{7,3},{8,14},{9,13},{10,... | collective-permute-start | bytes 221192 | tf_op jit(solution)/shard_map/ppermute | solution.py:269
  10.0 4.2 %collective-permute-start.4 = (bf16[2,72,128]{2,1,0:T(8,128)(2,1)S(1)}, bf16[2,72,128]{2,1,0:T(8,128)(2,1)S(1)}, u32[]{:S(2)}, u32[]{:S(2)}) collective-permute-start(bf16[2,72,128]{2,1,0:T(8,128)(2,1)S(1)} %get-tuple-element.30), channel_id=1, source_target_pairs={{0,2},{1,3},{2,0},{3,1},{4,6},{5,7},{6,4},{7,5},{8,10},{9,11},{10,... | collective-permute-start | bytes 110600 | tf_op jit(solution)/shard_map/ppermute | solution.py:269
  15.6 1.4 %collective-permute-start.5 = (bf16[8,72,128]{2,1,0:T(8,128)(2,1)S(1)}, bf16[8,72,128]{2,1,0:T(8,128)(2,1)S(1)}, u32[]{:S(2)}, u32[]{:S(2)}) collective-permute-start(bf16[8,72,128]{2,1,0:T(8,128)(2,1)S(1)} %get-tuple-element.33), channel_id=1, source_target_pairs={{0,1},{1,0},{2,3},{3,2},{4,5},{5,4},{6,7},{7,6},{8,9},{9,8},{10,11... | collective-permute-start | bytes 442376 | tf_op jit(solution)/shard_map/ppermute | solution.py:269
  18.4 11.9 %copy-start = (bf16[256,256]{1,0:T(8,128)(2,1)S(1)}, bf16[256,256]{1,0:T(8,128)(2,1)}, u32[]{:S(2)}) copy-start(bf16[256,256]{1,0:T(8,128)(2,1)} %w_ref.1) | copy-start | bytes 393220
  18.5 1.3 %collective-permute-start.6 = (bf16[3,2,16,256]{3,2,1,0:T(8,128)(2,1)S(1)}, bf16[3,2,16,256]{3,2,1,0:T(8,128)(2,1)S(1)}, u32[]{:S(2)}, u32[]{:S(2)}) collective-permute-start(bf16[3,2,16,256]{3,2,1,0:T(8,128)(2,1)S(1)} %get-tuple-element.35), channel_id=1, source_target_pairs={{0,1},{1,0},{2,3},{3,2},{4,5},{5,4},{6,7},{7,6},{8,9},{9,8},{10,11... | collective-permute-start | bytes 147464 | tf_op jit(solution)/shard_map/ppermute | solution.py:269
  19.8 8.6 %collective-permute-start.7 = (bf16[2,2,16,256]{3,2,1,0:T(8,128)(2,1)S(1)}, bf16[2,2,16,256]{3,2,1,0:T(8,128)(2,1)S(1)}, u32[]{:S(2)}, u32[]{:S(2)}) collective-permute-start(bf16[2,2,16,256]{3,2,1,0:T(8,128)(2,1)S(1)} %get-tuple-element.36), channel_id=1, source_target_pairs={{0,10},{1,9},{2,8},{3,11},{4,14},{5,13},{6,12},{7,15},{8,2},{9,1},... | collective-permute-start | bytes 98312 | tf_op jit(solution)/shard_map/ppermute | solution.py:269
  22.7 5.7 %collective-permute-start.8 = (bf16[2,2,16,256]{3,2,1,0:T(8,128)(2,1)S(1)}, bf16[2,2,16,256]{3,2,1,0:T(8,128)(2,1)S(1)}, u32[]{:S(2)}, u32[]{:S(2)}) collective-permute-start(bf16[2,2,16,256]{3,2,1,0:T(8,128)(2,1)S(1)} %get-tuple-element.37), channel_id=1, source_target_pairs={{0,12},{1,15},{2,14},{3,13},{4,8},{5,11},{6,10},{7,9},{8,4},{9,7},... | collective-permute-start | bytes 98312 | tf_op jit(solution)/shard_map/ppermute | solution.py:269
  23.9 5.2 %collective-permute-start.9 = (bf16[2,2,16,256]{3,2,1,0:T(8,128)(2,1)S(1)}, bf16[2,2,16,256]{3,2,1,0:T(8,128)(2,1)S(1)}, u32[]{:S(2)}, u32[]{:S(2)}) collective-permute-start(bf16[2,2,16,256]{3,2,1,0:T(8,128)(2,1)S(1)} %get-tuple-element.38), channel_id=1, source_target_pairs={{0,6},{1,5},{2,4},{3,7},{4,2},{5,1},{6,0},{7,3},{8,14},{9,13},{10,... | collective-permute-start | bytes 98312 | tf_op jit(solution)/shard_map/ppermute | solution.py:269
  24.6 3.7 %collective-permute-start.10 = (bf16[2,16,256]{2,1,0:T(8,128)(2,1)S(1)}, bf16[2,16,256]{2,1,0:T(8,128)(2,1)S(1)}, u32[]{:S(2)}, u32[]{:S(2)}) collective-permute-start(bf16[2,16,256]{2,1,0:T(8,128)(2,1)S(1)} %get-tuple-element.39), channel_id=1, source_target_pairs={{0,2},{1,3},{2,0},{3,1},{4,6},{5,7},{6,4},{7,5},{8,10},{9,11},{10,... | collective-permute-start | bytes 49160 | tf_op jit(solution)/shard_map/ppermute | solution.py:269
  29.1 1.3 %collective-permute-start.11 = (bf16[8,16,256]{2,1,0:T(8,128)(2,1)S(1)}, bf16[8,16,256]{2,1,0:T(8,128)(2,1)S(1)}, u32[]{:S(2)}, u32[]{:S(2)}) collective-permute-start(bf16[8,16,256]{2,1,0:T(8,128)(2,1)S(1)} %get-tuple-element.42), channel_id=1, source_target_pairs={{0,1},{1,0},{2,3},{3,2},{4,5},{5,4},{6,7},{7,6},{8,9},{9,8},{10,11... | collective-permute-start | bytes 196616 | tf_op jit(solution)/shard_map/ppermute | solution.py:269

commit v10 on v9

--- a/solution.py
+++ b/solution.py
@@ -64,17 +64,19 @@
     return jnp.where(core == 0, mine, others), jnp.where(core == 0, others, mine)
 
 
-def put_routes(source_ref, keep_ref, give_ref, near_ref, home_ref):
+def put_routes(source_ref, keep_ref, give_ref, home_ref):
     chip, core = lax.axis_index("chip"), lax.axis_index("core")
 
     def blocks(distance):
         return source_ref[pl.ds((chip ^ distance) * 2, 2)]
 
-    for turn, route in enumerate(routes_of(source_ref.shape[0] // 2)):
+    routes = routes_of(source_ref.shape[0] // 2)
+    for turn, route in enumerate(routes):
         own, other = carried(route, core)
         keep_ref[turn] = blocks(own)
         give_ref[turn] = blocks(other)
-    near_ref[...] = blocks(1)
+    keep_ref[len(routes)] = blocks(1)
+    give_ref[len(routes)] = blocks(1)
     home_ref[...] = blocks(0)
 
 
@@ -85,14 +87,13 @@
 
 
 def split_body(*refs):
-    far_refs, (near_ref, home_ref, keep_ref, give_ref) = refs[:-4], refs[-4:]
+    moved_refs, (home_ref, keep_ref, give_ref) = refs[:-3], refs[-3:]
     core = lax.axis_index("core")
     for out_ref, target in ((keep_ref, core), (give_ref, 1 - core)):
-        for turn, far_ref in enumerate(far_refs):
+        for turn, moved_ref in enumerate(moved_refs):
             for sender in range(2):
-                out_ref[2 * turn + sender] = far_ref[sender, target]
-        out_ref[2 * len(far_refs)] = near_ref[target]
-        out_ref[2 * len(far_refs) + 1] = home_ref[target]
+                out_ref[2 * turn + sender] = moved_ref[sender, target]
+        out_ref[2 * len(moved_refs)] = home_ref[target]
 
 
 def take_routes(keep_ref, got_ref, target_ref):
@@ -104,13 +105,44 @@
         target_ref[(chip ^ own) * 2 + 1 - core] = keep_ref[2 * turn + 1]
         target_ref[(chip ^ other) * 2 + 1 - core] = got_ref[2 * turn]
         target_ref[(chip ^ other) * 2 + core] = got_ref[2 * turn + 1]
-    for place, distance in ((2 * len(routes), 1), (2 * len(routes) + 1, 0)):
-        target_ref[(chip ^ distance) * 2 + core] = keep_ref[place]
-        target_ref[(chip ^ distance) * 2 + 1 - core] = got_ref[place]
+    near, home = 2 * len(routes), 2 * len(routes) + 2
+    for sender in range(2):
+        block = jnp.where(core == 1, keep_ref[near + sender], got_ref[near + sender])
+        target_ref[(chip ^ 1) * 2 + 1 - sender] = block
+    target_ref[chip * 2 + core] = keep_ref[home]
+    target_ref[chip * 2 + 1 - core] = got_ref[home]
+
+
+def normed_of(tokens_ref, gain_ref):
+    inputs = tokens_ref[...].astype(jnp.float32)
+    mean_sq = jnp.mean(inputs * inputs, axis=-1, keepdims=True)
+    return (inputs * lax.rsqrt(mean_sq + epsilon) * gain_ref[...]).astype(jnp.bfloat16)
+
+
+def projected_of(normed, weights):
+    projected = jnp.dot(normed, weights, preferred_element_type=jnp.float32)
+    projected = projected.astype(jnp.bfloat16).astype(jnp.float32)
+    return jnp.concatenate([projected, jnp.zeros((edge, projected.shape[1]), jnp.float32)])
+
+
+def short_mix(projected, taps):
+    acc = taps[0:1] * projected
+    for tap_num in range(1, taps.shape[0]):
+        acc = acc + taps[tap_num : tap_num + 1] * pltpu.roll(projected, tap_num, 0)
+    return acc
+
+
+def query_body(tokens_ref, gain_ref, w_ref, short_ref, query_ref):
+    rows, width = tokens_ref.shape
+    cols = slice(0, width)
+    query = short_mix(projected_of(normed_of(tokens_ref, gain_ref), w_ref[:, cols]), short_ref[:, cols])
+    query_ref[...] = query[0:rows]
+    row = lax.broadcasted_iota(jnp.int32, (edge, width), 0)
+    query_ref[0:edge, :] = jnp.where(row < short_ref.shape[0] - 1, 1.0, query[0:edge])
 
 
 def prepare_body(*refs):
-    hbm, query_ref, outs, held, sems = refs[:7], refs[7], refs[8:-8], refs[-8:-1], refs[-1]
+    hbm, outs, held, sems = refs[:7], refs[7:-8], refs[-8:-1], refs[-1]
     staged = len(outs) > 1
     outs, packed_ref = (outs[:-1], outs[-1]) if staged else (outs, outs[0])
     tokens_ref, gain_ref, w_ref, short_ref, long_ref, medium_ref, skip_ref = held
@@ -120,31 +152,17 @@
         copy.start()
     copies[0].wait()
     copies[1].wait()
-    inputs = tokens_ref[...].astype(jnp.float32)
-    mean_sq = jnp.mean(inputs * inputs, axis=-1, keepdims=True)
-    normed = (inputs * lax.rsqrt(mean_sq + epsilon) * gain_ref[...]).astype(jnp.bfloat16)
+    normed = normed_of(tokens_ref, gain_ref)
     copies[2].wait()
     copies[3].wait()
-    projected = jnp.dot(normed, w_ref[...], preferred_element_type=jnp.float32)
-    projected = projected.astype(jnp.bfloat16).astype(jnp.float32)
-    projected = jnp.concatenate([projected, jnp.zeros((edge, 3 * width), jnp.float32)])
-    taps_count = short_ref.shape[0]
-
-    def mixed(part):
-        cols = slice(part * width, (part + 1) * width)
-        acc = short_ref[0:1, cols] * projected[:, cols]
-        for tap_num in range(1, taps_count):
-            acc = acc + short_ref[tap_num : tap_num + 1, cols] * pltpu.roll(projected[:, cols], tap_num, 0)
-        return acc
-
-    query, key, value = mixed(0), mixed(1), mixed(2)
-    query_ref[...] = query[0:rows]
-    row = lax.broadcasted_iota(jnp.int32, (edge, width), 0)
-    query_ref[0:edge, :] = jnp.where(row < taps_count - 1, 1.0, query[0:edge])
+    query_cols, cols = slice(0, width), slice(width, 3 * width)
+    mixed = short_mix(projected_of(normed, w_ref[:, cols]), short_ref[:, cols])
+    key, value = mixed[:, 0:width], mixed[:, width:]
     put_columns(packed_ref, 0, (key[0:rows] * value[0:rows]).astype(jnp.bfloat16).T)
-    rims = []
-    for part in (key, value, query):
-        rims += [part[0:edge], part[rows:]]
+    rims = [key[0:edge], key[rows:], value[0:edge], value[rows:]]
+    for begin, place in ((0, 0), (rows - 2 * edge, 2 * edge)):
+        some = projected_of(normed[begin : begin + 2 * edge], w_ref[:, query_cols])
+        rims.append(short_mix(some, short_ref[:, query_cols])[place : place + edge])
     rims.append(jnp.zeros((lane - 3 * rim_step, width), jnp.float32))
     put_rim(packed_ref, 2 * rows, jnp.concatenate(rims).T)
     for copy in copies[4:]:
@@ -266,25 +284,25 @@
 
 
 def permute(array, partner):
-    return lax.ppermute(array, seq, [(i, partner(i)) for i in range(lax.axis_size(seq))])
+    pairs = [(i, partner(i)) for i in range(lax.axis_size(seq))]
+    return lax.ppermute(array, seq, [(i, j) for i, j in pairs if j != i])
 
 
 def bf16(*shape):
     return jax.ShapeDtypeStruct(shape, jnp.bfloat16)
 
 
-def exchange(keep, give, near, home):
+def exchange(keep, give, home):
     block, turns = keep.shape[2:], keep.shape[0]
     got = permute(give, lambda i: i ^ 1)
-    near = permute(near, lambda i: i ^ 2)
-    far = call(
+    moved = call(
         merge_body, (bf16(2, 2, *block),) * turns, (keep, got), [pltpu.VMEM] * 2, moved=4 * keep.size
     )
-    routes = routes_of(lax.axis_size("chip"))
-    far = [permute(part, lambda i: i ^ 2 * route[i % 2]) for part, route in zip(far, routes)]
-    half = bf16(2 * turns + 2, *block)
+    routes = routes_of(lax.axis_size("chip")) + [(0, 1)]
+    moved = [permute(part, lambda i: i ^ 2 * route[i % 2]) for part, route in zip(moved, routes)]
+    half = bf16(2 * turns + 1, *block)
     keep, give = call(
-        split_body, (half, half), (*far, near, home), [pltpu.VMEM] * (turns + 2), moved=4 * keep.size
+        split_body, (half, half), (*moved, home), [pltpu.VMEM] * (turns + 1), moved=4 * keep.size
     )
     return keep, permute(give, lambda i: i ^ 1)
 
@@ -304,8 +322,8 @@
     def pieces(shape):
         if not staged:
             return (bf16(*shape),), []
-        block, turns = shape[1:], len(routes_of(chips))
-        outs = [bf16(turns, 2, *block)] * 2 + [bf16(2, *block)] * 2
+        block, turns = shape[1:], len(routes_of(chips)) + 1
+        outs = [bf16(turns, 2, *block)] * 2 + [bf16(2, *block)]
         return tuple(outs), [pltpu.VMEM(shape, jnp.bfloat16)]
 
     def swap(parts):
@@ -315,12 +333,20 @@
         blocks = array.reshape(devices, -1, array.shape[-1])
         return (lax.all_to_all(blocks, seq, split_axis=0, concat_axis=0).reshape(array.shape),)
 
+    query = call(
+        query_body,
+        jax.ShapeDtypeStruct((rows, width), jnp.float32),
+        (tokens, norm_gain[None, :], w_in, short_filter),
+        [pltpu.VMEM] * 4,
+        flops=2 * rows * width * width,
+        moved=800_000,
+    )
     args = (tokens, norm_gain[None, :], w_in, short_filter, long_filter, medium_filter, skip_gain[None, :])
     args = tuple(pltpu.with_memory_space_constraint(arg, pltpu.HBM) for arg in args)
     outs, packed_scratch = pieces(packed_shape)
-    query, *parts = call(
+    parts = call(
         prepare_body,
-        (jax.ShapeDtypeStruct((rows, width), jnp.float32), *outs),
+        outs,
         args,
         [pltpu.HBM] * len(args),
         packed_scratch

time: 31.4 us -> 32.8 us (1.045)
  waiting for transfers between devices: 12.3 us -> 13.3 us
    ppermute x12, waiting for transfers between devices: 12.3 us -> 13.3 us  [permute(): return lax.ppermute(array, seq, [(i, j) for i, j in pairs if j != i])]
    pallas_call x7 -> x8, Pallas kernels: 4.32 us -> 4.57 us  [call(): pl.pallas_call(body, out_shape=outs, in_specs=[whole(space) for space in...]
  transfers between devices with their start and end apart: 12 -> 12, of which waited for: 10 -> 10; matrix products, arithmetic and copies ran while one was open for 0% -> 0% of each run, Pallas kernels for 0% -> 1%
where the time goes in v10:
time: 32.8 us; the launch traced here: 32.6 us
  starting transfers between devices  14.7 us (45%)
  waiting for transfers between devices  13.3 us (41%)
  Pallas kernels  4.57 us (14%)
    ppermute x12, starting transfers between devices, permute(): return lax.ppermute(array, seq, [(i, j) for i, j in pairs if j != i])  14.7 us
    ppermute x12, waiting for transfers between devices, permute(): return lax.ppermute(array, seq, [(i, j) for i, j in pairs if j != i])  13.3 us
    pallas_call x8, Pallas kernels, call(): pl.pallas_call(body, out_shape=outs, in_specs=[whole(space) for space in...  4.57 us
  transfers between devices with their start and end apart: 12, of which 10 were waited for; matrix products, arithmetic and copies ran while one was open for 0% of the time, Pallas kernels for 1%

profile of v10, /device:TPU:0, one launch (start us, length us, event | category | flops | bytes accessed | tf_op | source)
XLA Modules:
  0.0 32.6 jit_solution(2259191874315076008)
XLA Ops:
  0.0 1.9 %shard_map.110 = (bf16[4,2,72,128]{3,2,1,0:T(8,128)(2,1)S(1)}, bf16[4,2,72,128]{3,2,1,0:T(8,128)(2,1)S(1)}, bf16[2,72,128]{2,1,0:T(8,128)(2,1)S(1)}) custom-call(bf16[256,256]{1,0:T(8,128)(2,1)} %refs_0_.1, f32[1,256]{1,0:T(1,128)} %bitcast.2, bf16[256,768]{1,0:T(8,128)(2,1)} %refs_2_.1, f32[3,768]{1,0:T(4,128)} %refs_3_.1, f32[256,256]{1,0:T(8,128)} %refs_4_.1, ...), custom_call_target="tpu_custom_call" | custom-call | flops 100663296 | bytes 1500000 | tf_op jit(solution)/shard_map/pallas_call | solution.py:25
  1.9 0.5 %collective-permute-start = (bf16[4,2,72,128]{3,2,1,0:T(8,128)(2,1)S(1)}, bf16[4,2,72,128]{3,2,1,0:T(8,128)(2,1)S(1)}, u32[]{:S(2)}, u32[]{:S(2)}) collective-permute-start(bf16[4,2,72,128]{3,2,1,0:T(8,128)(2,1)S(1)} %get-tuple-element.24), channel_id=1, source_target_pairs={{0,1},{1,0},{2,3},{3,2},{4,5},{5,4},{6,7},{7,6},{8,9},{9,8},{10,11... | collective-permute-start | bytes 442376 | tf_op jit(solution)/shard_map/ppermute | solution.py:288
  2.4 1.0 %collective-permute-done.got_ref = bf16[4,2,72,128]{3,2,1,0:T(8,128)(2,1)S(1)} collective-permute-done((bf16[4,2,72,128]{3,2,1,0:T(8,128)(2,1)S(1)}, bf16[4,2,72,128]{3,2,1,0:T(8,128)(2,1)S(1)}, u32[]{:S(2)}, u32[]{:S(2)}) %collective-permute-start) | collective-permute-done | bytes 147488 | tf_op jit(solution)/shard_map/ppermute | solution.py:288
  3.4 0.0 copy-start.5
  3.4 0.0 copy-start.6
  3.4 5.0 %collective-permute-start.1 = (bf16[2,2,72,128]{3,2,1,0:T(8,128)(2,1)S(1)}, bf16[2,2,72,128]{3,2,1,0:T(8,128)(2,1)S(1)}, u32[]{:S(2)}, u32[]{:S(2)}) collective-permute-start(bf16[2,2,72,128]{3,2,1,0:T(8,128)(2,1)S(1)} %get-tuple-element.25), channel_id=1, source_target_pairs={{0,10},{1,9},{2,8},{3,11},{4,14},{5,13},{6,12},{7,15},{8,2},{9,1},... | collective-permute-start | bytes 221192 | tf_op jit(solution)/shard_map/ppermute | solution.py:288
  8.4 1.3 %collective-permute-start.2 = (bf16[2,2,72,128]{3,2,1,0:T(8,128)(2,1)S(1)}, bf16[2,2,72,128]{3,2,1,0:T(8,128)(2,1)S(1)}, u32[]{:S(2)}, u32[]{:S(2)}) collective-permute-start(bf16[2,2,72,128]{3,2,1,0:T(8,128)(2,1)S(1)} %get-tuple-element.26), channel_id=1, source_target_pairs={{0,12},{1,15},{2,14},{3,13},{4,8},{5,11},{6,10},{7,9},{8,4},{9,7},... | collective-permute-start | bytes 221192 | tf_op jit(solution)/shard_map/ppermute | solution.py:288
  9.7 0.2 collective-permute-start.3
  9.9 0.7 %collective-permute-start.4 = (bf16[2,2,72,128]{3,2,1,0:T(8,128)(2,1)S(1)}, bf16[2,2,72,128]{3,2,1,0:T(8,128)(2,1)S(1)}, u32[]{:S(2)}, u32[]{:S(2)}) collective-permute-start(bf16[2,2,72,128]{3,2,1,0:T(8,128)(2,1)S(1)} %get-tuple-element.28), channel_id=1, source_target_pairs={{1,3},{3,1},{5,7},{7,5},{9,11},{11,9},{13,15},{15,13},{17,19},{19,... | collective-permute-start | bytes 221192 | tf_op jit(solution)/shard_map/ppermute | solution.py:288
  10.6 3.3 %collective-permute-done.1.refs_0_ = bf16[2,2,72,128]{3,2,1,0:T(8,128)(2,1)S(1)} collective-permute-done((bf16[2,2,72,128]{3,2,1,0:T(8,128)(2,1)S(1)}, bf16[2,2,72,128]{3,2,1,0:T(8,128)(2,1)S(1)}, u32[]{:S(2)}, u32[]{:S(2)}) %collective-permute-start.1) | collective-permute-done | bytes 73760 | tf_op jit(solution)/shard_map/ppermute | solution.py:288
  13.9 1.1 %collective-permute-done.2.refs_1_ = bf16[2,2,72,128]{3,2,1,0:T(8,128)(2,1)S(1)} collective-permute-done((bf16[2,2,72,128]{3,2,1,0:T(8,128)(2,1)S(1)}, bf16[2,2,72,128]{3,2,1,0:T(8,128)(2,1)S(1)}, u32[]{:S(2)}, u32[]{:S(2)}) %collective-permute-start.2) | collective-permute-done | bytes 73760 | tf_op jit(solution)/shard_map/ppermute | solution.py:288
  15.1 0.5 %collective-permute-done.3.refs_2_ = bf16[2,2,72,128]{3,2,1,0:T(8,128)(2,1)S(1)} collective-permute-done((bf16[2,2,72,128]{3,2,1,0:T(8,128)(2,1)S(1)}, bf16[2,2,72,128]{3,2,1,0:T(8,128)(2,1)S(1)}, u32[]{:S(2)}, u32[]{:S(2)}) %collective-permute-start.3) | collective-permute-done | bytes 73760 | tf_op jit(solution)/shard_map/ppermute | solution.py:288
  15.5 0.0 collective-permute-done.4.refs_3_
  15.5 0.0 copy-start.7
  15.6 0.1 collective-permute-start.5
  15.7 1.4 %collective-permute-done.5.refs_1_ = bf16[9,72,128]{2,1,0:T(8,128)(2,1)S(1)} collective-permute-done((bf16[9,72,128]{2,1,0:T(8,128)(2,1)S(1)}, bf16[9,72,128]{2,1,0:T(8,128)(2,1)S(1)}, u32[]{:S(2)}, u32[]{:S(2)}) %collective-permute-start.5) | collective-permute-done | bytes 165920 | tf_op jit(solution)/shard_map/ppermute | solution.py:288
  17.0 0.0 copy-done.5
  17.0 0.0 copy-done.6
  17.0 0.0 copy-done.7
  17.1 0.0 copy-start
  17.1 1.4 %shard_map.113 = (bf16[4,2,16,256]{3,2,1,0:T(8,128)(2,1)S(1)}, bf16[4,2,16,256]{3,2,1,0:T(8,128)(2,1)S(1)}, bf16[2,16,256]{2,1,0:T(8,128)(2,1)S(1)}) custom-call(bf16[512,256]{1,0:T(8,128)(2,1)S(1)} %copy-done.5, f32[32,256]{1,0:T(8,128)S(1)} %copy-done.7, bf16[256,512]{1,0:T(8,128)(2,1)S(1)} %copy-done.6, ...), custom_call_target="tpu_custom_call" | custom-call | flops 603979776 | bytes 2000000 | tf_op jit(solution)/shard_map/pallas_call | solution.py:25
  18.5 0.2 collective-permute-start.6
  18.7 1.1 %collective-permute-done.6.got_ref = bf16[4,2,16,256]{3,2,1,0:T(8,128)(2,1)S(1)} collective-permute-done((bf16[4,2,16,256]{3,2,1,0:T(8,128)(2,1)S(1)}, bf16[4,2,16,256]{3,2,1,0:T(8,128)(2,1)S(1)}, u32[]{:S(2)}, u32[]{:S(2)}) %collective-permute-start.6) | collective-permute-done | bytes 65568 | tf_op jit(solution)/shard_map/ppermute | solution.py:288
  19.8 0.0 copy-start.1
  19.8 0.8 %collective-permute-start.10 = (bf16[2,2,16,256]{3,2,1,0:T(8,128)(2,1)S(1)}, bf16[2,2,16,256]{3,2,1,0:T(8,128)(2,1)S(1)}, u32[]{:S(2)}, u32[]{:S(2)}) collective-permute-start(bf16[2,2,16,256]{3,2,1,0:T(8,128)(2,1)S(1)} %get-tuple-element.37), channel_id=1, source_target_pairs={{1,3},{3,1},{5,7},{7,5},{9,11},{11,9},{13,15},{15,13},{17,19},{19,... | collective-permute-start | bytes 98312 | tf_op jit(solution)/shard_map/ppermute | solution.py:288
  20.6 2.9 %collective-permute-start.7 = (bf16[2,2,16,256]{3,2,1,0:T(8,128)(2,1)S(1)}, bf16[2,2,16,256]{3,2,1,0:T(8,128)(2,1)S(1)}, u32[]{:S(2)}, u32[]{:S(2)}) collective-permute-start(bf16[2,2,16,256]{3,2,1,0:T(8,128)(2,1)S(1)} %get-tuple-element.34), channel_id=1, source_target_pairs={{0,10},{1,9},{2,8},{3,11},{4,14},{5,13},{6,12},{7,15},{8,2},{9,1},... | collective-permute-start | bytes 98312 | tf_op jit(solution)/shard_map/ppermute | solution.py:288
  23.6 0.9 %collective-permute-start.8 = (bf16[2,2,16,256]{3,2,1,0:T(8,128)(2,1)S(1)}, bf16[2,2,16,256]{3,2,1,0:T(8,128)(2,1)S(1)}, u32[]{:S(2)}, u32[]{:S(2)}) collective-permute-start(bf16[2,2,16,256]{3,2,1,0:T(8,128)(2,1)S(1)} %get-tuple-element.35), channel_id=1, source_target_pairs={{0,12},{1,15},{2,14},{3,13},{4,8},{5,11},{6,10},{7,9},{8,4},{9,7},... | collective-permute-start | bytes 98312 | tf_op jit(solution)/shard_map/ppermute | solution.py:288
  24.5 1.0 %collective-permute-start.9 = (bf16[2,2,16,256]{3,2,1,0:T(8,128)(2,1)S(1)}, bf16[2,2,16,256]{3,2,1,0:T(8,128)(2,1)S(1)}, u32[]{:S(2)}, u32[]{:S(2)}) collective-permute-start(bf16[2,2,16,256]{3,2,1,0:T(8,128)(2,1)S(1)} %get-tuple-element.36), channel_id=1, source_target_pairs={{0,6},{1,5},{2,4},{3,7},{4,2},{5,1},{6,0},{7,3},{8,14},{9,13},{10,... | collective-permute-start | bytes 98312 | tf_op jit(solution)/shard_map/ppermute | solution.py:288
  25.4 0.0 collective-permute-done.10.refs_3_
  25.5 1.0 %collective-permute-done.7.refs_0_ = bf16[2,2,16,256]{3,2,1,0:T(8,128)(2,1)S(1)} collective-permute-done((bf16[2,2,16,256]{3,2,1,0:T(8,128)(2,1)S(1)}, bf16[2,2,16,256]{3,2,1,0:T(8,128)(2,1)S(1)}, u32[]{:S(2)}, u32[]{:S(2)}) %collective-permute-start.7) | collective-permute-done | bytes 32800 | tf_op jit(solution)/shard_map/ppermute | solution.py:288
  26.4 3.1 %collective-permute-done.8.refs_1_ = bf16[2,2,16,256]{3,2,1,0:T(8,128)(2,1)S(1)} collective-permute-done((bf16[2,2,16,256]{3,2,1,0:T(8,128)(2,1)S(1)}, bf16[2,2,16,256]{3,2,1,0:T(8,128)(2,1)S(1)}, u32[]{:S(2)}, u32[]{:S(2)}) %collective-permute-start.8) | collective-permute-done | bytes 32800 | tf_op jit(solution)/shard_map/ppermute | solution.py:288
  29.5 0.2 collective-permute-done.9.refs_2_
  29.7 0.0 copy-start.3
  29.7 0.0 copy-start.4
  29.7 0.0 copy-start.2
  29.7 1.1 %collective-permute-start.11 = (bf16[9,16,256]{2,1,0:T(8,128)(2,1)S(1)}, bf16[9,16,256]{2,1,0:T(8,128)(2,1)S(1)}, u32[]{:S(2)}, u32[]{:S(2)}) collective-permute-start(bf16[9,16,256]{2,1,0:T(8,128)(2,1)S(1)} %get-tuple-element.40), channel_id=1, source_target_pairs={{0,1},{1,0},{2,3},{3,2},{4,5},{5,4},{6,7},{7,6},{8,9},{9,8},{10,11... | collective-permute-start | bytes 221192 | tf_op jit(solution)/shard_map/ppermute | solution.py:288
  30.8 0.0 copy-done
  30.8 0.0 copy-done.1
  30.8 0.0 copy-done.3
  30.8 0.0 copy-done.4
  30.8 0.3 shard_map.109.query_ref
  31.1 0.6 %collective-permute-done.11.refs_1_ = bf16[9,16,256]{2,1,0:T(8,128)(2,1)S(1)} collective-permute-done((bf16[9,16,256]{2,1,0:T(8,128)(2,1)S(1)}, bf16[9,16,256]{2,1,0:T(8,128)(2,1)S(1)}, u32[]{:S(2)}, u32[]{:S(2)}) %collective-permute-start.11) | collective-permute-done | bytes 73760 | tf_op jit(solution)/shard_map/ppermute | solution.py:288
  31.7 0.0 copy-done.2
  31.7 0.9 %shard_map.116 = bf16[256,256]{1,0:T(8,128)(2,1)} custom-call(f32[256,256]{1,0:T(8,128)S(1)} %shard_map.109.query_ref, bf16[256,256]{1,0:T(8,128)(2,1)S(1)} %copy-done.2, bf16[9,16,256]{2,1,0:T(8,128)(2,1)S(1)} %get-tuple-element.39.refs_0_, bf16[9,16,256]{2,1,0:T(8,128)(2,1)S(1)} %collective-permute-done.11.refs_1_), custom_call_target="tpu_custom_call" | custom-call | flops 33554432 | bytes 600000 | tf_op jit(solution)/shard_map/pallas_call | solution.py:25
  (4 shorter events, 0.1 us)
Async XLA Ops:
  1.9 1.5 %collective-permute-start = (bf16[4,2,72,128]{3,2,1,0:T(8,128)(2,1)S(1)}, bf16[4,2,72,128]{3,2,1,0:T(8,128)(2,1)S(1)}, u32[]{:S(2)}, u32[]{:S(2)}) collective-permute-start(bf16[4,2,72,128]{3,2,1,0:T(8,128)(2,1)S(1)} %get-tuple-element.24), channel_id=1, source_target_pairs={{0,1},{1,0},{2,3},{3,2},{4,5},{5,4},{6,7},{7,6},{8,9},{9,8},{10,11... | collective-permute-start | bytes 442376 | tf_op jit(solution)/shard_map/ppermute | solution.py:288
  3.4 13.6 %copy-start.5 = (bf16[512,256]{1,0:T(8,128)(2,1)S(1)}, bf16[512,256]{1,0:T(8,128)(2,1)}, u32[]{:S(2)}) copy-start(bf16[512,256]{1,0:T(8,128)(2,1)} %constant.6.clone.first_ref) | copy-start | bytes 786436
  3.4 13.6 %copy-start.6 = (bf16[256,512]{1,0:T(8,128)(2,1)S(1)}, bf16[256,512]{1,0:T(8,128)(2,1)}, u32[]{:S(2)}) copy-start(bf16[256,512]{1,0:T(8,128)(2,1)} %constant.8.clone.inner_ref) | copy-start | bytes 786436
  3.4 10.5 %collective-permute-start.1 = (bf16[2,2,72,128]{3,2,1,0:T(8,128)(2,1)S(1)}, bf16[2,2,72,128]{3,2,1,0:T(8,128)(2,1)S(1)}, u32[]{:S(2)}, u32[]{:S(2)}) collective-permute-start(bf16[2,2,72,128]{3,2,1,0:T(8,128)(2,1)S(1)} %get-tuple-element.25), channel_id=1, source_target_pairs={{0,10},{1,9},{2,8},{3,11},{4,14},{5,13},{6,12},{7,15},{8,2},{9,1},... | collective-permute-start | bytes 221192 | tf_op jit(solution)/shard_map/ppermute | solution.py:288
  8.4 6.7 %collective-permute-start.2 = (bf16[2,2,72,128]{3,2,1,0:T(8,128)(2,1)S(1)}, bf16[2,2,72,128]{3,2,1,0:T(8,128)(2,1)S(1)}, u32[]{:S(2)}, u32[]{:S(2)}) collective-permute-start(bf16[2,2,72,128]{3,2,1,0:T(8,128)(2,1)S(1)} %get-tuple-element.26), channel_id=1, source_target_pairs={{0,12},{1,15},{2,14},{3,13},{4,8},{5,11},{6,10},{7,9},{8,4},{9,7},... | collective-permute-start | bytes 221192 | tf_op jit(solution)/shard_map/ppermute | solution.py:288
  9.7 5.8 %collective-permute-start.3 = (bf16[2,2,72,128]{3,2,1,0:T(8,128)(2,1)S(1)}, bf16[2,2,72,128]{3,2,1,0:T(8,128)(2,1)S(1)}, u32[]{:S(2)}, u32[]{:S(2)}) collective-permute-start(bf16[2,2,72,128]{3,2,1,0:T(8,128)(2,1)S(1)} %get-tuple-element.27), channel_id=1, source_target_pairs={{0,6},{1,5},{2,4},{3,7},{4,2},{5,1},{6,0},{7,3},{8,14},{9,13},{10,... | collective-permute-start | bytes 221192 | tf_op jit(solution)/shard_map/ppermute | solution.py:288
  9.9 5.6 %collective-permute-start.4 = (bf16[2,2,72,128]{3,2,1,0:T(8,128)(2,1)S(1)}, bf16[2,2,72,128]{3,2,1,0:T(8,128)(2,1)S(1)}, u32[]{:S(2)}, u32[]{:S(2)}) collective-permute-start(bf16[2,2,72,128]{3,2,1,0:T(8,128)(2,1)S(1)} %get-tuple-element.28), channel_id=1, source_target_pairs={{1,3},{3,1},{5,7},{7,5},{9,11},{11,9},{13,15},{15,13},{17,19},{19,... | collective-permute-start | bytes 221192 | tf_op jit(solution)/shard_map/ppermute | solution.py:288
  15.5 1.5 %copy-start.7 = (f32[32,256]{1,0:T(8,128)S(1)}, f32[32,256]{1,0:T(8,128)}, u32[]{:S(2)}) copy-start(f32[32,256]{1,0:T(8,128)} %constant.7.clone.twist_ref) | copy-start | bytes 98308
  15.6 1.5 %collective-permute-start.5 = (bf16[9,72,128]{2,1,0:T(8,128)(2,1)S(1)}, bf16[9,72,128]{2,1,0:T(8,128)(2,1)S(1)}, u32[]{:S(2)}, u32[]{:S(2)}) collective-permute-start(bf16[9,72,128]{2,1,0:T(8,128)(2,1)S(1)} %get-tuple-element.31), channel_id=1, source_target_pairs={{0,1},{1,0},{2,3},{3,2},{4,5},{5,4},{6,7},{7,6},{8,9},{9,8},{10,11... | collective-permute-start | bytes 497672 | tf_op jit(solution)/shard_map/ppermute | solution.py:288
  17.1 13.8 %copy-start = (bf16[256,768]{1,0:T(8,128)(2,1)S(1)}, bf16[256,768]{1,0:T(8,128)(2,1)}, u32[]{:S(2)}) copy-start(bf16[256,768]{1,0:T(8,128)(2,1)} %refs_2_.1) | copy-start | bytes 1179652
  18.5 1.3 %collective-permute-start.6 = (bf16[4,2,16,256]{3,2,1,0:T(8,128)(2,1)S(1)}, bf16[4,2,16,256]{3,2,1,0:T(8,128)(2,1)S(1)}, u32[]{:S(2)}, u32[]{:S(2)}) collective-permute-start(bf16[4,2,16,256]{3,2,1,0:T(8,128)(2,1)S(1)} %get-tuple-element.33), channel_id=1, source_target_pairs={{0,1},{1,0},{2,3},{3,2},{4,5},{5,4},{6,7},{7,6},{8,9},{9,8},{10,11... | collective-permute-start | bytes 196616 | tf_op jit(solution)/shard_map/ppermute | solution.py:288
  19.8 11.0 %copy-start.1 = (bf16[256,256]{1,0:T(8,128)(2,1)S(1)}, bf16[256,256]{1,0:T(8,128)(2,1)}, u32[]{:S(2)}) copy-start(bf16[256,256]{1,0:T(8,128)(2,1)} %refs_0_.1) | copy-start | bytes 393220
  19.8 5.6 %collective-permute-start.10 = (bf16[2,2,16,256]{3,2,1,0:T(8,128)(2,1)S(1)}, bf16[2,2,16,256]{3,2,1,0:T(8,128)(2,1)S(1)}, u32[]{:S(2)}, u32[]{:S(2)}) collective-permute-start(bf16[2,2,16,256]{3,2,1,0:T(8,128)(2,1)S(1)} %get-tuple-element.37), channel_id=1, source_target_pairs={{1,3},{3,1},{5,7},{7,5},{9,11},{11,9},{13,15},{15,13},{17,19},{19,... | collective-permute-start | bytes 98312 | tf_op jit(solution)/shard_map/ppermute | solution.py:288
  20.6 5.8 %collective-permute-start.7 = (bf16[2,2,16,256]{3,2,1,0:T(8,128)(2,1)S(1)}, bf16[2,2,16,256]{3,2,1,0:T(8,128)(2,1)S(1)}, u32[]{:S(2)}, u32[]{:S(2)}) collective-permute-start(bf16[2,2,16,256]{3,2,1,0:T(8,128)(2,1)S(1)} %get-tuple-element.34), channel_id=1, source_target_pairs={{0,10},{1,9},{2,8},{3,11},{4,14},{5,13},{6,12},{7,15},{8,2},{9,1},... | collective-permute-start | bytes 98312 | tf_op jit(solution)/shard_map/ppermute | solution.py:288
  23.6 5.9 %collective-permute-start.8 = (bf16[2,2,16,256]{3,2,1,0:T(8,128)(2,1)S(1)}, bf16[2,2,16,256]{3,2,1,0:T(8,128)(2,1)S(1)}, u32[]{:S(2)}, u32[]{:S(2)}) collective-permute-start(bf16[2,2,16,256]{3,2,1,0:T(8,128)(2,1)S(1)} %get-tuple-element.35), channel_id=1, source_target_pairs={{0,12},{1,15},{2,14},{3,13},{4,8},{5,11},{6,10},{7,9},{8,4},{9,7},... | collective-permute-start | bytes 98312 | tf_op jit(solution)/shard_map/ppermute | solution.py:288
  24.5 5.2 %collective-permute-start.9 = (bf16[2,2,16,256]{3,2,1,0:T(8,128)(2,1)S(1)}, bf16[2,2,16,256]{3,2,1,0:T(8,128)(2,1)S(1)}, u32[]{:S(2)}, u32[]{:S(2)}) collective-permute-start(bf16[2,2,16,256]{3,2,1,0:T(8,128)(2,1)S(1)} %get-tuple-element.36), channel_id=1, source_target_pairs={{0,6},{1,5},{2,4},{3,7},{4,2},{5,1},{6,0},{7,3},{8,14},{9,13},{10,... | collective-permute-start | bytes 98312 | tf_op jit(solution)/shard_map/ppermute | solution.py:288
  29.7 1.1 %copy-start.3 = (f32[3,768]{1,0:T(4,128)S(1)}, f32[3,768]{1,0:T(4,128)}, u32[]{:S(2)}) copy-start(f32[3,768]{1,0:T(4,128)} %refs_3_.1) | copy-start | bytes 27652
  29.7 1.1 %copy-start.4 = (f32[256]{0:T(256)S(1)}, f32[256]{0:T(256)}, u32[]{:S(2)}) copy-start(f32[256]{0:T(256)} %param.12) | copy-start | bytes 3076
  29.7 2.0 %copy-start.2 = (bf16[256,256]{1,0:T(8,128)(2,1)S(1)}, bf16[256,256]{1,0:T(8,128)(2,1)}, u32[]{:S(2)}) copy-start(bf16[256,256]{1,0:T(8,128)(2,1)} %w_ref.3) | copy-start | bytes 393220
  29.7 2.0 %collective-permute-start.11 = (bf16[9,16,256]{2,1,0:T(8,128)(2,1)S(1)}, bf16[9,16,256]{2,1,0:T(8,128)(2,1)S(1)}, u32[]{:S(2)}, u32[]{:S(2)}) collective-permute-start(bf16[9,16,256]{2,1,0:T(8,128)(2,1)S(1)} %get-tuple-element.40), channel_id=1, source_target_pairs={{0,1},{1,0},{2,3},{3,2},{4,5},{5,4},{6,7},{7,6},{8,9},{9,8},{10,11... | collective-permute-start | bytes 221192 | tf_op jit(solution)/shard_map/ppermute | solution.py:288

commit v11 on v10

--- a/solution.py
+++ b/solution.py
@@ -56,7 +56,7 @@
 
 def routes_of(chips):
     far = sorted(range(2, chips, 2), key=lambda d: (-d.bit_length(), d))
-    return [(d + 1, d) if turn % 2 == 0 else (d, d + 1) for turn, d in enumerate(far)]
+    return [(d, d + 1) for d in far]
 
 
 def carried(route, core):
@@ -64,19 +64,17 @@
     return jnp.where(core == 0, mine, others), jnp.where(core == 0, others, mine)
 
 
-def put_routes(source_ref, keep_ref, give_ref, home_ref):
+def put_routes(source_ref, keep_ref, give_ref, near_ref, home_ref):
     chip, core = lax.axis_index("chip"), lax.axis_index("core")
 
     def blocks(distance):
         return source_ref[pl.ds((chip ^ distance) * 2, 2)]
 
-    routes = routes_of(source_ref.shape[0] // 2)
-    for turn, route in enumerate(routes):
+    for turn, route in enumerate(routes_of(source_ref.shape[0] // 2)):
         own, other = carried(route, core)
         keep_ref[turn] = blocks(own)
         give_ref[turn] = blocks(other)
-    keep_ref[len(routes)] = blocks(1)
-    give_ref[len(routes)] = blocks(1)
+    near_ref[...] = blocks(1)
     home_ref[...] = blocks(0)
 
 
@@ -87,13 +85,14 @@
 
 
 def split_body(*refs):
-    moved_refs, (home_ref, keep_ref, give_ref) = refs[:-3], refs[-3:]
+    far_refs, (near_ref, home_ref, keep_ref, give_ref) = refs[:-4], refs[-4:]
     core = lax.axis_index("core")
     for out_ref, target in ((keep_ref, core), (give_ref, 1 - core)):
-        for turn, moved_ref in enumerate(moved_refs):
+        for turn, far_ref in enumerate(far_refs):
             for sender in range(2):
-                out_ref[2 * turn + sender] = moved_ref[sender, target]
-        out_ref[2 * len(moved_refs)] = home_ref[target]
+                out_ref[2 * turn + sender] = far_ref[sender, target]
+        out_ref[2 * len(far_refs)] = near_ref[target]
+        out_ref[2 * len(far_refs) + 1] = home_ref[target]
 
 
 def take_routes(keep_ref, got_ref, target_ref):
@@ -105,12 +104,9 @@
         target_ref[(chip ^ own) * 2 + 1 - core] = keep_ref[2 * turn + 1]
         target_ref[(chip ^ other) * 2 + 1 - core] = got_ref[2 * turn]
         target_ref[(chip ^ other) * 2 + core] = got_ref[2 * turn + 1]
-    near, home = 2 * len(routes), 2 * len(routes) + 2
-    for sender in range(2):
-        block = jnp.where(core == 1, keep_ref[near + sender], got_ref[near + sender])
-        target_ref[(chip ^ 1) * 2 + 1 - sender] = block
-    target_ref[chip * 2 + core] = keep_ref[home]
-    target_ref[chip * 2 + 1 - core] = got_ref[home]
+    for place, distance in ((2 * len(routes), 1), (2 * len(routes) + 1, 0)):
+        target_ref[(chip ^ distance) * 2 + core] = keep_ref[place]
+        target_ref[(chip ^ distance) * 2 + 1 - core] = got_ref[place]
 
 
 def normed_of(tokens_ref, gain_ref):
@@ -147,33 +143,50 @@
     outs, packed_ref = (outs[:-1], outs[-1]) if staged else (outs, outs[0])
     tokens_ref, gain_ref, w_ref, short_ref, long_ref, medium_ref, skip_ref = held
     rows, width = tokens_ref.shape
-    copies = [pltpu.make_async_copy(h, v, sems.at[i]) for i, (h, v) in enumerate(zip(hbm, held))]
+    is_first = lax.axis_index(seq) == 0
+    query_cols, cols = slice(0, width), slice(width, 3 * width)
+
+    def copy_of(index, sem, part=slice(None)):
+        return pltpu.make_async_copy(hbm[index].at[:, part], held[index].at[:, part], sems.at[sem])
+
+    copies = [copy_of(0, 0), copy_of(1, 1), copy_of(2, 2, cols), copy_of(3, 3), copy_of(4, 4)]
+    copies.append(copy_of(2, 7, query_cols))
+    extra = [copy_of(5, 5), copy_of(6, 6)]
     for copy in copies:
         copy.start()
+
+    @pl.when(is_first)
+    def _():
+        for copy in extra:
+            copy.start()
+
     copies[0].wait()
     copies[1].wait()
     normed = normed_of(tokens_ref, gain_ref)
     copies[2].wait()
     copies[3].wait()
-    query_cols, cols = slice(0, width), slice(width, 3 * width)
     mixed = short_mix(projected_of(normed, w_ref[:, cols]), short_ref[:, cols])
     key, value = mixed[:, 0:width], mixed[:, width:]
     put_columns(packed_ref, 0, (key[0:rows] * value[0:rows]).astype(jnp.bfloat16).T)
+    copies[5].wait()
     rims = [key[0:edge], key[rows:], value[0:edge], value[rows:]]
     for begin, place in ((0, 0), (rows - 2 * edge, 2 * edge)):
         some = projected_of(normed[begin : begin + 2 * edge], w_ref[:, query_cols])
         rims.append(short_mix(some, short_ref[:, query_cols])[place : place + edge])
     rims.append(jnp.zeros((lane - 3 * rim_step, width), jnp.float32))
     put_rim(packed_ref, 2 * rows, jnp.concatenate(rims).T)
-    for copy in copies[4:]:
-        copy.wait()
-    med_len = medium_ref.shape[0]
-    is_first = jnp.where(lax.axis_index(seq) == 0, 1.0, 0.0)
-    head = long_ref[0:med_len, :] + is_first * medium_ref[...]
-    head_row = lax.broadcasted_iota(jnp.int32, head.shape, 0)
-    head = head + jnp.where(head_row == 0, is_first * skip_ref[...], 0.0)
-    taps = jnp.concatenate([head, long_ref[med_len:, :]]).astype(jnp.bfloat16)
-    put_columns(packed_ref, rows, taps.T)
+    copies[4].wait()
+
+    @pl.when(is_first)
+    def _():
+        for copy in extra:
+            copy.wait()
+        med_len = medium_ref.shape[0]
+        head_row = lax.broadcasted_iota(jnp.int32, medium_ref.shape, 0)
+        direct = jnp.where(head_row == 0, skip_ref[...], 0.0)
+        long_ref[0:med_len, :] = long_ref[0:med_len, :] + medium_ref[...] + direct
+
+    put_columns(packed_ref, rows, long_ref[...].astype(jnp.bfloat16).T)
     if staged:
         put_routes(packed_ref, *outs)
 
@@ -284,25 +297,25 @@
 
 
 def permute(array, partner):
-    pairs = [(i, partner(i)) for i in range(lax.axis_size(seq))]
-    return lax.ppermute(array, seq, [(i, j) for i, j in pairs if j != i])
+    return lax.ppermute(array, seq, [(i, partner(i)) for i in range(lax.axis_size(seq))])
 
 
 def bf16(*shape):
     return jax.ShapeDtypeStruct(shape, jnp.bfloat16)
 
 
-def exchange(keep, give, home):
+def exchange(keep, give, near, home):
     block, turns = keep.shape[2:], keep.shape[0]
     got = permute(give, lambda i: i ^ 1)
-    moved = call(
+    near = permute(near, lambda i: i ^ 2)
+    far = call(
         merge_body, (bf16(2, 2, *block),) * turns, (keep, got), [pltpu.VMEM] * 2, moved=4 * keep.size
     )
-    routes = routes_of(lax.axis_size("chip")) + [(0, 1)]
-    moved = [permute(part, lambda i: i ^ 2 * route[i % 2]) for part, route in zip(moved, routes)]
-    half = bf16(2 * turns + 1, *block)
+    routes = routes_of(lax.axis_size("chip"))
+    far = [permute(part, lambda i: i ^ 2 * route[i % 2]) for part, route in zip(far, routes)]
+    half = bf16(2 * turns + 2, *block)
     keep, give = call(
-        split_body, (half, half), (*moved, home), [pltpu.VMEM] * (turns + 1), moved=4 * keep.size
+        split_body, (half, half), (*far, near, home), [pltpu.VMEM] * (turns + 2), moved=4 * keep.size
     )
     return keep, permute(give, lambda i: i ^ 1)
 
@@ -322,8 +335,8 @@
     def pieces(shape):
         if not staged:
             return (bf16(*shape),), []
-        block, turns = shape[1:], len(routes_of(chips)) + 1
-        outs = [bf16(turns, 2, *block)] * 2 + [bf16(2, *block)]
+        block, turns = shape[1:], len(routes_of(chips))
+        outs = [bf16(turns, 2, *block)] * 2 + [bf16(2, *block)] * 2
         return tuple(outs), [pltpu.VMEM(shape, jnp.bfloat16)]
 
     def swap(parts):
@@ -351,7 +364,7 @@
         [pltpu.HBM] * len(args),
         packed_scratch
         + [pltpu.VMEM(arg.shape, arg.dtype) for arg in args]
-        + [pltpu.SemaphoreType.DMA((len(args),))],
+        + [pltpu.SemaphoreType.DMA((len(args) + 1,))],
         flops=2 * rows * width * 3 * width,
         moved=1_500_000,
     )

time: 32.8 us -> 31 us (0.945)
  waiting for transfers between devices: 13.3 us -> 11.7 us
  starting transfers between devices: 14.7 us -> 14.1 us
    ppermute x12, waiting for transfers between devices: 13.3 us -> 11.7 us  [permute(): lax.ppermute(array, seq, [(i, partner(i)) for i in range(lax.axis_size(se...]
    ppermute x12, starting transfers between devices: 14.7 us -> 14.1 us  [permute(): lax.ppermute(array, seq, [(i, partner(i)) for i in range(lax.axis_size(se...]
  transfers between devices with their start and end apart: 12 -> 12, of which waited for: 10 -> 9; matrix products, arithmetic and copies ran while one was open for 0% -> 0% of each run, Pallas kernels for 1% -> 1%
where the time goes in v11:
time: 31 us; the launch traced here: 30.8 us
  starting transfers between devices  14.1 us (45%)
  waiting for transfers between devices  11.7 us (38%)
  Pallas kernels  4.7 us (15%)
    ppermute x12, starting transfers between devices, permute(): lax.ppermute(array, seq, [(i, partner(i)) for i in range(lax.axis_size(se...  14.1 us
    ppermute x12, waiting for transfers between devices, permute(): lax.ppermute(array, seq, [(i, partner(i)) for i in range(lax.axis_size(se...  11.7 us
    pallas_call x8, Pallas kernels, call(): pl.pallas_call(body, out_shape=outs, in_specs=[whole(space) for space in...  4.7 us
  transfers between devices with their start and end apart: 12, of which 9 were waited for; matrix products, arithmetic and copies ran while one was open for 0% of the time, Pallas kernels for 1%

profile of v11, /device:TPU:0, one launch (start us, length us, event | category | flops | bytes accessed | tf_op | source)
XLA Modules:
  0.0 30.8 jit_solution(8263597295822176533)
XLA Ops:
  0.0 0.0 copy-start.7
  0.0 2.0 %shard_map.110 = (bf16[3,2,72,128]{3,2,1,0:T(8,128)(2,1)S(1)}, bf16[3,2,72,128]{3,2,1,0:T(8,128)(2,1)S(1)}, bf16[2,72,128]{2,1,0:T(8,128)(2,1)S(1)}, bf16[2,72,128]{2,1,0:T(8,128)(2,1)S(1)}) custom-call(bf16[256,256]{1,0:T(8,128)(2,1)} %refs_0_.1, f32[1,256]{1,0:T(1,128)} %bitcast.2, bf16[256,768]{1,0:T(8,128)(2,1)} %refs_2_.1, f32[3,768]{1,0:T(4,128)} %refs_3_.1, ...), custom_call_target="tpu_custom_call" | custom-call | flops 100663296 | bytes 1500000 | tf_op jit(solution)/shard_map/pallas_call | solution.py:25
  2.0 0.5 %collective-permute-start = (bf16[3,2,72,128]{3,2,1,0:T(8,128)(2,1)S(1)}, bf16[3,2,72,128]{3,2,1,0:T(8,128)(2,1)S(1)}, u32[]{:S(2)}, u32[]{:S(2)}) collective-permute-start(bf16[3,2,72,128]{3,2,1,0:T(8,128)(2,1)S(1)} %get-tuple-element.24), channel_id=1, source_target_pairs={{0,1},{1,0},{2,3},{3,2},{4,5},{5,4},{6,7},{7,6},{8,9},{9,8},{10,11... | collective-permute-start | bytes 331784 | tf_op jit(solution)/shard_map/ppermute | solution.py:300
  2.5 1.0 %collective-permute-done.got_ref = bf16[3,2,72,128]{3,2,1,0:T(8,128)(2,1)S(1)} collective-permute-done((bf16[3,2,72,128]{3,2,1,0:T(8,128)(2,1)S(1)}, bf16[3,2,72,128]{3,2,1,0:T(8,128)(2,1)S(1)}, u32[]{:S(2)}, u32[]{:S(2)}) %collective-permute-start) | collective-permute-done | bytes 110624 | tf_op jit(solution)/shard_map/ppermute | solution.py:300
  3.5 0.0 copy-start.5
  3.5 0.0 copy-start.6
  3.5 4.0 %collective-permute-start.1 = (bf16[2,2,72,128]{3,2,1,0:T(8,128)(2,1)S(1)}, bf16[2,2,72,128]{3,2,1,0:T(8,128)(2,1)S(1)}, u32[]{:S(2)}, u32[]{:S(2)}) collective-permute-start(bf16[2,2,72,128]{3,2,1,0:T(8,128)(2,1)S(1)} %get-tuple-element.25), channel_id=1, source_target_pairs={{0,8},{1,11},{2,10},{3,9},{4,12},{5,15},{6,14},{7,13},{8,0},{9,3},... | collective-permute-start | bytes 221192 | tf_op jit(solution)/shard_map/ppermute | solution.py:300
  7.5 1.3 %collective-permute-start.2 = (bf16[2,2,72,128]{3,2,1,0:T(8,128)(2,1)S(1)}, bf16[2,2,72,128]{3,2,1,0:T(8,128)(2,1)S(1)}, u32[]{:S(2)}, u32[]{:S(2)}) collective-permute-start(bf16[2,2,72,128]{3,2,1,0:T(8,128)(2,1)S(1)} %get-tuple-element.26), channel_id=1, source_target_pairs={{0,12},{1,15},{2,14},{3,13},{4,8},{5,11},{6,10},{7,9},{8,4},{9,7},... | collective-permute-start | bytes 221192 | tf_op jit(solution)/shard_map/ppermute | solution.py:300
  8.9 0.2 collective-permute-start.3
  9.1 1.5 %collective-permute-start.4 = (bf16[2,72,128]{2,1,0:T(8,128)(2,1)S(1)}, bf16[2,72,128]{2,1,0:T(8,128)(2,1)S(1)}, u32[]{:S(2)}, u32[]{:S(2)}) collective-permute-start(bf16[2,72,128]{2,1,0:T(8,128)(2,1)S(1)} %get-tuple-element.28), channel_id=1, source_target_pairs={{0,2},{1,3},{2,0},{3,1},{4,6},{5,7},{6,4},{7,5},{8,10},{9,11},{10,... | collective-permute-start | bytes 110600 | tf_op jit(solution)/shard_map/ppermute | solution.py:300
  10.6 2.9 %collective-permute-done.4.refs_3_ = bf16[2,72,128]{2,1,0:T(8,128)(2,1)S(1)} collective-permute-done((bf16[2,72,128]{2,1,0:T(8,128)(2,1)S(1)}, bf16[2,72,128]{2,1,0:T(8,128)(2,1)S(1)}, u32[]{:S(2)}, u32[]{:S(2)}) %collective-permute-start.4) | collective-permute-done | bytes 36896 | tf_op jit(solution)/shard_map/ppermute | solution.py:300
  13.6 0.0 collective-permute-done.1.refs_0_
  13.6 0.9 %collective-permute-done.2.refs_1_ = bf16[2,2,72,128]{3,2,1,0:T(8,128)(2,1)S(1)} collective-permute-done((bf16[2,2,72,128]{3,2,1,0:T(8,128)(2,1)S(1)}, bf16[2,2,72,128]{3,2,1,0:T(8,128)(2,1)S(1)}, u32[]{:S(2)}, u32[]{:S(2)}) %collective-permute-start.2) | collective-permute-done | bytes 73760 | tf_op jit(solution)/shard_map/ppermute | solution.py:300
  14.5 0.8 %collective-permute-done.3.refs_2_ = bf16[2,2,72,128]{3,2,1,0:T(8,128)(2,1)S(1)} collective-permute-done((bf16[2,2,72,128]{3,2,1,0:T(8,128)(2,1)S(1)}, bf16[2,2,72,128]{3,2,1,0:T(8,128)(2,1)S(1)}, u32[]{:S(2)}, u32[]{:S(2)}) %collective-permute-start.3) | collective-permute-done | bytes 73760 | tf_op jit(solution)/shard_map/ppermute | solution.py:300
  15.3 0.3 collective-permute-start.5
  15.6 1.1 %collective-permute-done.5.refs_1_ = bf16[8,72,128]{2,1,0:T(8,128)(2,1)S(1)} collective-permute-done((bf16[8,72,128]{2,1,0:T(8,128)(2,1)S(1)}, bf16[8,72,128]{2,1,0:T(8,128)(2,1)S(1)}, u32[]{:S(2)}, u32[]{:S(2)}) %collective-permute-start.5) | collective-permute-done | bytes 147488 | tf_op jit(solution)/shard_map/ppermute | solution.py:300
  16.8 0.0 copy-done.7
  16.8 0.0 copy-done.5
  16.8 0.0 copy-done.6
  16.8 0.0 copy-start
  16.8 1.4 %shard_map.113 = (bf16[3,2,16,256]{3,2,1,0:T(8,128)(2,1)S(1)}, bf16[3,2,16,256]{3,2,1,0:T(8,128)(2,1)S(1)}, bf16[2,16,256]{2,1,0:T(8,128)(2,1)S(1)}, bf16[2,16,256]{2,1,0:T(8,128)(2,1)S(1)}) custom-call(bf16[512,256]{1,0:T(8,128)(2,1)S(1)} %copy-done.5, f32[32,256]{1,0:T(8,128)S(1)} %copy-done.7, bf16[256,512]{1,0:T(8,128)(2,1)S(1)} %copy-done.6, ...), custom_call_target="tpu_custom_call" | custom-call | flops 603979776 | bytes 2000000 | tf_op jit(solution)/shard_map/pallas_call | solution.py:25
  18.2 0.0 copy-start.1
  18.2 0.3 collective-permute-start.6
  18.5 1.0 %collective-permute-done.6.got_ref = bf16[3,2,16,256]{3,2,1,0:T(8,128)(2,1)S(1)} collective-permute-done((bf16[3,2,16,256]{3,2,1,0:T(8,128)(2,1)S(1)}, bf16[3,2,16,256]{3,2,1,0:T(8,128)(2,1)S(1)}, u32[]{:S(2)}, u32[]{:S(2)}) %collective-permute-start.6) | collective-permute-done | bytes 49184 | tf_op jit(solution)/shard_map/ppermute | solution.py:300
  19.5 3.1 %collective-permute-start.7 = (bf16[2,2,16,256]{3,2,1,0:T(8,128)(2,1)S(1)}, bf16[2,2,16,256]{3,2,1,0:T(8,128)(2,1)S(1)}, u32[]{:S(2)}, u32[]{:S(2)}) collective-permute-start(bf16[2,2,16,256]{3,2,1,0:T(8,128)(2,1)S(1)} %get-tuple-element.34), channel_id=1, source_target_pairs={{0,8},{1,11},{2,10},{3,9},{4,12},{5,15},{6,14},{7,13},{8,0},{9,3},... | collective-permute-start | bytes 98312 | tf_op jit(solution)/shard_map/ppermute | solution.py:300
  22.6 0.9 %collective-permute-start.8 = (bf16[2,2,16,256]{3,2,1,0:T(8,128)(2,1)S(1)}, bf16[2,2,16,256]{3,2,1,0:T(8,128)(2,1)S(1)}, u32[]{:S(2)}, u32[]{:S(2)}) collective-permute-start(bf16[2,2,16,256]{3,2,1,0:T(8,128)(2,1)S(1)} %get-tuple-element.35), channel_id=1, source_target_pairs={{0,12},{1,15},{2,14},{3,13},{4,8},{5,11},{6,10},{7,9},{8,4},{9,7},... | collective-permute-start | bytes 98312 | tf_op jit(solution)/shard_map/ppermute | solution.py:300
  23.5 0.5 %collective-permute-start.9 = (bf16[2,2,16,256]{3,2,1,0:T(8,128)(2,1)S(1)}, bf16[2,2,16,256]{3,2,1,0:T(8,128)(2,1)S(1)}, u32[]{:S(2)}, u32[]{:S(2)}) collective-permute-start(bf16[2,2,16,256]{3,2,1,0:T(8,128)(2,1)S(1)} %get-tuple-element.36), channel_id=1, source_target_pairs={{0,4},{1,7},{2,6},{3,5},{4,0},{5,3},{6,2},{7,1},{8,12},{9,15},{10,... | collective-permute-start | bytes 98312 | tf_op jit(solution)/shard_map/ppermute | solution.py:300
  24.0 1.0 %collective-permute-start.10 = (bf16[2,16,256]{2,1,0:T(8,128)(2,1)S(1)}, bf16[2,16,256]{2,1,0:T(8,128)(2,1)S(1)}, u32[]{:S(2)}, u32[]{:S(2)}) collective-permute-start(bf16[2,16,256]{2,1,0:T(8,128)(2,1)S(1)} %get-tuple-element.37), channel_id=1, source_target_pairs={{0,2},{1,3},{2,0},{3,1},{4,6},{5,7},{6,4},{7,5},{8,10},{9,11},{10,... | collective-permute-start | bytes 49160 | tf_op jit(solution)/shard_map/ppermute | solution.py:300
  25.0 2.9 %collective-permute-done.10.refs_3_ = bf16[2,16,256]{2,1,0:T(8,128)(2,1)S(1)} collective-permute-done((bf16[2,16,256]{2,1,0:T(8,128)(2,1)S(1)}, bf16[2,16,256]{2,1,0:T(8,128)(2,1)S(1)}, u32[]{:S(2)}, u32[]{:S(2)}) %collective-permute-start.10) | collective-permute-done | bytes 16416 | tf_op jit(solution)/shard_map/ppermute | solution.py:300
  27.9 0.0 collective-permute-done.7.refs_0_
  27.9 0.6 %collective-permute-done.8.refs_1_ = bf16[2,2,16,256]{3,2,1,0:T(8,128)(2,1)S(1)} collective-permute-done((bf16[2,2,16,256]{3,2,1,0:T(8,128)(2,1)S(1)}, bf16[2,2,16,256]{3,2,1,0:T(8,128)(2,1)S(1)}, u32[]{:S(2)}, u32[]{:S(2)}) %collective-permute-start.8) | collective-permute-done | bytes 32800 | tf_op jit(solution)/shard_map/ppermute | solution.py:300
  28.5 0.0 collective-permute-done.9.refs_2_
  28.5 0.0 copy-start.3
  28.5 0.0 copy-start.4
  28.5 0.0 copy-start.2
  28.5 0.5 %collective-permute-start.11 = (bf16[8,16,256]{2,1,0:T(8,128)(2,1)S(1)}, bf16[8,16,256]{2,1,0:T(8,128)(2,1)S(1)}, u32[]{:S(2)}, u32[]{:S(2)}) collective-permute-start(bf16[8,16,256]{2,1,0:T(8,128)(2,1)S(1)} %get-tuple-element.40), channel_id=1, source_target_pairs={{0,1},{1,0},{2,3},{3,2},{4,5},{5,4},{6,7},{7,6},{8,9},{9,8},{10,11... | collective-permute-start | bytes 196616 | tf_op jit(solution)/shard_map/ppermute | solution.py:300
  29.0 0.0 copy-done
  29.0 0.0 copy-done.1
  29.0 0.2 copy-done.3
  29.2 0.0 copy-done.4
  29.2 0.3 %shard_map.109.query_ref = f32[256,256]{1,0:T(8,128)S(1)} custom-call(bf16[256,256]{1,0:T(8,128)(2,1)S(1)} %copy-done.1, f32[1,256]{1,0:T(1,128)S(1)} %bitcast.3, bf16[256,768]{1,0:T(8,128)(2,1)S(1)} %copy-done, f32[3,768]{1,0:T(4,128)S(1)} %copy-done.3), custom_call_target="tpu_custom_call" | custom-call | flops 33554432 | bytes 800000 | tf_op jit(solution)/shard_map/pallas_call | solution.py:25
  29.5 0.4 %collective-permute-done.11.refs_1_ = bf16[8,16,256]{2,1,0:T(8,128)(2,1)S(1)} collective-permute-done((bf16[8,16,256]{2,1,0:T(8,128)(2,1)S(1)}, bf16[8,16,256]{2,1,0:T(8,128)(2,1)S(1)}, u32[]{:S(2)}, u32[]{:S(2)}) %collective-permute-start.11) | collective-permute-done | bytes 65568 | tf_op jit(solution)/shard_map/ppermute | solution.py:300
  29.9 0.0 copy-done.2
  29.9 0.9 %shard_map.116 = bf16[256,256]{1,0:T(8,128)(2,1)} custom-call(f32[256,256]{1,0:T(8,128)S(1)} %shard_map.109.query_ref, bf16[256,256]{1,0:T(8,128)(2,1)S(1)} %copy-done.2, bf16[8,16,256]{2,1,0:T(8,128)(2,1)S(1)} %get-tuple-element.39.refs_0_, bf16[8,16,256]{2,1,0:T(8,128)(2,1)S(1)} %collective-permute-done.11.refs_1_), custom_call_target="tpu_custom_call" | custom-call | flops 33554432 | bytes 600000 | tf_op jit(solution)/shard_map/pallas_call | solution.py:25
  (4 shorter events, 0.1 us)
Async XLA Ops:
  0.0 16.8 %copy-start.7 = (f32[32,256]{1,0:T(8,128)S(1)}, f32[32,256]{1,0:T(8,128)}, u32[]{:S(2)}) copy-start(f32[32,256]{1,0:T(8,128)} %constant.7.clone.twist_ref) | copy-start | bytes 98308
  2.0 1.5 %collective-permute-start = (bf16[3,2,72,128]{3,2,1,0:T(8,128)(2,1)S(1)}, bf16[3,2,72,128]{3,2,1,0:T(8,128)(2,1)S(1)}, u32[]{:S(2)}, u32[]{:S(2)}) collective-permute-start(bf16[3,2,72,128]{3,2,1,0:T(8,128)(2,1)S(1)} %get-tuple-element.24), channel_id=1, source_target_pairs={{0,1},{1,0},{2,3},{3,2},{4,5},{5,4},{6,7},{7,6},{8,9},{9,8},{10,11... | collective-permute-start | bytes 331784 | tf_op jit(solution)/shard_map/ppermute | solution.py:300
  3.5 13.3 %copy-start.5 = (bf16[512,256]{1,0:T(8,128)(2,1)S(1)}, bf16[512,256]{1,0:T(8,128)(2,1)}, u32[]{:S(2)}) copy-start(bf16[512,256]{1,0:T(8,128)(2,1)} %constant.6.clone.first_ref) | copy-start | bytes 786436
  3.5 13.3 %copy-start.6 = (bf16[256,512]{1,0:T(8,128)(2,1)S(1)}, bf16[256,512]{1,0:T(8,128)(2,1)}, u32[]{:S(2)}) copy-start(bf16[256,512]{1,0:T(8,128)(2,1)} %constant.8.clone.inner_ref) | copy-start | bytes 786436
  3.5 10.1 %collective-permute-start.1 = (bf16[2,2,72,128]{3,2,1,0:T(8,128)(2,1)S(1)}, bf16[2,2,72,128]{3,2,1,0:T(8,128)(2,1)S(1)}, u32[]{:S(2)}, u32[]{:S(2)}) collective-permute-start(bf16[2,2,72,128]{3,2,1,0:T(8,128)(2,1)S(1)} %get-tuple-element.25), channel_id=1, source_target_pairs={{0,8},{1,11},{2,10},{3,9},{4,12},{5,15},{6,14},{7,13},{8,0},{9,3},... | collective-permute-start | bytes 221192 | tf_op jit(solution)/shard_map/ppermute | solution.py:300
  7.5 7.0 %collective-permute-start.2 = (bf16[2,2,72,128]{3,2,1,0:T(8,128)(2,1)S(1)}, bf16[2,2,72,128]{3,2,1,0:T(8,128)(2,1)S(1)}, u32[]{:S(2)}, u32[]{:S(2)}) collective-permute-start(bf16[2,2,72,128]{3,2,1,0:T(8,128)(2,1)S(1)} %get-tuple-element.26), channel_id=1, source_target_pairs={{0,12},{1,15},{2,14},{3,13},{4,8},{5,11},{6,10},{7,9},{8,4},{9,7},... | collective-permute-start | bytes 221192 | tf_op jit(solution)/shard_map/ppermute | solution.py:300
  8.9 6.4 %collective-permute-start.3 = (bf16[2,2,72,128]{3,2,1,0:T(8,128)(2,1)S(1)}, bf16[2,2,72,128]{3,2,1,0:T(8,128)(2,1)S(1)}, u32[]{:S(2)}, u32[]{:S(2)}) collective-permute-start(bf16[2,2,72,128]{3,2,1,0:T(8,128)(2,1)S(1)} %get-tuple-element.27), channel_id=1, source_target_pairs={{0,4},{1,7},{2,6},{3,5},{4,0},{5,3},{6,2},{7,1},{8,12},{9,15},{10,... | collective-permute-start | bytes 221192 | tf_op jit(solution)/shard_map/ppermute | solution.py:300
  9.1 4.5 %collective-permute-start.4 = (bf16[2,72,128]{2,1,0:T(8,128)(2,1)S(1)}, bf16[2,72,128]{2,1,0:T(8,128)(2,1)S(1)}, u32[]{:S(2)}, u32[]{:S(2)}) collective-permute-start(bf16[2,72,128]{2,1,0:T(8,128)(2,1)S(1)} %get-tuple-element.28), channel_id=1, source_target_pairs={{0,2},{1,3},{2,0},{3,1},{4,6},{5,7},{6,4},{7,5},{8,10},{9,11},{10,... | collective-permute-start | bytes 110600 | tf_op jit(solution)/shard_map/ppermute | solution.py:300
  15.3 1.4 %collective-permute-start.5 = (bf16[8,72,128]{2,1,0:T(8,128)(2,1)S(1)}, bf16[8,72,128]{2,1,0:T(8,128)(2,1)S(1)}, u32[]{:S(2)}, u32[]{:S(2)}) collective-permute-start(bf16[8,72,128]{2,1,0:T(8,128)(2,1)S(1)} %get-tuple-element.31), channel_id=1, source_target_pairs={{0,1},{1,0},{2,3},{3,2},{4,5},{5,4},{6,7},{7,6},{8,9},{9,8},{10,11... | collective-permute-start | bytes 442376 | tf_op jit(solution)/shard_map/ppermute | solution.py:300
  16.8 12.2 %copy-start = (bf16[256,768]{1,0:T(8,128)(2,1)S(1)}, bf16[256,768]{1,0:T(8,128)(2,1)}, u32[]{:S(2)}) copy-start(bf16[256,768]{1,0:T(8,128)(2,1)} %refs_2_.1) | copy-start | bytes 1179652
  18.2 10.8 %copy-start.1 = (bf16[256,256]{1,0:T(8,128)(2,1)S(1)}, bf16[256,256]{1,0:T(8,128)(2,1)}, u32[]{:S(2)}) copy-start(bf16[256,256]{1,0:T(8,128)(2,1)} %refs_0_.1) | copy-start | bytes 393220
  18.2 1.3 %collective-permute-start.6 = (bf16[3,2,16,256]{3,2,1,0:T(8,128)(2,1)S(1)}, bf16[3,2,16,256]{3,2,1,0:T(8,128)(2,1)S(1)}, u32[]{:S(2)}, u32[]{:S(2)}) collective-permute-start(bf16[3,2,16,256]{3,2,1,0:T(8,128)(2,1)S(1)} %get-tuple-element.33), channel_id=1, source_target_pairs={{0,1},{1,0},{2,3},{3,2},{4,5},{5,4},{6,7},{7,6},{8,9},{9,8},{10,11... | collective-permute-start | bytes 147464 | tf_op jit(solution)/shard_map/ppermute | solution.py:300
  19.5 8.4 %collective-permute-start.7 = (bf16[2,2,16,256]{3,2,1,0:T(8,128)(2,1)S(1)}, bf16[2,2,16,256]{3,2,1,0:T(8,128)(2,1)S(1)}, u32[]{:S(2)}, u32[]{:S(2)}) collective-permute-start(bf16[2,2,16,256]{3,2,1,0:T(8,128)(2,1)S(1)} %get-tuple-element.34), channel_id=1, source_target_pairs={{0,8},{1,11},{2,10},{3,9},{4,12},{5,15},{6,14},{7,13},{8,0},{9,3},... | collective-permute-start | bytes 98312 | tf_op jit(solution)/shard_map/ppermute | solution.py:300
  22.6 5.9 %collective-permute-start.8 = (bf16[2,2,16,256]{3,2,1,0:T(8,128)(2,1)S(1)}, bf16[2,2,16,256]{3,2,1,0:T(8,128)(2,1)S(1)}, u32[]{:S(2)}, u32[]{:S(2)}) collective-permute-start(bf16[2,2,16,256]{3,2,1,0:T(8,128)(2,1)S(1)} %get-tuple-element.35), channel_id=1, source_target_pairs={{0,12},{1,15},{2,14},{3,13},{4,8},{5,11},{6,10},{7,9},{8,4},{9,7},... | collective-permute-start | bytes 98312 | tf_op jit(solution)/shard_map/ppermute | solution.py:300
  23.5 5.0 %collective-permute-start.9 = (bf16[2,2,16,256]{3,2,1,0:T(8,128)(2,1)S(1)}, bf16[2,2,16,256]{3,2,1,0:T(8,128)(2,1)S(1)}, u32[]{:S(2)}, u32[]{:S(2)}) collective-permute-start(bf16[2,2,16,256]{3,2,1,0:T(8,128)(2,1)S(1)} %get-tuple-element.36), channel_id=1, source_target_pairs={{0,4},{1,7},{2,6},{3,5},{4,0},{5,3},{6,2},{7,1},{8,12},{9,15},{10,... | collective-permute-start | bytes 98312 | tf_op jit(solution)/shard_map/ppermute | solution.py:300
  24.0 3.9 %collective-permute-start.10 = (bf16[2,16,256]{2,1,0:T(8,128)(2,1)S(1)}, bf16[2,16,256]{2,1,0:T(8,128)(2,1)S(1)}, u32[]{:S(2)}, u32[]{:S(2)}) collective-permute-start(bf16[2,16,256]{2,1,0:T(8,128)(2,1)S(1)} %get-tuple-element.37), channel_id=1, source_target_pairs={{0,2},{1,3},{2,0},{3,1},{4,6},{5,7},{6,4},{7,5},{8,10},{9,11},{10,... | collective-permute-start | bytes 49160 | tf_op jit(solution)/shard_map/ppermute | solution.py:300
  28.5 0.7 %copy-start.3 = (f32[3,768]{1,0:T(4,128)S(1)}, f32[3,768]{1,0:T(4,128)}, u32[]{:S(2)}) copy-start(f32[3,768]{1,0:T(4,128)} %refs_3_.1) | copy-start | bytes 27652
  28.5 0.7 %copy-start.4 = (f32[256]{0:T(256)S(1)}, f32[256]{0:T(256)}, u32[]{:S(2)}) copy-start(f32[256]{0:T(256)} %param.12) | copy-start | bytes 3076
  28.5 1.4 %copy-start.2 = (bf16[256,256]{1,0:T(8,128)(2,1)S(1)}, bf16[256,256]{1,0:T(8,128)(2,1)}, u32[]{:S(2)}) copy-start(bf16[256,256]{1,0:T(8,128)(2,1)} %w_ref.3) | copy-start | bytes 393220
  28.5 1.4 %collective-permute-start.11 = (bf16[8,16,256]{2,1,0:T(8,128)(2,1)S(1)}, bf16[8,16,256]{2,1,0:T(8,128)(2,1)S(1)}, u32[]{:S(2)}, u32[]{:S(2)}) collective-permute-start(bf16[8,16,256]{2,1,0:T(8,128)(2,1)S(1)} %get-tuple-element.40), channel_id=1, source_target_pairs={{0,1},{1,0},{2,3},{3,2},{4,5},{5,4},{6,7},{7,6},{8,9},{9,8},{10,11... | collective-permute-start | bytes 196616 | tf_op jit(solution)/shard_map/ppermute | solution.py:300

commit v12 on v10

v12 whole, which is shorter than its diff:
```python
import functools
import math

import jax
import jax.numpy as jnp
import numpy as np
from jax import lax
from jax.experimental import pallas as pl
from jax.experimental.pallas import tpu as pltpu
from jax.sharding import PartitionSpec as P

epsilon = 1e-06
edge = 8
lane = 128
seq = ("chip", "core")
rim_step = 2 * edge
chan_tile = 16
vmem_bytes = 32 * 2**20


def whole(space):
    return pl.BlockSpec(memory_space=space)


def call(body, outs, args, spaces, scratch=(), flops=0, moved=0):
    return pl.pallas_call(
        body,
        out_shape=outs,
        in_specs=[whole(space) for space in spaces],
        out_specs=jax.tree.map(lambda _: whole(pltpu.VMEM), outs),
        scratch_shapes=list(scratch),
        compiler_params=pltpu.CompilerParams(vmem_limit_bytes=vmem_bytes),
        cost_estimate=pl.CostEstimate(flops=flops, bytes_accessed=moved, transcendentals=0),
    )(*args)


def spectral_tables(devices, rows, chans):
    full_len = devices * rows
    freqs = 4 * np.arange(devices) + 1
    eye = np.eye(chans)
    angle = 2.0 * math.pi / (4 * devices) * (freqs[:, None] * np.arange(devices)[None, :] % (4 * devices))
    cosine, sine = np.kron(np.cos(angle), eye), np.kron(np.sin(angle), eye)
    first = np.concatenate([cosine, -sine])
    offsets = np.arange(rows)
    twist = 2.0 * math.pi / (4 * full_len) * (freqs[:, None] * offsets[None, :] % (4 * full_len))
    twist = np.concatenate([np.cos(twist), np.sin(twist)])
    if chans % 8:
        twist = np.repeat(twist, chans, axis=0)
    turn = 2.0 * math.pi / rows * (offsets[:, None] * offsets[None, :] % rows)
    inner = np.concatenate([np.cos(turn), np.sin(turn)], axis=1)
    return (
        jnp.asarray(first, jnp.bfloat16),
        jnp.asarray(twist, jnp.float32),
        jnp.asarray(inner, jnp.bfloat16),
    )


def routes_of(chips):
    far = sorted(range(2, chips, 2), key=lambda d: (-d.bit_length(), d))
    return [(d, d + 1) for d in far]


def carried(route, core):
    mine, others = route
    return jnp.where(core == 0, mine, others), jnp.where(core == 0, others, mine)


def put_routes(source_ref, rim_ref, keep_ref, give_ref, near_ref, home_ref):
    chip, core = lax.axis_index("chip"), lax.axis_index("core")
    size = source_ref.shape[0] // 2 // (lax.axis_size("chip"))

    def put(out_ref, distance):
        start = pl.multiple_of((chip ^ distance) * 2 * size, 2 * size)
        out_ref[0 : 2 * size, :] = source_ref[pl.ds(start, 2 * size), :]
        if rim_ref is not None:
            out_ref[2 * size :, :] = rim_ref[chip ^ distance]

    for turn, route in enumerate(routes_of(lax.axis_size("chip"))):
        own, other = carried(route, core)
        put(keep_ref.at[turn], own)
        put(give_ref.at[turn], other)
    put(near_ref, 1)
    put(home_ref, 0)


def half_rims(first_ref, second_ref, begin):
    pair = [ref[begin:, :].astype(jnp.float32)[0 : edge // 2] for ref in (first_ref, second_ref)]
    return jnp.concatenate(pair).astype(jnp.bfloat16)


def merge_body(size, keep_ref, got_ref, *out_refs):
    for turn, out_ref in enumerate(out_refs):
        out_ref[0 : 2 * size, :] = keep_ref[turn, 0 : 2 * size, :]
        out_ref[2 * size : 4 * size, :] = got_ref[turn, 0 : 2 * size, :]
        if out_ref.shape[0] > 4 * size:
            out_ref[4 * size :, :] = half_rims(keep_ref.at[turn], got_ref.at[turn], 2 * size)


def split_body(size, *refs):
    far_refs, (near_ref, home_ref, keep_ref, give_ref) = refs[:-4], refs[-4:]
    core = lax.axis_index("core")
    sources = [(far_ref, 2 * sender) for far_ref in far_refs for sender in range(2)]
    sources += [(near_ref, 0), (home_ref, 0)]
    for out_ref, target in ((keep_ref, core), (give_ref, 1 - core)):
        for place, (source_ref, block) in enumerate(sources):
            start = pl.multiple_of((block + target) * size, size)
            out_ref[place * size : (place + 1) * size, :] = source_ref[pl.ds(start, size), :]
        begin = len(sources) * size
        if out_ref.shape[0] > begin:
            for far_ref in far_refs:
                out_ref[begin : begin + edge, :] = far_ref[4 * size :, :]
                begin += edge
            out_ref[begin:, :] = half_rims(near_ref, home_ref, 2 * size)


def take_routes(keep_ref, got_ref, target_ref, rim_ref=None):
    chip, core = lax.axis_index("chip"), lax.axis_index("core")
    routes = routes_of(lax.axis_size("chip"))
    count = 2 * len(routes) + 2
    size = target_ref.shape[0] // (2 * lax.axis_size("chip"))
    places = [(*carried(route, core), sender) for route in routes for sender in range(2)]
    places += [(1, 1, 0), (0, 0, 0)]
    for place, (own, other, sender) in enumerate(places):
        for ref, distance, carrier in ((keep_ref, own, core), (got_ref, other, 1 - core)):
            device = (chip ^ distance) * 2 + (carrier if sender == 0 else 1 - carrier)
            start = pl.multiple_of(device * size, size)
            target_ref[pl.ds(start, size), :] = ref[place * size : (place + 1) * size, :]
            if rim_ref is not None:
                begin = count * size + place // 2 * edge
                rims = ref[begin : begin + edge, :].astype(jnp.float32)
                rim_ref[device, 0 : edge // 2, :] = rims[place % 2 * edge // 2 : (place % 2 + 1) * edge // 2]


def normed_of(tokens_ref, gain_ref):
    inputs = tokens_ref[...].astype(jnp.float32)
    mean_sq = jnp.mean(inputs * inputs, axis=-1, keepdims=True)
    return (inputs * lax.rsqrt(mean_sq + epsilon) * gain_ref[...]).astype(jnp.bfloat16)


def projected_of(normed, weights):
    projected = jnp.dot(normed, weights, preferred_element_type=jnp.float32)
    projected = projected.astype(jnp.bfloat16).astype(jnp.float32)
    return jnp.concatenate([projected, jnp.zeros((edge, projected.shape[1]), jnp.float32)])


def short_mix(projected, taps):
    acc = taps[0:1] * projected
    for tap_num in range(1, taps.shape[0]):
        acc = acc + taps[tap_num : tap_num + 1] * pltpu.roll(projected, tap_num, 0)
    return acc


def query_body(tokens_ref, gain_ref, w_ref, short_ref, query_ref):
    rows, width = tokens_ref.shape
    cols = slice(0, width)
    query = short_mix(projected_of(normed_of(tokens_ref, gain_ref), w_ref[:, cols]), short_ref[:, cols])
    query_ref[...] = query[0:rows]
    row = lax.broadcasted_iota(jnp.int32, (edge, width), 0)
    query_ref[0:edge, :] = jnp.where(row < short_ref.shape[0] - 1, 1.0, query[0:edge])


def prepare_body(*refs):
    hbm, outs, held, sems = refs[:7], refs[7:-8], refs[-8:-1], refs[-1]
    staged = len(outs) > 1
    outs, (packed_ref, rim_ref) = (outs[:-2], outs[-2:]) if staged else (outs, (outs[0], None))
    tokens_ref, gain_ref, w_ref, short_ref, long_ref, medium_ref, skip_ref = held
    rows, width = tokens_ref.shape
    copies = [pltpu.make_async_copy(h, v, sems.at[i]) for i, (h, v) in enumerate(zip(hbm, held))]
    for copy in copies:
        copy.start()
    copies[0].wait()
    copies[1].wait()
    normed = normed_of(tokens_ref, gain_ref)
    copies[2].wait()
    copies[3].wait()
    query_cols, cols = slice(0, width), slice(width, 3 * width)
    mixed = short_mix(projected_of(normed, w_ref[:, cols]), short_ref[:, cols])
    key, value = mixed[:, 0:width], mixed[:, width:]
    put_columns(packed_ref, 0, (key[0:rows] * value[0:rows]).astype(jnp.bfloat16).T)
    rims = [(key[0:edge], key[rows:]), (value[0:edge], value[rows:])]
    ends = []
    for begin, place in ((0, 0), (rows - 2 * edge, 2 * edge)):
        some = projected_of(normed[begin : begin + 2 * edge], w_ref[:, query_cols])
        ends.append(short_mix(some, short_ref[:, query_cols])[place : place + edge])
    put_rim(packed_ref, rim_ref, [*rims, ends])
    for copy in copies[4:]:
        copy.wait()
    med_len = medium_ref.shape[0]
    is_first = jnp.where(lax.axis_index(seq) == 0, 1.0, 0.0)
    head = long_ref[0:med_len, :] + is_first * medium_ref[...]
    head_row = lax.broadcasted_iota(jnp.int32, head.shape, 0)
    head = head + jnp.where(head_row == 0, is_first * skip_ref[...], 0.0)
    taps = jnp.concatenate([head, long_ref[med_len:, :]]).astype(jnp.bfloat16)
    put_columns(packed_ref, rows, taps.T)
    if staged:
        put_routes(packed_ref, rim_ref, *outs)


def put_columns(packed_ref, begin, values):
    if packed_ref.shape[1] > lane:
        packed_ref[:, begin : begin + values.shape[1]] = values
        return
    devices = lax.axis_size(seq)
    chans = values.shape[0] // devices
    size = packed_ref.shape[0] // devices
    for device in range(devices):
        for column in range(values.shape[1] // lane):
            start = device * size + (begin // lane + column) * chans
            packed_ref[start : start + chans, :] = values[
                device * chans : (device + 1) * chans, column * lane : (column + 1) * lane
            ]


def put_rim(packed_ref, rim_ref, parts):
    width = parts[0][0].shape[1]
    if rim_ref is None:
        rows = [row for part in parts for row in part]
        rows.append(jnp.zeros((lane - 3 * rim_step, width), jnp.float32))
        rim = jnp.concatenate(rows).T
        packed_ref[:, packed_ref.shape[1] - lane :] = rim.astype(jnp.bfloat16)
        return
    chips = rim_ref.shape[0]
    span = width // chips
    half = edge // 4
    group = lax.broadcasted_iota(jnp.int32, (edge // 2, lane), 1) // span
    parts = [jnp.concatenate([own[0:half], after[0:half]]) for own, after in parts]
    for chip in range(chips):
        begin = chip * span // lane * lane
        place = chip * span % lane
        rim = jnp.zeros((edge // 2, lane), jnp.float32)
        for index, part in enumerate(parts):
            shift = (index * span - place) % lane
            moved = part[:, begin : begin + lane]
            moved = pltpu.roll(moved, shift, 1) if shift else moved
            rim = jnp.where(group == index, moved, rim)
        rim = jnp.concatenate([rim, jnp.zeros((edge // 2, lane), jnp.float32)])
        rim_ref[chip] = rim.astype(jnp.bfloat16)


def columns_of(packed_ref, chans, rows):
    devices, count = lax.axis_size(seq), 2 * rows // lane
    blocks = packed_ref[...].reshape(devices, count * chans, lane)
    columns = [blocks[:, i * chans : (i + 1) * chans].reshape(-1, lane) for i in range(count)]
    return jnp.concatenate(columns, axis=1)


def rim_of(rim_ref, turned_ref, chans):
    span = 2 * chans
    rim = rim_ref[...].reshape(-1, lane)
    row = lax.broadcasted_iota(jnp.int32, rim.shape, 0)
    column = lax.broadcasted_iota(jnp.int32, rim.shape, 1)
    before = pltpu.roll(rim, edge - edge // 4, 0)
    rim = rim + jnp.where(row < edge, 0.0, before)
    signal = rim * pltpu.roll(rim, lane - span, 1)
    turned_ref[...] = jnp.where(column < span, signal, rim).T
    found = []
    for begin in (0, 2 * span):
        start = pl.multiple_of(begin + lax.axis_index("core") * chans, chans)
        part = turned_ref[pl.ds(start, chans), :]
        blocks = [part] + [pltpu.roll(part, lane - edge * k, 1) for k in range(1, rim_ref.shape[0])]
        found.append(jnp.concatenate(blocks))
    return found


def twist_rows(twist_ref, chans):
    half, rows = twist_ref.shape[0] // 2, twist_ref.shape[1]
    tables = twist_ref[0:half, :], twist_ref[half:, :]
    if chans % 8:
        return tables
    return tuple(
        jnp.broadcast_to(table[:, None, :], (half, chans, rows)).reshape(half * chans, rows)
        for table in tables
    )


def convolve_body(chans, rim_count, first_ref, twist_ref, inner_ref, *refs):
    rows = twist_ref.shape[1]
    half = first_ref.shape[0] // 2
    scale = chans / (half * rows)
    staged = len(refs) > 2
    if staged:
        keep_ref, got_ref, *outs, packed_ref, rim_ref, turned_ref, out_ref = refs
        rim_ref[...] = jnp.zeros_like(rim_ref)
        take_routes(keep_ref, got_ref, packed_ref, rim_ref)
        values = columns_of(packed_ref, chans, rows)
        rim_signal, rim_query = rim_of(rim_ref, turned_ref, chans)
    else:
        packed_ref, out_ref = refs
        values = packed_ref[:, : 2 * rows]
        rim = packed_ref[:, 2 * rows :].astype(jnp.float32)
        before = jnp.concatenate([jnp.zeros((chans, lane), jnp.float32), rim[:-chans]])
        rim = rim + pltpu.roll(before, lane - edge, 1)
        rim_signal = rim * pltpu.roll(rim, lane - rim_step, 1)
        rim_query = pltpu.roll(rim, lane - 2 * rim_step, 1)
    in_rim = lax.broadcasted_iota(jnp.int32, rim_signal.shape, 1) < rim_count
    rim_signal = rim_signal.astype(jnp.bfloat16)
    rim_query = scale * jnp.where(in_rim, rim_query, 1.0)
    values = jnp.concatenate(
        [jnp.where(in_rim, rim_signal, values[:, 0:lane]), values[:, lane:]], axis=1
    )
    cosine, sine = inner_ref[:, 0:rows], inner_ref[:, rows:]
    inner = jnp.concatenate(
        [jnp.concatenate([cosine, -sine], axis=1), jnp.concatenate([sine, cosine], axis=1)]
    )
    spread = jnp.dot(first_ref[...], values, preferred_element_type=jnp.float32)
    tw_cos, tw_sin = twist_rows(twist_ref, chans)
    turned = []
    for begin in (0, rows):
        real, imag = spread[0:half, begin : begin + rows], spread[half:, begin : begin + rows]
        turned.append([real * tw_cos + imag * tw_sin, imag * tw_cos - real * tw_sin])
    turned = jnp.concatenate([jnp.concatenate(pair, axis=1).astype(jnp.bfloat16) for pair in turned])
    spectra = jnp.dot(turned, inner, preferred_element_type=jnp.float32)
    real, imag = spectra[0:half, 0:rows], spectra[0:half, rows:]
    fil_re, fil_im = spectra[half:, 0:rows], spectra[half:, rows:]
    product = [real * fil_im + imag * fil_re, real * fil_re - imag * fil_im]
    product = jnp.concatenate(product, axis=1).astype(jnp.bfloat16)
    back = jnp.dot(product, inner, preferred_element_type=jnp.float32)
    imag, real = back[:, 0:rows], back[:, rows:]
    turned = jnp.concatenate([real * tw_cos - imag * tw_sin, imag * tw_cos + real * tw_sin])
    last = jnp.concatenate([first_ref[0:half, :].T, first_ref[half:, :].T], axis=1)
    conv = jnp.dot(last, turned.astype(jnp.bfloat16), preferred_element_type=jnp.float32)
    conv = jnp.concatenate([conv[:, 0:lane] * rim_query, conv[:, lane:] * scale], axis=1)
    out_ref[...] = conv.astype(jnp.bfloat16)
    if staged:
        put_routes(out_ref, None, *outs)


def output_body(query_ref, w_ref, *refs):
    if len(refs) > 2:
        keep_ref, got_ref, out_ref, conv_ref = refs
        take_routes(keep_ref, got_ref, conv_ref)
    else:
        conv_ref, out_ref = refs
    conv = conv_ref[...].T.astype(jnp.float32)
    mixed_out = (query_ref[...] * conv).astype(jnp.bfloat16)
    out_ref[...] = jnp.dot(mixed_out, w_ref[...], preferred_element_type=jnp.float32).astype(
        jnp.bfloat16
    )


def permute(array, partner):
    return lax.ppermute(array, seq, [(i, partner(i)) for i in range(lax.axis_size(seq))])


def bf16(*shape):
    return jax.ShapeDtypeStruct(shape, jnp.bfloat16)


def exchange(keep, give, near, home):
    turns, size = keep.shape[0], keep.shape[1] // 2 // chan_tile * chan_tile
    lanes, extra = keep.shape[2], keep.shape[1] - 2 * size
    got = permute(give, lambda i: i ^ 1)
    near = permute(near, lambda i: i ^ 2)
    far = call(
        functools.partial(merge_body, size),
        (bf16(4 * size + extra, lanes),) * turns,
        (keep, got),
        [pltpu.VMEM] * 2,
        moved=4 * keep.size,
    )
    routes = routes_of(lax.axis_size("chip"))
    far = [permute(part, lambda i: i ^ 2 * route[i % 2]) for part, route in zip(far, routes)]
    count = 2 * turns + 2
    half = bf16(count * size + count // 2 * extra, lanes)
    keep, give = call(
        functools.partial(split_body, size),
        (half, half),
        (*far, near, home),
        [pltpu.VMEM] * (turns + 2),
        moved=4 * keep.size,
    )
    return keep, permute(give, lambda i: i ^ 1)


def local(tokens, norm_gain, w_in, short_filter, long_filter, medium_filter, skip_gain, w_out):
    rows, width = tokens.shape
    devices, chips = lax.axis_size(seq), lax.axis_size("chip")
    chans = width // devices
    first, twist, inner = spectral_tables(devices, rows, chans)
    staged = chans == chan_tile and chips >= 4 and short_filter.shape[0] <= 3
    if staged:
        packed_shape = (2 * rows // lane * width, lane)
    else:
        packed_shape = (width, 2 * rows + lane)

    def pieces(shape, extra):
        if not staged:
            return (bf16(*shape),)
        size, turns = 2 * shape[0] // devices + extra, len(routes_of(chips))
        return (bf16(turns, size, shape[1]),) * 2 + (bf16(size, shape[1]),) * 2

    def scratch(*shapes):
        return [pltpu.VMEM(*shape) for shape in shapes] if staged else []

    def swap(parts):
        if staged:
            return exchange(*parts)
        (array,) = parts
        blocks = array.reshape(devices, -1, array.shape[-1])
        return (lax.all_to_all(blocks, seq, split_axis=0, concat_axis=0).reshape(array.shape),)

    query = call(
        query_body,
        jax.ShapeDtypeStruct((rows, width), jnp.float32),
        (tokens, norm_gain[None, :], w_in, short_filter),
        [pltpu.VMEM] * 4,
        flops=2 * rows * width * width,
        moved=800_000,
    )
    args = (tokens, norm_gain[None, :], w_in, short_filter, long_filter, medium_filter, skip_gain[None, :])
    args = tuple(pltpu.with_memory_space_constraint(arg, pltpu.HBM) for arg in args)
    packed = (packed_shape, jnp.bfloat16)
    parts = call(
        prepare_body,
        pieces(packed_shape, edge),
        args,
        [pltpu.HBM] * len(args),
        scratch(packed, ((chips, edge, lane), jnp.bfloat16))
        + [pltpu.VMEM(arg.shape, arg.dtype) for arg in args]
        + [pltpu.SemaphoreType.DMA((len(args),))],
        flops=2 * rows * width * 3 * width,
        moved=1_500_000,
    )
    conv = ((width, rows), jnp.bfloat16)
    parts = swap(parts)
    parts = call(
        functools.partial(convolve_body, chans, short_filter.shape[0] - 1),
        pieces((width, rows), 0),
        (first, twist, inner, *parts),
        [pltpu.VMEM] * (3 + len(parts)),
        scratch(packed, ((devices, edge, lane), jnp.float32), ((lane, lane), jnp.float32), conv),
        flops=18 * first.shape[0] * width * rows,
        moved=2_000_000,
    )
    parts = swap(parts)
    return call(
        output_body,
        bf16(rows, width),
        (query, w_out, *parts),
        [pltpu.VMEM] * (2 + len(parts)),
        scratch(conv),
        flops=2 * rows * width * width,
        moved=600_000,
    )


def solution(mesh):
    groups, devices = mesh.devices.shape
    split = jax.sharding.Mesh(mesh.devices.reshape(groups, devices // 2, 2), ("groups", *seq))
    rows = P(("groups", *seq), None)
    placed = (rows, P(), P(), P(), P(seq, None), P(), P(), P())
    return jax.shard_map(local, mesh=split, in_specs=placed, out_specs=rows, check_vma=False)
```

time: 32.8 us -> 30.2 us (0.921)
  waiting for transfers between devices: 13.3 us -> 11.4 us
  starting transfers between devices: 14.7 us -> 13.9 us
    ppermute x12, waiting for transfers between devices: 13.3 us -> 11.4 us  [permute(): lax.ppermute(array, seq, [(i, partner(i)) for i in range(lax.axis_size(se...]
    ppermute x12, starting transfers between devices: 14.7 us -> 13.9 us  [permute(): lax.ppermute(array, seq, [(i, partner(i)) for i in range(lax.axis_size(se...]
  transfers between devices with their start and end apart: 12 -> 12, of which waited for: 10 -> 9; matrix products, arithmetic and copies ran while one was open for 0% -> 0% of each run, Pallas kernels for 1% -> 1%
where the time goes in v12:
time: 30.2 us; the launch traced here: 30.1 us
  starting transfers between devices  13.9 us (46%)
  waiting for transfers between devices  11.4 us (38%)
  Pallas kernels  4.5 us (15%)
    ppermute x12, starting transfers between devices, permute(): lax.ppermute(array, seq, [(i, partner(i)) for i in range(lax.axis_size(se...  13.9 us
    ppermute x12, waiting for transfers between devices, permute(): lax.ppermute(array, seq, [(i, partner(i)) for i in range(lax.axis_size(se...  11.4 us
    pallas_call x8, Pallas kernels, call(): pl.pallas_call(body, out_shape=outs, in_specs=[whole(space) for space in...  4.5 us
  transfers between devices with their start and end apart: 12, of which 9 were waited for; matrix products, arithmetic and copies ran while one was open for 0% of the time, Pallas kernels for 1%

profile of v12, /device:TPU:0, one launch (start us, length us, event | category | flops | bytes accessed | tf_op | source)
XLA Modules:
  0.0 30.1 jit_solution(14007024665060216468)
XLA Ops:
  0.0 0.0 copy-start.6
  0.0 1.8 %shard_map.110 = (bf16[3,136,128]{2,1,0:T(8,128)(2,1)S(1)}, bf16[3,136,128]{2,1,0:T(8,128)(2,1)S(1)}, bf16[136,128]{1,0:T(8,128)(2,1)S(1)}, bf16[136,128]{1,0:T(8,128)(2,1)S(1)}) custom-call(bf16[256,256]{1,0:T(8,128)(2,1)} %refs_0_.1, f32[1,256]{1,0:T(1,128)} %bitcast.2, bf16[256,768]{1,0:T(8,128)(2,1)} %refs_2_.1, f32[3,768]{1,0:T(4,128)} %refs_3_.1, ...), custom_call_target="tpu_custom_call" | custom-call | flops 100663296 | bytes 1500000 | tf_op jit(solution)/shard_map/pallas_call | solution.py:26
  1.8 0.0 copy-start.5
  1.8 0.5 %collective-permute-start = (bf16[3,136,128]{2,1,0:T(8,128)(2,1)S(1)}, bf16[3,136,128]{2,1,0:T(8,128)(2,1)S(1)}, u32[]{:S(2)}, u32[]{:S(2)}) collective-permute-start(bf16[3,136,128]{2,1,0:T(8,128)(2,1)S(1)} %get-tuple-element.24), channel_id=1, source_target_pairs={{0,1},{1,0},{2,3},{3,2},{4,5},{5,4},{6,7},{7,6},{8,9},{9,8},{10,11... | collective-permute-start | bytes 313352 | tf_op jit(solution)/shard_map/ppermute | solution.py:342
  2.3 1.0 %collective-permute-done.got_ref = bf16[3,136,128]{2,1,0:T(8,128)(2,1)S(1)} collective-permute-done((bf16[3,136,128]{2,1,0:T(8,128)(2,1)S(1)}, bf16[3,136,128]{2,1,0:T(8,128)(2,1)S(1)}, u32[]{:S(2)}, u32[]{:S(2)}) %collective-permute-start) | collective-permute-done | bytes 104480 | tf_op jit(solution)/shard_map/ppermute | solution.py:342
  3.3 4.0 %collective-permute-start.1 = (bf16[264,128]{1,0:T(8,128)(2,1)S(1)}, bf16[264,128]{1,0:T(8,128)(2,1)S(1)}, u32[]{:S(2)}, u32[]{:S(2)}) collective-permute-start(bf16[264,128]{1,0:T(8,128)(2,1)S(1)} %get-tuple-element.25), channel_id=1, source_target_pairs={{0,8},{1,11},{2,10},{3,9},{4,12},{5,15},{6,14},{7,13},{8,0},{9,3},... | collective-permute-start | bytes 202760 | tf_op jit(solution)/shard_map/ppermute | solution.py:342
  7.3 1.3 %collective-permute-start.2 = (bf16[264,128]{1,0:T(8,128)(2,1)S(1)}, bf16[264,128]{1,0:T(8,128)(2,1)S(1)}, u32[]{:S(2)}, u32[]{:S(2)}) collective-permute-start(bf16[264,128]{1,0:T(8,128)(2,1)S(1)} %get-tuple-element.26), channel_id=1, source_target_pairs={{0,12},{1,15},{2,14},{3,13},{4,8},{5,11},{6,10},{7,9},{8,4},{9,7},... | collective-permute-start | bytes 202760 | tf_op jit(solution)/shard_map/ppermute | solution.py:342
  8.7 0.2 collective-permute-start.3
  8.9 1.5 %collective-permute-start.4 = (bf16[136,128]{1,0:T(8,128)(2,1)S(1)}, bf16[136,128]{1,0:T(8,128)(2,1)S(1)}, u32[]{:S(2)}, u32[]{:S(2)}) collective-permute-start(bf16[136,128]{1,0:T(8,128)(2,1)S(1)} %get-tuple-element.28), channel_id=1, source_target_pairs={{0,2},{1,3},{2,0},{3,1},{4,6},{5,7},{6,4},{7,5},{8,10},{9,11},{10,... | collective-permute-start | bytes 104456 | tf_op jit(solution)/shard_map/ppermute | solution.py:342
  10.4 2.4 %collective-permute-done.4.refs_3_ = bf16[136,128]{1,0:T(8,128)(2,1)S(1)} collective-permute-done((bf16[136,128]{1,0:T(8,128)(2,1)S(1)}, bf16[136,128]{1,0:T(8,128)(2,1)S(1)}, u32[]{:S(2)}, u32[]{:S(2)}) %collective-permute-start.4) | collective-permute-done | bytes 34848 | tf_op jit(solution)/shard_map/ppermute | solution.py:342
  12.9 0.0 collective-permute-done.1.refs_0_
  12.9 1.2 %collective-permute-done.2.refs_1_ = bf16[264,128]{1,0:T(8,128)(2,1)S(1)} collective-permute-done((bf16[264,128]{1,0:T(8,128)(2,1)S(1)}, bf16[264,128]{1,0:T(8,128)(2,1)S(1)}, u32[]{:S(2)}, u32[]{:S(2)}) %collective-permute-start.2) | collective-permute-done | bytes 67616 | tf_op jit(solution)/shard_map/ppermute | solution.py:342
  14.1 0.8 %collective-permute-done.3.refs_2_ = bf16[264,128]{1,0:T(8,128)(2,1)S(1)} collective-permute-done((bf16[264,128]{1,0:T(8,128)(2,1)S(1)}, bf16[264,128]{1,0:T(8,128)(2,1)S(1)}, u32[]{:S(2)}, u32[]{:S(2)}) %collective-permute-start.3) | collective-permute-done | bytes 67616 | tf_op jit(solution)/shard_map/ppermute | solution.py:342
  14.9 0.0 copy-start.7
  14.9 0.3 collective-permute-start.5
  15.2 1.1 %collective-permute-done.5.refs_1_ = bf16[544,128]{1,0:T(8,128)(2,1)S(1)} collective-permute-done((bf16[544,128]{1,0:T(8,128)(2,1)S(1)}, bf16[544,128]{1,0:T(8,128)(2,1)S(1)}, u32[]{:S(2)}, u32[]{:S(2)}) %collective-permute-start.5) | collective-permute-done | bytes 139296 | tf_op jit(solution)/shard_map/ppermute | solution.py:342
  16.3 0.0 copy-done.6
  16.3 0.0 copy-done.5
  16.3 0.0 copy-done.7
  16.3 0.0 copy-start
  16.3 1.4 %shard_map.113 = (bf16[3,32,256]{2,1,0:T(8,128)(2,1)S(1)}, bf16[3,32,256]{2,1,0:T(8,128)(2,1)S(1)}, bf16[32,256]{1,0:T(8,128)(2,1)S(1)}, bf16[32,256]{1,0:T(8,128)(2,1)S(1)}) custom-call(bf16[512,256]{1,0:T(8,128)(2,1)S(1)} %copy-done.5, f32[32,256]{1,0:T(8,128)S(1)} %copy-done.7, bf16[256,512]{1,0:T(8,128)(2,1)S(1)} %copy-done.6, ...), custom_call_target="tpu_custom_call" | custom-call | flops 603979776 | bytes 2000000 | tf_op jit(solution)/shard_map/pallas_call | solution.py:26
  17.7 0.0 copy-start.1
  17.8 0.3 collective-permute-start.6
  18.0 1.0 %collective-permute-done.6.got_ref = bf16[3,32,256]{2,1,0:T(8,128)(2,1)S(1)} collective-permute-done((bf16[3,32,256]{2,1,0:T(8,128)(2,1)S(1)}, bf16[3,32,256]{2,1,0:T(8,128)(2,1)S(1)}, u32[]{:S(2)}, u32[]{:S(2)}) %collective-permute-start.6) | collective-permute-done | bytes 49184 | tf_op jit(solution)/shard_map/ppermute | solution.py:342
  19.1 2.8 %collective-permute-start.7 = (bf16[64,256]{1,0:T(8,128)(2,1)S(1)}, bf16[64,256]{1,0:T(8,128)(2,1)S(1)}, u32[]{:S(2)}, u32[]{:S(2)}) collective-permute-start(bf16[64,256]{1,0:T(8,128)(2,1)S(1)} %get-tuple-element.34), channel_id=1, source_target_pairs={{0,8},{1,11},{2,10},{3,9},{4,12},{5,15},{6,14},{7,13},{8,0},{9,3},... | collective-permute-start | bytes 98312 | tf_op jit(solution)/shard_map/ppermute | solution.py:342
  21.9 0.9 %collective-permute-start.8 = (bf16[64,256]{1,0:T(8,128)(2,1)S(1)}, bf16[64,256]{1,0:T(8,128)(2,1)S(1)}, u32[]{:S(2)}, u32[]{:S(2)}) collective-permute-start(bf16[64,256]{1,0:T(8,128)(2,1)S(1)} %get-tuple-element.35), channel_id=1, source_target_pairs={{0,12},{1,15},{2,14},{3,13},{4,8},{5,11},{6,10},{7,9},{8,4},{9,7},... | collective-permute-start | bytes 98312 | tf_op jit(solution)/shard_map/ppermute | solution.py:342
  22.8 0.5 %collective-permute-start.9 = (bf16[64,256]{1,0:T(8,128)(2,1)S(1)}, bf16[64,256]{1,0:T(8,128)(2,1)S(1)}, u32[]{:S(2)}, u32[]{:S(2)}) collective-permute-start(bf16[64,256]{1,0:T(8,128)(2,1)S(1)} %get-tuple-element.36), channel_id=1, source_target_pairs={{0,4},{1,7},{2,6},{3,5},{4,0},{5,3},{6,2},{7,1},{8,12},{9,15},{10,... | collective-permute-start | bytes 98312 | tf_op jit(solution)/shard_map/ppermute | solution.py:342
  23.3 1.0 %collective-permute-start.10 = (bf16[32,256]{1,0:T(8,128)(2,1)S(1)}, bf16[32,256]{1,0:T(8,128)(2,1)S(1)}, u32[]{:S(2)}, u32[]{:S(2)}) collective-permute-start(bf16[32,256]{1,0:T(8,128)(2,1)S(1)} %get-tuple-element.37), channel_id=1, source_target_pairs={{0,2},{1,3},{2,0},{3,1},{4,6},{5,7},{6,4},{7,5},{8,10},{9,11},{10,... | collective-permute-start | bytes 49160 | tf_op jit(solution)/shard_map/ppermute | solution.py:342
  24.2 2.9 %collective-permute-done.10.refs_3_ = bf16[32,256]{1,0:T(8,128)(2,1)S(1)} collective-permute-done((bf16[32,256]{1,0:T(8,128)(2,1)S(1)}, bf16[32,256]{1,0:T(8,128)(2,1)S(1)}, u32[]{:S(2)}, u32[]{:S(2)}) %collective-permute-start.10) | collective-permute-done | bytes 16416 | tf_op jit(solution)/shard_map/ppermute | solution.py:342
  27.2 0.0 collective-permute-done.7.refs_0_
  27.2 0.6 %collective-permute-done.8.refs_1_ = bf16[64,256]{1,0:T(8,128)(2,1)S(1)} collective-permute-done((bf16[64,256]{1,0:T(8,128)(2,1)S(1)}, bf16[64,256]{1,0:T(8,128)(2,1)S(1)}, u32[]{:S(2)}, u32[]{:S(2)}) %collective-permute-start.8) | collective-permute-done | bytes 32800 | tf_op jit(solution)/shard_map/ppermute | solution.py:342
  27.8 0.0 collective-permute-done.9.refs_2_
  27.8 0.0 copy-start.3
  27.8 0.0 copy-start.4
  27.8 0.0 copy-start.2
  27.8 0.5 %collective-permute-start.11 = (bf16[128,256]{1,0:T(8,128)(2,1)S(1)}, bf16[128,256]{1,0:T(8,128)(2,1)S(1)}, u32[]{:S(2)}, u32[]{:S(2)}) collective-permute-start(bf16[128,256]{1,0:T(8,128)(2,1)S(1)} %get-tuple-element.40), channel_id=1, source_target_pairs={{0,1},{1,0},{2,3},{3,2},{4,5},{5,4},{6,7},{7,6},{8,9},{9,8},{10,11... | collective-permute-start | bytes 196616 | tf_op jit(solution)/shard_map/ppermute | solution.py:342
  28.3 0.0 copy-done
  28.3 0.0 copy-done.1
  28.3 0.2 copy-done.3
  28.5 0.0 copy-done.4
  28.5 0.3 %shard_map.109.query_ref = f32[256,256]{1,0:T(8,128)S(1)} custom-call(bf16[256,256]{1,0:T(8,128)(2,1)S(1)} %copy-done.1, f32[1,256]{1,0:T(1,128)S(1)} %bitcast.3, bf16[256,768]{1,0:T(8,128)(2,1)S(1)} %copy-done, f32[3,768]{1,0:T(4,128)S(1)} %copy-done.3), custom_call_target="tpu_custom_call" | custom-call | flops 33554432 | bytes 800000 | tf_op jit(solution)/shard_map/pallas_call | solution.py:26
  28.8 0.4 %collective-permute-done.11.refs_1_ = bf16[128,256]{1,0:T(8,128)(2,1)S(1)} collective-permute-done((bf16[128,256]{1,0:T(8,128)(2,1)S(1)}, bf16[128,256]{1,0:T(8,128)(2,1)S(1)}, u32[]{:S(2)}, u32[]{:S(2)}) %collective-permute-start.11) | collective-permute-done | bytes 65568 | tf_op jit(solution)/shard_map/ppermute | solution.py:342
  29.2 0.0 copy-done.2
  29.2 0.9 %shard_map.116 = bf16[256,256]{1,0:T(8,128)(2,1)} custom-call(f32[256,256]{1,0:T(8,128)S(1)} %shard_map.109.query_ref, bf16[256,256]{1,0:T(8,128)(2,1)S(1)} %copy-done.2, bf16[128,256]{1,0:T(8,128)(2,1)S(1)} %get-tuple-element.39.refs_0_, bf16[128,256]{1,0:T(8,128)(2,1)S(1)} %collective-permute-done.11.refs_1_), custom_call_target="tpu_custom_call" | custom-call | flops 33554432 | bytes 600000 | tf_op jit(solution)/shard_map/pallas_call | solution.py:26
  (4 shorter events, 0.1 us)
Async XLA Ops:
  0.0 16.3 %copy-start.6 = (bf16[256,512]{1,0:T(8,128)(2,1)S(1)}, bf16[256,512]{1,0:T(8,128)(2,1)}, u32[]{:S(2)}) copy-start(bf16[256,512]{1,0:T(8,128)(2,1)} %constant.8.clone.inner_ref) | copy-start | bytes 786436
  1.8 14.5 %copy-start.5 = (bf16[512,256]{1,0:T(8,128)(2,1)S(1)}, bf16[512,256]{1,0:T(8,128)(2,1)}, u32[]{:S(2)}) copy-start(bf16[512,256]{1,0:T(8,128)(2,1)} %constant.6.clone.first_ref) | copy-start | bytes 786436
  1.8 1.5 %collective-permute-start = (bf16[3,136,128]{2,1,0:T(8,128)(2,1)S(1)}, bf16[3,136,128]{2,1,0:T(8,128)(2,1)S(1)}, u32[]{:S(2)}, u32[]{:S(2)}) collective-permute-start(bf16[3,136,128]{2,1,0:T(8,128)(2,1)S(1)} %get-tuple-element.24), channel_id=1, source_target_pairs={{0,1},{1,0},{2,3},{3,2},{4,5},{5,4},{6,7},{7,6},{8,9},{9,8},{10,11... | collective-permute-start | bytes 313352 | tf_op jit(solution)/shard_map/ppermute | solution.py:342
  3.3 9.5 %collective-permute-start.1 = (bf16[264,128]{1,0:T(8,128)(2,1)S(1)}, bf16[264,128]{1,0:T(8,128)(2,1)S(1)}, u32[]{:S(2)}, u32[]{:S(2)}) collective-permute-start(bf16[264,128]{1,0:T(8,128)(2,1)S(1)} %get-tuple-element.25), channel_id=1, source_target_pairs={{0,8},{1,11},{2,10},{3,9},{4,12},{5,15},{6,14},{7,13},{8,0},{9,3},... | collective-permute-start | bytes 202760 | tf_op jit(solution)/shard_map/ppermute | solution.py:342
  7.3 6.8 %collective-permute-start.2 = (bf16[264,128]{1,0:T(8,128)(2,1)S(1)}, bf16[264,128]{1,0:T(8,128)(2,1)S(1)}, u32[]{:S(2)}, u32[]{:S(2)}) collective-permute-start(bf16[264,128]{1,0:T(8,128)(2,1)S(1)} %get-tuple-element.26), channel_id=1, source_target_pairs={{0,12},{1,15},{2,14},{3,13},{4,8},{5,11},{6,10},{7,9},{8,4},{9,7},... | collective-permute-start | bytes 202760 | tf_op jit(solution)/shard_map/ppermute | solution.py:342
  8.7 6.2 %collective-permute-start.3 = (bf16[264,128]{1,0:T(8,128)(2,1)S(1)}, bf16[264,128]{1,0:T(8,128)(2,1)S(1)}, u32[]{:S(2)}, u32[]{:S(2)}) collective-permute-start(bf16[264,128]{1,0:T(8,128)(2,1)S(1)} %get-tuple-element.27), channel_id=1, source_target_pairs={{0,4},{1,7},{2,6},{3,5},{4,0},{5,3},{6,2},{7,1},{8,12},{9,15},{10,... | collective-permute-start | bytes 202760 | tf_op jit(solution)/shard_map/ppermute | solution.py:342
  8.9 3.9 %collective-permute-start.4 = (bf16[136,128]{1,0:T(8,128)(2,1)S(1)}, bf16[136,128]{1,0:T(8,128)(2,1)S(1)}, u32[]{:S(2)}, u32[]{:S(2)}) collective-permute-start(bf16[136,128]{1,0:T(8,128)(2,1)S(1)} %get-tuple-element.28), channel_id=1, source_target_pairs={{0,2},{1,3},{2,0},{3,1},{4,6},{5,7},{6,4},{7,5},{8,10},{9,11},{10,... | collective-permute-start | bytes 104456 | tf_op jit(solution)/shard_map/ppermute | solution.py:342
  14.9 1.5 %copy-start.7 = (f32[32,256]{1,0:T(8,128)S(1)}, f32[32,256]{1,0:T(8,128)}, u32[]{:S(2)}) copy-start(f32[32,256]{1,0:T(8,128)} %constant.7.clone.twist_ref) | copy-start | bytes 98308
  14.9 1.4 %collective-permute-start.5 = (bf16[544,128]{1,0:T(8,128)(2,1)S(1)}, bf16[544,128]{1,0:T(8,128)(2,1)S(1)}, u32[]{:S(2)}, u32[]{:S(2)}) collective-permute-start(bf16[544,128]{1,0:T(8,128)(2,1)S(1)} %get-tuple-element.31), channel_id=1, source_target_pairs={{0,1},{1,0},{2,3},{3,2},{4,5},{5,4},{6,7},{7,6},{8,9},{9,8},{10,11... | collective-permute-start | bytes 417800 | tf_op jit(solution)/shard_map/ppermute | solution.py:342
  16.3 11.9 %copy-start = (bf16[256,768]{1,0:T(8,128)(2,1)S(1)}, bf16[256,768]{1,0:T(8,128)(2,1)}, u32[]{:S(2)}) copy-start(bf16[256,768]{1,0:T(8,128)(2,1)} %refs_2_.1) | copy-start | bytes 1179652
  17.7 10.5 %copy-start.1 = (bf16[256,256]{1,0:T(8,128)(2,1)S(1)}, bf16[256,256]{1,0:T(8,128)(2,1)}, u32[]{:S(2)}) copy-start(bf16[256,256]{1,0:T(8,128)(2,1)} %refs_0_.1) | copy-start | bytes 393220
  17.8 1.3 %collective-permute-start.6 = (bf16[3,32,256]{2,1,0:T(8,128)(2,1)S(1)}, bf16[3,32,256]{2,1,0:T(8,128)(2,1)S(1)}, u32[]{:S(2)}, u32[]{:S(2)}) collective-permute-start(bf16[3,32,256]{2,1,0:T(8,128)(2,1)S(1)} %get-tuple-element.33), channel_id=1, source_target_pairs={{0,1},{1,0},{2,3},{3,2},{4,5},{5,4},{6,7},{7,6},{8,9},{9,8},{10,11... | collective-permute-start | bytes 147464 | tf_op jit(solution)/shard_map/ppermute | solution.py:342
  19.1 8.1 %collective-permute-start.7 = (bf16[64,256]{1,0:T(8,128)(2,1)S(1)}, bf16[64,256]{1,0:T(8,128)(2,1)S(1)}, u32[]{:S(2)}, u32[]{:S(2)}) collective-permute-start(bf16[64,256]{1,0:T(8,128)(2,1)S(1)} %get-tuple-element.34), channel_id=1, source_target_pairs={{0,8},{1,11},{2,10},{3,9},{4,12},{5,15},{6,14},{7,13},{8,0},{9,3},... | collective-permute-start | bytes 98312 | tf_op jit(solution)/shard_map/ppermute | solution.py:342
  21.9 5.9 %collective-permute-start.8 = (bf16[64,256]{1,0:T(8,128)(2,1)S(1)}, bf16[64,256]{1,0:T(8,128)(2,1)S(1)}, u32[]{:S(2)}, u32[]{:S(2)}) collective-permute-start(bf16[64,256]{1,0:T(8,128)(2,1)S(1)} %get-tuple-element.35), channel_id=1, source_target_pairs={{0,12},{1,15},{2,14},{3,13},{4,8},{5,11},{6,10},{7,9},{8,4},{9,7},... | collective-permute-start | bytes 98312 | tf_op jit(solution)/shard_map/ppermute | solution.py:342
  22.8 5.0 %collective-permute-start.9 = (bf16[64,256]{1,0:T(8,128)(2,1)S(1)}, bf16[64,256]{1,0:T(8,128)(2,1)S(1)}, u32[]{:S(2)}, u32[]{:S(2)}) collective-permute-start(bf16[64,256]{1,0:T(8,128)(2,1)S(1)} %get-tuple-element.36), channel_id=1, source_target_pairs={{0,4},{1,7},{2,6},{3,5},{4,0},{5,3},{6,2},{7,1},{8,12},{9,15},{10,... | collective-permute-start | bytes 98312 | tf_op jit(solution)/shard_map/ppermute | solution.py:342
  23.3 3.9 %collective-permute-start.10 = (bf16[32,256]{1,0:T(8,128)(2,1)S(1)}, bf16[32,256]{1,0:T(8,128)(2,1)S(1)}, u32[]{:S(2)}, u32[]{:S(2)}) collective-permute-start(bf16[32,256]{1,0:T(8,128)(2,1)S(1)} %get-tuple-element.37), channel_id=1, source_target_pairs={{0,2},{1,3},{2,0},{3,1},{4,6},{5,7},{6,4},{7,5},{8,10},{9,11},{10,... | collective-permute-start | bytes 49160 | tf_op jit(solution)/shard_map/ppermute | solution.py:342
  27.8 0.7 %copy-start.3 = (f32[3,768]{1,0:T(4,128)S(1)}, f32[3,768]{1,0:T(4,128)}, u32[]{:S(2)}) copy-start(f32[3,768]{1,0:T(4,128)} %refs_3_.1) | copy-start | bytes 27652
  27.8 0.7 %copy-start.4 = (f32[256]{0:T(256)S(1)}, f32[256]{0:T(256)}, u32[]{:S(2)}) copy-start(f32[256]{0:T(256)} %param.12) | copy-start | bytes 3076
  27.8 1.4 %copy-start.2 = (bf16[256,256]{1,0:T(8,128)(2,1)S(1)}, bf16[256,256]{1,0:T(8,128)(2,1)}, u32[]{:S(2)}) copy-start(bf16[256,256]{1,0:T(8,128)(2,1)} %w_ref.3) | copy-start | bytes 393220
  27.8 1.4 %collective-permute-start.11 = (bf16[128,256]{1,0:T(8,128)(2,1)S(1)}, bf16[128,256]{1,0:T(8,128)(2,1)S(1)}, u32[]{:S(2)}, u32[]{:S(2)}) collective-permute-start(bf16[128,256]{1,0:T(8,128)(2,1)S(1)} %get-tuple-element.40), channel_id=1, source_target_pairs={{0,1},{1,0},{2,3},{3,2},{4,5},{5,4},{6,7},{7,6},{8,9},{9,8},{10,11... | collective-permute-start | bytes 196616 | tf_op jit(solution)/shard_map/ppermute | solution.py:342

commit v13 on v12

--- a/solution.py
+++ b/solution.py
@@ -15,6 +15,7 @@
 seq = ("chip", "core")
 rim_step = 2 * edge
 chan_tile = 16
+near_pads = 2
 vmem_bytes = 32 * 2**20
 
 
@@ -68,23 +69,27 @@
 def put_routes(source_ref, rim_ref, keep_ref, give_ref, near_ref, home_ref):
     chip, core = lax.axis_index("chip"), lax.axis_index("core")
     size = source_ref.shape[0] // 2 // (lax.axis_size("chip"))
+    extra = home_ref.shape[0] - 2 * size
 
     def put(out_ref, distance):
         start = pl.multiple_of((chip ^ distance) * 2 * size, 2 * size)
         out_ref[0 : 2 * size, :] = source_ref[pl.ds(start, 2 * size), :]
-        if rim_ref is not None:
-            out_ref[2 * size :, :] = rim_ref[chip ^ distance]
+        if extra:
+            out_ref[2 * size : 2 * size + extra, :] = rim_ref[chip ^ distance]
 
     for turn, route in enumerate(routes_of(lax.axis_size("chip"))):
         own, other = carried(route, core)
         put(keep_ref.at[turn], own)
         put(give_ref.at[turn], other)
+    put(home_ref, 0)
     put(near_ref, 1)
-    put(home_ref, 0)
+    for begin in range(2 * size + extra, near_ref.shape[0], 2 * size):
+        near_ref[begin : begin + 2 * size, :] = home_ref[0 : 2 * size, :]
 
 
 def half_rims(first_ref, second_ref, begin):
-    pair = [ref[begin:, :].astype(jnp.float32)[0 : edge // 2] for ref in (first_ref, second_ref)]
+    pair = [ref[begin : begin + edge, :].astype(jnp.float32) for ref in (first_ref, second_ref)]
+    pair = [rims[0 : edge // 2] for rims in pair]
     return jnp.concatenate(pair).astype(jnp.bfloat16)
 
 
@@ -387,7 +392,8 @@
         if not staged:
             return (bf16(*shape),)
         size, turns = 2 * shape[0] // devices + extra, len(routes_of(chips))
-        return (bf16(turns, size, shape[1]),) * 2 + (bf16(size, shape[1]),) * 2
+        near = size + near_pads * (size - extra)
+        return (bf16(turns, size, shape[1]),) * 2 + (bf16(near, shape[1]), bf16(size, shape[1]))
 
     def scratch(*shapes):
         return [pltpu.VMEM(*shape) for shape in shapes] if staged else []

time: 30.2 us -> 30.3 us (level)
  starting transfers between devices: 13.9 us -> 13.4 us
  waiting for transfers between devices: 11.4 us -> 11.9 us
    ppermute x12, waiting for transfers between devices: 11.4 us -> 11.9 us  [permute(): lax.ppermute(array, seq, [(i, partner(i)) for i in range(lax.axis_size(se...]
    ppermute x12, starting transfers between devices: 13.9 us -> 13.4 us  [permute(): lax.ppermute(array, seq, [(i, partner(i)) for i in range(lax.axis_size(se...]
  transfers between devices with their start and end apart: 12 -> 12, of which waited for: 9 -> 7; matrix products, arithmetic and copies ran while one was open for 0% -> 0% of each run, Pallas kernels for 1% -> 1%
where the time goes in v13:
time: 30.3 us; the launch traced here: 30.2 us
  starting transfers between devices  13.4 us (44%)
  waiting for transfers between devices  11.9 us (39%)
  Pallas kernels  4.47 us (15%)
    ppermute x12, starting transfers between devices, permute(): lax.ppermute(array, seq, [(i, partner(i)) for i in range(lax.axis_size(se...  13.4 us
    ppermute x12, waiting for transfers between devices, permute(): lax.ppermute(array, seq, [(i, partner(i)) for i in range(lax.axis_size(se...  11.9 us
    pallas_call x8, Pallas kernels, call(): pl.pallas_call(body, out_shape=outs, in_specs=[whole(space) for space in...  4.47 us
  transfers between devices with their start and end apart: 12, of which 7 were waited for; matrix products, arithmetic and copies ran while one was open for 0% of the time, Pallas kernels for 1%

profile of v13, /device:TPU:0, one launch (start us, length us, event | category | flops | bytes accessed | tf_op | source)
XLA Modules:
  0.0 30.2 jit_solution(11999444715436000519)
XLA Ops:
  0.0 1.8 %shard_map.110 = (bf16[3,136,128]{2,1,0:T(8,128)(2,1)S(1)}, bf16[3,136,128]{2,1,0:T(8,128)(2,1)S(1)}, bf16[392,128]{1,0:T(8,128)(2,1)S(1)}, bf16[136,128]{1,0:T(8,128)(2,1)S(1)}) custom-call(bf16[256,256]{1,0:T(8,128)(2,1)} %refs_0_.1, f32[1,256]{1,0:T(1,128)} %bitcast.2, bf16[256,768]{1,0:T(8,128)(2,1)} %refs_2_.1, f32[3,768]{1,0:T(4,128)} %refs_3_.1, ...), custom_call_target="tpu_custom_call" | custom-call | flops 100663296 | bytes 1500000 | tf_op jit(solution)/shard_map/pallas_call | solution.py:27
  1.8 0.5 %collective-permute-start = (bf16[3,136,128]{2,1,0:T(8,128)(2,1)S(1)}, bf16[3,136,128]{2,1,0:T(8,128)(2,1)S(1)}, u32[]{:S(2)}, u32[]{:S(2)}) collective-permute-start(bf16[3,136,128]{2,1,0:T(8,128)(2,1)S(1)} %get-tuple-element.24), channel_id=1, source_target_pairs={{0,1},{1,0},{2,3},{3,2},{4,5},{5,4},{6,7},{7,6},{8,9},{9,8},{10,11... | collective-permute-start | bytes 313352 | tf_op jit(solution)/shard_map/ppermute | solution.py:347
  2.3 2.6 %collective-permute-start.4 = (bf16[392,128]{1,0:T(8,128)(2,1)S(1)}, bf16[392,128]{1,0:T(8,128)(2,1)S(1)}, u32[]{:S(2)}, u32[]{:S(2)}) collective-permute-start(bf16[392,128]{1,0:T(8,128)(2,1)S(1)} %get-tuple-element.28), channel_id=1, source_target_pairs={{0,2},{1,3},{2,0},{3,1},{4,6},{5,7},{6,4},{7,5},{8,10},{9,11},{10,... | collective-permute-start | bytes 301064 | tf_op jit(solution)/shard_map/ppermute | solution.py:347
  4.9 0.0 collective-permute-done.got_ref
  4.9 0.0 copy-start.5
  4.9 0.0 copy-start.6
  4.9 2.7 %collective-permute-start.1 = (bf16[264,128]{1,0:T(8,128)(2,1)S(1)}, bf16[264,128]{1,0:T(8,128)(2,1)S(1)}, u32[]{:S(2)}, u32[]{:S(2)}) collective-permute-start(bf16[264,128]{1,0:T(8,128)(2,1)S(1)} %get-tuple-element.25), channel_id=1, source_target_pairs={{0,8},{1,11},{2,10},{3,9},{4,12},{5,15},{6,14},{7,13},{8,0},{9,3},... | collective-permute-start | bytes 202760 | tf_op jit(solution)/shard_map/ppermute | solution.py:347
  7.6 1.4 %collective-permute-start.2 = (bf16[264,128]{1,0:T(8,128)(2,1)S(1)}, bf16[264,128]{1,0:T(8,128)(2,1)S(1)}, u32[]{:S(2)}, u32[]{:S(2)}) collective-permute-start(bf16[264,128]{1,0:T(8,128)(2,1)S(1)} %get-tuple-element.26), channel_id=1, source_target_pairs={{0,12},{1,15},{2,14},{3,13},{4,8},{5,11},{6,10},{7,9},{8,4},{9,7},... | collective-permute-start | bytes 202760 | tf_op jit(solution)/shard_map/ppermute | solution.py:347
  8.9 0.2 collective-permute-start.3
  9.2 0.0 collective-permute-done.4.refs_3_
  9.2 3.2 %collective-permute-done.1.refs_0_ = bf16[264,128]{1,0:T(8,128)(2,1)S(1)} collective-permute-done((bf16[264,128]{1,0:T(8,128)(2,1)S(1)}, bf16[264,128]{1,0:T(8,128)(2,1)S(1)}, u32[]{:S(2)}, u32[]{:S(2)}) %collective-permute-start.1) | collective-permute-done | bytes 67616 | tf_op jit(solution)/shard_map/ppermute | solution.py:347
  12.4 2.1 %collective-permute-done.2.refs_1_ = bf16[264,128]{1,0:T(8,128)(2,1)S(1)} collective-permute-done((bf16[264,128]{1,0:T(8,128)(2,1)S(1)}, bf16[264,128]{1,0:T(8,128)(2,1)S(1)}, u32[]{:S(2)}, u32[]{:S(2)}) %collective-permute-start.2) | collective-permute-done | bytes 67616 | tf_op jit(solution)/shard_map/ppermute | solution.py:347
  14.4 0.8 %collective-permute-done.3.refs_2_ = bf16[264,128]{1,0:T(8,128)(2,1)S(1)} collective-permute-done((bf16[264,128]{1,0:T(8,128)(2,1)S(1)}, bf16[264,128]{1,0:T(8,128)(2,1)S(1)}, u32[]{:S(2)}, u32[]{:S(2)}) %collective-permute-start.3) | collective-permute-done | bytes 67616 | tf_op jit(solution)/shard_map/ppermute | solution.py:347
  15.2 0.0 copy-start.7
  15.2 0.3 collective-permute-start.5
  15.5 1.1 %collective-permute-done.5.refs_1_ = bf16[544,128]{1,0:T(8,128)(2,1)S(1)} collective-permute-done((bf16[544,128]{1,0:T(8,128)(2,1)S(1)}, bf16[544,128]{1,0:T(8,128)(2,1)S(1)}, u32[]{:S(2)}, u32[]{:S(2)}) %collective-permute-start.5) | collective-permute-done | bytes 139296 | tf_op jit(solution)/shard_map/ppermute | solution.py:347
  16.7 0.0 copy-done.5
  16.7 0.0 copy-done.6
  16.7 0.0 copy-done.7
  16.7 0.0 copy-start
  16.7 1.4 %shard_map.113 = (bf16[3,32,256]{2,1,0:T(8,128)(2,1)S(1)}, bf16[3,32,256]{2,1,0:T(8,128)(2,1)S(1)}, bf16[96,256]{1,0:T(8,128)(2,1)S(1)}, bf16[32,256]{1,0:T(8,128)(2,1)S(1)}) custom-call(bf16[512,256]{1,0:T(8,128)(2,1)S(1)} %copy-done.5, f32[32,256]{1,0:T(8,128)S(1)} %copy-done.7, bf16[256,512]{1,0:T(8,128)(2,1)S(1)} %copy-done.6, ...), custom_call_target="tpu_custom_call" | custom-call | flops 603979776 | bytes 2000000 | tf_op jit(solution)/shard_map/pallas_call | solution.py:27
  18.1 0.3 collective-permute-start.6
  18.4 1.3 %collective-permute-start.10 = (bf16[96,256]{1,0:T(8,128)(2,1)S(1)}, bf16[96,256]{1,0:T(8,128)(2,1)S(1)}, u32[]{:S(2)}, u32[]{:S(2)}) collective-permute-start(bf16[96,256]{1,0:T(8,128)(2,1)S(1)} %get-tuple-element.37), channel_id=1, source_target_pairs={{0,2},{1,3},{2,0},{3,1},{4,6},{5,7},{6,4},{7,5},{8,10},{9,11},{10,... | collective-permute-start | bytes 147464 | tf_op jit(solution)/shard_map/ppermute | solution.py:347
  19.6 0.0 collective-permute-done.6.got_ref
  19.6 0.0 copy-start.1
  19.7 2.4 %collective-permute-start.7 = (bf16[64,256]{1,0:T(8,128)(2,1)S(1)}, bf16[64,256]{1,0:T(8,128)(2,1)S(1)}, u32[]{:S(2)}, u32[]{:S(2)}) collective-permute-start(bf16[64,256]{1,0:T(8,128)(2,1)S(1)} %get-tuple-element.34), channel_id=1, source_target_pairs={{0,8},{1,11},{2,10},{3,9},{4,12},{5,15},{6,14},{7,13},{8,0},{9,3},... | collective-permute-start | bytes 98312 | tf_op jit(solution)/shard_map/ppermute | solution.py:347
  22.0 0.9 %collective-permute-start.8 = (bf16[64,256]{1,0:T(8,128)(2,1)S(1)}, bf16[64,256]{1,0:T(8,128)(2,1)S(1)}, u32[]{:S(2)}, u32[]{:S(2)}) collective-permute-start(bf16[64,256]{1,0:T(8,128)(2,1)S(1)} %get-tuple-element.35), channel_id=1, source_target_pairs={{0,12},{1,15},{2,14},{3,13},{4,8},{5,11},{6,10},{7,9},{8,4},{9,7},... | collective-permute-start | bytes 98312 | tf_op jit(solution)/shard_map/ppermute | solution.py:347
  23.0 0.5 %collective-permute-start.9 = (bf16[64,256]{1,0:T(8,128)(2,1)S(1)}, bf16[64,256]{1,0:T(8,128)(2,1)S(1)}, u32[]{:S(2)}, u32[]{:S(2)}) collective-permute-start(bf16[64,256]{1,0:T(8,128)(2,1)S(1)} %get-tuple-element.36), channel_id=1, source_target_pairs={{0,4},{1,7},{2,6},{3,5},{4,0},{5,3},{6,2},{7,1},{8,12},{9,15},{10,... | collective-permute-start | bytes 98312 | tf_op jit(solution)/shard_map/ppermute | solution.py:347
  23.5 0.0 collective-permute-done.10.refs_3_
  23.5 1.8 %collective-permute-done.7.refs_0_ = bf16[64,256]{1,0:T(8,128)(2,1)S(1)} collective-permute-done((bf16[64,256]{1,0:T(8,128)(2,1)S(1)}, bf16[64,256]{1,0:T(8,128)(2,1)S(1)}, u32[]{:S(2)}, u32[]{:S(2)}) %collective-permute-start.7) | collective-permute-done | bytes 32800 | tf_op jit(solution)/shard_map/ppermute | solution.py:347
  25.3 2.6 %collective-permute-done.8.refs_1_ = bf16[64,256]{1,0:T(8,128)(2,1)S(1)} collective-permute-done((bf16[64,256]{1,0:T(8,128)(2,1)S(1)}, bf16[64,256]{1,0:T(8,128)(2,1)S(1)}, u32[]{:S(2)}, u32[]{:S(2)}) %collective-permute-start.8) | collective-permute-done | bytes 32800 | tf_op jit(solution)/shard_map/ppermute | solution.py:347
  27.9 0.0 collective-permute-done.9.refs_2_
  27.9 0.0 copy-start.3
  27.9 0.0 copy-start.4
  27.9 0.0 copy-start.2
  27.9 0.4 %collective-permute-start.11 = (bf16[128,256]{1,0:T(8,128)(2,1)S(1)}, bf16[128,256]{1,0:T(8,128)(2,1)S(1)}, u32[]{:S(2)}, u32[]{:S(2)}) collective-permute-start(bf16[128,256]{1,0:T(8,128)(2,1)S(1)} %get-tuple-element.40), channel_id=1, source_target_pairs={{0,1},{1,0},{2,3},{3,2},{4,5},{5,4},{6,7},{7,6},{8,9},{9,8},{10,11... | collective-permute-start | bytes 196616 | tf_op jit(solution)/shard_map/ppermute | solution.py:347
  28.3 0.0 copy-done
  28.3 0.0 copy-done.1
  28.3 0.3 copy-done.3
  28.6 0.0 copy-done.4
  28.6 0.3 %shard_map.109.query_ref = f32[256,256]{1,0:T(8,128)S(1)} custom-call(bf16[256,256]{1,0:T(8,128)(2,1)S(1)} %copy-done.1, f32[1,256]{1,0:T(1,128)S(1)} %bitcast.3, bf16[256,768]{1,0:T(8,128)(2,1)S(1)} %copy-done, f32[3,768]{1,0:T(4,128)S(1)} %copy-done.3), custom_call_target="tpu_custom_call" | custom-call | flops 33554432 | bytes 800000 | tf_op jit(solution)/shard_map/pallas_call | solution.py:27
  28.9 0.3 %collective-permute-done.11.refs_1_ = bf16[128,256]{1,0:T(8,128)(2,1)S(1)} collective-permute-done((bf16[128,256]{1,0:T(8,128)(2,1)S(1)}, bf16[128,256]{1,0:T(8,128)(2,1)S(1)}, u32[]{:S(2)}, u32[]{:S(2)}) %collective-permute-start.11) | collective-permute-done | bytes 65568 | tf_op jit(solution)/shard_map/ppermute | solution.py:347
  29.2 0.0 copy-done.2
  29.2 0.9 %shard_map.116 = bf16[256,256]{1,0:T(8,128)(2,1)} custom-call(f32[256,256]{1,0:T(8,128)S(1)} %shard_map.109.query_ref, bf16[256,256]{1,0:T(8,128)(2,1)S(1)} %copy-done.2, bf16[128,256]{1,0:T(8,128)(2,1)S(1)} %get-tuple-element.39.refs_0_, bf16[128,256]{1,0:T(8,128)(2,1)S(1)} %collective-permute-done.11.refs_1_), custom_call_target="tpu_custom_call" | custom-call | flops 33554432 | bytes 600000 | tf_op jit(solution)/shard_map/pallas_call | solution.py:27
  (4 shorter events, 0.1 us)
Async XLA Ops:
  1.8 3.1 %collective-permute-start = (bf16[3,136,128]{2,1,0:T(8,128)(2,1)S(1)}, bf16[3,136,128]{2,1,0:T(8,128)(2,1)S(1)}, u32[]{:S(2)}, u32[]{:S(2)}) collective-permute-start(bf16[3,136,128]{2,1,0:T(8,128)(2,1)S(1)} %get-tuple-element.24), channel_id=1, source_target_pairs={{0,1},{1,0},{2,3},{3,2},{4,5},{5,4},{6,7},{7,6},{8,9},{9,8},{10,11... | collective-permute-start | bytes 313352 | tf_op jit(solution)/shard_map/ppermute | solution.py:347
  2.3 6.9 %collective-permute-start.4 = (bf16[392,128]{1,0:T(8,128)(2,1)S(1)}, bf16[392,128]{1,0:T(8,128)(2,1)S(1)}, u32[]{:S(2)}, u32[]{:S(2)}) collective-permute-start(bf16[392,128]{1,0:T(8,128)(2,1)S(1)} %get-tuple-element.28), channel_id=1, source_target_pairs={{0,2},{1,3},{2,0},{3,1},{4,6},{5,7},{6,4},{7,5},{8,10},{9,11},{10,... | collective-permute-start | bytes 301064 | tf_op jit(solution)/shard_map/ppermute | solution.py:347
  4.9 11.8 %copy-start.5 = (bf16[512,256]{1,0:T(8,128)(2,1)S(1)}, bf16[512,256]{1,0:T(8,128)(2,1)}, u32[]{:S(2)}) copy-start(bf16[512,256]{1,0:T(8,128)(2,1)} %constant.6.clone.first_ref) | copy-start | bytes 786436
  4.9 11.8 %copy-start.6 = (bf16[256,512]{1,0:T(8,128)(2,1)S(1)}, bf16[256,512]{1,0:T(8,128)(2,1)}, u32[]{:S(2)}) copy-start(bf16[256,512]{1,0:T(8,128)(2,1)} %constant.8.clone.inner_ref) | copy-start | bytes 786436
  4.9 7.4 %collective-permute-start.1 = (bf16[264,128]{1,0:T(8,128)(2,1)S(1)}, bf16[264,128]{1,0:T(8,128)(2,1)S(1)}, u32[]{:S(2)}, u32[]{:S(2)}) collective-permute-start(bf16[264,128]{1,0:T(8,128)(2,1)S(1)} %get-tuple-element.25), channel_id=1, source_target_pairs={{0,8},{1,11},{2,10},{3,9},{4,12},{5,15},{6,14},{7,13},{8,0},{9,3},... | collective-permute-start | bytes 202760 | tf_op jit(solution)/shard_map/ppermute | solution.py:347
  7.6 6.9 %collective-permute-start.2 = (bf16[264,128]{1,0:T(8,128)(2,1)S(1)}, bf16[264,128]{1,0:T(8,128)(2,1)S(1)}, u32[]{:S(2)}, u32[]{:S(2)}) collective-permute-start(bf16[264,128]{1,0:T(8,128)(2,1)S(1)} %get-tuple-element.26), channel_id=1, source_target_pairs={{0,12},{1,15},{2,14},{3,13},{4,8},{5,11},{6,10},{7,9},{8,4},{9,7},... | collective-permute-start | bytes 202760 | tf_op jit(solution)/shard_map/ppermute | solution.py:347
  8.9 6.3 %collective-permute-start.3 = (bf16[264,128]{1,0:T(8,128)(2,1)S(1)}, bf16[264,128]{1,0:T(8,128)(2,1)S(1)}, u32[]{:S(2)}, u32[]{:S(2)}) collective-permute-start(bf16[264,128]{1,0:T(8,128)(2,1)S(1)} %get-tuple-element.27), channel_id=1, source_target_pairs={{0,4},{1,7},{2,6},{3,5},{4,0},{5,3},{6,2},{7,1},{8,12},{9,15},{10,... | collective-permute-start | bytes 202760 | tf_op jit(solution)/shard_map/ppermute | solution.py:347
  15.2 1.5 %copy-start.7 = (f32[32,256]{1,0:T(8,128)S(1)}, f32[32,256]{1,0:T(8,128)}, u32[]{:S(2)}) copy-start(f32[32,256]{1,0:T(8,128)} %constant.7.clone.twist_ref) | copy-start | bytes 98308
  15.2 1.4 %collective-permute-start.5 = (bf16[544,128]{1,0:T(8,128)(2,1)S(1)}, bf16[544,128]{1,0:T(8,128)(2,1)S(1)}, u32[]{:S(2)}, u32[]{:S(2)}) collective-permute-start(bf16[544,128]{1,0:T(8,128)(2,1)S(1)} %get-tuple-element.31), channel_id=1, source_target_pairs={{0,1},{1,0},{2,3},{3,2},{4,5},{5,4},{6,7},{7,6},{8,9},{9,8},{10,11... | collective-permute-start | bytes 417800 | tf_op jit(solution)/shard_map/ppermute | solution.py:347
  16.7 11.6 %copy-start = (bf16[256,768]{1,0:T(8,128)(2,1)S(1)}, bf16[256,768]{1,0:T(8,128)(2,1)}, u32[]{:S(2)}) copy-start(bf16[256,768]{1,0:T(8,128)(2,1)} %refs_2_.1) | copy-start | bytes 1179652
  18.1 1.5 %collective-permute-start.6 = (bf16[3,32,256]{2,1,0:T(8,128)(2,1)S(1)}, bf16[3,32,256]{2,1,0:T(8,128)(2,1)S(1)}, u32[]{:S(2)}, u32[]{:S(2)}) collective-permute-start(bf16[3,32,256]{2,1,0:T(8,128)(2,1)S(1)} %get-tuple-element.33), channel_id=1, source_target_pairs={{0,1},{1,0},{2,3},{3,2},{4,5},{5,4},{6,7},{7,6},{8,9},{9,8},{10,11... | collective-permute-start | bytes 147464 | tf_op jit(solution)/shard_map/ppermute | solution.py:347
  18.4 5.1 %collective-permute-start.10 = (bf16[96,256]{1,0:T(8,128)(2,1)S(1)}, bf16[96,256]{1,0:T(8,128)(2,1)S(1)}, u32[]{:S(2)}, u32[]{:S(2)}) collective-permute-start(bf16[96,256]{1,0:T(8,128)(2,1)S(1)} %get-tuple-element.37), channel_id=1, source_target_pairs={{0,2},{1,3},{2,0},{3,1},{4,6},{5,7},{6,4},{7,5},{8,10},{9,11},{10,... | collective-permute-start | bytes 147464 | tf_op jit(solution)/shard_map/ppermute | solution.py:347
  19.6 8.7 %copy-start.1 = (bf16[256,256]{1,0:T(8,128)(2,1)S(1)}, bf16[256,256]{1,0:T(8,128)(2,1)}, u32[]{:S(2)}) copy-start(bf16[256,256]{1,0:T(8,128)(2,1)} %refs_0_.1) | copy-start | bytes 393220
  19.7 5.6 %collective-permute-start.7 = (bf16[64,256]{1,0:T(8,128)(2,1)S(1)}, bf16[64,256]{1,0:T(8,128)(2,1)S(1)}, u32[]{:S(2)}, u32[]{:S(2)}) collective-permute-start(bf16[64,256]{1,0:T(8,128)(2,1)S(1)} %get-tuple-element.34), channel_id=1, source_target_pairs={{0,8},{1,11},{2,10},{3,9},{4,12},{5,15},{6,14},{7,13},{8,0},{9,3},... | collective-permute-start | bytes 98312 | tf_op jit(solution)/shard_map/ppermute | solution.py:347
  22.0 5.8 %collective-permute-start.8 = (bf16[64,256]{1,0:T(8,128)(2,1)S(1)}, bf16[64,256]{1,0:T(8,128)(2,1)S(1)}, u32[]{:S(2)}, u32[]{:S(2)}) collective-permute-start(bf16[64,256]{1,0:T(8,128)(2,1)S(1)} %get-tuple-element.35), channel_id=1, source_target_pairs={{0,12},{1,15},{2,14},{3,13},{4,8},{5,11},{6,10},{7,9},{8,4},{9,7},... | collective-permute-start | bytes 98312 | tf_op jit(solution)/shard_map/ppermute | solution.py:347
  23.0 4.9 %collective-permute-start.9 = (bf16[64,256]{1,0:T(8,128)(2,1)S(1)}, bf16[64,256]{1,0:T(8,128)(2,1)S(1)}, u32[]{:S(2)}, u32[]{:S(2)}) collective-permute-start(bf16[64,256]{1,0:T(8,128)(2,1)S(1)} %get-tuple-element.36), channel_id=1, source_target_pairs={{0,4},{1,7},{2,6},{3,5},{4,0},{5,3},{6,2},{7,1},{8,12},{9,15},{10,... | collective-permute-start | bytes 98312 | tf_op jit(solution)/shard_map/ppermute | solution.py:347
  27.9 0.7 %copy-start.3 = (f32[3,768]{1,0:T(4,128)S(1)}, f32[3,768]{1,0:T(4,128)}, u32[]{:S(2)}) copy-start(f32[3,768]{1,0:T(4,128)} %refs_3_.1) | copy-start | bytes 27652
  27.9 0.7 %copy-start.4 = (f32[256]{0:T(256)S(1)}, f32[256]{0:T(256)}, u32[]{:S(2)}) copy-start(f32[256]{0:T(256)} %param.12) | copy-start | bytes 3076
  27.9 1.3 %copy-start.2 = (bf16[256,256]{1,0:T(8,128)(2,1)S(1)}, bf16[256,256]{1,0:T(8,128)(2,1)}, u32[]{:S(2)}) copy-start(bf16[256,256]{1,0:T(8,128)(2,1)} %w_ref.3) | copy-start | bytes 393220
  27.9 1.3 %collective-permute-start.11 = (bf16[128,256]{1,0:T(8,128)(2,1)S(1)}, bf16[128,256]{1,0:T(8,128)(2,1)S(1)}, u32[]{:S(2)}, u32[]{:S(2)}) collective-permute-start(bf16[128,256]{1,0:T(8,128)(2,1)S(1)} %get-tuple-element.40), channel_id=1, source_target_pairs={{0,1},{1,0},{2,3},{3,2},{4,5},{5,4},{6,7},{7,6},{8,9},{9,8},{10,11... | collective-permute-start | bytes 196616 | tf_op jit(solution)/shard_map/ppermute | solution.py:347

commit v14 on v13

--- a/solution.py
+++ b/solution.py
@@ -15,7 +15,6 @@
 seq = ("chip", "core")
 rim_step = 2 * edge
 chan_tile = 16
-near_pads = 2
 vmem_bytes = 32 * 2**20
 
 
@@ -23,12 +22,12 @@
     return pl.BlockSpec(memory_space=space)
 
 
-def call(body, outs, args, spaces, scratch=(), flops=0, moved=0):
+def call(body, outs, args, spaces, scratch=(), flops=0, moved=0, out_space=pltpu.VMEM):
     return pl.pallas_call(
         body,
         out_shape=outs,
         in_specs=[whole(space) for space in spaces],
-        out_specs=jax.tree.map(lambda _: whole(pltpu.VMEM), outs),
+        out_specs=jax.tree.map(lambda _: whole(out_space), outs),
         scratch_shapes=list(scratch),
         compiler_params=pltpu.CompilerParams(vmem_limit_bytes=vmem_bytes),
         cost_estimate=pl.CostEstimate(flops=flops, bytes_accessed=moved, transcendentals=0),
@@ -83,8 +82,9 @@
         put(give_ref.at[turn], other)
     put(home_ref, 0)
     put(near_ref, 1)
-    for begin in range(2 * size + extra, near_ref.shape[0], 2 * size):
-        near_ref[begin : begin + 2 * size, :] = home_ref[0 : 2 * size, :]
+    begin = 2 * size + extra
+    near_ref[begin : begin + 2 * size, :] = home_ref[0 : 2 * size, :]
+    near_ref[begin + 2 * size :, :] = home_ref[0:chan_tile, :]
 
 
 def half_rims(first_ref, second_ref, begin):
@@ -171,8 +171,15 @@
     tokens_ref, gain_ref, w_ref, short_ref, long_ref, medium_ref, skip_ref = held
     rows, width = tokens_ref.shape
     copies = [pltpu.make_async_copy(h, v, sems.at[i]) for i, (h, v) in enumerate(zip(hbm, held))]
-    for copy in copies:
+    is_first = lax.axis_index(seq) == 0
+    for copy in copies[:5]:
         copy.start()
+
+    @pl.when(is_first)
+    def _():
+        for copy in copies[5:]:
+            copy.start()
+
     copies[0].wait()
     copies[1].wait()
     normed = normed_of(tokens_ref, gain_ref)
@@ -188,15 +195,18 @@
         some = projected_of(normed[begin : begin + 2 * edge], w_ref[:, query_cols])
         ends.append(short_mix(some, short_ref[:, query_cols])[place : place + edge])
     put_rim(packed_ref, rim_ref, [*rims, ends])
-    for copy in copies[4:]:
-        copy.wait()
-    med_len = medium_ref.shape[0]
-    is_first = jnp.where(lax.axis_index(seq) == 0, 1.0, 0.0)
-    head = long_ref[0:med_len, :] + is_first * medium_ref[...]
-    head_row = lax.broadcasted_iota(jnp.int32, head.shape, 0)
-    head = head + jnp.where(head_row == 0, is_first * skip_ref[...], 0.0)
-    taps = jnp.concatenate([head, long_ref[med_len:, :]]).astype(jnp.bfloat16)
-    put_columns(packed_ref, rows, taps.T)
+    copies[4].wait()
+
+    @pl.when(is_first)
+    def _():
+        for copy in copies[5:]:
+            copy.wait()
+        med_len = medium_ref.shape[0]
+        head_row = lax.broadcasted_iota(jnp.int32, medium_ref.shape, 0)
+        direct = jnp.where(head_row == 0, skip_ref[...], 0.0)
+        long_ref[0:med_len, :] = long_ref[0:med_len, :] + medium_ref[...] + direct
+
+    put_columns(packed_ref, rows, long_ref[...].astype(jnp.bfloat16).T)
     if staged:
         put_routes(packed_ref, rim_ref, *outs)
 
@@ -331,16 +341,23 @@
 
 
 def output_body(query_ref, w_ref, *refs):
-    if len(refs) > 2:
-        keep_ref, got_ref, out_ref, conv_ref = refs
+    if len(refs) > 5:
+        keep_ref, got_ref, out_ref, conv_ref, result_ref, sems = refs
         take_routes(keep_ref, got_ref, conv_ref)
     else:
-        conv_ref, out_ref = refs
-    conv = conv_ref[...].T.astype(jnp.float32)
-    mixed_out = (query_ref[...] * conv).astype(jnp.bfloat16)
-    out_ref[...] = jnp.dot(mixed_out, w_ref[...], preferred_element_type=jnp.float32).astype(
-        jnp.bfloat16
-    )
+        conv_ref, out_ref, result_ref, sems = refs
+    rows = query_ref.shape[0]
+    copies = []
+    for part in range(2):
+        place = slice(part * rows // 2, (part + 1) * rows // 2)
+        conv = conv_ref[:, place].T.astype(jnp.float32)
+        mixed_out = (query_ref[place, :] * conv).astype(jnp.bfloat16)
+        result = jnp.dot(mixed_out, w_ref[...], preferred_element_type=jnp.float32)
+        result_ref[place, :] = result.astype(jnp.bfloat16)
+        copies.append(pltpu.make_async_copy(result_ref.at[place], out_ref.at[place], sems.at[part]))
+        copies[-1].start()
+    for copy in copies:
+        copy.wait()
 
 
 def permute(array, partner):
@@ -392,7 +409,7 @@
         if not staged:
             return (bf16(*shape),)
         size, turns = 2 * shape[0] // devices + extra, len(routes_of(chips))
-        near = size + near_pads * (size - extra)
+        near = size + size - extra + chan_tile
         return (bf16(turns, size, shape[1]),) * 2 + (bf16(near, shape[1]), bf16(size, shape[1]))
 
     def scratch(*shapes):
@@ -444,9 +461,10 @@
         bf16(rows, width),
         (query, w_out, *parts),
         [pltpu.VMEM] * (2 + len(parts)),
-        scratch(conv),
+        scratch(conv) + [pltpu.VMEM((rows, width), jnp.bfloat16), pltpu.SemaphoreType.DMA((2,))],
         flops=2 * rows * width * width,
         moved=600_000,
+        out_space=pltpu.HBM,
     )
 
 

time: 30.3 us -> 30.3 us (level)
  no operation moved by 1% of the time
where the time goes in v14:
time: 30.3 us; the launch traced here: 30.1 us
  starting transfers between devices  13.4 us (44%)
  waiting for transfers between devices  11.9 us (39%)
  Pallas kernels  4.47 us (15%)
    ppermute x12, starting transfers between devices, permute(): lax.ppermute(array, seq, [(i, partner(i)) for i in range(lax.axis_size(se...  13.4 us
    ppermute x12, waiting for transfers between devices, permute(): lax.ppermute(array, seq, [(i, partner(i)) for i in range(lax.axis_size(se...  11.9 us
    pallas_call x8, Pallas kernels, call(): pl.pallas_call(body, out_shape=outs, in_specs=[whole(space) for space in...  4.47 us
  transfers between devices with their start and end apart: 12, of which 7 were waited for; matrix products, arithmetic and copies ran while one was open for 0% of the time, Pallas kernels for 1%

profile of v14, /device:TPU:0, one launch (start us, length us, event | category | flops | bytes accessed | tf_op | source)
XLA Modules:
  0.0 30.1 jit_solution(16253529807107624628)
XLA Ops:
  0.0 0.0 copy-start.7
  0.0 1.8 %shard_map.110 = (bf16[3,136,128]{2,1,0:T(8,128)(2,1)S(1)}, bf16[3,136,128]{2,1,0:T(8,128)(2,1)S(1)}, bf16[280,128]{1,0:T(8,128)(2,1)S(1)}, bf16[136,128]{1,0:T(8,128)(2,1)S(1)}) custom-call(bf16[256,256]{1,0:T(8,128)(2,1)} %refs_0_.1, f32[1,256]{1,0:T(1,128)} %bitcast.2, bf16[256,768]{1,0:T(8,128)(2,1)} %refs_2_.1, f32[3,768]{1,0:T(4,128)} %refs_3_.1, ...), custom_call_target="tpu_custom_call" | custom-call | flops 100663296 | bytes 1500000 | tf_op jit(solution)/shard_map/pallas_call | solution.py:26
  1.8 0.5 %collective-permute-start = (bf16[3,136,128]{2,1,0:T(8,128)(2,1)S(1)}, bf16[3,136,128]{2,1,0:T(8,128)(2,1)S(1)}, u32[]{:S(2)}, u32[]{:S(2)}) collective-permute-start(bf16[3,136,128]{2,1,0:T(8,128)(2,1)S(1)} %get-tuple-element.24), channel_id=1, source_target_pairs={{0,1},{1,0},{2,3},{3,2},{4,5},{5,4},{6,7},{7,6},{8,9},{9,8},{10,11... | collective-permute-start | bytes 313352 | tf_op jit(solution)/shard_map/ppermute | solution.py:364
  2.3 2.6 %collective-permute-start.4 = (bf16[280,128]{1,0:T(8,128)(2,1)S(1)}, bf16[280,128]{1,0:T(8,128)(2,1)S(1)}, u32[]{:S(2)}, u32[]{:S(2)}) collective-permute-start(bf16[280,128]{1,0:T(8,128)(2,1)S(1)} %get-tuple-element.28), channel_id=1, source_target_pairs={{0,2},{1,3},{2,0},{3,1},{4,6},{5,7},{6,4},{7,5},{8,10},{9,11},{10,... | collective-permute-start | bytes 215048 | tf_op jit(solution)/shard_map/ppermute | solution.py:364
  4.9 0.0 collective-permute-done.got_ref
  4.9 0.0 copy-start.5
  4.9 0.0 copy-start.6
  4.9 2.7 %collective-permute-start.1 = (bf16[264,128]{1,0:T(8,128)(2,1)S(1)}, bf16[264,128]{1,0:T(8,128)(2,1)S(1)}, u32[]{:S(2)}, u32[]{:S(2)}) collective-permute-start(bf16[264,128]{1,0:T(8,128)(2,1)S(1)} %get-tuple-element.25), channel_id=1, source_target_pairs={{0,8},{1,11},{2,10},{3,9},{4,12},{5,15},{6,14},{7,13},{8,0},{9,3},... | collective-permute-start | bytes 202760 | tf_op jit(solution)/shard_map/ppermute | solution.py:364
  7.6 1.4 %collective-permute-start.2 = (bf16[264,128]{1,0:T(8,128)(2,1)S(1)}, bf16[264,128]{1,0:T(8,128)(2,1)S(1)}, u32[]{:S(2)}, u32[]{:S(2)}) collective-permute-start(bf16[264,128]{1,0:T(8,128)(2,1)S(1)} %get-tuple-element.26), channel_id=1, source_target_pairs={{0,12},{1,15},{2,14},{3,13},{4,8},{5,11},{6,10},{7,9},{8,4},{9,7},... | collective-permute-start | bytes 202760 | tf_op jit(solution)/shard_map/ppermute | solution.py:364
  8.9 0.2 collective-permute-start.3
  9.2 0.0 collective-permute-done.4.refs_3_
  9.2 3.2 %collective-permute-done.1.refs_0_ = bf16[264,128]{1,0:T(8,128)(2,1)S(1)} collective-permute-done((bf16[264,128]{1,0:T(8,128)(2,1)S(1)}, bf16[264,128]{1,0:T(8,128)(2,1)S(1)}, u32[]{:S(2)}, u32[]{:S(2)}) %collective-permute-start.1) | collective-permute-done | bytes 67616 | tf_op jit(solution)/shard_map/ppermute | solution.py:364
  12.3 2.1 %collective-permute-done.2.refs_1_ = bf16[264,128]{1,0:T(8,128)(2,1)S(1)} collective-permute-done((bf16[264,128]{1,0:T(8,128)(2,1)S(1)}, bf16[264,128]{1,0:T(8,128)(2,1)S(1)}, u32[]{:S(2)}, u32[]{:S(2)}) %collective-permute-start.2) | collective-permute-done | bytes 67616 | tf_op jit(solution)/shard_map/ppermute | solution.py:364
  14.4 0.8 %collective-permute-done.3.refs_2_ = bf16[264,128]{1,0:T(8,128)(2,1)S(1)} collective-permute-done((bf16[264,128]{1,0:T(8,128)(2,1)S(1)}, bf16[264,128]{1,0:T(8,128)(2,1)S(1)}, u32[]{:S(2)}, u32[]{:S(2)}) %collective-permute-start.3) | collective-permute-done | bytes 67616 | tf_op jit(solution)/shard_map/ppermute | solution.py:364
  15.2 0.3 collective-permute-start.5
  15.5 1.1 %collective-permute-done.5.refs_1_ = bf16[544,128]{1,0:T(8,128)(2,1)S(1)} collective-permute-done((bf16[544,128]{1,0:T(8,128)(2,1)S(1)}, bf16[544,128]{1,0:T(8,128)(2,1)S(1)}, u32[]{:S(2)}, u32[]{:S(2)}) %collective-permute-start.5) | collective-permute-done | bytes 139296 | tf_op jit(solution)/shard_map/ppermute | solution.py:364
  16.7 0.0 copy-done.7
  16.7 0.0 copy-done.5
  16.7 0.0 copy-done.6
  16.7 0.0 copy-start
  16.7 1.4 %shard_map.113 = (bf16[3,32,256]{2,1,0:T(8,128)(2,1)S(1)}, bf16[3,32,256]{2,1,0:T(8,128)(2,1)S(1)}, bf16[80,256]{1,0:T(8,128)(2,1)S(1)}, bf16[32,256]{1,0:T(8,128)(2,1)S(1)}) custom-call(bf16[512,256]{1,0:T(8,128)(2,1)S(1)} %copy-done.5, f32[32,256]{1,0:T(8,128)S(1)} %copy-done.7, bf16[256,512]{1,0:T(8,128)(2,1)S(1)} %copy-done.6, ...), custom_call_target="tpu_custom_call" | custom-call | flops 603979776 | bytes 2000000 | tf_op jit(solution)/shard_map/pallas_call | solution.py:26
  18.1 0.3 collective-permute-start.6
  18.4 1.3 %collective-permute-start.10 = (bf16[80,256]{1,0:T(8,128)(2,1)S(1)}, bf16[80,256]{1,0:T(8,128)(2,1)S(1)}, u32[]{:S(2)}, u32[]{:S(2)}) collective-permute-start(bf16[80,256]{1,0:T(8,128)(2,1)S(1)} %get-tuple-element.37), channel_id=1, source_target_pairs={{0,2},{1,3},{2,0},{3,1},{4,6},{5,7},{6,4},{7,5},{8,10},{9,11},{10,... | collective-permute-start | bytes 122888 | tf_op jit(solution)/shard_map/ppermute | solution.py:364
  19.6 0.0 collective-permute-done.6.got_ref
  19.6 0.0 copy-start.1
  19.6 2.4 %collective-permute-start.7 = (bf16[64,256]{1,0:T(8,128)(2,1)S(1)}, bf16[64,256]{1,0:T(8,128)(2,1)S(1)}, u32[]{:S(2)}, u32[]{:S(2)}) collective-permute-start(bf16[64,256]{1,0:T(8,128)(2,1)S(1)} %get-tuple-element.34), channel_id=1, source_target_pairs={{0,8},{1,11},{2,10},{3,9},{4,12},{5,15},{6,14},{7,13},{8,0},{9,3},... | collective-permute-start | bytes 98312 | tf_op jit(solution)/shard_map/ppermute | solution.py:364
  22.0 0.9 %collective-permute-start.8 = (bf16[64,256]{1,0:T(8,128)(2,1)S(1)}, bf16[64,256]{1,0:T(8,128)(2,1)S(1)}, u32[]{:S(2)}, u32[]{:S(2)}) collective-permute-start(bf16[64,256]{1,0:T(8,128)(2,1)S(1)} %get-tuple-element.35), channel_id=1, source_target_pairs={{0,12},{1,15},{2,14},{3,13},{4,8},{5,11},{6,10},{7,9},{8,4},{9,7},... | collective-permute-start | bytes 98312 | tf_op jit(solution)/shard_map/ppermute | solution.py:364
  23.0 0.5 %collective-permute-start.9 = (bf16[64,256]{1,0:T(8,128)(2,1)S(1)}, bf16[64,256]{1,0:T(8,128)(2,1)S(1)}, u32[]{:S(2)}, u32[]{:S(2)}) collective-permute-start(bf16[64,256]{1,0:T(8,128)(2,1)S(1)} %get-tuple-element.36), channel_id=1, source_target_pairs={{0,4},{1,7},{2,6},{3,5},{4,0},{5,3},{6,2},{7,1},{8,12},{9,15},{10,... | collective-permute-start | bytes 98312 | tf_op jit(solution)/shard_map/ppermute | solution.py:364
  23.5 0.0 collective-permute-done.10.refs_3_
  23.5 1.8 %collective-permute-done.7.refs_0_ = bf16[64,256]{1,0:T(8,128)(2,1)S(1)} collective-permute-done((bf16[64,256]{1,0:T(8,128)(2,1)S(1)}, bf16[64,256]{1,0:T(8,128)(2,1)S(1)}, u32[]{:S(2)}, u32[]{:S(2)}) %collective-permute-start.7) | collective-permute-done | bytes 32800 | tf_op jit(solution)/shard_map/ppermute | solution.py:364
  25.2 2.6 %collective-permute-done.8.refs_1_ = bf16[64,256]{1,0:T(8,128)(2,1)S(1)} collective-permute-done((bf16[64,256]{1,0:T(8,128)(2,1)S(1)}, bf16[64,256]{1,0:T(8,128)(2,1)S(1)}, u32[]{:S(2)}, u32[]{:S(2)}) %collective-permute-start.8) | collective-permute-done | bytes 32800 | tf_op jit(solution)/shard_map/ppermute | solution.py:364
  27.9 0.0 collective-permute-done.9.refs_2_
  27.9 0.0 copy-start.3
  27.9 0.0 copy-start.4
  27.9 0.0 copy-start.2
  27.9 0.4 %collective-permute-start.11 = (bf16[128,256]{1,0:T(8,128)(2,1)S(1)}, bf16[128,256]{1,0:T(8,128)(2,1)S(1)}, u32[]{:S(2)}, u32[]{:S(2)}) collective-permute-start(bf16[128,256]{1,0:T(8,128)(2,1)S(1)} %get-tuple-element.40), channel_id=1, source_target_pairs={{0,1},{1,0},{2,3},{3,2},{4,5},{5,4},{6,7},{7,6},{8,9},{9,8},{10,11... | collective-permute-start | bytes 196616 | tf_op jit(solution)/shard_map/ppermute | solution.py:364
  28.3 0.0 copy-done
  28.3 0.0 copy-done.1
  28.3 0.3 copy-done.3
  28.6 0.0 copy-done.4
  28.6 0.3 %shard_map.109.query_ref = f32[256,256]{1,0:T(8,128)S(1)} custom-call(bf16[256,256]{1,0:T(8,128)(2,1)S(1)} %copy-done.1, f32[1,256]{1,0:T(1,128)S(1)} %bitcast.3, bf16[256,768]{1,0:T(8,128)(2,1)S(1)} %copy-done, f32[3,768]{1,0:T(4,128)S(1)} %copy-done.3), custom_call_target="tpu_custom_call" | custom-call | flops 33554432 | bytes 800000 | tf_op jit(solution)/shard_map/pallas_call | solution.py:26
  28.9 0.3 %collective-permute-done.11.refs_1_ = bf16[128,256]{1,0:T(8,128)(2,1)S(1)} collective-permute-done((bf16[128,256]{1,0:T(8,128)(2,1)S(1)}, bf16[128,256]{1,0:T(8,128)(2,1)S(1)}, u32[]{:S(2)}, u32[]{:S(2)}) %collective-permute-start.11) | collective-permute-done | bytes 65568 | tf_op jit(solution)/shard_map/ppermute | solution.py:364
  29.2 0.0 copy-done.2
  29.2 0.9 %shard_map.116 = bf16[256,256]{1,0:T(8,128)(2,1)} custom-call(f32[256,256]{1,0:T(8,128)S(1)} %shard_map.109.query_ref, bf16[256,256]{1,0:T(8,128)(2,1)S(1)} %copy-done.2, bf16[128,256]{1,0:T(8,128)(2,1)S(1)} %get-tuple-element.39.refs_0_, bf16[128,256]{1,0:T(8,128)(2,1)S(1)} %collective-permute-done.11.refs_1_), custom_call_target="tpu_custom_call" | custom-call | flops 33554432 | bytes 600000 | tf_op jit(solution)/shard_map/pallas_call | solution.py:26
  (4 shorter events, 0.1 us)
Async XLA Ops:
  0.0 16.7 %copy-start.7 = (f32[32,256]{1,0:T(8,128)S(1)}, f32[32,256]{1,0:T(8,128)}, u32[]{:S(2)}) copy-start(f32[32,256]{1,0:T(8,128)} %constant.7.clone.twist_ref) | copy-start | bytes 98308
  1.8 3.1 %collective-permute-start = (bf16[3,136,128]{2,1,0:T(8,128)(2,1)S(1)}, bf16[3,136,128]{2,1,0:T(8,128)(2,1)S(1)}, u32[]{:S(2)}, u32[]{:S(2)}) collective-permute-start(bf16[3,136,128]{2,1,0:T(8,128)(2,1)S(1)} %get-tuple-element.24), channel_id=1, source_target_pairs={{0,1},{1,0},{2,3},{3,2},{4,5},{5,4},{6,7},{7,6},{8,9},{9,8},{10,11... | collective-permute-start | bytes 313352 | tf_op jit(solution)/shard_map/ppermute | solution.py:364
  2.3 6.9 %collective-permute-start.4 = (bf16[280,128]{1,0:T(8,128)(2,1)S(1)}, bf16[280,128]{1,0:T(8,128)(2,1)S(1)}, u32[]{:S(2)}, u32[]{:S(2)}) collective-permute-start(bf16[280,128]{1,0:T(8,128)(2,1)S(1)} %get-tuple-element.28), channel_id=1, source_target_pairs={{0,2},{1,3},{2,0},{3,1},{4,6},{5,7},{6,4},{7,5},{8,10},{9,11},{10,... | collective-permute-start | bytes 215048 | tf_op jit(solution)/shard_map/ppermute | solution.py:364
  4.9 11.8 %copy-start.5 = (bf16[512,256]{1,0:T(8,128)(2,1)S(1)}, bf16[512,256]{1,0:T(8,128)(2,1)}, u32[]{:S(2)}) copy-start(bf16[512,256]{1,0:T(8,128)(2,1)} %constant.6.clone.first_ref) | copy-start | bytes 786436
  4.9 11.8 %copy-start.6 = (bf16[256,512]{1,0:T(8,128)(2,1)S(1)}, bf16[256,512]{1,0:T(8,128)(2,1)}, u32[]{:S(2)}) copy-start(bf16[256,512]{1,0:T(8,128)(2,1)} %constant.8.clone.inner_ref) | copy-start | bytes 786436
  4.9 7.4 %collective-permute-start.1 = (bf16[264,128]{1,0:T(8,128)(2,1)S(1)}, bf16[264,128]{1,0:T(8,128)(2,1)S(1)}, u32[]{:S(2)}, u32[]{:S(2)}) collective-permute-start(bf16[264,128]{1,0:T(8,128)(2,1)S(1)} %get-tuple-element.25), channel_id=1, source_target_pairs={{0,8},{1,11},{2,10},{3,9},{4,12},{5,15},{6,14},{7,13},{8,0},{9,3},... | collective-permute-start | bytes 202760 | tf_op jit(solution)/shard_map/ppermute | solution.py:364
  7.6 6.9 %collective-permute-start.2 = (bf16[264,128]{1,0:T(8,128)(2,1)S(1)}, bf16[264,128]{1,0:T(8,128)(2,1)S(1)}, u32[]{:S(2)}, u32[]{:S(2)}) collective-permute-start(bf16[264,128]{1,0:T(8,128)(2,1)S(1)} %get-tuple-element.26), channel_id=1, source_target_pairs={{0,12},{1,15},{2,14},{3,13},{4,8},{5,11},{6,10},{7,9},{8,4},{9,7},... | collective-permute-start | bytes 202760 | tf_op jit(solution)/shard_map/ppermute | solution.py:364
  8.9 6.3 %collective-permute-start.3 = (bf16[264,128]{1,0:T(8,128)(2,1)S(1)}, bf16[264,128]{1,0:T(8,128)(2,1)S(1)}, u32[]{:S(2)}, u32[]{:S(2)}) collective-permute-start(bf16[264,128]{1,0:T(8,128)(2,1)S(1)} %get-tuple-element.27), channel_id=1, source_target_pairs={{0,4},{1,7},{2,6},{3,5},{4,0},{5,3},{6,2},{7,1},{8,12},{9,15},{10,... | collective-permute-start | bytes 202760 | tf_op jit(solution)/shard_map/ppermute | solution.py:364
  15.2 1.4 %collective-permute-start.5 = (bf16[544,128]{1,0:T(8,128)(2,1)S(1)}, bf16[544,128]{1,0:T(8,128)(2,1)S(1)}, u32[]{:S(2)}, u32[]{:S(2)}) collective-permute-start(bf16[544,128]{1,0:T(8,128)(2,1)S(1)} %get-tuple-element.31), channel_id=1, source_target_pairs={{0,1},{1,0},{2,3},{3,2},{4,5},{5,4},{6,7},{7,6},{8,9},{9,8},{10,11... | collective-permute-start | bytes 417800 | tf_op jit(solution)/shard_map/ppermute | solution.py:364
  16.7 11.6 %copy-start = (bf16[256,768]{1,0:T(8,128)(2,1)S(1)}, bf16[256,768]{1,0:T(8,128)(2,1)}, u32[]{:S(2)}) copy-start(bf16[256,768]{1,0:T(8,128)(2,1)} %refs_2_.1) | copy-start | bytes 1179652
  18.1 1.5 %collective-permute-start.6 = (bf16[3,32,256]{2,1,0:T(8,128)(2,1)S(1)}, bf16[3,32,256]{2,1,0:T(8,128)(2,1)S(1)}, u32[]{:S(2)}, u32[]{:S(2)}) collective-permute-start(bf16[3,32,256]{2,1,0:T(8,128)(2,1)S(1)} %get-tuple-element.33), channel_id=1, source_target_pairs={{0,1},{1,0},{2,3},{3,2},{4,5},{5,4},{6,7},{7,6},{8,9},{9,8},{10,11... | collective-permute-start | bytes 147464 | tf_op jit(solution)/shard_map/ppermute | solution.py:364
  18.4 5.1 %collective-permute-start.10 = (bf16[80,256]{1,0:T(8,128)(2,1)S(1)}, bf16[80,256]{1,0:T(8,128)(2,1)S(1)}, u32[]{:S(2)}, u32[]{:S(2)}) collective-permute-start(bf16[80,256]{1,0:T(8,128)(2,1)S(1)} %get-tuple-element.37), channel_id=1, source_target_pairs={{0,2},{1,3},{2,0},{3,1},{4,6},{5,7},{6,4},{7,5},{8,10},{9,11},{10,... | collective-permute-start | bytes 122888 | tf_op jit(solution)/shard_map/ppermute | solution.py:364
  19.6 8.7 %copy-start.1 = (bf16[256,256]{1,0:T(8,128)(2,1)S(1)}, bf16[256,256]{1,0:T(8,128)(2,1)}, u32[]{:S(2)}) copy-start(bf16[256,256]{1,0:T(8,128)(2,1)} %refs_0_.1) | copy-start | bytes 393220
  19.6 5.6 %collective-permute-start.7 = (bf16[64,256]{1,0:T(8,128)(2,1)S(1)}, bf16[64,256]{1,0:T(8,128)(2,1)S(1)}, u32[]{:S(2)}, u32[]{:S(2)}) collective-permute-start(bf16[64,256]{1,0:T(8,128)(2,1)S(1)} %get-tuple-element.34), channel_id=1, source_target_pairs={{0,8},{1,11},{2,10},{3,9},{4,12},{5,15},{6,14},{7,13},{8,0},{9,3},... | collective-permute-start | bytes 98312 | tf_op jit(solution)/shard_map/ppermute | solution.py:364
  22.0 5.8 %collective-permute-start.8 = (bf16[64,256]{1,0:T(8,128)(2,1)S(1)}, bf16[64,256]{1,0:T(8,128)(2,1)S(1)}, u32[]{:S(2)}, u32[]{:S(2)}) collective-permute-start(bf16[64,256]{1,0:T(8,128)(2,1)S(1)} %get-tuple-element.35), channel_id=1, source_target_pairs={{0,12},{1,15},{2,14},{3,13},{4,8},{5,11},{6,10},{7,9},{8,4},{9,7},... | collective-permute-start | bytes 98312 | tf_op jit(solution)/shard_map/ppermute | solution.py:364
  23.0 4.9 %collective-permute-start.9 = (bf16[64,256]{1,0:T(8,128)(2,1)S(1)}, bf16[64,256]{1,0:T(8,128)(2,1)S(1)}, u32[]{:S(2)}, u32[]{:S(2)}) collective-permute-start(bf16[64,256]{1,0:T(8,128)(2,1)S(1)} %get-tuple-element.36), channel_id=1, source_target_pairs={{0,4},{1,7},{2,6},{3,5},{4,0},{5,3},{6,2},{7,1},{8,12},{9,15},{10,... | collective-permute-start | bytes 98312 | tf_op jit(solution)/shard_map/ppermute | solution.py:364
  27.9 0.7 %copy-start.3 = (f32[3,768]{1,0:T(4,128)S(1)}, f32[3,768]{1,0:T(4,128)}, u32[]{:S(2)}) copy-start(f32[3,768]{1,0:T(4,128)} %refs_3_.1) | copy-start | bytes 27652
  27.9 0.7 %copy-start.4 = (f32[256]{0:T(256)S(1)}, f32[256]{0:T(256)}, u32[]{:S(2)}) copy-start(f32[256]{0:T(256)} %param.12) | copy-start | bytes 3076
  27.9 1.3 %copy-start.2 = (bf16[256,256]{1,0:T(8,128)(2,1)S(1)}, bf16[256,256]{1,0:T(8,128)(2,1)}, u32[]{:S(2)}) copy-start(bf16[256,256]{1,0:T(8,128)(2,1)} %w_ref.3) | copy-start | bytes 393220
  27.9 1.3 %collective-permute-start.11 = (bf16[128,256]{1,0:T(8,128)(2,1)S(1)}, bf16[128,256]{1,0:T(8,128)(2,1)S(1)}, u32[]{:S(2)}, u32[]{:S(2)}) collective-permute-start(bf16[128,256]{1,0:T(8,128)(2,1)S(1)} %get-tuple-element.40), channel_id=1, source_target_pairs={{0,1},{1,0},{2,3},{3,2},{4,5},{5,4},{6,7},{7,6},{8,9},{9,8},{10,11... | collective-permute-start | bytes 196616 | tf_op jit(solution)/shard_map/ppermute | solution.py:364

commit v15 on v13

--- a/solution.py
+++ b/solution.py
@@ -15,7 +15,6 @@
 seq = ("chip", "core")
 rim_step = 2 * edge
 chan_tile = 16
-near_pads = 2
 vmem_bytes = 32 * 2**20
 
 
@@ -56,8 +55,10 @@
     )
 
 
-def routes_of(chips):
+def routes_of(chips, forward):
     far = sorted(range(2, chips, 2), key=lambda d: (-d.bit_length(), d))
+    if forward:
+        far = far[:1] + far[:0:-1]
     return [(d, d + 1) for d in far]
 
 
@@ -77,14 +78,15 @@
         if extra:
             out_ref[2 * size : 2 * size + extra, :] = rim_ref[chip ^ distance]
 
-    for turn, route in enumerate(routes_of(lax.axis_size("chip"))):
+    for turn, route in enumerate(routes_of(lax.axis_size("chip"), extra > 0)):
         own, other = carried(route, core)
         put(keep_ref.at[turn], own)
         put(give_ref.at[turn], other)
     put(home_ref, 0)
     put(near_ref, 1)
-    for begin in range(2 * size + extra, near_ref.shape[0], 2 * size):
-        near_ref[begin : begin + 2 * size, :] = home_ref[0 : 2 * size, :]
+    begin = 2 * size + extra
+    near_ref[begin : begin + 2 * size, :] = home_ref[0 : 2 * size, :]
+    near_ref[begin + 2 * size :, :] = home_ref[0:chan_tile, :]
 
 
 def half_rims(first_ref, second_ref, begin):
@@ -120,7 +122,7 @@
 
 def take_routes(keep_ref, got_ref, target_ref, rim_ref=None):
     chip, core = lax.axis_index("chip"), lax.axis_index("core")
-    routes = routes_of(lax.axis_size("chip"))
+    routes = routes_of(lax.axis_size("chip"), rim_ref is not None)
     count = 2 * len(routes) + 2
     size = target_ref.shape[0] // (2 * lax.axis_size("chip"))
     places = [(*carried(route, core), sender) for route in routes for sender in range(2)]
@@ -183,11 +185,9 @@
     key, value = mixed[:, 0:width], mixed[:, width:]
     put_columns(packed_ref, 0, (key[0:rows] * value[0:rows]).astype(jnp.bfloat16).T)
     rims = [(key[0:edge], key[rows:]), (value[0:edge], value[rows:])]
-    ends = []
-    for begin, place in ((0, 0), (rows - 2 * edge, 2 * edge)):
-        some = projected_of(normed[begin : begin + 2 * edge], w_ref[:, query_cols])
-        ends.append(short_mix(some, short_ref[:, query_cols])[place : place + edge])
-    put_rim(packed_ref, rim_ref, [*rims, ends])
+    some = jnp.concatenate([normed[0 : 2 * edge], normed[rows - 2 * edge :]])
+    some = short_mix(projected_of(some, w_ref[:, query_cols]), short_ref[:, query_cols])
+    put_rim(packed_ref, rim_ref, [*rims, (some[0:edge], some[4 * edge :])])
     for copy in copies[4:]:
         copy.wait()
     med_len = medium_ref.shape[0]
@@ -363,7 +363,7 @@
         [pltpu.VMEM] * 2,
         moved=4 * keep.size,
     )
-    routes = routes_of(lax.axis_size("chip"))
+    routes = routes_of(lax.axis_size("chip"), extra > 0)
     far = [permute(part, lambda i: i ^ 2 * route[i % 2]) for part, route in zip(far, routes)]
     count = 2 * turns + 2
     half = bf16(count * size + count // 2 * extra, lanes)
@@ -391,8 +391,8 @@
     def pieces(shape, extra):
         if not staged:
             return (bf16(*shape),)
-        size, turns = 2 * shape[0] // devices + extra, len(routes_of(chips))
-        near = size + near_pads * (size - extra)
+        size, turns = 2 * shape[0] // devices + extra, chips // 2 - 1
+        near = size + size - extra + chan_tile
         return (bf16(turns, size, shape[1]),) * 2 + (bf16(near, shape[1]), bf16(size, shape[1]))
 
     def scratch(*shapes):

time: 30.3 us -> 30.5 us (level)
  no operation moved by 1% of the time
where the time goes in v15:
time: 30.5 us; the launch traced here: 30.3 us
  starting transfers between devices  13.1 us (43%)
  waiting for transfers between devices  12.2 us (40%)
  Pallas kernels  4.46 us (15%)
  local copies, waits for them, and re-layouts  0.53 us (2%)
    ppermute x12, starting transfers between devices, permute(): lax.ppermute(array, seq, [(i, partner(i)) for i in range(lax.axis_size(se...  13.1 us
    ppermute x12, waiting for transfers between devices, permute(): lax.ppermute(array, seq, [(i, partner(i)) for i in range(lax.axis_size(se...  12.2 us
    pallas_call x8, Pallas kernels, call(): pl.pallas_call(body, out_shape=outs, in_specs=[whole(space) for space in...  4.46 us
  transfers between devices with their start and end apart: 12, of which 7 were waited for; matrix products, arithmetic and copies ran while one was open for 0% of the time, Pallas kernels for 1%

profile of v15, /device:TPU:0, one launch (start us, length us, event | category | flops | bytes accessed | tf_op | source)
XLA Modules:
  0.0 30.3 jit_solution(11897802868889065366)
XLA Ops:
  0.0 0.0 copy-start.7
  0.0 1.8 %shard_map.110 = (bf16[3,136,128]{2,1,0:T(8,128)(2,1)S(1)}, bf16[3,136,128]{2,1,0:T(8,128)(2,1)S(1)}, bf16[280,128]{1,0:T(8,128)(2,1)S(1)}, bf16[136,128]{1,0:T(8,128)(2,1)S(1)}) custom-call(bf16[256,256]{1,0:T(8,128)(2,1)} %refs_0_.1, f32[1,256]{1,0:T(1,128)} %bitcast.2, bf16[256,768]{1,0:T(8,128)(2,1)} %refs_2_.1, f32[3,768]{1,0:T(4,128)} %refs_3_.1, ...), custom_call_target="tpu_custom_call" | custom-call | flops 100663296 | bytes 1500000 | tf_op jit(solution)/shard_map/pallas_call | solution.py:26
  1.8 0.5 %collective-permute-start = (bf16[3,136,128]{2,1,0:T(8,128)(2,1)S(1)}, bf16[3,136,128]{2,1,0:T(8,128)(2,1)S(1)}, u32[]{:S(2)}, u32[]{:S(2)}) collective-permute-start(bf16[3,136,128]{2,1,0:T(8,128)(2,1)S(1)} %get-tuple-element.24), channel_id=1, source_target_pairs={{0,1},{1,0},{2,3},{3,2},{4,5},{5,4},{6,7},{7,6},{8,9},{9,8},{10,11... | collective-permute-start | bytes 313352 | tf_op jit(solution)/shard_map/ppermute | solution.py:347
  2.3 2.6 %collective-permute-start.4 = (bf16[280,128]{1,0:T(8,128)(2,1)S(1)}, bf16[280,128]{1,0:T(8,128)(2,1)S(1)}, u32[]{:S(2)}, u32[]{:S(2)}) collective-permute-start(bf16[280,128]{1,0:T(8,128)(2,1)S(1)} %get-tuple-element.28), channel_id=1, source_target_pairs={{0,2},{1,3},{2,0},{3,1},{4,6},{5,7},{6,4},{7,5},{8,10},{9,11},{10,... | collective-permute-start | bytes 215048 | tf_op jit(solution)/shard_map/ppermute | solution.py:347
  4.9 0.0 collective-permute-done.got_ref
  4.9 0.0 copy-start.5
  4.9 0.0 copy-start.6
  4.9 2.7 %collective-permute-start.1 = (bf16[264,128]{1,0:T(8,128)(2,1)S(1)}, bf16[264,128]{1,0:T(8,128)(2,1)S(1)}, u32[]{:S(2)}, u32[]{:S(2)}) collective-permute-start(bf16[264,128]{1,0:T(8,128)(2,1)S(1)} %get-tuple-element.25), channel_id=1, source_target_pairs={{0,8},{1,11},{2,10},{3,9},{4,12},{5,15},{6,14},{7,13},{8,0},{9,3},... | collective-permute-start | bytes 202760 | tf_op jit(solution)/shard_map/ppermute | solution.py:347
  7.6 1.6 %collective-permute-start.2 = (bf16[264,128]{1,0:T(8,128)(2,1)S(1)}, bf16[264,128]{1,0:T(8,128)(2,1)S(1)}, u32[]{:S(2)}, u32[]{:S(2)}) collective-permute-start(bf16[264,128]{1,0:T(8,128)(2,1)S(1)} %get-tuple-element.26), channel_id=1, source_target_pairs={{0,4},{1,7},{2,6},{3,5},{4,0},{5,3},{6,2},{7,1},{8,12},{9,15},{10,... | collective-permute-start | bytes 202760 | tf_op jit(solution)/shard_map/ppermute | solution.py:347
  9.2 0.2 collective-permute-start.3
  9.4 0.0 collective-permute-done.4.refs_3_
  9.4 2.9 %collective-permute-done.1.refs_0_ = bf16[264,128]{1,0:T(8,128)(2,1)S(1)} collective-permute-done((bf16[264,128]{1,0:T(8,128)(2,1)S(1)}, bf16[264,128]{1,0:T(8,128)(2,1)S(1)}, u32[]{:S(2)}, u32[]{:S(2)}) %collective-permute-start.1) | collective-permute-done | bytes 67616 | tf_op jit(solution)/shard_map/ppermute | solution.py:347
  12.3 0.4 %collective-permute-done.2.refs_1_ = bf16[264,128]{1,0:T(8,128)(2,1)S(1)} collective-permute-done((bf16[264,128]{1,0:T(8,128)(2,1)S(1)}, bf16[264,128]{1,0:T(8,128)(2,1)S(1)}, u32[]{:S(2)}, u32[]{:S(2)}) %collective-permute-start.2) | collective-permute-done | bytes 67616 | tf_op jit(solution)/shard_map/ppermute | solution.py:347
  12.7 3.0 %collective-permute-done.3.refs_2_ = bf16[264,128]{1,0:T(8,128)(2,1)S(1)} collective-permute-done((bf16[264,128]{1,0:T(8,128)(2,1)S(1)}, bf16[264,128]{1,0:T(8,128)(2,1)S(1)}, u32[]{:S(2)}, u32[]{:S(2)}) %collective-permute-start.3) | collective-permute-done | bytes 67616 | tf_op jit(solution)/shard_map/ppermute | solution.py:347
  15.8 0.3 collective-permute-start.5
  16.1 1.1 %collective-permute-done.5.refs_1_ = bf16[544,128]{1,0:T(8,128)(2,1)S(1)} collective-permute-done((bf16[544,128]{1,0:T(8,128)(2,1)S(1)}, bf16[544,128]{1,0:T(8,128)(2,1)S(1)}, u32[]{:S(2)}, u32[]{:S(2)}) %collective-permute-start.5) | collective-permute-done | bytes 139296 | tf_op jit(solution)/shard_map/ppermute | solution.py:347
  17.2 0.0 copy-done.7
  17.2 0.0 copy-done.5
  17.2 0.0 copy-done.6
  17.3 0.0 copy-start
  17.3 1.4 %shard_map.113 = (bf16[3,32,256]{2,1,0:T(8,128)(2,1)S(1)}, bf16[3,32,256]{2,1,0:T(8,128)(2,1)S(1)}, bf16[80,256]{1,0:T(8,128)(2,1)S(1)}, bf16[32,256]{1,0:T(8,128)(2,1)S(1)}) custom-call(bf16[512,256]{1,0:T(8,128)(2,1)S(1)} %copy-done.5, f32[32,256]{1,0:T(8,128)S(1)} %copy-done.7, bf16[256,512]{1,0:T(8,128)(2,1)S(1)} %copy-done.6, ...), custom_call_target="tpu_custom_call" | custom-call | flops 603979776 | bytes 2000000 | tf_op jit(solution)/shard_map/pallas_call | solution.py:26
  18.7 0.3 collective-permute-start.6
  18.9 1.3 %collective-permute-start.10 = (bf16[80,256]{1,0:T(8,128)(2,1)S(1)}, bf16[80,256]{1,0:T(8,128)(2,1)S(1)}, u32[]{:S(2)}, u32[]{:S(2)}) collective-permute-start(bf16[80,256]{1,0:T(8,128)(2,1)S(1)} %get-tuple-element.37), channel_id=1, source_target_pairs={{0,2},{1,3},{2,0},{3,1},{4,6},{5,7},{6,4},{7,5},{8,10},{9,11},{10,... | collective-permute-start | bytes 122888 | tf_op jit(solution)/shard_map/ppermute | solution.py:347
  20.2 0.0 collective-permute-done.6.got_ref
  20.2 0.0 copy-start.1
  20.2 1.8 %collective-permute-start.7 = (bf16[64,256]{1,0:T(8,128)(2,1)S(1)}, bf16[64,256]{1,0:T(8,128)(2,1)S(1)}, u32[]{:S(2)}, u32[]{:S(2)}) collective-permute-start(bf16[64,256]{1,0:T(8,128)(2,1)S(1)} %get-tuple-element.34), channel_id=1, source_target_pairs={{0,8},{1,11},{2,10},{3,9},{4,12},{5,15},{6,14},{7,13},{8,0},{9,3},... | collective-permute-start | bytes 98312 | tf_op jit(solution)/shard_map/ppermute | solution.py:347
  22.0 0.4 %collective-permute-start.8 = (bf16[64,256]{1,0:T(8,128)(2,1)S(1)}, bf16[64,256]{1,0:T(8,128)(2,1)S(1)}, u32[]{:S(2)}, u32[]{:S(2)}) collective-permute-start(bf16[64,256]{1,0:T(8,128)(2,1)S(1)} %get-tuple-element.35), channel_id=1, source_target_pairs={{0,12},{1,15},{2,14},{3,13},{4,8},{5,11},{6,10},{7,9},{8,4},{9,7},... | collective-permute-start | bytes 98312 | tf_op jit(solution)/shard_map/ppermute | solution.py:347
  22.4 1.4 %collective-permute-start.9 = (bf16[64,256]{1,0:T(8,128)(2,1)S(1)}, bf16[64,256]{1,0:T(8,128)(2,1)S(1)}, u32[]{:S(2)}, u32[]{:S(2)}) collective-permute-start(bf16[64,256]{1,0:T(8,128)(2,1)S(1)} %get-tuple-element.36), channel_id=1, source_target_pairs={{0,4},{1,7},{2,6},{3,5},{4,0},{5,3},{6,2},{7,1},{8,12},{9,15},{10,... | collective-permute-start | bytes 98312 | tf_op jit(solution)/shard_map/ppermute | solution.py:347
  23.8 0.0 collective-permute-done.10.refs_3_
  23.8 1.4 %collective-permute-done.7.refs_0_ = bf16[64,256]{1,0:T(8,128)(2,1)S(1)} collective-permute-done((bf16[64,256]{1,0:T(8,128)(2,1)S(1)}, bf16[64,256]{1,0:T(8,128)(2,1)S(1)}, u32[]{:S(2)}, u32[]{:S(2)}) %collective-permute-start.7) | collective-permute-done | bytes 32800 | tf_op jit(solution)/shard_map/ppermute | solution.py:347
  25.2 2.8 %collective-permute-done.8.refs_1_ = bf16[64,256]{1,0:T(8,128)(2,1)S(1)} collective-permute-done((bf16[64,256]{1,0:T(8,128)(2,1)S(1)}, bf16[64,256]{1,0:T(8,128)(2,1)S(1)}, u32[]{:S(2)}, u32[]{:S(2)}) %collective-permute-start.8) | collective-permute-done | bytes 32800 | tf_op jit(solution)/shard_map/ppermute | solution.py:347
  28.0 0.0 collective-permute-done.9.refs_2_
  28.0 0.0 copy-start.3
  28.1 0.0 copy-start.4
  28.1 0.0 copy-start.2
  28.1 0.2 collective-permute-start.11
  28.3 0.0 copy-done
  28.3 0.0 copy-done.1
  28.3 0.5 %copy-done.3 = f32[3,768]{1,0:T(4,128)S(1)} copy-done((f32[3,768]{1,0:T(4,128)S(1)}, f32[3,768]{1,0:T(4,128)}, u32[]{:S(2)}) %copy-start.3) | copy-done | bytes 9240
  28.8 0.0 copy-done.4
  28.8 0.3 %shard_map.109.query_ref = f32[256,256]{1,0:T(8,128)S(1)} custom-call(bf16[256,256]{1,0:T(8,128)(2,1)S(1)} %copy-done.1, f32[1,256]{1,0:T(1,128)S(1)} %bitcast.3, bf16[256,768]{1,0:T(8,128)(2,1)S(1)} %copy-done, f32[3,768]{1,0:T(4,128)S(1)} %copy-done.3), custom_call_target="tpu_custom_call" | custom-call | flops 33554432 | bytes 800000 | tf_op jit(solution)/shard_map/pallas_call | solution.py:26
  29.1 0.3 %collective-permute-done.11.refs_1_ = bf16[128,256]{1,0:T(8,128)(2,1)S(1)} collective-permute-done((bf16[128,256]{1,0:T(8,128)(2,1)S(1)}, bf16[128,256]{1,0:T(8,128)(2,1)S(1)}, u32[]{:S(2)}, u32[]{:S(2)}) %collective-permute-start.11) | collective-permute-done | bytes 65568 | tf_op jit(solution)/shard_map/ppermute | solution.py:347
  29.4 0.0 copy-done.2
  29.4 0.9 %shard_map.116 = bf16[256,256]{1,0:T(8,128)(2,1)} custom-call(f32[256,256]{1,0:T(8,128)S(1)} %shard_map.109.query_ref, bf16[256,256]{1,0:T(8,128)(2,1)S(1)} %copy-done.2, bf16[128,256]{1,0:T(8,128)(2,1)S(1)} %get-tuple-element.39.refs_0_, bf16[128,256]{1,0:T(8,128)(2,1)S(1)} %collective-permute-done.11.refs_1_), custom_call_target="tpu_custom_call" | custom-call | flops 33554432 | bytes 600000 | tf_op jit(solution)/shard_map/pallas_call | solution.py:26
  (4 shorter events, 0.1 us)
Async XLA Ops:
  0.0 17.2 %copy-start.7 = (f32[32,256]{1,0:T(8,128)S(1)}, f32[32,256]{1,0:T(8,128)}, u32[]{:S(2)}) copy-start(f32[32,256]{1,0:T(8,128)} %constant.7.clone.twist_ref) | copy-start | bytes 98308
  1.8 3.1 %collective-permute-start = (bf16[3,136,128]{2,1,0:T(8,128)(2,1)S(1)}, bf16[3,136,128]{2,1,0:T(8,128)(2,1)S(1)}, u32[]{:S(2)}, u32[]{:S(2)}) collective-permute-start(bf16[3,136,128]{2,1,0:T(8,128)(2,1)S(1)} %get-tuple-element.24), channel_id=1, source_target_pairs={{0,1},{1,0},{2,3},{3,2},{4,5},{5,4},{6,7},{7,6},{8,9},{9,8},{10,11... | collective-permute-start | bytes 313352 | tf_op jit(solution)/shard_map/ppermute | solution.py:347
  2.3 7.1 %collective-permute-start.4 = (bf16[280,128]{1,0:T(8,128)(2,1)S(1)}, bf16[280,128]{1,0:T(8,128)(2,1)S(1)}, u32[]{:S(2)}, u32[]{:S(2)}) collective-permute-start(bf16[280,128]{1,0:T(8,128)(2,1)S(1)} %get-tuple-element.28), channel_id=1, source_target_pairs={{0,2},{1,3},{2,0},{3,1},{4,6},{5,7},{6,4},{7,5},{8,10},{9,11},{10,... | collective-permute-start | bytes 215048 | tf_op jit(solution)/shard_map/ppermute | solution.py:347
  4.9 12.3 %copy-start.5 = (bf16[512,256]{1,0:T(8,128)(2,1)S(1)}, bf16[512,256]{1,0:T(8,128)(2,1)}, u32[]{:S(2)}) copy-start(bf16[512,256]{1,0:T(8,128)(2,1)} %constant.6.clone.first_ref) | copy-start | bytes 786436
  4.9 12.3 %copy-start.6 = (bf16[256,512]{1,0:T(8,128)(2,1)S(1)}, bf16[256,512]{1,0:T(8,128)(2,1)}, u32[]{:S(2)}) copy-start(bf16[256,512]{1,0:T(8,128)(2,1)} %constant.8.clone.inner_ref) | copy-start | bytes 786436
  4.9 7.4 %collective-permute-start.1 = (bf16[264,128]{1,0:T(8,128)(2,1)S(1)}, bf16[264,128]{1,0:T(8,128)(2,1)S(1)}, u32[]{:S(2)}, u32[]{:S(2)}) collective-permute-start(bf16[264,128]{1,0:T(8,128)(2,1)S(1)} %get-tuple-element.25), channel_id=1, source_target_pairs={{0,8},{1,11},{2,10},{3,9},{4,12},{5,15},{6,14},{7,13},{8,0},{9,3},... | collective-permute-start | bytes 202760 | tf_op jit(solution)/shard_map/ppermute | solution.py:347
  7.6 5.2 %collective-permute-start.2 = (bf16[264,128]{1,0:T(8,128)(2,1)S(1)}, bf16[264,128]{1,0:T(8,128)(2,1)S(1)}, u32[]{:S(2)}, u32[]{:S(2)}) collective-permute-start(bf16[264,128]{1,0:T(8,128)(2,1)S(1)} %get-tuple-element.26), channel_id=1, source_target_pairs={{0,4},{1,7},{2,6},{3,5},{4,0},{5,3},{6,2},{7,1},{8,12},{9,15},{10,... | collective-permute-start | bytes 202760 | tf_op jit(solution)/shard_map/ppermute | solution.py:347
  9.2 6.6 %collective-permute-start.3 = (bf16[264,128]{1,0:T(8,128)(2,1)S(1)}, bf16[264,128]{1,0:T(8,128)(2,1)S(1)}, u32[]{:S(2)}, u32[]{:S(2)}) collective-permute-start(bf16[264,128]{1,0:T(8,128)(2,1)S(1)} %get-tuple-element.27), channel_id=1, source_target_pairs={{0,12},{1,15},{2,14},{3,13},{4,8},{5,11},{6,10},{7,9},{8,4},{9,7},... | collective-permute-start | bytes 202760 | tf_op jit(solution)/shard_map/ppermute | solution.py:347
  15.8 1.4 %collective-permute-start.5 = (bf16[544,128]{1,0:T(8,128)(2,1)S(1)}, bf16[544,128]{1,0:T(8,128)(2,1)S(1)}, u32[]{:S(2)}, u32[]{:S(2)}) collective-permute-start(bf16[544,128]{1,0:T(8,128)(2,1)S(1)} %get-tuple-element.31), channel_id=1, source_target_pairs={{0,1},{1,0},{2,3},{3,2},{4,5},{5,4},{6,7},{7,6},{8,9},{9,8},{10,11... | collective-permute-start | bytes 417800 | tf_op jit(solution)/shard_map/ppermute | solution.py:347
  17.3 11.0 %copy-start = (bf16[256,768]{1,0:T(8,128)(2,1)S(1)}, bf16[256,768]{1,0:T(8,128)(2,1)}, u32[]{:S(2)}) copy-start(bf16[256,768]{1,0:T(8,128)(2,1)} %refs_2_.1) | copy-start | bytes 1179652
  18.7 1.5 %collective-permute-start.6 = (bf16[3,32,256]{2,1,0:T(8,128)(2,1)S(1)}, bf16[3,32,256]{2,1,0:T(8,128)(2,1)S(1)}, u32[]{:S(2)}, u32[]{:S(2)}) collective-permute-start(bf16[3,32,256]{2,1,0:T(8,128)(2,1)S(1)} %get-tuple-element.33), channel_id=1, source_target_pairs={{0,1},{1,0},{2,3},{3,2},{4,5},{5,4},{6,7},{7,6},{8,9},{9,8},{10,11... | collective-permute-start | bytes 147464 | tf_op jit(solution)/shard_map/ppermute | solution.py:347
  18.9 4.8 %collective-permute-start.10 = (bf16[80,256]{1,0:T(8,128)(2,1)S(1)}, bf16[80,256]{1,0:T(8,128)(2,1)S(1)}, u32[]{:S(2)}, u32[]{:S(2)}) collective-permute-start(bf16[80,256]{1,0:T(8,128)(2,1)S(1)} %get-tuple-element.37), channel_id=1, source_target_pairs={{0,2},{1,3},{2,0},{3,1},{4,6},{5,7},{6,4},{7,5},{8,10},{9,11},{10,... | collective-permute-start | bytes 122888 | tf_op jit(solution)/shard_map/ppermute | solution.py:347
  20.2 8.1 %copy-start.1 = (bf16[256,256]{1,0:T(8,128)(2,1)S(1)}, bf16[256,256]{1,0:T(8,128)(2,1)}, u32[]{:S(2)}) copy-start(bf16[256,256]{1,0:T(8,128)(2,1)} %refs_0_.1) | copy-start | bytes 393220
  20.2 5.0 %collective-permute-start.7 = (bf16[64,256]{1,0:T(8,128)(2,1)S(1)}, bf16[64,256]{1,0:T(8,128)(2,1)S(1)}, u32[]{:S(2)}, u32[]{:S(2)}) collective-permute-start(bf16[64,256]{1,0:T(8,128)(2,1)S(1)} %get-tuple-element.34), channel_id=1, source_target_pairs={{0,8},{1,11},{2,10},{3,9},{4,12},{5,15},{6,14},{7,13},{8,0},{9,3},... | collective-permute-start | bytes 98312 | tf_op jit(solution)/shard_map/ppermute | solution.py:347
  22.0 6.1 %collective-permute-start.8 = (bf16[64,256]{1,0:T(8,128)(2,1)S(1)}, bf16[64,256]{1,0:T(8,128)(2,1)S(1)}, u32[]{:S(2)}, u32[]{:S(2)}) collective-permute-start(bf16[64,256]{1,0:T(8,128)(2,1)S(1)} %get-tuple-element.35), channel_id=1, source_target_pairs={{0,12},{1,15},{2,14},{3,13},{4,8},{5,11},{6,10},{7,9},{8,4},{9,7},... | collective-permute-start | bytes 98312 | tf_op jit(solution)/shard_map/ppermute | solution.py:347
  22.4 5.7 %collective-permute-start.9 = (bf16[64,256]{1,0:T(8,128)(2,1)S(1)}, bf16[64,256]{1,0:T(8,128)(2,1)S(1)}, u32[]{:S(2)}, u32[]{:S(2)}) collective-permute-start(bf16[64,256]{1,0:T(8,128)(2,1)S(1)} %get-tuple-element.36), channel_id=1, source_target_pairs={{0,4},{1,7},{2,6},{3,5},{4,0},{5,3},{6,2},{7,1},{8,12},{9,15},{10,... | collective-permute-start | bytes 98312 | tf_op jit(solution)/shard_map/ppermute | solution.py:347
  28.0 0.7 %copy-start.3 = (f32[3,768]{1,0:T(4,128)S(1)}, f32[3,768]{1,0:T(4,128)}, u32[]{:S(2)}) copy-start(f32[3,768]{1,0:T(4,128)} %refs_3_.1) | copy-start | bytes 27652
  28.1 0.7 %copy-start.4 = (f32[256]{0:T(256)S(1)}, f32[256]{0:T(256)}, u32[]{:S(2)}) copy-start(f32[256]{0:T(256)} %param.12) | copy-start | bytes 3076
  28.1 1.3 %copy-start.2 = (bf16[256,256]{1,0:T(8,128)(2,1)S(1)}, bf16[256,256]{1,0:T(8,128)(2,1)}, u32[]{:S(2)}) copy-start(bf16[256,256]{1,0:T(8,128)(2,1)} %w_ref.3) | copy-start | bytes 393220
  28.1 1.3 %collective-permute-start.11 = (bf16[128,256]{1,0:T(8,128)(2,1)S(1)}, bf16[128,256]{1,0:T(8,128)(2,1)S(1)}, u32[]{:S(2)}, u32[]{:S(2)}) collective-permute-start(bf16[128,256]{1,0:T(8,128)(2,1)S(1)} %get-tuple-element.40), channel_id=1, source_target_pairs={{0,1},{1,0},{2,3},{3,2},{4,5},{5,4},{6,7},{7,6},{8,9},{9,8},{10,11... | collective-permute-start | bytes 196616 | tf_op jit(solution)/shard_map/ppermute | solution.py:347

commit v16 on v15

--- a/solution.py
+++ b/solution.py
@@ -55,11 +55,8 @@
     )
 
 
-def routes_of(chips, forward):
-    far = sorted(range(2, chips, 2), key=lambda d: (-d.bit_length(), d))
-    if forward:
-        far = far[:1] + far[:0:-1]
-    return [(d, d + 1) for d in far]
+def routes_of(chips):
+    return [(d, d + 1) for d in range(chips - 2, 1, -2)]
 
 
 def carried(route, core):
@@ -78,7 +75,7 @@
         if extra:
             out_ref[2 * size : 2 * size + extra, :] = rim_ref[chip ^ distance]
 
-    for turn, route in enumerate(routes_of(lax.axis_size("chip"), extra > 0)):
+    for turn, route in enumerate(routes_of(lax.axis_size("chip"))):
         own, other = carried(route, core)
         put(keep_ref.at[turn], own)
         put(give_ref.at[turn], other)
@@ -122,7 +119,7 @@
 
 def take_routes(keep_ref, got_ref, target_ref, rim_ref=None):
     chip, core = lax.axis_index("chip"), lax.axis_index("core")
-    routes = routes_of(lax.axis_size("chip"), rim_ref is not None)
+    routes = routes_of(lax.axis_size("chip"))
     count = 2 * len(routes) + 2
     size = target_ref.shape[0] // (2 * lax.axis_size("chip"))
     places = [(*carried(route, core), sender) for route in routes for sender in range(2)]
@@ -363,7 +360,7 @@
         [pltpu.VMEM] * 2,
         moved=4 * keep.size,
     )
-    routes = routes_of(lax.axis_size("chip"), extra > 0)
+    routes = routes_of(lax.axis_size("chip"))
     far = [permute(part, lambda i: i ^ 2 * route[i % 2]) for part, route in zip(far, routes)]
     count = 2 * turns + 2
     half = bf16(count * size + count // 2 * extra, lanes)

time: 30.5 us -> 29.4 us (0.964)
  waiting for transfers between devices: 12.2 us -> 10.7 us
  starting transfers between devices: 13.1 us -> 13.7 us
    ppermute x12, waiting for transfers between devices: 12.2 us -> 10.7 us  [permute(): lax.ppermute(array, seq, [(i, partner(i)) for i in range(lax.axis_size(se...]
    ppermute x12, starting transfers between devices: 13.1 us -> 13.7 us  [permute(): lax.ppermute(array, seq, [(i, partner(i)) for i in range(lax.axis_size(se...]
where the time goes in v16:
time: 29.4 us; the launch traced here: 29.3 us
  starting transfers between devices  13.7 us (47%)
  waiting for transfers between devices  10.7 us (36%)
  Pallas kernels  4.46 us (15%)
  local copies, waits for them, and re-layouts  0.35 us (1%)
    ppermute x12, starting transfers between devices, permute(): lax.ppermute(array, seq, [(i, partner(i)) for i in range(lax.axis_size(se...  13.7 us
    ppermute x12, waiting for transfers between devices, permute(): lax.ppermute(array, seq, [(i, partner(i)) for i in range(lax.axis_size(se...  10.7 us
    pallas_call x8, Pallas kernels, call(): pl.pallas_call(body, out_shape=outs, in_specs=[whole(space) for space in...  4.46 us
  transfers between devices with their start and end apart: 12, of which 7 were waited for; matrix products, arithmetic and copies ran while one was open for 0% of the time, Pallas kernels for 1%

profile of v16, /device:TPU:0, one launch (start us, length us, event | category | flops | bytes accessed | tf_op | source)
XLA Modules:
  0.0 29.3 jit_solution(14091361283055965245)
XLA Ops:
  0.0 0.0 copy-start.7
  0.0 1.8 %shard_map.110 = (bf16[3,136,128]{2,1,0:T(8,128)(2,1)S(1)}, bf16[3,136,128]{2,1,0:T(8,128)(2,1)S(1)}, bf16[280,128]{1,0:T(8,128)(2,1)S(1)}, bf16[136,128]{1,0:T(8,128)(2,1)S(1)}) custom-call(bf16[256,256]{1,0:T(8,128)(2,1)} %refs_0_.1, f32[1,256]{1,0:T(1,128)} %bitcast.2, bf16[256,768]{1,0:T(8,128)(2,1)} %refs_2_.1, f32[3,768]{1,0:T(4,128)} %refs_3_.1, ...), custom_call_target="tpu_custom_call" | custom-call | flops 100663296 | bytes 1500000 | tf_op jit(solution)/shard_map/pallas_call | solution.py:26
  1.8 0.5 %collective-permute-start = (bf16[3,136,128]{2,1,0:T(8,128)(2,1)S(1)}, bf16[3,136,128]{2,1,0:T(8,128)(2,1)S(1)}, u32[]{:S(2)}, u32[]{:S(2)}) collective-permute-start(bf16[3,136,128]{2,1,0:T(8,128)(2,1)S(1)} %get-tuple-element.24), channel_id=1, source_target_pairs={{0,1},{1,0},{2,3},{3,2},{4,5},{5,4},{6,7},{7,6},{8,9},{9,8},{10,11... | collective-permute-start | bytes 313352 | tf_op jit(solution)/shard_map/ppermute | solution.py:344
  2.3 2.6 %collective-permute-start.4 = (bf16[280,128]{1,0:T(8,128)(2,1)S(1)}, bf16[280,128]{1,0:T(8,128)(2,1)S(1)}, u32[]{:S(2)}, u32[]{:S(2)}) collective-permute-start(bf16[280,128]{1,0:T(8,128)(2,1)S(1)} %get-tuple-element.28), channel_id=1, source_target_pairs={{0,2},{1,3},{2,0},{3,1},{4,6},{5,7},{6,4},{7,5},{8,10},{9,11},{10,... | collective-permute-start | bytes 215048 | tf_op jit(solution)/shard_map/ppermute | solution.py:344
  4.9 0.0 collective-permute-done.got_ref
  4.9 0.0 copy-start.5
  4.9 0.0 copy-start.6
  4.9 3.7 %collective-permute-start.1 = (bf16[264,128]{1,0:T(8,128)(2,1)S(1)}, bf16[264,128]{1,0:T(8,128)(2,1)S(1)}, u32[]{:S(2)}, u32[]{:S(2)}) collective-permute-start(bf16[264,128]{1,0:T(8,128)(2,1)S(1)} %get-tuple-element.25), channel_id=1, source_target_pairs={{0,12},{1,15},{2,14},{3,13},{4,8},{5,11},{6,10},{7,9},{8,4},{9,7},... | collective-permute-start | bytes 202760 | tf_op jit(solution)/shard_map/ppermute | solution.py:344
  8.6 0.0 collective-permute-start.2
  8.6 0.8 %collective-permute-start.3 = (bf16[264,128]{1,0:T(8,128)(2,1)S(1)}, bf16[264,128]{1,0:T(8,128)(2,1)S(1)}, u32[]{:S(2)}, u32[]{:S(2)}) collective-permute-start(bf16[264,128]{1,0:T(8,128)(2,1)S(1)} %get-tuple-element.27), channel_id=1, source_target_pairs={{0,4},{1,7},{2,6},{3,5},{4,0},{5,3},{6,2},{7,1},{8,12},{9,15},{10,... | collective-permute-start | bytes 202760 | tf_op jit(solution)/shard_map/ppermute | solution.py:344
  9.4 0.0 collective-permute-done.4.refs_3_
  9.4 2.4 %collective-permute-done.1.refs_0_ = bf16[264,128]{1,0:T(8,128)(2,1)S(1)} collective-permute-done((bf16[264,128]{1,0:T(8,128)(2,1)S(1)}, bf16[264,128]{1,0:T(8,128)(2,1)S(1)}, u32[]{:S(2)}, u32[]{:S(2)}) %collective-permute-start.1) | collective-permute-done | bytes 67616 | tf_op jit(solution)/shard_map/ppermute | solution.py:344
  11.8 3.5 %collective-permute-done.2.refs_1_ = bf16[264,128]{1,0:T(8,128)(2,1)S(1)} collective-permute-done((bf16[264,128]{1,0:T(8,128)(2,1)S(1)}, bf16[264,128]{1,0:T(8,128)(2,1)S(1)}, u32[]{:S(2)}, u32[]{:S(2)}) %collective-permute-start.2) | collective-permute-done | bytes 67616 | tf_op jit(solution)/shard_map/ppermute | solution.py:344
  15.2 0.0 collective-permute-done.3.refs_2_
  15.2 0.2 collective-permute-start.5
  15.4 1.2 %collective-permute-done.5.refs_1_ = bf16[544,128]{1,0:T(8,128)(2,1)S(1)} collective-permute-done((bf16[544,128]{1,0:T(8,128)(2,1)S(1)}, bf16[544,128]{1,0:T(8,128)(2,1)S(1)}, u32[]{:S(2)}, u32[]{:S(2)}) %collective-permute-start.5) | collective-permute-done | bytes 139296 | tf_op jit(solution)/shard_map/ppermute | solution.py:344
  16.7 0.0 copy-done.7
  16.7 0.0 copy-done.5
  16.7 0.0 copy-done.6
  16.7 0.0 copy-start
  16.7 1.4 %shard_map.113 = (bf16[3,32,256]{2,1,0:T(8,128)(2,1)S(1)}, bf16[3,32,256]{2,1,0:T(8,128)(2,1)S(1)}, bf16[80,256]{1,0:T(8,128)(2,1)S(1)}, bf16[32,256]{1,0:T(8,128)(2,1)S(1)}) custom-call(bf16[512,256]{1,0:T(8,128)(2,1)S(1)} %copy-done.5, f32[32,256]{1,0:T(8,128)S(1)} %copy-done.7, bf16[256,512]{1,0:T(8,128)(2,1)S(1)} %copy-done.6, ...), custom_call_target="tpu_custom_call" | custom-call | flops 603979776 | bytes 2000000 | tf_op jit(solution)/shard_map/pallas_call | solution.py:26
  18.1 0.2 collective-permute-start.6
  18.3 1.0 %collective-permute-start.10 = (bf16[80,256]{1,0:T(8,128)(2,1)S(1)}, bf16[80,256]{1,0:T(8,128)(2,1)S(1)}, u32[]{:S(2)}, u32[]{:S(2)}) collective-permute-start(bf16[80,256]{1,0:T(8,128)(2,1)S(1)} %get-tuple-element.37), channel_id=1, source_target_pairs={{0,2},{1,3},{2,0},{3,1},{4,6},{5,7},{6,4},{7,5},{8,10},{9,11},{10,... | collective-permute-start | bytes 122888 | tf_op jit(solution)/shard_map/ppermute | solution.py:344
  19.3 0.1 collective-permute-done.6.got_ref
  19.4 0.0 copy-start.1
  19.4 2.5 %collective-permute-start.7 = (bf16[64,256]{1,0:T(8,128)(2,1)S(1)}, bf16[64,256]{1,0:T(8,128)(2,1)S(1)}, u32[]{:S(2)}, u32[]{:S(2)}) collective-permute-start(bf16[64,256]{1,0:T(8,128)(2,1)S(1)} %get-tuple-element.34), channel_id=1, source_target_pairs={{0,12},{1,15},{2,14},{3,13},{4,8},{5,11},{6,10},{7,9},{8,4},{9,7},... | collective-permute-start | bytes 98312 | tf_op jit(solution)/shard_map/ppermute | solution.py:344
  21.9 0.2 collective-permute-start.8
  22.1 1.7 %collective-permute-start.9 = (bf16[64,256]{1,0:T(8,128)(2,1)S(1)}, bf16[64,256]{1,0:T(8,128)(2,1)S(1)}, u32[]{:S(2)}, u32[]{:S(2)}) collective-permute-start(bf16[64,256]{1,0:T(8,128)(2,1)S(1)} %get-tuple-element.36), channel_id=1, source_target_pairs={{0,4},{1,7},{2,6},{3,5},{4,0},{5,3},{6,2},{7,1},{8,12},{9,15},{10,... | collective-permute-start | bytes 98312 | tf_op jit(solution)/shard_map/ppermute | solution.py:344
  23.9 0.0 collective-permute-done.10.refs_3_
  23.9 1.6 %collective-permute-done.7.refs_0_ = bf16[64,256]{1,0:T(8,128)(2,1)S(1)} collective-permute-done((bf16[64,256]{1,0:T(8,128)(2,1)S(1)}, bf16[64,256]{1,0:T(8,128)(2,1)S(1)}, u32[]{:S(2)}, u32[]{:S(2)}) %collective-permute-start.7) | collective-permute-done | bytes 32800 | tf_op jit(solution)/shard_map/ppermute | solution.py:344
  25.4 1.6 %collective-permute-done.8.refs_1_ = bf16[64,256]{1,0:T(8,128)(2,1)S(1)} collective-permute-done((bf16[64,256]{1,0:T(8,128)(2,1)S(1)}, bf16[64,256]{1,0:T(8,128)(2,1)S(1)}, u32[]{:S(2)}, u32[]{:S(2)}) %collective-permute-start.8) | collective-permute-done | bytes 32800 | tf_op jit(solution)/shard_map/ppermute | solution.py:344
  27.0 0.0 collective-permute-done.9.refs_2_
  27.0 0.0 copy-start.3
  27.0 0.0 copy-start.4
  27.0 0.0 copy-start.2
  27.1 0.3 %collective-permute-start.11 = (bf16[128,256]{1,0:T(8,128)(2,1)S(1)}, bf16[128,256]{1,0:T(8,128)(2,1)S(1)}, u32[]{:S(2)}, u32[]{:S(2)}) collective-permute-start(bf16[128,256]{1,0:T(8,128)(2,1)S(1)} %get-tuple-element.40), channel_id=1, source_target_pairs={{0,1},{1,0},{2,3},{3,2},{4,5},{5,4},{6,7},{7,6},{8,9},{9,8},{10,11... | collective-permute-start | bytes 196616 | tf_op jit(solution)/shard_map/ppermute | solution.py:344
  27.4 0.0 copy-done
  27.4 0.0 copy-done.1
  27.4 0.3 %copy-done.3 = f32[3,768]{1,0:T(4,128)S(1)} copy-done((f32[3,768]{1,0:T(4,128)S(1)}, f32[3,768]{1,0:T(4,128)}, u32[]{:S(2)}) %copy-start.3) | copy-done | bytes 9240
  27.7 0.0 copy-done.4
  27.7 0.3 %shard_map.109.query_ref = f32[256,256]{1,0:T(8,128)S(1)} custom-call(bf16[256,256]{1,0:T(8,128)(2,1)S(1)} %copy-done.1, f32[1,256]{1,0:T(1,128)S(1)} %bitcast.3, bf16[256,768]{1,0:T(8,128)(2,1)S(1)} %copy-done, f32[3,768]{1,0:T(4,128)S(1)} %copy-done.3), custom_call_target="tpu_custom_call" | custom-call | flops 33554432 | bytes 800000 | tf_op jit(solution)/shard_map/pallas_call | solution.py:26
  28.0 0.3 %collective-permute-done.11.refs_1_ = bf16[128,256]{1,0:T(8,128)(2,1)S(1)} collective-permute-done((bf16[128,256]{1,0:T(8,128)(2,1)S(1)}, bf16[128,256]{1,0:T(8,128)(2,1)S(1)}, u32[]{:S(2)}, u32[]{:S(2)}) %collective-permute-start.11) | collective-permute-done | bytes 65568 | tf_op jit(solution)/shard_map/ppermute | solution.py:344
  28.4 0.0 copy-done.2
  28.4 0.9 %shard_map.116 = bf16[256,256]{1,0:T(8,128)(2,1)} custom-call(f32[256,256]{1,0:T(8,128)S(1)} %shard_map.109.query_ref, bf16[256,256]{1,0:T(8,128)(2,1)S(1)} %copy-done.2, bf16[128,256]{1,0:T(8,128)(2,1)S(1)} %get-tuple-element.39.refs_0_, bf16[128,256]{1,0:T(8,128)(2,1)S(1)} %collective-permute-done.11.refs_1_), custom_call_target="tpu_custom_call" | custom-call | flops 33554432 | bytes 600000 | tf_op jit(solution)/shard_map/pallas_call | solution.py:26
  (4 shorter events, 0.1 us)
Async XLA Ops:
  0.0 16.7 %copy-start.7 = (f32[32,256]{1,0:T(8,128)S(1)}, f32[32,256]{1,0:T(8,128)}, u32[]{:S(2)}) copy-start(f32[32,256]{1,0:T(8,128)} %constant.7.clone.twist_ref) | copy-start | bytes 98308
  1.8 3.1 %collective-permute-start = (bf16[3,136,128]{2,1,0:T(8,128)(2,1)S(1)}, bf16[3,136,128]{2,1,0:T(8,128)(2,1)S(1)}, u32[]{:S(2)}, u32[]{:S(2)}) collective-permute-start(bf16[3,136,128]{2,1,0:T(8,128)(2,1)S(1)} %get-tuple-element.24), channel_id=1, source_target_pairs={{0,1},{1,0},{2,3},{3,2},{4,5},{5,4},{6,7},{7,6},{8,9},{9,8},{10,11... | collective-permute-start | bytes 313352 | tf_op jit(solution)/shard_map/ppermute | solution.py:344
  2.3 7.1 %collective-permute-start.4 = (bf16[280,128]{1,0:T(8,128)(2,1)S(1)}, bf16[280,128]{1,0:T(8,128)(2,1)S(1)}, u32[]{:S(2)}, u32[]{:S(2)}) collective-permute-start(bf16[280,128]{1,0:T(8,128)(2,1)S(1)} %get-tuple-element.28), channel_id=1, source_target_pairs={{0,2},{1,3},{2,0},{3,1},{4,6},{5,7},{6,4},{7,5},{8,10},{9,11},{10,... | collective-permute-start | bytes 215048 | tf_op jit(solution)/shard_map/ppermute | solution.py:344
  4.9 11.8 %copy-start.5 = (bf16[512,256]{1,0:T(8,128)(2,1)S(1)}, bf16[512,256]{1,0:T(8,128)(2,1)}, u32[]{:S(2)}) copy-start(bf16[512,256]{1,0:T(8,128)(2,1)} %constant.6.clone.first_ref) | copy-start | bytes 786436
  4.9 11.8 %copy-start.6 = (bf16[256,512]{1,0:T(8,128)(2,1)S(1)}, bf16[256,512]{1,0:T(8,128)(2,1)}, u32[]{:S(2)}) copy-start(bf16[256,512]{1,0:T(8,128)(2,1)} %constant.8.clone.inner_ref) | copy-start | bytes 786436
  4.9 6.8 %collective-permute-start.1 = (bf16[264,128]{1,0:T(8,128)(2,1)S(1)}, bf16[264,128]{1,0:T(8,128)(2,1)S(1)}, u32[]{:S(2)}, u32[]{:S(2)}) collective-permute-start(bf16[264,128]{1,0:T(8,128)(2,1)S(1)} %get-tuple-element.25), channel_id=1, source_target_pairs={{0,12},{1,15},{2,14},{3,13},{4,8},{5,11},{6,10},{7,9},{8,4},{9,7},... | collective-permute-start | bytes 202760 | tf_op jit(solution)/shard_map/ppermute | solution.py:344
  8.6 6.6 %collective-permute-start.2 = (bf16[264,128]{1,0:T(8,128)(2,1)S(1)}, bf16[264,128]{1,0:T(8,128)(2,1)S(1)}, u32[]{:S(2)}, u32[]{:S(2)}) collective-permute-start(bf16[264,128]{1,0:T(8,128)(2,1)S(1)} %get-tuple-element.26), channel_id=1, source_target_pairs={{0,8},{1,11},{2,10},{3,9},{4,12},{5,15},{6,14},{7,13},{8,0},{9,3},... | collective-permute-start | bytes 202760 | tf_op jit(solution)/shard_map/ppermute | solution.py:344
  8.6 6.6 %collective-permute-start.3 = (bf16[264,128]{1,0:T(8,128)(2,1)S(1)}, bf16[264,128]{1,0:T(8,128)(2,1)S(1)}, u32[]{:S(2)}, u32[]{:S(2)}) collective-permute-start(bf16[264,128]{1,0:T(8,128)(2,1)S(1)} %get-tuple-element.27), channel_id=1, source_target_pairs={{0,4},{1,7},{2,6},{3,5},{4,0},{5,3},{6,2},{7,1},{8,12},{9,15},{10,... | collective-permute-start | bytes 202760 | tf_op jit(solution)/shard_map/ppermute | solution.py:344
  15.2 1.4 %collective-permute-start.5 = (bf16[544,128]{1,0:T(8,128)(2,1)S(1)}, bf16[544,128]{1,0:T(8,128)(2,1)S(1)}, u32[]{:S(2)}, u32[]{:S(2)}) collective-permute-start(bf16[544,128]{1,0:T(8,128)(2,1)S(1)} %get-tuple-element.31), channel_id=1, source_target_pairs={{0,1},{1,0},{2,3},{3,2},{4,5},{5,4},{6,7},{7,6},{8,9},{9,8},{10,11... | collective-permute-start | bytes 417800 | tf_op jit(solution)/shard_map/ppermute | solution.py:344
  16.7 10.7 %copy-start = (bf16[256,768]{1,0:T(8,128)(2,1)S(1)}, bf16[256,768]{1,0:T(8,128)(2,1)}, u32[]{:S(2)}) copy-start(bf16[256,768]{1,0:T(8,128)(2,1)} %refs_2_.1) | copy-start | bytes 1179652
  18.1 1.3 %collective-permute-start.6 = (bf16[3,32,256]{2,1,0:T(8,128)(2,1)S(1)}, bf16[3,32,256]{2,1,0:T(8,128)(2,1)S(1)}, u32[]{:S(2)}, u32[]{:S(2)}) collective-permute-start(bf16[3,32,256]{2,1,0:T(8,128)(2,1)S(1)} %get-tuple-element.33), channel_id=1, source_target_pairs={{0,1},{1,0},{2,3},{3,2},{4,5},{5,4},{6,7},{7,6},{8,9},{9,8},{10,11... | collective-permute-start | bytes 147464 | tf_op jit(solution)/shard_map/ppermute | solution.py:344
  18.3 5.6 %collective-permute-start.10 = (bf16[80,256]{1,0:T(8,128)(2,1)S(1)}, bf16[80,256]{1,0:T(8,128)(2,1)S(1)}, u32[]{:S(2)}, u32[]{:S(2)}) collective-permute-start(bf16[80,256]{1,0:T(8,128)(2,1)S(1)} %get-tuple-element.37), channel_id=1, source_target_pairs={{0,2},{1,3},{2,0},{3,1},{4,6},{5,7},{6,4},{7,5},{8,10},{9,11},{10,... | collective-permute-start | bytes 122888 | tf_op jit(solution)/shard_map/ppermute | solution.py:344
  19.4 8.0 %copy-start.1 = (bf16[256,256]{1,0:T(8,128)(2,1)S(1)}, bf16[256,256]{1,0:T(8,128)(2,1)}, u32[]{:S(2)}) copy-start(bf16[256,256]{1,0:T(8,128)(2,1)} %refs_0_.1) | copy-start | bytes 393220
  19.4 6.0 %collective-permute-start.7 = (bf16[64,256]{1,0:T(8,128)(2,1)S(1)}, bf16[64,256]{1,0:T(8,128)(2,1)S(1)}, u32[]{:S(2)}, u32[]{:S(2)}) collective-permute-start(bf16[64,256]{1,0:T(8,128)(2,1)S(1)} %get-tuple-element.34), channel_id=1, source_target_pairs={{0,12},{1,15},{2,14},{3,13},{4,8},{5,11},{6,10},{7,9},{8,4},{9,7},... | collective-permute-start | bytes 98312 | tf_op jit(solution)/shard_map/ppermute | solution.py:344
  21.9 5.1 %collective-permute-start.8 = (bf16[64,256]{1,0:T(8,128)(2,1)S(1)}, bf16[64,256]{1,0:T(8,128)(2,1)S(1)}, u32[]{:S(2)}, u32[]{:S(2)}) collective-permute-start(bf16[64,256]{1,0:T(8,128)(2,1)S(1)} %get-tuple-element.35), channel_id=1, source_target_pairs={{0,8},{1,11},{2,10},{3,9},{4,12},{5,15},{6,14},{7,13},{8,0},{9,3},... | collective-permute-start | bytes 98312 | tf_op jit(solution)/shard_map/ppermute | solution.py:344
  22.1 4.9 %collective-permute-start.9 = (bf16[64,256]{1,0:T(8,128)(2,1)S(1)}, bf16[64,256]{1,0:T(8,128)(2,1)S(1)}, u32[]{:S(2)}, u32[]{:S(2)}) collective-permute-start(bf16[64,256]{1,0:T(8,128)(2,1)S(1)} %get-tuple-element.36), channel_id=1, source_target_pairs={{0,4},{1,7},{2,6},{3,5},{4,0},{5,3},{6,2},{7,1},{8,12},{9,15},{10,... | collective-permute-start | bytes 98312 | tf_op jit(solution)/shard_map/ppermute | solution.py:344
  27.0 0.7 %copy-start.3 = (f32[3,768]{1,0:T(4,128)S(1)}, f32[3,768]{1,0:T(4,128)}, u32[]{:S(2)}) copy-start(f32[3,768]{1,0:T(4,128)} %refs_3_.1) | copy-start | bytes 27652
  27.0 0.7 %copy-start.4 = (f32[256]{0:T(256)S(1)}, f32[256]{0:T(256)}, u32[]{:S(2)}) copy-start(f32[256]{0:T(256)} %param.12) | copy-start | bytes 3076
  27.0 1.3 %copy-start.2 = (bf16[256,256]{1,0:T(8,128)(2,1)S(1)}, bf16[256,256]{1,0:T(8,128)(2,1)}, u32[]{:S(2)}) copy-start(bf16[256,256]{1,0:T(8,128)(2,1)} %w_ref.3) | copy-start | bytes 393220
  27.1 1.3 %collective-permute-start.11 = (bf16[128,256]{1,0:T(8,128)(2,1)S(1)}, bf16[128,256]{1,0:T(8,128)(2,1)S(1)}, u32[]{:S(2)}, u32[]{:S(2)}) collective-permute-start(bf16[128,256]{1,0:T(8,128)(2,1)S(1)} %get-tuple-element.40), channel_id=1, source_target_pairs={{0,1},{1,0},{2,3},{3,2},{4,5},{5,4},{6,7},{7,6},{8,9},{9,8},{10,11... | collective-permute-start | bytes 196616 | tf_op jit(solution)/shard_map/ppermute | solution.py:344

commit v17 on v16

--- a/solution.py
+++ b/solution.py
@@ -81,9 +81,9 @@
         put(give_ref.at[turn], other)
     put(home_ref, 0)
     put(near_ref, 1)
-    begin = 2 * size + extra
-    near_ref[begin : begin + 2 * size, :] = home_ref[0 : 2 * size, :]
-    near_ref[begin + 2 * size :, :] = home_ref[0:chan_tile, :]
+    if not extra:
+        near_ref[2 * size : 4 * size, :] = home_ref[...]
+        near_ref[4 * size :, :] = home_ref[0:chan_tile, :]
 
 
 def half_rims(first_ref, second_ref, begin):
@@ -389,7 +389,7 @@
         if not staged:
             return (bf16(*shape),)
         size, turns = 2 * shape[0] // devices + extra, chips // 2 - 1
-        near = size + size - extra + chan_tile
+        near = size if extra else 2 * size + chan_tile
         return (bf16(turns, size, shape[1]),) * 2 + (bf16(near, shape[1]), bf16(size, shape[1]))
 
     def scratch(*shapes):

time: 29.4 us -> 29.6 us (level)
  waiting for transfers between devices: 10.7 us -> 9.97 us
  starting transfers between devices: 13.7 us -> 14.4 us
    ppermute x12, waiting for transfers between devices: 10.7 us -> 9.97 us  [permute(): lax.ppermute(array, seq, [(i, partner(i)) for i in range(lax.axis_size(se...]
    ppermute x12, starting transfers between devices: 13.7 us -> 14.4 us  [permute(): lax.ppermute(array, seq, [(i, partner(i)) for i in range(lax.axis_size(se...]
where the time goes in v17:
time: 29.6 us; the launch traced here: 29.5 us
  starting transfers between devices  14.4 us (49%)
  waiting for transfers between devices  9.97 us (34%)
  Pallas kernels  4.5 us (15%)
  local copies, waits for them, and re-layouts  0.57 us (2%)
    ppermute x12, starting transfers between devices, permute(): lax.ppermute(array, seq, [(i, partner(i)) for i in range(lax.axis_size(se...  14.4 us
    ppermute x12, waiting for transfers between devices, permute(): lax.ppermute(array, seq, [(i, partner(i)) for i in range(lax.axis_size(se...  9.97 us
    pallas_call x8, Pallas kernels, call(): pl.pallas_call(body, out_shape=outs, in_specs=[whole(space) for space in...  4.5 us
  transfers between devices with their start and end apart: 12, of which 7 were waited for; matrix products, arithmetic and copies ran while one was open for 0% of the time, Pallas kernels for 1%

profile of v17, /device:TPU:0, one launch (start us, length us, event | category | flops | bytes accessed | tf_op | source)
XLA Modules:
  0.0 29.5 jit_solution(15983875161302610233)
XLA Ops:
  0.0 0.0 copy-start.6
  0.0 1.8 %shard_map.110 = (bf16[3,136,128]{2,1,0:T(8,128)(2,1)S(1)}, bf16[3,136,128]{2,1,0:T(8,128)(2,1)S(1)}, bf16[136,128]{1,0:T(8,128)(2,1)S(1)}, bf16[136,128]{1,0:T(8,128)(2,1)S(1)}) custom-call(bf16[256,256]{1,0:T(8,128)(2,1)} %refs_0_.1, f32[1,256]{1,0:T(1,128)} %bitcast.2, bf16[256,768]{1,0:T(8,128)(2,1)} %refs_2_.1, f32[3,768]{1,0:T(4,128)} %refs_3_.1, ...), custom_call_target="tpu_custom_call" | custom-call | flops 100663296 | bytes 1500000 | tf_op jit(solution)/shard_map/pallas_call | solution.py:26
  1.8 0.0 copy-start.5
  1.8 0.5 %collective-permute-start = (bf16[3,136,128]{2,1,0:T(8,128)(2,1)S(1)}, bf16[3,136,128]{2,1,0:T(8,128)(2,1)S(1)}, u32[]{:S(2)}, u32[]{:S(2)}) collective-permute-start(bf16[3,136,128]{2,1,0:T(8,128)(2,1)S(1)} %get-tuple-element.24), channel_id=1, source_target_pairs={{0,1},{1,0},{2,3},{3,2},{4,5},{5,4},{6,7},{7,6},{8,9},{9,8},{10,11... | collective-permute-start | bytes 313352 | tf_op jit(solution)/shard_map/ppermute | solution.py:344
  2.4 1.0 %collective-permute-done.got_ref = bf16[3,136,128]{2,1,0:T(8,128)(2,1)S(1)} collective-permute-done((bf16[3,136,128]{2,1,0:T(8,128)(2,1)S(1)}, bf16[3,136,128]{2,1,0:T(8,128)(2,1)S(1)}, u32[]{:S(2)}, u32[]{:S(2)}) %collective-permute-start) | collective-permute-done | bytes 104480 | tf_op jit(solution)/shard_map/ppermute | solution.py:344
  3.3 5.0 %collective-permute-start.1 = (bf16[264,128]{1,0:T(8,128)(2,1)S(1)}, bf16[264,128]{1,0:T(8,128)(2,1)S(1)}, u32[]{:S(2)}, u32[]{:S(2)}) collective-permute-start(bf16[264,128]{1,0:T(8,128)(2,1)S(1)} %get-tuple-element.25), channel_id=1, source_target_pairs={{0,12},{1,15},{2,14},{3,13},{4,8},{5,11},{6,10},{7,9},{8,4},{9,7},... | collective-permute-start | bytes 202760 | tf_op jit(solution)/shard_map/ppermute | solution.py:344
  8.3 0.0 collective-permute-start.2
  8.3 0.6 %collective-permute-start.3 = (bf16[264,128]{1,0:T(8,128)(2,1)S(1)}, bf16[264,128]{1,0:T(8,128)(2,1)S(1)}, u32[]{:S(2)}, u32[]{:S(2)}) collective-permute-start(bf16[264,128]{1,0:T(8,128)(2,1)S(1)} %get-tuple-element.27), channel_id=1, source_target_pairs={{0,4},{1,7},{2,6},{3,5},{4,0},{5,3},{6,2},{7,1},{8,12},{9,15},{10,... | collective-permute-start | bytes 202760 | tf_op jit(solution)/shard_map/ppermute | solution.py:344
  9.0 1.7 %collective-permute-start.4 = (bf16[136,128]{1,0:T(8,128)(2,1)S(1)}, bf16[136,128]{1,0:T(8,128)(2,1)S(1)}, u32[]{:S(2)}, u32[]{:S(2)}) collective-permute-start(bf16[136,128]{1,0:T(8,128)(2,1)S(1)} %get-tuple-element.28), channel_id=1, source_target_pairs={{0,2},{1,3},{2,0},{3,1},{4,6},{5,7},{6,4},{7,5},{8,10},{9,11},{10,... | collective-permute-start | bytes 104456 | tf_op jit(solution)/shard_map/ppermute | solution.py:344
  10.7 3.0 %collective-permute-done.4.refs_3_ = bf16[136,128]{1,0:T(8,128)(2,1)S(1)} collective-permute-done((bf16[136,128]{1,0:T(8,128)(2,1)S(1)}, bf16[136,128]{1,0:T(8,128)(2,1)S(1)}, u32[]{:S(2)}, u32[]{:S(2)}) %collective-permute-start.4) | collective-permute-done | bytes 34848 | tf_op jit(solution)/shard_map/ppermute | solution.py:344
  13.7 0.0 collective-permute-done.1.refs_0_
  13.7 1.3 %collective-permute-done.2.refs_1_ = bf16[264,128]{1,0:T(8,128)(2,1)S(1)} collective-permute-done((bf16[264,128]{1,0:T(8,128)(2,1)S(1)}, bf16[264,128]{1,0:T(8,128)(2,1)S(1)}, u32[]{:S(2)}, u32[]{:S(2)}) %collective-permute-start.2) | collective-permute-done | bytes 67616 | tf_op jit(solution)/shard_map/ppermute | solution.py:344
  15.0 0.0 collective-permute-done.3.refs_2_
  15.0 0.0 copy-start.7
  15.0 0.5 %collective-permute-start.5 = (bf16[544,128]{1,0:T(8,128)(2,1)S(1)}, bf16[544,128]{1,0:T(8,128)(2,1)S(1)}, u32[]{:S(2)}, u32[]{:S(2)}) collective-permute-start(bf16[544,128]{1,0:T(8,128)(2,1)S(1)} %get-tuple-element.31), channel_id=1, source_target_pairs={{0,1},{1,0},{2,3},{3,2},{4,5},{5,4},{6,7},{7,6},{8,9},{9,8},{10,11... | collective-permute-start | bytes 417800 | tf_op jit(solution)/shard_map/ppermute | solution.py:344
  15.5 1.0 %collective-permute-done.5.refs_1_ = bf16[544,128]{1,0:T(8,128)(2,1)S(1)} collective-permute-done((bf16[544,128]{1,0:T(8,128)(2,1)S(1)}, bf16[544,128]{1,0:T(8,128)(2,1)S(1)}, u32[]{:S(2)}, u32[]{:S(2)}) %collective-permute-start.5) | collective-permute-done | bytes 139296 | tf_op jit(solution)/shard_map/ppermute | solution.py:344
  16.5 0.0 copy-done.6
  16.5 0.0 copy-done.5
  16.5 0.0 copy-done.7
  16.5 0.0 copy-start
  16.5 1.4 %shard_map.113 = (bf16[3,32,256]{2,1,0:T(8,128)(2,1)S(1)}, bf16[3,32,256]{2,1,0:T(8,128)(2,1)S(1)}, bf16[80,256]{1,0:T(8,128)(2,1)S(1)}, bf16[32,256]{1,0:T(8,128)(2,1)S(1)}) custom-call(bf16[512,256]{1,0:T(8,128)(2,1)S(1)} %copy-done.5, f32[32,256]{1,0:T(8,128)S(1)} %copy-done.7, bf16[256,512]{1,0:T(8,128)(2,1)S(1)} %copy-done.6, ...), custom_call_target="tpu_custom_call" | custom-call | flops 603979776 | bytes 2000000 | tf_op jit(solution)/shard_map/pallas_call | solution.py:26
  17.9 0.4 %collective-permute-start.6 = (bf16[3,32,256]{2,1,0:T(8,128)(2,1)S(1)}, bf16[3,32,256]{2,1,0:T(8,128)(2,1)S(1)}, u32[]{:S(2)}, u32[]{:S(2)}) collective-permute-start(bf16[3,32,256]{2,1,0:T(8,128)(2,1)S(1)} %get-tuple-element.33), channel_id=1, source_target_pairs={{0,1},{1,0},{2,3},{3,2},{4,5},{5,4},{6,7},{7,6},{8,9},{9,8},{10,11... | collective-permute-start | bytes 147464 | tf_op jit(solution)/shard_map/ppermute | solution.py:344
  18.3 1.0 %collective-permute-start.10 = (bf16[80,256]{1,0:T(8,128)(2,1)S(1)}, bf16[80,256]{1,0:T(8,128)(2,1)S(1)}, u32[]{:S(2)}, u32[]{:S(2)}) collective-permute-start(bf16[80,256]{1,0:T(8,128)(2,1)S(1)} %get-tuple-element.37), channel_id=1, source_target_pairs={{0,2},{1,3},{2,0},{3,1},{4,6},{5,7},{6,4},{7,5},{8,10},{9,11},{10,... | collective-permute-start | bytes 122888 | tf_op jit(solution)/shard_map/ppermute | solution.py:344
  19.4 0.0 collective-permute-done.6.got_ref
  19.4 0.0 copy-start.1
  19.4 2.8 %collective-permute-start.7 = (bf16[64,256]{1,0:T(8,128)(2,1)S(1)}, bf16[64,256]{1,0:T(8,128)(2,1)S(1)}, u32[]{:S(2)}, u32[]{:S(2)}) collective-permute-start(bf16[64,256]{1,0:T(8,128)(2,1)S(1)} %get-tuple-element.34), channel_id=1, source_target_pairs={{0,12},{1,15},{2,14},{3,13},{4,8},{5,11},{6,10},{7,9},{8,4},{9,7},... | collective-permute-start | bytes 98312 | tf_op jit(solution)/shard_map/ppermute | solution.py:344
  22.2 0.0 collective-permute-start.8
  22.2 1.7 %collective-permute-start.9 = (bf16[64,256]{1,0:T(8,128)(2,1)S(1)}, bf16[64,256]{1,0:T(8,128)(2,1)S(1)}, u32[]{:S(2)}, u32[]{:S(2)}) collective-permute-start(bf16[64,256]{1,0:T(8,128)(2,1)S(1)} %get-tuple-element.36), channel_id=1, source_target_pairs={{0,4},{1,7},{2,6},{3,5},{4,0},{5,3},{6,2},{7,1},{8,12},{9,15},{10,... | collective-permute-start | bytes 98312 | tf_op jit(solution)/shard_map/ppermute | solution.py:344
  23.8 0.0 collective-permute-done.10.refs_3_
  23.8 1.4 %collective-permute-done.7.refs_0_ = bf16[64,256]{1,0:T(8,128)(2,1)S(1)} collective-permute-done((bf16[64,256]{1,0:T(8,128)(2,1)S(1)}, bf16[64,256]{1,0:T(8,128)(2,1)S(1)}, u32[]{:S(2)}, u32[]{:S(2)}) %collective-permute-start.7) | collective-permute-done | bytes 32800 | tf_op jit(solution)/shard_map/ppermute | solution.py:344
  25.2 2.0 %collective-permute-done.8.refs_1_ = bf16[64,256]{1,0:T(8,128)(2,1)S(1)} collective-permute-done((bf16[64,256]{1,0:T(8,128)(2,1)S(1)}, bf16[64,256]{1,0:T(8,128)(2,1)S(1)}, u32[]{:S(2)}, u32[]{:S(2)}) %collective-permute-start.8) | collective-permute-done | bytes 32800 | tf_op jit(solution)/shard_map/ppermute | solution.py:344
  27.2 0.0 collective-permute-done.9.refs_2_
  27.2 0.0 copy-start.3
  27.2 0.0 copy-start.4
  27.2 0.0 copy-start.2
  27.2 0.1 collective-permute-start.11
  27.4 0.0 copy-done
  27.4 0.0 copy-done.1
  27.4 0.5 %copy-done.3 = f32[3,768]{1,0:T(4,128)S(1)} copy-done((f32[3,768]{1,0:T(4,128)S(1)}, f32[3,768]{1,0:T(4,128)}, u32[]{:S(2)}) %copy-start.3) | copy-done | bytes 9240
  27.9 0.0 copy-done.4
  27.9 0.3 %shard_map.109.query_ref = f32[256,256]{1,0:T(8,128)S(1)} custom-call(bf16[256,256]{1,0:T(8,128)(2,1)S(1)} %copy-done.1, f32[1,256]{1,0:T(1,128)S(1)} %bitcast.3, bf16[256,768]{1,0:T(8,128)(2,1)S(1)} %copy-done, f32[3,768]{1,0:T(4,128)S(1)} %copy-done.3), custom_call_target="tpu_custom_call" | custom-call | flops 33554432 | bytes 800000 | tf_op jit(solution)/shard_map/pallas_call | solution.py:26
  28.2 0.3 %collective-permute-done.11.refs_1_ = bf16[128,256]{1,0:T(8,128)(2,1)S(1)} collective-permute-done((bf16[128,256]{1,0:T(8,128)(2,1)S(1)}, bf16[128,256]{1,0:T(8,128)(2,1)S(1)}, u32[]{:S(2)}, u32[]{:S(2)}) %collective-permute-start.11) | collective-permute-done | bytes 65568 | tf_op jit(solution)/shard_map/ppermute | solution.py:344
  28.6 0.0 copy-done.2
  28.6 0.9 %shard_map.116 = bf16[256,256]{1,0:T(8,128)(2,1)} custom-call(f32[256,256]{1,0:T(8,128)S(1)} %shard_map.109.query_ref, bf16[256,256]{1,0:T(8,128)(2,1)S(1)} %copy-done.2, bf16[128,256]{1,0:T(8,128)(2,1)S(1)} %get-tuple-element.39.refs_0_, bf16[128,256]{1,0:T(8,128)(2,1)S(1)} %collective-permute-done.11.refs_1_), custom_call_target="tpu_custom_call" | custom-call | flops 33554432 | bytes 600000 | tf_op jit(solution)/shard_map/pallas_call | solution.py:26
  (4 shorter events, 0.1 us)
Async XLA Ops:
  0.0 16.5 %copy-start.6 = (bf16[256,512]{1,0:T(8,128)(2,1)S(1)}, bf16[256,512]{1,0:T(8,128)(2,1)}, u32[]{:S(2)}) copy-start(bf16[256,512]{1,0:T(8,128)(2,1)} %constant.8.clone.inner_ref) | copy-start | bytes 786436
  1.8 14.6 %copy-start.5 = (bf16[512,256]{1,0:T(8,128)(2,1)S(1)}, bf16[512,256]{1,0:T(8,128)(2,1)}, u32[]{:S(2)}) copy-start(bf16[512,256]{1,0:T(8,128)(2,1)} %constant.6.clone.first_ref) | copy-start | bytes 786436
  1.8 1.5 %collective-permute-start = (bf16[3,136,128]{2,1,0:T(8,128)(2,1)S(1)}, bf16[3,136,128]{2,1,0:T(8,128)(2,1)S(1)}, u32[]{:S(2)}, u32[]{:S(2)}) collective-permute-start(bf16[3,136,128]{2,1,0:T(8,128)(2,1)S(1)} %get-tuple-element.24), channel_id=1, source_target_pairs={{0,1},{1,0},{2,3},{3,2},{4,5},{5,4},{6,7},{7,6},{8,9},{9,8},{10,11... | collective-permute-start | bytes 313352 | tf_op jit(solution)/shard_map/ppermute | solution.py:344
  3.3 10.4 %collective-permute-start.1 = (bf16[264,128]{1,0:T(8,128)(2,1)S(1)}, bf16[264,128]{1,0:T(8,128)(2,1)S(1)}, u32[]{:S(2)}, u32[]{:S(2)}) collective-permute-start(bf16[264,128]{1,0:T(8,128)(2,1)S(1)} %get-tuple-element.25), channel_id=1, source_target_pairs={{0,12},{1,15},{2,14},{3,13},{4,8},{5,11},{6,10},{7,9},{8,4},{9,7},... | collective-permute-start | bytes 202760 | tf_op jit(solution)/shard_map/ppermute | solution.py:344
  8.3 6.6 %collective-permute-start.2 = (bf16[264,128]{1,0:T(8,128)(2,1)S(1)}, bf16[264,128]{1,0:T(8,128)(2,1)S(1)}, u32[]{:S(2)}, u32[]{:S(2)}) collective-permute-start(bf16[264,128]{1,0:T(8,128)(2,1)S(1)} %get-tuple-element.26), channel_id=1, source_target_pairs={{0,8},{1,11},{2,10},{3,9},{4,12},{5,15},{6,14},{7,13},{8,0},{9,3},... | collective-permute-start | bytes 202760 | tf_op jit(solution)/shard_map/ppermute | solution.py:344
  8.3 6.6 %collective-permute-start.3 = (bf16[264,128]{1,0:T(8,128)(2,1)S(1)}, bf16[264,128]{1,0:T(8,128)(2,1)S(1)}, u32[]{:S(2)}, u32[]{:S(2)}) collective-permute-start(bf16[264,128]{1,0:T(8,128)(2,1)S(1)} %get-tuple-element.27), channel_id=1, source_target_pairs={{0,4},{1,7},{2,6},{3,5},{4,0},{5,3},{6,2},{7,1},{8,12},{9,15},{10,... | collective-permute-start | bytes 202760 | tf_op jit(solution)/shard_map/ppermute | solution.py:344
  9.0 4.7 %collective-permute-start.4 = (bf16[136,128]{1,0:T(8,128)(2,1)S(1)}, bf16[136,128]{1,0:T(8,128)(2,1)S(1)}, u32[]{:S(2)}, u32[]{:S(2)}) collective-permute-start(bf16[136,128]{1,0:T(8,128)(2,1)S(1)} %get-tuple-element.28), channel_id=1, source_target_pairs={{0,2},{1,3},{2,0},{3,1},{4,6},{5,7},{6,4},{7,5},{8,10},{9,11},{10,... | collective-permute-start | bytes 104456 | tf_op jit(solution)/shard_map/ppermute | solution.py:344
  15.0 1.5 %copy-start.7 = (f32[32,256]{1,0:T(8,128)S(1)}, f32[32,256]{1,0:T(8,128)}, u32[]{:S(2)}) copy-start(f32[32,256]{1,0:T(8,128)} %constant.7.clone.twist_ref) | copy-start | bytes 98308
  15.0 1.5 %collective-permute-start.5 = (bf16[544,128]{1,0:T(8,128)(2,1)S(1)}, bf16[544,128]{1,0:T(8,128)(2,1)S(1)}, u32[]{:S(2)}, u32[]{:S(2)}) collective-permute-start(bf16[544,128]{1,0:T(8,128)(2,1)S(1)} %get-tuple-element.31), channel_id=1, source_target_pairs={{0,1},{1,0},{2,3},{3,2},{4,5},{5,4},{6,7},{7,6},{8,9},{9,8},{10,11... | collective-permute-start | bytes 417800 | tf_op jit(solution)/shard_map/ppermute | solution.py:344
  16.5 10.9 %copy-start = (bf16[256,768]{1,0:T(8,128)(2,1)S(1)}, bf16[256,768]{1,0:T(8,128)(2,1)}, u32[]{:S(2)}) copy-start(bf16[256,768]{1,0:T(8,128)(2,1)} %refs_2_.1) | copy-start | bytes 1179652
  17.9 1.5 %collective-permute-start.6 = (bf16[3,32,256]{2,1,0:T(8,128)(2,1)S(1)}, bf16[3,32,256]{2,1,0:T(8,128)(2,1)S(1)}, u32[]{:S(2)}, u32[]{:S(2)}) collective-permute-start(bf16[3,32,256]{2,1,0:T(8,128)(2,1)S(1)} %get-tuple-element.33), channel_id=1, source_target_pairs={{0,1},{1,0},{2,3},{3,2},{4,5},{5,4},{6,7},{7,6},{8,9},{9,8},{10,11... | collective-permute-start | bytes 147464 | tf_op jit(solution)/shard_map/ppermute | solution.py:344
  18.3 5.5 %collective-permute-start.10 = (bf16[80,256]{1,0:T(8,128)(2,1)S(1)}, bf16[80,256]{1,0:T(8,128)(2,1)S(1)}, u32[]{:S(2)}, u32[]{:S(2)}) collective-permute-start(bf16[80,256]{1,0:T(8,128)(2,1)S(1)} %get-tuple-element.37), channel_id=1, source_target_pairs={{0,2},{1,3},{2,0},{3,1},{4,6},{5,7},{6,4},{7,5},{8,10},{9,11},{10,... | collective-permute-start | bytes 122888 | tf_op jit(solution)/shard_map/ppermute | solution.py:344
  19.4 8.0 %copy-start.1 = (bf16[256,256]{1,0:T(8,128)(2,1)S(1)}, bf16[256,256]{1,0:T(8,128)(2,1)}, u32[]{:S(2)}) copy-start(bf16[256,256]{1,0:T(8,128)(2,1)} %refs_0_.1) | copy-start | bytes 393220
  19.4 5.8 %collective-permute-start.7 = (bf16[64,256]{1,0:T(8,128)(2,1)S(1)}, bf16[64,256]{1,0:T(8,128)(2,1)S(1)}, u32[]{:S(2)}, u32[]{:S(2)}) collective-permute-start(bf16[64,256]{1,0:T(8,128)(2,1)S(1)} %get-tuple-element.34), channel_id=1, source_target_pairs={{0,12},{1,15},{2,14},{3,13},{4,8},{5,11},{6,10},{7,9},{8,4},{9,7},... | collective-permute-start | bytes 98312 | tf_op jit(solution)/shard_map/ppermute | solution.py:344
  22.2 5.0 %collective-permute-start.8 = (bf16[64,256]{1,0:T(8,128)(2,1)S(1)}, bf16[64,256]{1,0:T(8,128)(2,1)S(1)}, u32[]{:S(2)}, u32[]{:S(2)}) collective-permute-start(bf16[64,256]{1,0:T(8,128)(2,1)S(1)} %get-tuple-element.35), channel_id=1, source_target_pairs={{0,8},{1,11},{2,10},{3,9},{4,12},{5,15},{6,14},{7,13},{8,0},{9,3},... | collective-permute-start | bytes 98312 | tf_op jit(solution)/shard_map/ppermute | solution.py:344
  22.2 5.0 %collective-permute-start.9 = (bf16[64,256]{1,0:T(8,128)(2,1)S(1)}, bf16[64,256]{1,0:T(8,128)(2,1)S(1)}, u32[]{:S(2)}, u32[]{:S(2)}) collective-permute-start(bf16[64,256]{1,0:T(8,128)(2,1)S(1)} %get-tuple-element.36), channel_id=1, source_target_pairs={{0,4},{1,7},{2,6},{3,5},{4,0},{5,3},{6,2},{7,1},{8,12},{9,15},{10,... | collective-permute-start | bytes 98312 | tf_op jit(solution)/shard_map/ppermute | solution.py:344
  27.2 0.7 %copy-start.3 = (f32[3,768]{1,0:T(4,128)S(1)}, f32[3,768]{1,0:T(4,128)}, u32[]{:S(2)}) copy-start(f32[3,768]{1,0:T(4,128)} %refs_3_.1) | copy-start | bytes 27652
  27.2 0.7 %copy-start.4 = (f32[256]{0:T(256)S(1)}, f32[256]{0:T(256)}, u32[]{:S(2)}) copy-start(f32[256]{0:T(256)} %param.12) | copy-start | bytes 3076
  27.2 1.3 %copy-start.2 = (bf16[256,256]{1,0:T(8,128)(2,1)S(1)}, bf16[256,256]{1,0:T(8,128)(2,1)}, u32[]{:S(2)}) copy-start(bf16[256,256]{1,0:T(8,128)(2,1)} %w_ref.3) | copy-start | bytes 393220
  27.2 1.3 %collective-permute-start.11 = (bf16[128,256]{1,0:T(8,128)(2,1)S(1)}, bf16[128,256]{1,0:T(8,128)(2,1)S(1)}, u32[]{:S(2)}, u32[]{:S(2)}) collective-permute-start(bf16[128,256]{1,0:T(8,128)(2,1)S(1)} %get-tuple-element.40), channel_id=1, source_target_pairs={{0,1},{1,0},{2,3},{3,2},{4,5},{5,4},{6,7},{7,6},{8,9},{9,8},{10,11... | collective-permute-start | bytes 196616 | tf_op jit(solution)/shard_map/ppermute | solution.py:344

commit v18 on v16

--- a/solution.py
+++ b/solution.py
@@ -175,8 +175,8 @@
     copies[0].wait()
     copies[1].wait()
     normed = normed_of(tokens_ref, gain_ref)
-    copies[2].wait()
-    copies[3].wait()
+    for copy in copies[2:]:
+        copy.wait()
     query_cols, cols = slice(0, width), slice(width, 3 * width)
     mixed = short_mix(projected_of(normed, w_ref[:, cols]), short_ref[:, cols])
     key, value = mixed[:, 0:width], mixed[:, width:]
@@ -185,8 +185,6 @@
     some = jnp.concatenate([normed[0 : 2 * edge], normed[rows - 2 * edge :]])
     some = short_mix(projected_of(some, w_ref[:, query_cols]), short_ref[:, query_cols])
     put_rim(packed_ref, rim_ref, [*rims, (some[0:edge], some[4 * edge :])])
-    for copy in copies[4:]:
-        copy.wait()
     med_len = medium_ref.shape[0]
     is_first = jnp.where(lax.axis_index(seq) == 0, 1.0, 0.0)
     head = long_ref[0:med_len, :] + is_first * medium_ref[...]
@@ -297,23 +295,24 @@
     in_rim = lax.broadcasted_iota(jnp.int32, rim_signal.shape, 1) < rim_count
     rim_signal = rim_signal.astype(jnp.bfloat16)
     rim_query = scale * jnp.where(in_rim, rim_query, 1.0)
-    values = jnp.concatenate(
-        [jnp.where(in_rim, rim_signal, values[:, 0:lane]), values[:, lane:]], axis=1
+    signal = jnp.concatenate(
+        [jnp.where(in_rim, rim_signal, values[:, 0:lane]), values[:, lane:rows]], axis=1
     )
     cosine, sine = inner_ref[:, 0:rows], inner_ref[:, rows:]
     inner = jnp.concatenate(
         [jnp.concatenate([cosine, -sine], axis=1), jnp.concatenate([sine, cosine], axis=1)]
     )
-    spread = jnp.dot(first_ref[...], values, preferred_element_type=jnp.float32)
+    spread_of = functools.partial(jnp.dot, first_ref[...], preferred_element_type=jnp.float32)
+    spreads = [spread_of(values[:, rows : 2 * rows]), spread_of(signal)]
     tw_cos, tw_sin = twist_rows(twist_ref, chans)
     turned = []
-    for begin in (0, rows):
-        real, imag = spread[0:half, begin : begin + rows], spread[half:, begin : begin + rows]
+    for spread in spreads:
+        real, imag = spread[0:half], spread[half:]
         turned.append([real * tw_cos + imag * tw_sin, imag * tw_cos - real * tw_sin])
     turned = jnp.concatenate([jnp.concatenate(pair, axis=1).astype(jnp.bfloat16) for pair in turned])
     spectra = jnp.dot(turned, inner, preferred_element_type=jnp.float32)
-    real, imag = spectra[0:half, 0:rows], spectra[0:half, rows:]
-    fil_re, fil_im = spectra[half:, 0:rows], spectra[half:, rows:]
+    fil_re, fil_im = spectra[0:half, 0:rows], spectra[0:half, rows:]
+    real, imag = spectra[half:, 0:rows], spectra[half:, rows:]
     product = [real * fil_im + imag * fil_re, real * fil_re - imag * fil_im]
     product = jnp.concatenate(product, axis=1).astype(jnp.bfloat16)
     back = jnp.dot(product, inner, preferred_element_type=jnp.float32)

time: 29.4 us -> 29.4 us (level)
  no operation moved by 1% of the time
where the time goes in v18:
time: 29.4 us; the launch traced here: 29.3 us
  starting transfers between devices  13.7 us (47%)
  waiting for transfers between devices  10.7 us (36%)
  Pallas kernels  4.46 us (15%)
  local copies, waits for them, and re-layouts  0.35 us (1%)
    ppermute x12, starting transfers between devices, permute(): lax.ppermute(array, seq, [(i, partner(i)) for i in range(lax.axis_size(se...  13.7 us
    ppermute x12, waiting for transfers between devices, permute(): lax.ppermute(array, seq, [(i, partner(i)) for i in range(lax.axis_size(se...  10.7 us
    pallas_call x8, Pallas kernels, call(): pl.pallas_call(body, out_shape=outs, in_specs=[whole(space) for space in...  4.46 us
  transfers between devices with their start and end apart: 12, of which 7 were waited for; matrix products, arithmetic and copies ran while one was open for 0% of the time, Pallas kernels for 1%

profile of v18, /device:TPU:0, one launch (start us, length us, event | category | flops | bytes accessed | tf_op | source)
XLA Modules:
  0.0 29.3 jit_solution(3237830982362669494)
XLA Ops:
  0.0 0.0 copy-start.7
  0.0 1.8 %shard_map.110 = (bf16[3,136,128]{2,1,0:T(8,128)(2,1)S(1)}, bf16[3,136,128]{2,1,0:T(8,128)(2,1)S(1)}, bf16[280,128]{1,0:T(8,128)(2,1)S(1)}, bf16[136,128]{1,0:T(8,128)(2,1)S(1)}) custom-call(bf16[256,256]{1,0:T(8,128)(2,1)} %refs_0_.1, f32[1,256]{1,0:T(1,128)} %bitcast.2, bf16[256,768]{1,0:T(8,128)(2,1)} %refs_2_.1, f32[3,768]{1,0:T(4,128)} %refs_3_.1, ...), custom_call_target="tpu_custom_call" | custom-call | flops 100663296 | bytes 1500000 | tf_op jit(solution)/shard_map/pallas_call | solution.py:26
  1.8 0.5 %collective-permute-start = (bf16[3,136,128]{2,1,0:T(8,128)(2,1)S(1)}, bf16[3,136,128]{2,1,0:T(8,128)(2,1)S(1)}, u32[]{:S(2)}, u32[]{:S(2)}) collective-permute-start(bf16[3,136,128]{2,1,0:T(8,128)(2,1)S(1)} %get-tuple-element.24), channel_id=1, source_target_pairs={{0,1},{1,0},{2,3},{3,2},{4,5},{5,4},{6,7},{7,6},{8,9},{9,8},{10,11... | collective-permute-start | bytes 313352 | tf_op jit(solution)/shard_map/ppermute | solution.py:343
  2.4 2.6 %collective-permute-start.4 = (bf16[280,128]{1,0:T(8,128)(2,1)S(1)}, bf16[280,128]{1,0:T(8,128)(2,1)S(1)}, u32[]{:S(2)}, u32[]{:S(2)}) collective-permute-start(bf16[280,128]{1,0:T(8,128)(2,1)S(1)} %get-tuple-element.28), channel_id=1, source_target_pairs={{0,2},{1,3},{2,0},{3,1},{4,6},{5,7},{6,4},{7,5},{8,10},{9,11},{10,... | collective-permute-start | bytes 215048 | tf_op jit(solution)/shard_map/ppermute | solution.py:343
  5.0 0.0 collective-permute-done.got_ref
  5.0 0.0 copy-start.5
  5.0 0.0 copy-start.6
  5.0 3.7 %collective-permute-start.1 = (bf16[264,128]{1,0:T(8,128)(2,1)S(1)}, bf16[264,128]{1,0:T(8,128)(2,1)S(1)}, u32[]{:S(2)}, u32[]{:S(2)}) collective-permute-start(bf16[264,128]{1,0:T(8,128)(2,1)S(1)} %get-tuple-element.25), channel_id=1, source_target_pairs={{0,12},{1,15},{2,14},{3,13},{4,8},{5,11},{6,10},{7,9},{8,4},{9,7},... | collective-permute-start | bytes 202760 | tf_op jit(solution)/shard_map/ppermute | solution.py:343
  8.6 0.0 collective-permute-start.2
  8.6 0.8 %collective-permute-start.3 = (bf16[264,128]{1,0:T(8,128)(2,1)S(1)}, bf16[264,128]{1,0:T(8,128)(2,1)S(1)}, u32[]{:S(2)}, u32[]{:S(2)}) collective-permute-start(bf16[264,128]{1,0:T(8,128)(2,1)S(1)} %get-tuple-element.27), channel_id=1, source_target_pairs={{0,4},{1,7},{2,6},{3,5},{4,0},{5,3},{6,2},{7,1},{8,12},{9,15},{10,... | collective-permute-start | bytes 202760 | tf_op jit(solution)/shard_map/ppermute | solution.py:343
  9.4 0.0 collective-permute-done.4.refs_3_
  9.4 2.4 %collective-permute-done.1.refs_0_ = bf16[264,128]{1,0:T(8,128)(2,1)S(1)} collective-permute-done((bf16[264,128]{1,0:T(8,128)(2,1)S(1)}, bf16[264,128]{1,0:T(8,128)(2,1)S(1)}, u32[]{:S(2)}, u32[]{:S(2)}) %collective-permute-start.1) | collective-permute-done | bytes 67616 | tf_op jit(solution)/shard_map/ppermute | solution.py:343
  11.8 3.5 %collective-permute-done.2.refs_1_ = bf16[264,128]{1,0:T(8,128)(2,1)S(1)} collective-permute-done((bf16[264,128]{1,0:T(8,128)(2,1)S(1)}, bf16[264,128]{1,0:T(8,128)(2,1)S(1)}, u32[]{:S(2)}, u32[]{:S(2)}) %collective-permute-start.2) | collective-permute-done | bytes 67616 | tf_op jit(solution)/shard_map/ppermute | solution.py:343
  15.3 0.0 collective-permute-done.3.refs_2_
  15.3 0.2 collective-permute-start.5
  15.5 1.2 %collective-permute-done.5.refs_1_ = bf16[544,128]{1,0:T(8,128)(2,1)S(1)} collective-permute-done((bf16[544,128]{1,0:T(8,128)(2,1)S(1)}, bf16[544,128]{1,0:T(8,128)(2,1)S(1)}, u32[]{:S(2)}, u32[]{:S(2)}) %collective-permute-start.5) | collective-permute-done | bytes 139296 | tf_op jit(solution)/shard_map/ppermute | solution.py:343
  16.7 0.0 copy-done.7
  16.7 0.0 copy-done.5
  16.7 0.0 copy-done.6
  16.7 0.0 copy-start
  16.7 1.3 %shard_map.113 = (bf16[3,32,256]{2,1,0:T(8,128)(2,1)S(1)}, bf16[3,32,256]{2,1,0:T(8,128)(2,1)S(1)}, bf16[80,256]{1,0:T(8,128)(2,1)S(1)}, bf16[32,256]{1,0:T(8,128)(2,1)S(1)}) custom-call(bf16[512,256]{1,0:T(8,128)(2,1)S(1)} %copy-done.5, f32[32,256]{1,0:T(8,128)S(1)} %copy-done.7, bf16[256,512]{1,0:T(8,128)(2,1)S(1)} %copy-done.6, ...), custom_call_target="tpu_custom_call" | custom-call | flops 603979776 | bytes 2000000 | tf_op jit(solution)/shard_map/pallas_call | solution.py:26
  18.1 0.2 collective-permute-start.6
  18.3 1.0 %collective-permute-start.10 = (bf16[80,256]{1,0:T(8,128)(2,1)S(1)}, bf16[80,256]{1,0:T(8,128)(2,1)S(1)}, u32[]{:S(2)}, u32[]{:S(2)}) collective-permute-start(bf16[80,256]{1,0:T(8,128)(2,1)S(1)} %get-tuple-element.37), channel_id=1, source_target_pairs={{0,2},{1,3},{2,0},{3,1},{4,6},{5,7},{6,4},{7,5},{8,10},{9,11},{10,... | collective-permute-start | bytes 122888 | tf_op jit(solution)/shard_map/ppermute | solution.py:343
  19.3 0.1 collective-permute-done.6.got_ref
  19.4 0.0 copy-start.1
  19.4 2.5 %collective-permute-start.7 = (bf16[64,256]{1,0:T(8,128)(2,1)S(1)}, bf16[64,256]{1,0:T(8,128)(2,1)S(1)}, u32[]{:S(2)}, u32[]{:S(2)}) collective-permute-start(bf16[64,256]{1,0:T(8,128)(2,1)S(1)} %get-tuple-element.34), channel_id=1, source_target_pairs={{0,12},{1,15},{2,14},{3,13},{4,8},{5,11},{6,10},{7,9},{8,4},{9,7},... | collective-permute-start | bytes 98312 | tf_op jit(solution)/shard_map/ppermute | solution.py:343
  21.9 0.2 collective-permute-start.8
  22.1 1.7 %collective-permute-start.9 = (bf16[64,256]{1,0:T(8,128)(2,1)S(1)}, bf16[64,256]{1,0:T(8,128)(2,1)S(1)}, u32[]{:S(2)}, u32[]{:S(2)}) collective-permute-start(bf16[64,256]{1,0:T(8,128)(2,1)S(1)} %get-tuple-element.36), channel_id=1, source_target_pairs={{0,4},{1,7},{2,6},{3,5},{4,0},{5,3},{6,2},{7,1},{8,12},{9,15},{10,... | collective-permute-start | bytes 98312 | tf_op jit(solution)/shard_map/ppermute | solution.py:343
  23.9 0.0 collective-permute-done.10.refs_3_
  23.9 1.6 %collective-permute-done.7.refs_0_ = bf16[64,256]{1,0:T(8,128)(2,1)S(1)} collective-permute-done((bf16[64,256]{1,0:T(8,128)(2,1)S(1)}, bf16[64,256]{1,0:T(8,128)(2,1)S(1)}, u32[]{:S(2)}, u32[]{:S(2)}) %collective-permute-start.7) | collective-permute-done | bytes 32800 | tf_op jit(solution)/shard_map/ppermute | solution.py:343
  25.4 1.6 %collective-permute-done.8.refs_1_ = bf16[64,256]{1,0:T(8,128)(2,1)S(1)} collective-permute-done((bf16[64,256]{1,0:T(8,128)(2,1)S(1)}, bf16[64,256]{1,0:T(8,128)(2,1)S(1)}, u32[]{:S(2)}, u32[]{:S(2)}) %collective-permute-start.8) | collective-permute-done | bytes 32800 | tf_op jit(solution)/shard_map/ppermute | solution.py:343
  27.0 0.0 collective-permute-done.9.refs_2_
  27.0 0.0 copy-start.3
  27.0 0.0 copy-start.4
  27.0 0.0 copy-start.2
  27.0 0.3 %collective-permute-start.11 = (bf16[128,256]{1,0:T(8,128)(2,1)S(1)}, bf16[128,256]{1,0:T(8,128)(2,1)S(1)}, u32[]{:S(2)}, u32[]{:S(2)}) collective-permute-start(bf16[128,256]{1,0:T(8,128)(2,1)S(1)} %get-tuple-element.40), channel_id=1, source_target_pairs={{0,1},{1,0},{2,3},{3,2},{4,5},{5,4},{6,7},{7,6},{8,9},{9,8},{10,11... | collective-permute-start | bytes 196616 | tf_op jit(solution)/shard_map/ppermute | solution.py:343
  27.4 0.0 copy-done
  27.4 0.0 copy-done.1
  27.4 0.3 %copy-done.3 = f32[3,768]{1,0:T(4,128)S(1)} copy-done((f32[3,768]{1,0:T(4,128)S(1)}, f32[3,768]{1,0:T(4,128)}, u32[]{:S(2)}) %copy-start.3) | copy-done | bytes 9240
  27.7 0.0 copy-done.4
  27.7 0.3 %shard_map.109.query_ref = f32[256,256]{1,0:T(8,128)S(1)} custom-call(bf16[256,256]{1,0:T(8,128)(2,1)S(1)} %copy-done.1, f32[1,256]{1,0:T(1,128)S(1)} %bitcast.3, bf16[256,768]{1,0:T(8,128)(2,1)S(1)} %copy-done, f32[3,768]{1,0:T(4,128)S(1)} %copy-done.3), custom_call_target="tpu_custom_call" | custom-call | flops 33554432 | bytes 800000 | tf_op jit(solution)/shard_map/pallas_call | solution.py:26
  28.0 0.3 %collective-permute-done.11.refs_1_ = bf16[128,256]{1,0:T(8,128)(2,1)S(1)} collective-permute-done((bf16[128,256]{1,0:T(8,128)(2,1)S(1)}, bf16[128,256]{1,0:T(8,128)(2,1)S(1)}, u32[]{:S(2)}, u32[]{:S(2)}) %collective-permute-start.11) | collective-permute-done | bytes 65568 | tf_op jit(solution)/shard_map/ppermute | solution.py:343
  28.4 0.0 copy-done.2
  28.4 0.9 %shard_map.116 = bf16[256,256]{1,0:T(8,128)(2,1)} custom-call(f32[256,256]{1,0:T(8,128)S(1)} %shard_map.109.query_ref, bf16[256,256]{1,0:T(8,128)(2,1)S(1)} %copy-done.2, bf16[128,256]{1,0:T(8,128)(2,1)S(1)} %get-tuple-element.39.refs_0_, bf16[128,256]{1,0:T(8,128)(2,1)S(1)} %collective-permute-done.11.refs_1_), custom_call_target="tpu_custom_call" | custom-call | flops 33554432 | bytes 600000 | tf_op jit(solution)/shard_map/pallas_call | solution.py:26
  (4 shorter events, 0.1 us)
Async XLA Ops:
  0.0 16.7 %copy-start.7 = (f32[32,256]{1,0:T(8,128)S(1)}, f32[32,256]{1,0:T(8,128)}, u32[]{:S(2)}) copy-start(f32[32,256]{1,0:T(8,128)} %constant.7.clone.twist_ref) | copy-start | bytes 98308
  1.8 3.1 %collective-permute-start = (bf16[3,136,128]{2,1,0:T(8,128)(2,1)S(1)}, bf16[3,136,128]{2,1,0:T(8,128)(2,1)S(1)}, u32[]{:S(2)}, u32[]{:S(2)}) collective-permute-start(bf16[3,136,128]{2,1,0:T(8,128)(2,1)S(1)} %get-tuple-element.24), channel_id=1, source_target_pairs={{0,1},{1,0},{2,3},{3,2},{4,5},{5,4},{6,7},{7,6},{8,9},{9,8},{10,11... | collective-permute-start | bytes 313352 | tf_op jit(solution)/shard_map/ppermute | solution.py:343
  2.4 7.1 %collective-permute-start.4 = (bf16[280,128]{1,0:T(8,128)(2,1)S(1)}, bf16[280,128]{1,0:T(8,128)(2,1)S(1)}, u32[]{:S(2)}, u32[]{:S(2)}) collective-permute-start(bf16[280,128]{1,0:T(8,128)(2,1)S(1)} %get-tuple-element.28), channel_id=1, source_target_pairs={{0,2},{1,3},{2,0},{3,1},{4,6},{5,7},{6,4},{7,5},{8,10},{9,11},{10,... | collective-permute-start | bytes 215048 | tf_op jit(solution)/shard_map/ppermute | solution.py:343
  5.0 11.8 %copy-start.5 = (bf16[512,256]{1,0:T(8,128)(2,1)S(1)}, bf16[512,256]{1,0:T(8,128)(2,1)}, u32[]{:S(2)}) copy-start(bf16[512,256]{1,0:T(8,128)(2,1)} %constant.6.clone.first_ref) | copy-start | bytes 786436
  5.0 11.8 %copy-start.6 = (bf16[256,512]{1,0:T(8,128)(2,1)S(1)}, bf16[256,512]{1,0:T(8,128)(2,1)}, u32[]{:S(2)}) copy-start(bf16[256,512]{1,0:T(8,128)(2,1)} %constant.8.clone.inner_ref) | copy-start | bytes 786436
  5.0 6.8 %collective-permute-start.1 = (bf16[264,128]{1,0:T(8,128)(2,1)S(1)}, bf16[264,128]{1,0:T(8,128)(2,1)S(1)}, u32[]{:S(2)}, u32[]{:S(2)}) collective-permute-start(bf16[264,128]{1,0:T(8,128)(2,1)S(1)} %get-tuple-element.25), channel_id=1, source_target_pairs={{0,12},{1,15},{2,14},{3,13},{4,8},{5,11},{6,10},{7,9},{8,4},{9,7},... | collective-permute-start | bytes 202760 | tf_op jit(solution)/shard_map/ppermute | solution.py:343
  8.6 6.6 %collective-permute-start.2 = (bf16[264,128]{1,0:T(8,128)(2,1)S(1)}, bf16[264,128]{1,0:T(8,128)(2,1)S(1)}, u32[]{:S(2)}, u32[]{:S(2)}) collective-permute-start(bf16[264,128]{1,0:T(8,128)(2,1)S(1)} %get-tuple-element.26), channel_id=1, source_target_pairs={{0,8},{1,11},{2,10},{3,9},{4,12},{5,15},{6,14},{7,13},{8,0},{9,3},... | collective-permute-start | bytes 202760 | tf_op jit(solution)/shard_map/ppermute | solution.py:343
  8.6 6.6 %collective-permute-start.3 = (bf16[264,128]{1,0:T(8,128)(2,1)S(1)}, bf16[264,128]{1,0:T(8,128)(2,1)S(1)}, u32[]{:S(2)}, u32[]{:S(2)}) collective-permute-start(bf16[264,128]{1,0:T(8,128)(2,1)S(1)} %get-tuple-element.27), channel_id=1, source_target_pairs={{0,4},{1,7},{2,6},{3,5},{4,0},{5,3},{6,2},{7,1},{8,12},{9,15},{10,... | collective-permute-start | bytes 202760 | tf_op jit(solution)/shard_map/ppermute | solution.py:343
  15.3 1.4 %collective-permute-start.5 = (bf16[544,128]{1,0:T(8,128)(2,1)S(1)}, bf16[544,128]{1,0:T(8,128)(2,1)S(1)}, u32[]{:S(2)}, u32[]{:S(2)}) collective-permute-start(bf16[544,128]{1,0:T(8,128)(2,1)S(1)} %get-tuple-element.31), channel_id=1, source_target_pairs={{0,1},{1,0},{2,3},{3,2},{4,5},{5,4},{6,7},{7,6},{8,9},{9,8},{10,11... | collective-permute-start | bytes 417800 | tf_op jit(solution)/shard_map/ppermute | solution.py:343
  16.7 10.7 %copy-start = (bf16[256,768]{1,0:T(8,128)(2,1)S(1)}, bf16[256,768]{1,0:T(8,128)(2,1)}, u32[]{:S(2)}) copy-start(bf16[256,768]{1,0:T(8,128)(2,1)} %refs_2_.1) | copy-start | bytes 1179652
  18.1 1.3 %collective-permute-start.6 = (bf16[3,32,256]{2,1,0:T(8,128)(2,1)S(1)}, bf16[3,32,256]{2,1,0:T(8,128)(2,1)S(1)}, u32[]{:S(2)}, u32[]{:S(2)}) collective-permute-start(bf16[3,32,256]{2,1,0:T(8,128)(2,1)S(1)} %get-tuple-element.33), channel_id=1, source_target_pairs={{0,1},{1,0},{2,3},{3,2},{4,5},{5,4},{6,7},{7,6},{8,9},{9,8},{10,11... | collective-permute-start | bytes 147464 | tf_op jit(solution)/shard_map/ppermute | solution.py:343
  18.3 5.6 %collective-permute-start.10 = (bf16[80,256]{1,0:T(8,128)(2,1)S(1)}, bf16[80,256]{1,0:T(8,128)(2,1)S(1)}, u32[]{:S(2)}, u32[]{:S(2)}) collective-permute-start(bf16[80,256]{1,0:T(8,128)(2,1)S(1)} %get-tuple-element.37), channel_id=1, source_target_pairs={{0,2},{1,3},{2,0},{3,1},{4,6},{5,7},{6,4},{7,5},{8,10},{9,11},{10,... | collective-permute-start | bytes 122888 | tf_op jit(solution)/shard_map/ppermute | solution.py:343
  19.4 8.0 %copy-start.1 = (bf16[256,256]{1,0:T(8,128)(2,1)S(1)}, bf16[256,256]{1,0:T(8,128)(2,1)}, u32[]{:S(2)}) copy-start(bf16[256,256]{1,0:T(8,128)(2,1)} %refs_0_.1) | copy-start | bytes 393220
  19.4 6.0 %collective-permute-start.7 = (bf16[64,256]{1,0:T(8,128)(2,1)S(1)}, bf16[64,256]{1,0:T(8,128)(2,1)S(1)}, u32[]{:S(2)}, u32[]{:S(2)}) collective-permute-start(bf16[64,256]{1,0:T(8,128)(2,1)S(1)} %get-tuple-element.34), channel_id=1, source_target_pairs={{0,12},{1,15},{2,14},{3,13},{4,8},{5,11},{6,10},{7,9},{8,4},{9,7},... | collective-permute-start | bytes 98312 | tf_op jit(solution)/shard_map/ppermute | solution.py:343
  21.9 5.1 %collective-permute-start.8 = (bf16[64,256]{1,0:T(8,128)(2,1)S(1)}, bf16[64,256]{1,0:T(8,128)(2,1)S(1)}, u32[]{:S(2)}, u32[]{:S(2)}) collective-permute-start(bf16[64,256]{1,0:T(8,128)(2,1)S(1)} %get-tuple-element.35), channel_id=1, source_target_pairs={{0,8},{1,11},{2,10},{3,9},{4,12},{5,15},{6,14},{7,13},{8,0},{9,3},... | collective-permute-start | bytes 98312 | tf_op jit(solution)/shard_map/ppermute | solution.py:343
  22.1 4.9 %collective-permute-start.9 = (bf16[64,256]{1,0:T(8,128)(2,1)S(1)}, bf16[64,256]{1,0:T(8,128)(2,1)S(1)}, u32[]{:S(2)}, u32[]{:S(2)}) collective-permute-start(bf16[64,256]{1,0:T(8,128)(2,1)S(1)} %get-tuple-element.36), channel_id=1, source_target_pairs={{0,4},{1,7},{2,6},{3,5},{4,0},{5,3},{6,2},{7,1},{8,12},{9,15},{10,... | collective-permute-start | bytes 98312 | tf_op jit(solution)/shard_map/ppermute | solution.py:343
  27.0 0.7 %copy-start.3 = (f32[3,768]{1,0:T(4,128)S(1)}, f32[3,768]{1,0:T(4,128)}, u32[]{:S(2)}) copy-start(f32[3,768]{1,0:T(4,128)} %refs_3_.1) | copy-start | bytes 27652
  27.0 0.7 %copy-start.4 = (f32[256]{0:T(256)S(1)}, f32[256]{0:T(256)}, u32[]{:S(2)}) copy-start(f32[256]{0:T(256)} %param.12) | copy-start | bytes 3076
  27.0 1.3 %copy-start.2 = (bf16[256,256]{1,0:T(8,128)(2,1)S(1)}, bf16[256,256]{1,0:T(8,128)(2,1)}, u32[]{:S(2)}) copy-start(bf16[256,256]{1,0:T(8,128)(2,1)} %w_ref.3) | copy-start | bytes 393220
  27.0 1.3 %collective-permute-start.11 = (bf16[128,256]{1,0:T(8,128)(2,1)S(1)}, bf16[128,256]{1,0:T(8,128)(2,1)S(1)}, u32[]{:S(2)}, u32[]{:S(2)}) collective-permute-start(bf16[128,256]{1,0:T(8,128)(2,1)S(1)} %get-tuple-element.40), channel_id=1, source_target_pairs={{0,1},{1,0},{2,3},{3,2},{4,5},{5,4},{6,7},{7,6},{8,9},{9,8},{10,11... | collective-permute-start | bytes 196616 | tf_op jit(solution)/shard_map/ppermute | solution.py:343

commit v19 on v18

--- a/solution.py
+++ b/solution.py
@@ -15,6 +15,7 @@
 seq = ("chip", "core")
 rim_step = 2 * edge
 chan_tile = 16
+copy_parts = 4
 vmem_bytes = 32 * 2**20
 
 
@@ -169,14 +170,28 @@
     outs, (packed_ref, rim_ref) = (outs[:-2], outs[-2:]) if staged else (outs, (outs[0], None))
     tokens_ref, gain_ref, w_ref, short_ref, long_ref, medium_ref, skip_ref = held
     rows, width = tokens_ref.shape
-    copies = [pltpu.make_async_copy(h, v, sems.at[i]) for i, (h, v) in enumerate(zip(hbm, held))]
-    for copy in copies:
+    copies = []
+    for index, (source, target) in enumerate(zip(hbm, held)):
+        parts = copy_parts if source.shape[0] % (16 * copy_parts) == 0 else 1
+        step = source.shape[0] // parts
+        places = [slice(part * step, (part + 1) * step) for part in range(parts)]
+        copies.append(
+            [
+                pltpu.make_async_copy(source.at[place], target.at[place], sems.at[index, part])
+                for part, place in enumerate(places)
+            ]
+        )
+    for copy in sum(copies, []):
         copy.start()
-    copies[0].wait()
-    copies[1].wait()
+
+    def wait_for(*operands):
+        for operand in operands:
+            for copy in copies[operand]:
+                copy.wait()
+
+    wait_for(0, 1)
     normed = normed_of(tokens_ref, gain_ref)
-    for copy in copies[2:]:
-        copy.wait()
+    wait_for(2, 3)
     query_cols, cols = slice(0, width), slice(width, 3 * width)
     mixed = short_mix(projected_of(normed, w_ref[:, cols]), short_ref[:, cols])
     key, value = mixed[:, 0:width], mixed[:, width:]
@@ -185,6 +200,7 @@
     some = jnp.concatenate([normed[0 : 2 * edge], normed[rows - 2 * edge :]])
     some = short_mix(projected_of(some, w_ref[:, query_cols]), short_ref[:, query_cols])
     put_rim(packed_ref, rim_ref, [*rims, (some[0:edge], some[4 * edge :])])
+    wait_for(4, 5, 6)
     med_len = medium_ref.shape[0]
     is_first = jnp.where(lax.axis_index(seq) == 0, 1.0, 0.0)
     head = long_ref[0:med_len, :] + is_first * medium_ref[...]
@@ -419,7 +435,7 @@
         [pltpu.HBM] * len(args),
         scratch(packed, ((chips, edge, lane), jnp.bfloat16))
         + [pltpu.VMEM(arg.shape, arg.dtype) for arg in args]
-        + [pltpu.SemaphoreType.DMA((len(args),))],
+        + [pltpu.SemaphoreType.DMA((len(args), copy_parts))],
         flops=2 * rows * width * 3 * width,
         moved=1_500_000,
     )

time: 29.4 us -> 29.6 us (level)
  no operation moved by 1% of the time
where the time goes in v19:
time: 29.6 us; the launch traced here: 29.5 us
  starting transfers between devices  13.7 us (46%)
  waiting for transfers between devices  10.7 us (36%)
  Pallas kernels  4.65 us (16%)
  local copies, waits for them, and re-layouts  0.36 us (1%)
    ppermute x12, starting transfers between devices, permute(): lax.ppermute(array, seq, [(i, partner(i)) for i in range(lax.axis_size(se...  13.7 us
    ppermute x12, waiting for transfers between devices, permute(): lax.ppermute(array, seq, [(i, partner(i)) for i in range(lax.axis_size(se...  10.7 us
    pallas_call x8, Pallas kernels, call(): pl.pallas_call(body, out_shape=outs, in_specs=[whole(space) for space in...  4.65 us
  transfers between devices with their start and end apart: 12, of which 7 were waited for; matrix products, arithmetic and copies ran while one was open for 0% of the time, Pallas kernels for 1%

profile of v19, /device:TPU:0, one launch (start us, length us, event | category | flops | bytes accessed | tf_op | source)
XLA Modules:
  0.0 29.5 jit_solution(14190992638989008369)
XLA Ops:
  0.0 0.0 copy-start.7
  0.0 2.0 %shard_map.110 = (bf16[3,136,128]{2,1,0:T(8,128)(2,1)S(1)}, bf16[3,136,128]{2,1,0:T(8,128)(2,1)S(1)}, bf16[280,128]{1,0:T(8,128)(2,1)S(1)}, bf16[136,128]{1,0:T(8,128)(2,1)S(1)}) custom-call(bf16[256,256]{1,0:T(8,128)(2,1)} %refs_0_.1, f32[1,256]{1,0:T(1,128)} %bitcast.2, bf16[256,768]{1,0:T(8,128)(2,1)} %refs_2_.1, f32[3,768]{1,0:T(4,128)} %refs_3_.1, ...), custom_call_target="tpu_custom_call" | custom-call | flops 100663296 | bytes 1500000 | tf_op jit(solution)/shard_map/pallas_call | solution.py:27
  2.0 0.5 %collective-permute-start = (bf16[3,136,128]{2,1,0:T(8,128)(2,1)S(1)}, bf16[3,136,128]{2,1,0:T(8,128)(2,1)S(1)}, u32[]{:S(2)}, u32[]{:S(2)}) collective-permute-start(bf16[3,136,128]{2,1,0:T(8,128)(2,1)S(1)} %get-tuple-element.24), channel_id=1, source_target_pairs={{0,1},{1,0},{2,3},{3,2},{4,5},{5,4},{6,7},{7,6},{8,9},{9,8},{10,11... | collective-permute-start | bytes 313352 | tf_op jit(solution)/shard_map/ppermute | solution.py:359
  2.6 2.6 %collective-permute-start.4 = (bf16[280,128]{1,0:T(8,128)(2,1)S(1)}, bf16[280,128]{1,0:T(8,128)(2,1)S(1)}, u32[]{:S(2)}, u32[]{:S(2)}) collective-permute-start(bf16[280,128]{1,0:T(8,128)(2,1)S(1)} %get-tuple-element.28), channel_id=1, source_target_pairs={{0,2},{1,3},{2,0},{3,1},{4,6},{5,7},{6,4},{7,5},{8,10},{9,11},{10,... | collective-permute-start | bytes 215048 | tf_op jit(solution)/shard_map/ppermute | solution.py:359
  5.1 0.0 collective-permute-done.got_ref
  5.1 0.0 copy-start.5
  5.2 0.0 copy-start.6
  5.2 3.7 %collective-permute-start.1 = (bf16[264,128]{1,0:T(8,128)(2,1)S(1)}, bf16[264,128]{1,0:T(8,128)(2,1)S(1)}, u32[]{:S(2)}, u32[]{:S(2)}) collective-permute-start(bf16[264,128]{1,0:T(8,128)(2,1)S(1)} %get-tuple-element.25), channel_id=1, source_target_pairs={{0,12},{1,15},{2,14},{3,13},{4,8},{5,11},{6,10},{7,9},{8,4},{9,7},... | collective-permute-start | bytes 202760 | tf_op jit(solution)/shard_map/ppermute | solution.py:359
  8.8 0.0 collective-permute-start.2
  8.8 0.8 %collective-permute-start.3 = (bf16[264,128]{1,0:T(8,128)(2,1)S(1)}, bf16[264,128]{1,0:T(8,128)(2,1)S(1)}, u32[]{:S(2)}, u32[]{:S(2)}) collective-permute-start(bf16[264,128]{1,0:T(8,128)(2,1)S(1)} %get-tuple-element.27), channel_id=1, source_target_pairs={{0,4},{1,7},{2,6},{3,5},{4,0},{5,3},{6,2},{7,1},{8,12},{9,15},{10,... | collective-permute-start | bytes 202760 | tf_op jit(solution)/shard_map/ppermute | solution.py:359
  9.6 0.0 collective-permute-done.4.refs_3_
  9.6 2.4 %collective-permute-done.1.refs_0_ = bf16[264,128]{1,0:T(8,128)(2,1)S(1)} collective-permute-done((bf16[264,128]{1,0:T(8,128)(2,1)S(1)}, bf16[264,128]{1,0:T(8,128)(2,1)S(1)}, u32[]{:S(2)}, u32[]{:S(2)}) %collective-permute-start.1) | collective-permute-done | bytes 67616 | tf_op jit(solution)/shard_map/ppermute | solution.py:359
  12.0 3.5 %collective-permute-done.2.refs_1_ = bf16[264,128]{1,0:T(8,128)(2,1)S(1)} collective-permute-done((bf16[264,128]{1,0:T(8,128)(2,1)S(1)}, bf16[264,128]{1,0:T(8,128)(2,1)S(1)}, u32[]{:S(2)}, u32[]{:S(2)}) %collective-permute-start.2) | collective-permute-done | bytes 67616 | tf_op jit(solution)/shard_map/ppermute | solution.py:359
  15.5 0.0 collective-permute-done.3.refs_2_
  15.5 0.2 collective-permute-start.5
  15.7 1.2 %collective-permute-done.5.refs_1_ = bf16[544,128]{1,0:T(8,128)(2,1)S(1)} collective-permute-done((bf16[544,128]{1,0:T(8,128)(2,1)S(1)}, bf16[544,128]{1,0:T(8,128)(2,1)S(1)}, u32[]{:S(2)}, u32[]{:S(2)}) %collective-permute-start.5) | collective-permute-done | bytes 139296 | tf_op jit(solution)/shard_map/ppermute | solution.py:359
  16.9 0.0 copy-done.7
  16.9 0.0 copy-done.5
  16.9 0.0 copy-done.6
  16.9 0.0 copy-start
  16.9 1.3 %shard_map.113 = (bf16[3,32,256]{2,1,0:T(8,128)(2,1)S(1)}, bf16[3,32,256]{2,1,0:T(8,128)(2,1)S(1)}, bf16[80,256]{1,0:T(8,128)(2,1)S(1)}, bf16[32,256]{1,0:T(8,128)(2,1)S(1)}) custom-call(bf16[512,256]{1,0:T(8,128)(2,1)S(1)} %copy-done.5, f32[32,256]{1,0:T(8,128)S(1)} %copy-done.7, bf16[256,512]{1,0:T(8,128)(2,1)S(1)} %copy-done.6, ...), custom_call_target="tpu_custom_call" | custom-call | flops 603979776 | bytes 2000000 | tf_op jit(solution)/shard_map/pallas_call | solution.py:27
  18.3 0.2 collective-permute-start.6
  18.5 1.0 %collective-permute-start.10 = (bf16[80,256]{1,0:T(8,128)(2,1)S(1)}, bf16[80,256]{1,0:T(8,128)(2,1)S(1)}, u32[]{:S(2)}, u32[]{:S(2)}) collective-permute-start(bf16[80,256]{1,0:T(8,128)(2,1)S(1)} %get-tuple-element.37), channel_id=1, source_target_pairs={{0,2},{1,3},{2,0},{3,1},{4,6},{5,7},{6,4},{7,5},{8,10},{9,11},{10,... | collective-permute-start | bytes 122888 | tf_op jit(solution)/shard_map/ppermute | solution.py:359
  19.5 0.1 collective-permute-done.6.got_ref
  19.6 0.0 copy-start.1
  19.6 2.5 %collective-permute-start.7 = (bf16[64,256]{1,0:T(8,128)(2,1)S(1)}, bf16[64,256]{1,0:T(8,128)(2,1)S(1)}, u32[]{:S(2)}, u32[]{:S(2)}) collective-permute-start(bf16[64,256]{1,0:T(8,128)(2,1)S(1)} %get-tuple-element.34), channel_id=1, source_target_pairs={{0,12},{1,15},{2,14},{3,13},{4,8},{5,11},{6,10},{7,9},{8,4},{9,7},... | collective-permute-start | bytes 98312 | tf_op jit(solution)/shard_map/ppermute | solution.py:359
  22.1 0.2 collective-permute-start.8
  22.3 1.7 %collective-permute-start.9 = (bf16[64,256]{1,0:T(8,128)(2,1)S(1)}, bf16[64,256]{1,0:T(8,128)(2,1)S(1)}, u32[]{:S(2)}, u32[]{:S(2)}) collective-permute-start(bf16[64,256]{1,0:T(8,128)(2,1)S(1)} %get-tuple-element.36), channel_id=1, source_target_pairs={{0,4},{1,7},{2,6},{3,5},{4,0},{5,3},{6,2},{7,1},{8,12},{9,15},{10,... | collective-permute-start | bytes 98312 | tf_op jit(solution)/shard_map/ppermute | solution.py:359
  24.0 0.0 collective-permute-done.10.refs_3_
  24.0 1.6 %collective-permute-done.7.refs_0_ = bf16[64,256]{1,0:T(8,128)(2,1)S(1)} collective-permute-done((bf16[64,256]{1,0:T(8,128)(2,1)S(1)}, bf16[64,256]{1,0:T(8,128)(2,1)S(1)}, u32[]{:S(2)}, u32[]{:S(2)}) %collective-permute-start.7) | collective-permute-done | bytes 32800 | tf_op jit(solution)/shard_map/ppermute | solution.py:359
  25.6 1.6 %collective-permute-done.8.refs_1_ = bf16[64,256]{1,0:T(8,128)(2,1)S(1)} collective-permute-done((bf16[64,256]{1,0:T(8,128)(2,1)S(1)}, bf16[64,256]{1,0:T(8,128)(2,1)S(1)}, u32[]{:S(2)}, u32[]{:S(2)}) %collective-permute-start.8) | collective-permute-done | bytes 32800 | tf_op jit(solution)/shard_map/ppermute | solution.py:359
  27.2 0.0 collective-permute-done.9.refs_2_
  27.2 0.0 copy-start.3
  27.2 0.0 copy-start.4
  27.2 0.0 copy-start.2
  27.2 0.3 %collective-permute-start.11 = (bf16[128,256]{1,0:T(8,128)(2,1)S(1)}, bf16[128,256]{1,0:T(8,128)(2,1)S(1)}, u32[]{:S(2)}, u32[]{:S(2)}) collective-permute-start(bf16[128,256]{1,0:T(8,128)(2,1)S(1)} %get-tuple-element.40), channel_id=1, source_target_pairs={{0,1},{1,0},{2,3},{3,2},{4,5},{5,4},{6,7},{7,6},{8,9},{9,8},{10,11... | collective-permute-start | bytes 196616 | tf_op jit(solution)/shard_map/ppermute | solution.py:359
  27.6 0.0 copy-done
  27.6 0.0 copy-done.1
  27.6 0.3 %copy-done.3 = f32[3,768]{1,0:T(4,128)S(1)} copy-done((f32[3,768]{1,0:T(4,128)S(1)}, f32[3,768]{1,0:T(4,128)}, u32[]{:S(2)}) %copy-start.3) | copy-done | bytes 9240
  27.9 0.0 copy-done.4
  27.9 0.3 %shard_map.109.query_ref = f32[256,256]{1,0:T(8,128)S(1)} custom-call(bf16[256,256]{1,0:T(8,128)(2,1)S(1)} %copy-done.1, f32[1,256]{1,0:T(1,128)S(1)} %bitcast.3, bf16[256,768]{1,0:T(8,128)(2,1)S(1)} %copy-done, f32[3,768]{1,0:T(4,128)S(1)} %copy-done.3), custom_call_target="tpu_custom_call" | custom-call | flops 33554432 | bytes 800000 | tf_op jit(solution)/shard_map/pallas_call | solution.py:27
  28.2 0.3 %collective-permute-done.11.refs_1_ = bf16[128,256]{1,0:T(8,128)(2,1)S(1)} collective-permute-done((bf16[128,256]{1,0:T(8,128)(2,1)S(1)}, bf16[128,256]{1,0:T(8,128)(2,1)S(1)}, u32[]{:S(2)}, u32[]{:S(2)}) %collective-permute-start.11) | collective-permute-done | bytes 65568 | tf_op jit(solution)/shard_map/ppermute | solution.py:359
  28.6 0.0 copy-done.2
  28.6 0.9 %shard_map.116 = bf16[256,256]{1,0:T(8,128)(2,1)} custom-call(f32[256,256]{1,0:T(8,128)S(1)} %shard_map.109.query_ref, bf16[256,256]{1,0:T(8,128)(2,1)S(1)} %copy-done.2, bf16[128,256]{1,0:T(8,128)(2,1)S(1)} %get-tuple-element.39.refs_0_, bf16[128,256]{1,0:T(8,128)(2,1)S(1)} %collective-permute-done.11.refs_1_), custom_call_target="tpu_custom_call" | custom-call | flops 33554432 | bytes 600000 | tf_op jit(solution)/shard_map/pallas_call | solution.py:27
  (4 shorter events, 0.1 us)
Async XLA Ops:
  0.0 16.9 %copy-start.7 = (f32[32,256]{1,0:T(8,128)S(1)}, f32[32,256]{1,0:T(8,128)}, u32[]{:S(2)}) copy-start(f32[32,256]{1,0:T(8,128)} %constant.7.clone.twist_ref) | copy-start | bytes 98308
  2.0 3.1 %collective-permute-start = (bf16[3,136,128]{2,1,0:T(8,128)(2,1)S(1)}, bf16[3,136,128]{2,1,0:T(8,128)(2,1)S(1)}, u32[]{:S(2)}, u32[]{:S(2)}) collective-permute-start(bf16[3,136,128]{2,1,0:T(8,128)(2,1)S(1)} %get-tuple-element.24), channel_id=1, source_target_pairs={{0,1},{1,0},{2,3},{3,2},{4,5},{5,4},{6,7},{7,6},{8,9},{9,8},{10,11... | collective-permute-start | bytes 313352 | tf_op jit(solution)/shard_map/ppermute | solution.py:359
  2.6 7.1 %collective-permute-start.4 = (bf16[280,128]{1,0:T(8,128)(2,1)S(1)}, bf16[280,128]{1,0:T(8,128)(2,1)S(1)}, u32[]{:S(2)}, u32[]{:S(2)}) collective-permute-start(bf16[280,128]{1,0:T(8,128)(2,1)S(1)} %get-tuple-element.28), channel_id=1, source_target_pairs={{0,2},{1,3},{2,0},{3,1},{4,6},{5,7},{6,4},{7,5},{8,10},{9,11},{10,... | collective-permute-start | bytes 215048 | tf_op jit(solution)/shard_map/ppermute | solution.py:359
  5.1 11.8 %copy-start.5 = (bf16[512,256]{1,0:T(8,128)(2,1)S(1)}, bf16[512,256]{1,0:T(8,128)(2,1)}, u32[]{:S(2)}) copy-start(bf16[512,256]{1,0:T(8,128)(2,1)} %constant.6.clone.first_ref) | copy-start | bytes 786436
  5.2 11.8 %copy-start.6 = (bf16[256,512]{1,0:T(8,128)(2,1)S(1)}, bf16[256,512]{1,0:T(8,128)(2,1)}, u32[]{:S(2)}) copy-start(bf16[256,512]{1,0:T(8,128)(2,1)} %constant.8.clone.inner_ref) | copy-start | bytes 786436
  5.2 6.8 %collective-permute-start.1 = (bf16[264,128]{1,0:T(8,128)(2,1)S(1)}, bf16[264,128]{1,0:T(8,128)(2,1)S(1)}, u32[]{:S(2)}, u32[]{:S(2)}) collective-permute-start(bf16[264,128]{1,0:T(8,128)(2,1)S(1)} %get-tuple-element.25), channel_id=1, source_target_pairs={{0,12},{1,15},{2,14},{3,13},{4,8},{5,11},{6,10},{7,9},{8,4},{9,7},... | collective-permute-start | bytes 202760 | tf_op jit(solution)/shard_map/ppermute | solution.py:359
  8.8 6.6 %collective-permute-start.2 = (bf16[264,128]{1,0:T(8,128)(2,1)S(1)}, bf16[264,128]{1,0:T(8,128)(2,1)S(1)}, u32[]{:S(2)}, u32[]{:S(2)}) collective-permute-start(bf16[264,128]{1,0:T(8,128)(2,1)S(1)} %get-tuple-element.26), channel_id=1, source_target_pairs={{0,8},{1,11},{2,10},{3,9},{4,12},{5,15},{6,14},{7,13},{8,0},{9,3},... | collective-permute-start | bytes 202760 | tf_op jit(solution)/shard_map/ppermute | solution.py:359
  8.8 6.6 %collective-permute-start.3 = (bf16[264,128]{1,0:T(8,128)(2,1)S(1)}, bf16[264,128]{1,0:T(8,128)(2,1)S(1)}, u32[]{:S(2)}, u32[]{:S(2)}) collective-permute-start(bf16[264,128]{1,0:T(8,128)(2,1)S(1)} %get-tuple-element.27), channel_id=1, source_target_pairs={{0,4},{1,7},{2,6},{3,5},{4,0},{5,3},{6,2},{7,1},{8,12},{9,15},{10,... | collective-permute-start | bytes 202760 | tf_op jit(solution)/shard_map/ppermute | solution.py:359
  15.5 1.4 %collective-permute-start.5 = (bf16[544,128]{1,0:T(8,128)(2,1)S(1)}, bf16[544,128]{1,0:T(8,128)(2,1)S(1)}, u32[]{:S(2)}, u32[]{:S(2)}) collective-permute-start(bf16[544,128]{1,0:T(8,128)(2,1)S(1)} %get-tuple-element.31), channel_id=1, source_target_pairs={{0,1},{1,0},{2,3},{3,2},{4,5},{5,4},{6,7},{7,6},{8,9},{9,8},{10,11... | collective-permute-start | bytes 417800 | tf_op jit(solution)/shard_map/ppermute | solution.py:359
  16.9 10.7 %copy-start = (bf16[256,768]{1,0:T(8,128)(2,1)S(1)}, bf16[256,768]{1,0:T(8,128)(2,1)}, u32[]{:S(2)}) copy-start(bf16[256,768]{1,0:T(8,128)(2,1)} %refs_2_.1) | copy-start | bytes 1179652
  18.3 1.3 %collective-permute-start.6 = (bf16[3,32,256]{2,1,0:T(8,128)(2,1)S(1)}, bf16[3,32,256]{2,1,0:T(8,128)(2,1)S(1)}, u32[]{:S(2)}, u32[]{:S(2)}) collective-permute-start(bf16[3,32,256]{2,1,0:T(8,128)(2,1)S(1)} %get-tuple-element.33), channel_id=1, source_target_pairs={{0,1},{1,0},{2,3},{3,2},{4,5},{5,4},{6,7},{7,6},{8,9},{9,8},{10,11... | collective-permute-start | bytes 147464 | tf_op jit(solution)/shard_map/ppermute | solution.py:359
  18.5 5.6 %collective-permute-start.10 = (bf16[80,256]{1,0:T(8,128)(2,1)S(1)}, bf16[80,256]{1,0:T(8,128)(2,1)S(1)}, u32[]{:S(2)}, u32[]{:S(2)}) collective-permute-start(bf16[80,256]{1,0:T(8,128)(2,1)S(1)} %get-tuple-element.37), channel_id=1, source_target_pairs={{0,2},{1,3},{2,0},{3,1},{4,6},{5,7},{6,4},{7,5},{8,10},{9,11},{10,... | collective-permute-start | bytes 122888 | tf_op jit(solution)/shard_map/ppermute | solution.py:359
  19.6 8.0 %copy-start.1 = (bf16[256,256]{1,0:T(8,128)(2,1)S(1)}, bf16[256,256]{1,0:T(8,128)(2,1)}, u32[]{:S(2)}) copy-start(bf16[256,256]{1,0:T(8,128)(2,1)} %refs_0_.1) | copy-start | bytes 393220
  19.6 6.0 %collective-permute-start.7 = (bf16[64,256]{1,0:T(8,128)(2,1)S(1)}, bf16[64,256]{1,0:T(8,128)(2,1)S(1)}, u32[]{:S(2)}, u32[]{:S(2)}) collective-permute-start(bf16[64,256]{1,0:T(8,128)(2,1)S(1)} %get-tuple-element.34), channel_id=1, source_target_pairs={{0,12},{1,15},{2,14},{3,13},{4,8},{5,11},{6,10},{7,9},{8,4},{9,7},... | collective-permute-start | bytes 98312 | tf_op jit(solution)/shard_map/ppermute | solution.py:359
  22.1 5.1 %collective-permute-start.8 = (bf16[64,256]{1,0:T(8,128)(2,1)S(1)}, bf16[64,256]{1,0:T(8,128)(2,1)S(1)}, u32[]{:S(2)}, u32[]{:S(2)}) collective-permute-start(bf16[64,256]{1,0:T(8,128)(2,1)S(1)} %get-tuple-element.35), channel_id=1, source_target_pairs={{0,8},{1,11},{2,10},{3,9},{4,12},{5,15},{6,14},{7,13},{8,0},{9,3},... | collective-permute-start | bytes 98312 | tf_op jit(solution)/shard_map/ppermute | solution.py:359
  22.3 4.9 %collective-permute-start.9 = (bf16[64,256]{1,0:T(8,128)(2,1)S(1)}, bf16[64,256]{1,0:T(8,128)(2,1)S(1)}, u32[]{:S(2)}, u32[]{:S(2)}) collective-permute-start(bf16[64,256]{1,0:T(8,128)(2,1)S(1)} %get-tuple-element.36), channel_id=1, source_target_pairs={{0,4},{1,7},{2,6},{3,5},{4,0},{5,3},{6,2},{7,1},{8,12},{9,15},{10,... | collective-permute-start | bytes 98312 | tf_op jit(solution)/shard_map/ppermute | solution.py:359
  27.2 0.7 %copy-start.3 = (f32[3,768]{1,0:T(4,128)S(1)}, f32[3,768]{1,0:T(4,128)}, u32[]{:S(2)}) copy-start(f32[3,768]{1,0:T(4,128)} %refs_3_.1) | copy-start | bytes 27652
  27.2 0.7 %copy-start.4 = (f32[256]{0:T(256)S(1)}, f32[256]{0:T(256)}, u32[]{:S(2)}) copy-start(f32[256]{0:T(256)} %param.12) | copy-start | bytes 3076
  27.2 1.3 %copy-start.2 = (bf16[256,256]{1,0:T(8,128)(2,1)S(1)}, bf16[256,256]{1,0:T(8,128)(2,1)}, u32[]{:S(2)}) copy-start(bf16[256,256]{1,0:T(8,128)(2,1)} %w_ref.3) | copy-start | bytes 393220
  27.2 1.3 %collective-permute-start.11 = (bf16[128,256]{1,0:T(8,128)(2,1)S(1)}, bf16[128,256]{1,0:T(8,128)(2,1)S(1)}, u32[]{:S(2)}, u32[]{:S(2)}) collective-permute-start(bf16[128,256]{1,0:T(8,128)(2,1)S(1)} %get-tuple-element.40), channel_id=1, source_target_pairs={{0,1},{1,0},{2,3},{3,2},{4,5},{5,4},{6,7},{7,6},{8,9},{9,8},{10,11... | collective-permute-start | bytes 196616 | tf_op jit(solution)/shard_map/ppermute | solution.py:359

commit v20 on v18

--- a/solution.py
+++ b/solution.py
@@ -175,8 +175,8 @@
     copies[0].wait()
     copies[1].wait()
     normed = normed_of(tokens_ref, gain_ref)
-    for copy in copies[2:]:
-        copy.wait()
+    copies[2].wait()
+    copies[3].wait()
     query_cols, cols = slice(0, width), slice(width, 3 * width)
     mixed = short_mix(projected_of(normed, w_ref[:, cols]), short_ref[:, cols])
     key, value = mixed[:, 0:width], mixed[:, width:]
@@ -185,12 +185,14 @@
     some = jnp.concatenate([normed[0 : 2 * edge], normed[rows - 2 * edge :]])
     some = short_mix(projected_of(some, w_ref[:, query_cols]), short_ref[:, query_cols])
     put_rim(packed_ref, rim_ref, [*rims, (some[0:edge], some[4 * edge :])])
+    for copy in copies[4:]:
+        copy.wait()
     med_len = medium_ref.shape[0]
     is_first = jnp.where(lax.axis_index(seq) == 0, 1.0, 0.0)
     head = long_ref[0:med_len, :] + is_first * medium_ref[...]
-    head_row = lax.broadcasted_iota(jnp.int32, head.shape, 0)
-    head = head + jnp.where(head_row == 0, is_first * skip_ref[...], 0.0)
-    taps = jnp.concatenate([head, long_ref[med_len:, :]]).astype(jnp.bfloat16)
+    row = lax.broadcasted_iota(jnp.int32, (edge, width), 0)
+    top = head[0:edge] + jnp.where(row == 0, is_first * skip_ref[...], 0.0)
+    taps = jnp.concatenate([top, head[edge:], long_ref[med_len:, :]]).astype(jnp.bfloat16)
     put_columns(packed_ref, rows, taps.T)
     if staged:
         put_routes(packed_ref, rim_ref, *outs)

time: 29.4 us -> 29.4 us (level)
  no operation moved by 1% of the time
where the time goes in v20:
time: 29.4 us; the launch traced here: 29.2 us
  starting transfers between devices  13.7 us (47%)
  waiting for transfers between devices  10.7 us (36%)
  Pallas kernels  4.41 us (15%)
  local copies, waits for them, and re-layouts  0.36 us (1%)
    ppermute x12, starting transfers between devices, permute(): lax.ppermute(array, seq, [(i, partner(i)) for i in range(lax.axis_size(se...  13.7 us
    ppermute x12, waiting for transfers between devices, permute(): lax.ppermute(array, seq, [(i, partner(i)) for i in range(lax.axis_size(se...  10.7 us
    pallas_call x8, Pallas kernels, call(): pl.pallas_call(body, out_shape=outs, in_specs=[whole(space) for space in...  4.41 us
  transfers between devices with their start and end apart: 12, of which 7 were waited for; matrix products, arithmetic and copies ran while one was open for 0% of the time, Pallas kernels for 1%

profile of v20, /device:TPU:0, one launch (start us, length us, event | category | flops | bytes accessed | tf_op | source)
XLA Modules:
  0.0 29.2 jit_solution(4936193135065315468)
XLA Ops:
  0.0 0.0 copy-start.7
  0.0 1.8 %shard_map.110 = (bf16[3,136,128]{2,1,0:T(8,128)(2,1)S(1)}, bf16[3,136,128]{2,1,0:T(8,128)(2,1)S(1)}, bf16[280,128]{1,0:T(8,128)(2,1)S(1)}, bf16[136,128]{1,0:T(8,128)(2,1)S(1)}) custom-call(bf16[256,256]{1,0:T(8,128)(2,1)} %refs_0_.1, f32[1,256]{1,0:T(1,128)} %bitcast.2, bf16[256,768]{1,0:T(8,128)(2,1)} %refs_2_.1, f32[3,768]{1,0:T(4,128)} %refs_3_.1, ...), custom_call_target="tpu_custom_call" | custom-call | flops 100663296 | bytes 1500000 | tf_op jit(solution)/shard_map/pallas_call | solution.py:26
  1.8 0.5 %collective-permute-start = (bf16[3,136,128]{2,1,0:T(8,128)(2,1)S(1)}, bf16[3,136,128]{2,1,0:T(8,128)(2,1)S(1)}, u32[]{:S(2)}, u32[]{:S(2)}) collective-permute-start(bf16[3,136,128]{2,1,0:T(8,128)(2,1)S(1)} %get-tuple-element.24), channel_id=1, source_target_pairs={{0,1},{1,0},{2,3},{3,2},{4,5},{5,4},{6,7},{7,6},{8,9},{9,8},{10,11... | collective-permute-start | bytes 313352 | tf_op jit(solution)/shard_map/ppermute | solution.py:345
  2.3 2.6 %collective-permute-start.4 = (bf16[280,128]{1,0:T(8,128)(2,1)S(1)}, bf16[280,128]{1,0:T(8,128)(2,1)S(1)}, u32[]{:S(2)}, u32[]{:S(2)}) collective-permute-start(bf16[280,128]{1,0:T(8,128)(2,1)S(1)} %get-tuple-element.28), channel_id=1, source_target_pairs={{0,2},{1,3},{2,0},{3,1},{4,6},{5,7},{6,4},{7,5},{8,10},{9,11},{10,... | collective-permute-start | bytes 215048 | tf_op jit(solution)/shard_map/ppermute | solution.py:345
  4.9 0.0 collective-permute-done.got_ref
  4.9 0.0 copy-start.5
  4.9 0.0 copy-start.6
  4.9 3.7 %collective-permute-start.1 = (bf16[264,128]{1,0:T(8,128)(2,1)S(1)}, bf16[264,128]{1,0:T(8,128)(2,1)S(1)}, u32[]{:S(2)}, u32[]{:S(2)}) collective-permute-start(bf16[264,128]{1,0:T(8,128)(2,1)S(1)} %get-tuple-element.25), channel_id=1, source_target_pairs={{0,12},{1,15},{2,14},{3,13},{4,8},{5,11},{6,10},{7,9},{8,4},{9,7},... | collective-permute-start | bytes 202760 | tf_op jit(solution)/shard_map/ppermute | solution.py:345
  8.6 0.0 collective-permute-start.2
  8.6 0.8 %collective-permute-start.3 = (bf16[264,128]{1,0:T(8,128)(2,1)S(1)}, bf16[264,128]{1,0:T(8,128)(2,1)S(1)}, u32[]{:S(2)}, u32[]{:S(2)}) collective-permute-start(bf16[264,128]{1,0:T(8,128)(2,1)S(1)} %get-tuple-element.27), channel_id=1, source_target_pairs={{0,4},{1,7},{2,6},{3,5},{4,0},{5,3},{6,2},{7,1},{8,12},{9,15},{10,... | collective-permute-start | bytes 202760 | tf_op jit(solution)/shard_map/ppermute | solution.py:345
  9.4 0.0 collective-permute-done.4.refs_3_
  9.4 2.4 %collective-permute-done.1.refs_0_ = bf16[264,128]{1,0:T(8,128)(2,1)S(1)} collective-permute-done((bf16[264,128]{1,0:T(8,128)(2,1)S(1)}, bf16[264,128]{1,0:T(8,128)(2,1)S(1)}, u32[]{:S(2)}, u32[]{:S(2)}) %collective-permute-start.1) | collective-permute-done | bytes 67616 | tf_op jit(solution)/shard_map/ppermute | solution.py:345
  11.8 3.5 %collective-permute-done.2.refs_1_ = bf16[264,128]{1,0:T(8,128)(2,1)S(1)} collective-permute-done((bf16[264,128]{1,0:T(8,128)(2,1)S(1)}, bf16[264,128]{1,0:T(8,128)(2,1)S(1)}, u32[]{:S(2)}, u32[]{:S(2)}) %collective-permute-start.2) | collective-permute-done | bytes 67616 | tf_op jit(solution)/shard_map/ppermute | solution.py:345
  15.2 0.0 collective-permute-done.3.refs_2_
  15.2 0.2 collective-permute-start.5
  15.4 1.2 %collective-permute-done.5.refs_1_ = bf16[544,128]{1,0:T(8,128)(2,1)S(1)} collective-permute-done((bf16[544,128]{1,0:T(8,128)(2,1)S(1)}, bf16[544,128]{1,0:T(8,128)(2,1)S(1)}, u32[]{:S(2)}, u32[]{:S(2)}) %collective-permute-start.5) | collective-permute-done | bytes 139296 | tf_op jit(solution)/shard_map/ppermute | solution.py:345
  16.7 0.0 copy-done.7
  16.7 0.0 copy-done.5
  16.7 0.0 copy-done.6
  16.7 0.0 copy-start
  16.7 1.3 %shard_map.113 = (bf16[3,32,256]{2,1,0:T(8,128)(2,1)S(1)}, bf16[3,32,256]{2,1,0:T(8,128)(2,1)S(1)}, bf16[80,256]{1,0:T(8,128)(2,1)S(1)}, bf16[32,256]{1,0:T(8,128)(2,1)S(1)}) custom-call(bf16[512,256]{1,0:T(8,128)(2,1)S(1)} %copy-done.5, f32[32,256]{1,0:T(8,128)S(1)} %copy-done.7, bf16[256,512]{1,0:T(8,128)(2,1)S(1)} %copy-done.6, ...), custom_call_target="tpu_custom_call" | custom-call | flops 603979776 | bytes 2000000 | tf_op jit(solution)/shard_map/pallas_call | solution.py:26
  18.0 0.2 collective-permute-start.6
  18.2 1.0 %collective-permute-start.10 = (bf16[80,256]{1,0:T(8,128)(2,1)S(1)}, bf16[80,256]{1,0:T(8,128)(2,1)S(1)}, u32[]{:S(2)}, u32[]{:S(2)}) collective-permute-start(bf16[80,256]{1,0:T(8,128)(2,1)S(1)} %get-tuple-element.37), channel_id=1, source_target_pairs={{0,2},{1,3},{2,0},{3,1},{4,6},{5,7},{6,4},{7,5},{8,10},{9,11},{10,... | collective-permute-start | bytes 122888 | tf_op jit(solution)/shard_map/ppermute | solution.py:345
  19.2 0.1 collective-permute-done.6.got_ref
  19.3 0.0 copy-start.1
  19.3 2.5 %collective-permute-start.7 = (bf16[64,256]{1,0:T(8,128)(2,1)S(1)}, bf16[64,256]{1,0:T(8,128)(2,1)S(1)}, u32[]{:S(2)}, u32[]{:S(2)}) collective-permute-start(bf16[64,256]{1,0:T(8,128)(2,1)S(1)} %get-tuple-element.34), channel_id=1, source_target_pairs={{0,12},{1,15},{2,14},{3,13},{4,8},{5,11},{6,10},{7,9},{8,4},{9,7},... | collective-permute-start | bytes 98312 | tf_op jit(solution)/shard_map/ppermute | solution.py:345
  21.9 0.2 collective-permute-start.8
  22.1 1.7 %collective-permute-start.9 = (bf16[64,256]{1,0:T(8,128)(2,1)S(1)}, bf16[64,256]{1,0:T(8,128)(2,1)S(1)}, u32[]{:S(2)}, u32[]{:S(2)}) collective-permute-start(bf16[64,256]{1,0:T(8,128)(2,1)S(1)} %get-tuple-element.36), channel_id=1, source_target_pairs={{0,4},{1,7},{2,6},{3,5},{4,0},{5,3},{6,2},{7,1},{8,12},{9,15},{10,... | collective-permute-start | bytes 98312 | tf_op jit(solution)/shard_map/ppermute | solution.py:345
  23.8 0.0 collective-permute-done.10.refs_3_
  23.8 1.6 %collective-permute-done.7.refs_0_ = bf16[64,256]{1,0:T(8,128)(2,1)S(1)} collective-permute-done((bf16[64,256]{1,0:T(8,128)(2,1)S(1)}, bf16[64,256]{1,0:T(8,128)(2,1)S(1)}, u32[]{:S(2)}, u32[]{:S(2)}) %collective-permute-start.7) | collective-permute-done | bytes 32800 | tf_op jit(solution)/shard_map/ppermute | solution.py:345
  25.4 1.6 %collective-permute-done.8.refs_1_ = bf16[64,256]{1,0:T(8,128)(2,1)S(1)} collective-permute-done((bf16[64,256]{1,0:T(8,128)(2,1)S(1)}, bf16[64,256]{1,0:T(8,128)(2,1)S(1)}, u32[]{:S(2)}, u32[]{:S(2)}) %collective-permute-start.8) | collective-permute-done | bytes 32800 | tf_op jit(solution)/shard_map/ppermute | solution.py:345
  27.0 0.0 collective-permute-done.9.refs_2_
  27.0 0.0 copy-start.3
  27.0 0.0 copy-start.4
  27.0 0.0 copy-start.2
  27.0 0.3 %collective-permute-start.11 = (bf16[128,256]{1,0:T(8,128)(2,1)S(1)}, bf16[128,256]{1,0:T(8,128)(2,1)S(1)}, u32[]{:S(2)}, u32[]{:S(2)}) collective-permute-start(bf16[128,256]{1,0:T(8,128)(2,1)S(1)} %get-tuple-element.40), channel_id=1, source_target_pairs={{0,1},{1,0},{2,3},{3,2},{4,5},{5,4},{6,7},{7,6},{8,9},{9,8},{10,11... | collective-permute-start | bytes 196616 | tf_op jit(solution)/shard_map/ppermute | solution.py:345
  27.3 0.0 copy-done
  27.3 0.0 copy-done.1
  27.3 0.3 %copy-done.3 = f32[3,768]{1,0:T(4,128)S(1)} copy-done((f32[3,768]{1,0:T(4,128)S(1)}, f32[3,768]{1,0:T(4,128)}, u32[]{:S(2)}) %copy-start.3) | copy-done | bytes 9240
  27.7 0.0 copy-done.4
  27.7 0.3 %shard_map.109.query_ref = f32[256,256]{1,0:T(8,128)S(1)} custom-call(bf16[256,256]{1,0:T(8,128)(2,1)S(1)} %copy-done.1, f32[1,256]{1,0:T(1,128)S(1)} %bitcast.3, bf16[256,768]{1,0:T(8,128)(2,1)S(1)} %copy-done, f32[3,768]{1,0:T(4,128)S(1)} %copy-done.3), custom_call_target="tpu_custom_call" | custom-call | flops 33554432 | bytes 800000 | tf_op jit(solution)/shard_map/pallas_call | solution.py:26
  28.0 0.3 %collective-permute-done.11.refs_1_ = bf16[128,256]{1,0:T(8,128)(2,1)S(1)} collective-permute-done((bf16[128,256]{1,0:T(8,128)(2,1)S(1)}, bf16[128,256]{1,0:T(8,128)(2,1)S(1)}, u32[]{:S(2)}, u32[]{:S(2)}) %collective-permute-start.11) | collective-permute-done | bytes 65568 | tf_op jit(solution)/shard_map/ppermute | solution.py:345
  28.3 0.0 copy-done.2
  28.3 0.9 %shard_map.116 = bf16[256,256]{1,0:T(8,128)(2,1)} custom-call(f32[256,256]{1,0:T(8,128)S(1)} %shard_map.109.query_ref, bf16[256,256]{1,0:T(8,128)(2,1)S(1)} %copy-done.2, bf16[128,256]{1,0:T(8,128)(2,1)S(1)} %get-tuple-element.39.refs_0_, bf16[128,256]{1,0:T(8,128)(2,1)S(1)} %collective-permute-done.11.refs_1_), custom_call_target="tpu_custom_call" | custom-call | flops 33554432 | bytes 600000 | tf_op jit(solution)/shard_map/pallas_call | solution.py:26
  (4 shorter events, 0.1 us)
Async XLA Ops:
  0.0 16.7 %copy-start.7 = (f32[32,256]{1,0:T(8,128)S(1)}, f32[32,256]{1,0:T(8,128)}, u32[]{:S(2)}) copy-start(f32[32,256]{1,0:T(8,128)} %constant.7.clone.twist_ref) | copy-start | bytes 98308
  1.8 3.1 %collective-permute-start = (bf16[3,136,128]{2,1,0:T(8,128)(2,1)S(1)}, bf16[3,136,128]{2,1,0:T(8,128)(2,1)S(1)}, u32[]{:S(2)}, u32[]{:S(2)}) collective-permute-start(bf16[3,136,128]{2,1,0:T(8,128)(2,1)S(1)} %get-tuple-element.24), channel_id=1, source_target_pairs={{0,1},{1,0},{2,3},{3,2},{4,5},{5,4},{6,7},{7,6},{8,9},{9,8},{10,11... | collective-permute-start | bytes 313352 | tf_op jit(solution)/shard_map/ppermute | solution.py:345
  2.3 7.1 %collective-permute-start.4 = (bf16[280,128]{1,0:T(8,128)(2,1)S(1)}, bf16[280,128]{1,0:T(8,128)(2,1)S(1)}, u32[]{:S(2)}, u32[]{:S(2)}) collective-permute-start(bf16[280,128]{1,0:T(8,128)(2,1)S(1)} %get-tuple-element.28), channel_id=1, source_target_pairs={{0,2},{1,3},{2,0},{3,1},{4,6},{5,7},{6,4},{7,5},{8,10},{9,11},{10,... | collective-permute-start | bytes 215048 | tf_op jit(solution)/shard_map/ppermute | solution.py:345
  4.9 11.8 %copy-start.5 = (bf16[512,256]{1,0:T(8,128)(2,1)S(1)}, bf16[512,256]{1,0:T(8,128)(2,1)}, u32[]{:S(2)}) copy-start(bf16[512,256]{1,0:T(8,128)(2,1)} %constant.6.clone.first_ref) | copy-start | bytes 786436
  4.9 11.8 %copy-start.6 = (bf16[256,512]{1,0:T(8,128)(2,1)S(1)}, bf16[256,512]{1,0:T(8,128)(2,1)}, u32[]{:S(2)}) copy-start(bf16[256,512]{1,0:T(8,128)(2,1)} %constant.8.clone.inner_ref) | copy-start | bytes 786436
  4.9 6.8 %collective-permute-start.1 = (bf16[264,128]{1,0:T(8,128)(2,1)S(1)}, bf16[264,128]{1,0:T(8,128)(2,1)S(1)}, u32[]{:S(2)}, u32[]{:S(2)}) collective-permute-start(bf16[264,128]{1,0:T(8,128)(2,1)S(1)} %get-tuple-element.25), channel_id=1, source_target_pairs={{0,12},{1,15},{2,14},{3,13},{4,8},{5,11},{6,10},{7,9},{8,4},{9,7},... | collective-permute-start | bytes 202760 | tf_op jit(solution)/shard_map/ppermute | solution.py:345
  8.6 6.6 %collective-permute-start.2 = (bf16[264,128]{1,0:T(8,128)(2,1)S(1)}, bf16[264,128]{1,0:T(8,128)(2,1)S(1)}, u32[]{:S(2)}, u32[]{:S(2)}) collective-permute-start(bf16[264,128]{1,0:T(8,128)(2,1)S(1)} %get-tuple-element.26), channel_id=1, source_target_pairs={{0,8},{1,11},{2,10},{3,9},{4,12},{5,15},{6,14},{7,13},{8,0},{9,3},... | collective-permute-start | bytes 202760 | tf_op jit(solution)/shard_map/ppermute | solution.py:345
  8.6 6.6 %collective-permute-start.3 = (bf16[264,128]{1,0:T(8,128)(2,1)S(1)}, bf16[264,128]{1,0:T(8,128)(2,1)S(1)}, u32[]{:S(2)}, u32[]{:S(2)}) collective-permute-start(bf16[264,128]{1,0:T(8,128)(2,1)S(1)} %get-tuple-element.27), channel_id=1, source_target_pairs={{0,4},{1,7},{2,6},{3,5},{4,0},{5,3},{6,2},{7,1},{8,12},{9,15},{10,... | collective-permute-start | bytes 202760 | tf_op jit(solution)/shard_map/ppermute | solution.py:345
  15.2 1.4 %collective-permute-start.5 = (bf16[544,128]{1,0:T(8,128)(2,1)S(1)}, bf16[544,128]{1,0:T(8,128)(2,1)S(1)}, u32[]{:S(2)}, u32[]{:S(2)}) collective-permute-start(bf16[544,128]{1,0:T(8,128)(2,1)S(1)} %get-tuple-element.31), channel_id=1, source_target_pairs={{0,1},{1,0},{2,3},{3,2},{4,5},{5,4},{6,7},{7,6},{8,9},{9,8},{10,11... | collective-permute-start | bytes 417800 | tf_op jit(solution)/shard_map/ppermute | solution.py:345
  16.7 10.7 %copy-start = (bf16[256,768]{1,0:T(8,128)(2,1)S(1)}, bf16[256,768]{1,0:T(8,128)(2,1)}, u32[]{:S(2)}) copy-start(bf16[256,768]{1,0:T(8,128)(2,1)} %refs_2_.1) | copy-start | bytes 1179652
  18.0 1.3 %collective-permute-start.6 = (bf16[3,32,256]{2,1,0:T(8,128)(2,1)S(1)}, bf16[3,32,256]{2,1,0:T(8,128)(2,1)S(1)}, u32[]{:S(2)}, u32[]{:S(2)}) collective-permute-start(bf16[3,32,256]{2,1,0:T(8,128)(2,1)S(1)} %get-tuple-element.33), channel_id=1, source_target_pairs={{0,1},{1,0},{2,3},{3,2},{4,5},{5,4},{6,7},{7,6},{8,9},{9,8},{10,11... | collective-permute-start | bytes 147464 | tf_op jit(solution)/shard_map/ppermute | solution.py:345
  18.2 5.6 %collective-permute-start.10 = (bf16[80,256]{1,0:T(8,128)(2,1)S(1)}, bf16[80,256]{1,0:T(8,128)(2,1)S(1)}, u32[]{:S(2)}, u32[]{:S(2)}) collective-permute-start(bf16[80,256]{1,0:T(8,128)(2,1)S(1)} %get-tuple-element.37), channel_id=1, source_target_pairs={{0,2},{1,3},{2,0},{3,1},{4,6},{5,7},{6,4},{7,5},{8,10},{9,11},{10,... | collective-permute-start | bytes 122888 | tf_op jit(solution)/shard_map/ppermute | solution.py:345
  19.3 8.0 %copy-start.1 = (bf16[256,256]{1,0:T(8,128)(2,1)S(1)}, bf16[256,256]{1,0:T(8,128)(2,1)}, u32[]{:S(2)}) copy-start(bf16[256,256]{1,0:T(8,128)(2,1)} %refs_0_.1) | copy-start | bytes 393220
  19.3 6.0 %collective-permute-start.7 = (bf16[64,256]{1,0:T(8,128)(2,1)S(1)}, bf16[64,256]{1,0:T(8,128)(2,1)S(1)}, u32[]{:S(2)}, u32[]{:S(2)}) collective-permute-start(bf16[64,256]{1,0:T(8,128)(2,1)S(1)} %get-tuple-element.34), channel_id=1, source_target_pairs={{0,12},{1,15},{2,14},{3,13},{4,8},{5,11},{6,10},{7,9},{8,4},{9,7},... | collective-permute-start | bytes 98312 | tf_op jit(solution)/shard_map/ppermute | solution.py:345
  21.9 5.1 %collective-permute-start.8 = (bf16[64,256]{1,0:T(8,128)(2,1)S(1)}, bf16[64,256]{1,0:T(8,128)(2,1)S(1)}, u32[]{:S(2)}, u32[]{:S(2)}) collective-permute-start(bf16[64,256]{1,0:T(8,128)(2,1)S(1)} %get-tuple-element.35), channel_id=1, source_target_pairs={{0,8},{1,11},{2,10},{3,9},{4,12},{5,15},{6,14},{7,13},{8,0},{9,3},... | collective-permute-start | bytes 98312 | tf_op jit(solution)/shard_map/ppermute | solution.py:345
  22.1 4.9 %collective-permute-start.9 = (bf16[64,256]{1,0:T(8,128)(2,1)S(1)}, bf16[64,256]{1,0:T(8,128)(2,1)S(1)}, u32[]{:S(2)}, u32[]{:S(2)}) collective-permute-start(bf16[64,256]{1,0:T(8,128)(2,1)S(1)} %get-tuple-element.36), channel_id=1, source_target_pairs={{0,4},{1,7},{2,6},{3,5},{4,0},{5,3},{6,2},{7,1},{8,12},{9,15},{10,... | collective-permute-start | bytes 98312 | tf_op jit(solution)/shard_map/ppermute | solution.py:345
  27.0 0.7 %copy-start.3 = (f32[3,768]{1,0:T(4,128)S(1)}, f32[3,768]{1,0:T(4,128)}, u32[]{:S(2)}) copy-start(f32[3,768]{1,0:T(4,128)} %refs_3_.1) | copy-start | bytes 27652
  27.0 0.7 %copy-start.4 = (f32[256]{0:T(256)S(1)}, f32[256]{0:T(256)}, u32[]{:S(2)}) copy-start(f32[256]{0:T(256)} %param.12) | copy-start | bytes 3076
  27.0 1.3 %copy-start.2 = (bf16[256,256]{1,0:T(8,128)(2,1)S(1)}, bf16[256,256]{1,0:T(8,128)(2,1)}, u32[]{:S(2)}) copy-start(bf16[256,256]{1,0:T(8,128)(2,1)} %w_ref.3) | copy-start | bytes 393220
  27.0 1.3 %collective-permute-start.11 = (bf16[128,256]{1,0:T(8,128)(2,1)S(1)}, bf16[128,256]{1,0:T(8,128)(2,1)S(1)}, u32[]{:S(2)}, u32[]{:S(2)}) collective-permute-start(bf16[128,256]{1,0:T(8,128)(2,1)S(1)} %get-tuple-element.40), channel_id=1, source_target_pairs={{0,1},{1,0},{2,3},{3,2},{4,5},{5,4},{6,7},{7,6},{8,9},{9,8},{10,11... | collective-permute-start | bytes 196616 | tf_op jit(solution)/shard_map/ppermute | solution.py:345

commit v21 on v20

--- a/solution.py
+++ b/solution.py
@@ -81,15 +81,19 @@
         put(give_ref.at[turn], other)
     put(home_ref, 0)
     put(near_ref, 1)
-    begin = 2 * size + extra
+    begin = 2 * size
+    if extra:
+        rim = rim_ref[chip ^ 1].astype(jnp.float32)
+        near_ref[begin : begin + chan_tile, :] = jnp.concatenate([rim, rim]).astype(jnp.bfloat16)
+        begin += chan_tile
     near_ref[begin : begin + 2 * size, :] = home_ref[0 : 2 * size, :]
-    near_ref[begin + 2 * size :, :] = home_ref[0:chan_tile, :]
+    begin += 2 * size
+    near_ref[begin:, :] = home_ref[0 : near_ref.shape[0] - begin, :]
 
 
 def half_rims(first_ref, second_ref, begin):
     pair = [ref[begin : begin + edge, :].astype(jnp.float32) for ref in (first_ref, second_ref)]
-    pair = [rims[0 : edge // 2] for rims in pair]
-    return jnp.concatenate(pair).astype(jnp.bfloat16)
+    return jnp.concatenate([rims[0 : edge // 2] for rims in pair])
 
 
 def merge_body(size, keep_ref, got_ref, *out_refs):
@@ -97,7 +101,8 @@
         out_ref[0 : 2 * size, :] = keep_ref[turn, 0 : 2 * size, :]
         out_ref[2 * size : 4 * size, :] = got_ref[turn, 0 : 2 * size, :]
         if out_ref.shape[0] > 4 * size:
-            out_ref[4 * size :, :] = half_rims(keep_ref.at[turn], got_ref.at[turn], 2 * size)
+            rims = half_rims(keep_ref.at[turn], got_ref.at[turn], 2 * size)
+            out_ref[4 * size :, :] = rims.astype(jnp.bfloat16)
 
 
 def split_body(size, *refs):
@@ -111,10 +116,9 @@
             out_ref[place * size : (place + 1) * size, :] = source_ref[pl.ds(start, size), :]
         begin = len(sources) * size
         if out_ref.shape[0] > begin:
-            for far_ref in far_refs:
-                out_ref[begin : begin + edge, :] = far_ref[4 * size :, :]
-                begin += edge
-            out_ref[begin:, :] = half_rims(near_ref, home_ref, 2 * size)
+            rims = [far_ref[4 * size :, :].astype(jnp.float32) for far_ref in far_refs]
+            rims.append(half_rims(near_ref, home_ref, 2 * size))
+            out_ref[begin:, :] = jnp.concatenate(rims).astype(jnp.bfloat16)
 
 
 def take_routes(keep_ref, got_ref, target_ref, rim_ref=None):
@@ -130,9 +134,9 @@
             start = pl.multiple_of(device * size, size)
             target_ref[pl.ds(start, size), :] = ref[place * size : (place + 1) * size, :]
             if rim_ref is not None:
-                begin = count * size + place // 2 * edge
-                rims = ref[begin : begin + edge, :].astype(jnp.float32)
-                rim_ref[device, 0 : edge // 2, :] = rims[place % 2 * edge // 2 : (place % 2 + 1) * edge // 2]
+                begin = place * edge // 2
+                rims = ref[count * size :, :].astype(jnp.float32)
+                rim_ref[device, 0 : edge // 2, :] = rims[begin : begin + edge // 2]
 
 
 def normed_of(tokens_ref, gain_ref):

time: 29.4 us -> 29.4 us (level)
  no operation moved by 1% of the time
where the time goes in v21:
time: 29.4 us; the launch traced here: 29.2 us
  starting transfers between devices  13.7 us (47%)
  waiting for transfers between devices  10.7 us (36%)
  Pallas kernels  4.41 us (15%)
  local copies, waits for them, and re-layouts  0.36 us (1%)
    ppermute x12, starting transfers between devices, permute(): lax.ppermute(array, seq, [(i, partner(i)) for i in range(lax.axis_size(se...  13.7 us
    ppermute x12, waiting for transfers between devices, permute(): lax.ppermute(array, seq, [(i, partner(i)) for i in range(lax.axis_size(se...  10.7 us
    pallas_call x8, Pallas kernels, call(): pl.pallas_call(body, out_shape=outs, in_specs=[whole(space) for space in...  4.41 us
  transfers between devices with their start and end apart: 12, of which 7 were waited for; matrix products, arithmetic and copies ran while one was open for 0% of the time, Pallas kernels for 1%

profile of v21, /device:TPU:0, one launch (start us, length us, event | category | flops | bytes accessed | tf_op | source)
XLA Modules:
  0.0 29.2 jit_solution(14306768957826688942)
XLA Ops:
  0.0 0.0 copy-start.7
  0.0 1.8 %shard_map.110 = (bf16[3,136,128]{2,1,0:T(8,128)(2,1)S(1)}, bf16[3,136,128]{2,1,0:T(8,128)(2,1)S(1)}, bf16[280,128]{1,0:T(8,128)(2,1)S(1)}, bf16[136,128]{1,0:T(8,128)(2,1)S(1)}) custom-call(bf16[256,256]{1,0:T(8,128)(2,1)} %refs_0_.1, f32[1,256]{1,0:T(1,128)} %bitcast.2, bf16[256,768]{1,0:T(8,128)(2,1)} %refs_2_.1, f32[3,768]{1,0:T(4,128)} %refs_3_.1, ...), custom_call_target="tpu_custom_call" | custom-call | flops 100663296 | bytes 1500000 | tf_op jit(solution)/shard_map/pallas_call | solution.py:26
  1.8 0.5 %collective-permute-start = (bf16[3,136,128]{2,1,0:T(8,128)(2,1)S(1)}, bf16[3,136,128]{2,1,0:T(8,128)(2,1)S(1)}, u32[]{:S(2)}, u32[]{:S(2)}) collective-permute-start(bf16[3,136,128]{2,1,0:T(8,128)(2,1)S(1)} %get-tuple-element.24), channel_id=1, source_target_pairs={{0,1},{1,0},{2,3},{3,2},{4,5},{5,4},{6,7},{7,6},{8,9},{9,8},{10,11... | collective-permute-start | bytes 313352 | tf_op jit(solution)/shard_map/ppermute | solution.py:349
  2.3 2.6 %collective-permute-start.4 = (bf16[280,128]{1,0:T(8,128)(2,1)S(1)}, bf16[280,128]{1,0:T(8,128)(2,1)S(1)}, u32[]{:S(2)}, u32[]{:S(2)}) collective-permute-start(bf16[280,128]{1,0:T(8,128)(2,1)S(1)} %get-tuple-element.28), channel_id=1, source_target_pairs={{0,2},{1,3},{2,0},{3,1},{4,6},{5,7},{6,4},{7,5},{8,10},{9,11},{10,... | collective-permute-start | bytes 215048 | tf_op jit(solution)/shard_map/ppermute | solution.py:349
  4.9 0.0 collective-permute-done.got_ref
  4.9 0.0 copy-start.5
  4.9 0.0 copy-start.6
  4.9 3.7 %collective-permute-start.1 = (bf16[264,128]{1,0:T(8,128)(2,1)S(1)}, bf16[264,128]{1,0:T(8,128)(2,1)S(1)}, u32[]{:S(2)}, u32[]{:S(2)}) collective-permute-start(bf16[264,128]{1,0:T(8,128)(2,1)S(1)} %get-tuple-element.25), channel_id=1, source_target_pairs={{0,12},{1,15},{2,14},{3,13},{4,8},{5,11},{6,10},{7,9},{8,4},{9,7},... | collective-permute-start | bytes 202760 | tf_op jit(solution)/shard_map/ppermute | solution.py:349
  8.6 0.0 collective-permute-start.2
  8.6 0.8 %collective-permute-start.3 = (bf16[264,128]{1,0:T(8,128)(2,1)S(1)}, bf16[264,128]{1,0:T(8,128)(2,1)S(1)}, u32[]{:S(2)}, u32[]{:S(2)}) collective-permute-start(bf16[264,128]{1,0:T(8,128)(2,1)S(1)} %get-tuple-element.27), channel_id=1, source_target_pairs={{0,4},{1,7},{2,6},{3,5},{4,0},{5,3},{6,2},{7,1},{8,12},{9,15},{10,... | collective-permute-start | bytes 202760 | tf_op jit(solution)/shard_map/ppermute | solution.py:349
  9.4 0.0 collective-permute-done.4.refs_3_
  9.4 2.4 %collective-permute-done.1.refs_0_ = bf16[264,128]{1,0:T(8,128)(2,1)S(1)} collective-permute-done((bf16[264,128]{1,0:T(8,128)(2,1)S(1)}, bf16[264,128]{1,0:T(8,128)(2,1)S(1)}, u32[]{:S(2)}, u32[]{:S(2)}) %collective-permute-start.1) | collective-permute-done | bytes 67616 | tf_op jit(solution)/shard_map/ppermute | solution.py:349
  11.8 3.5 %collective-permute-done.2.refs_1_ = bf16[264,128]{1,0:T(8,128)(2,1)S(1)} collective-permute-done((bf16[264,128]{1,0:T(8,128)(2,1)S(1)}, bf16[264,128]{1,0:T(8,128)(2,1)S(1)}, u32[]{:S(2)}, u32[]{:S(2)}) %collective-permute-start.2) | collective-permute-done | bytes 67616 | tf_op jit(solution)/shard_map/ppermute | solution.py:349
  15.2 0.0 collective-permute-done.3.refs_2_
  15.2 0.2 collective-permute-start.5
  15.4 1.2 %collective-permute-done.5.refs_1_ = bf16[544,128]{1,0:T(8,128)(2,1)S(1)} collective-permute-done((bf16[544,128]{1,0:T(8,128)(2,1)S(1)}, bf16[544,128]{1,0:T(8,128)(2,1)S(1)}, u32[]{:S(2)}, u32[]{:S(2)}) %collective-permute-start.5) | collective-permute-done | bytes 139296 | tf_op jit(solution)/shard_map/ppermute | solution.py:349
  16.7 0.0 copy-done.7
  16.7 0.0 copy-done.5
  16.7 0.0 copy-done.6
  16.7 0.0 copy-start
  16.7 1.3 %shard_map.113 = (bf16[3,32,256]{2,1,0:T(8,128)(2,1)S(1)}, bf16[3,32,256]{2,1,0:T(8,128)(2,1)S(1)}, bf16[80,256]{1,0:T(8,128)(2,1)S(1)}, bf16[32,256]{1,0:T(8,128)(2,1)S(1)}) custom-call(bf16[512,256]{1,0:T(8,128)(2,1)S(1)} %copy-done.5, f32[32,256]{1,0:T(8,128)S(1)} %copy-done.7, bf16[256,512]{1,0:T(8,128)(2,1)S(1)} %copy-done.6, ...), custom_call_target="tpu_custom_call" | custom-call | flops 603979776 | bytes 2000000 | tf_op jit(solution)/shard_map/pallas_call | solution.py:26
  18.0 0.2 collective-permute-start.6
  18.2 1.0 %collective-permute-start.10 = (bf16[80,256]{1,0:T(8,128)(2,1)S(1)}, bf16[80,256]{1,0:T(8,128)(2,1)S(1)}, u32[]{:S(2)}, u32[]{:S(2)}) collective-permute-start(bf16[80,256]{1,0:T(8,128)(2,1)S(1)} %get-tuple-element.37), channel_id=1, source_target_pairs={{0,2},{1,3},{2,0},{3,1},{4,6},{5,7},{6,4},{7,5},{8,10},{9,11},{10,... | collective-permute-start | bytes 122888 | tf_op jit(solution)/shard_map/ppermute | solution.py:349
  19.2 0.1 collective-permute-done.6.got_ref
  19.3 0.0 copy-start.1
  19.3 2.5 %collective-permute-start.7 = (bf16[64,256]{1,0:T(8,128)(2,1)S(1)}, bf16[64,256]{1,0:T(8,128)(2,1)S(1)}, u32[]{:S(2)}, u32[]{:S(2)}) collective-permute-start(bf16[64,256]{1,0:T(8,128)(2,1)S(1)} %get-tuple-element.34), channel_id=1, source_target_pairs={{0,12},{1,15},{2,14},{3,13},{4,8},{5,11},{6,10},{7,9},{8,4},{9,7},... | collective-permute-start | bytes 98312 | tf_op jit(solution)/shard_map/ppermute | solution.py:349
  21.9 0.2 collective-permute-start.8
  22.1 1.7 %collective-permute-start.9 = (bf16[64,256]{1,0:T(8,128)(2,1)S(1)}, bf16[64,256]{1,0:T(8,128)(2,1)S(1)}, u32[]{:S(2)}, u32[]{:S(2)}) collective-permute-start(bf16[64,256]{1,0:T(8,128)(2,1)S(1)} %get-tuple-element.36), channel_id=1, source_target_pairs={{0,4},{1,7},{2,6},{3,5},{4,0},{5,3},{6,2},{7,1},{8,12},{9,15},{10,... | collective-permute-start | bytes 98312 | tf_op jit(solution)/shard_map/ppermute | solution.py:349
  23.8 0.0 collective-permute-done.10.refs_3_
  23.8 1.6 %collective-permute-done.7.refs_0_ = bf16[64,256]{1,0:T(8,128)(2,1)S(1)} collective-permute-done((bf16[64,256]{1,0:T(8,128)(2,1)S(1)}, bf16[64,256]{1,0:T(8,128)(2,1)S(1)}, u32[]{:S(2)}, u32[]{:S(2)}) %collective-permute-start.7) | collective-permute-done | bytes 32800 | tf_op jit(solution)/shard_map/ppermute | solution.py:349
  25.4 1.6 %collective-permute-done.8.refs_1_ = bf16[64,256]{1,0:T(8,128)(2,1)S(1)} collective-permute-done((bf16[64,256]{1,0:T(8,128)(2,1)S(1)}, bf16[64,256]{1,0:T(8,128)(2,1)S(1)}, u32[]{:S(2)}, u32[]{:S(2)}) %collective-permute-start.8) | collective-permute-done | bytes 32800 | tf_op jit(solution)/shard_map/ppermute | solution.py:349
  27.0 0.0 collective-permute-done.9.refs_2_
  27.0 0.0 copy-start.3
  27.0 0.0 copy-start.4
  27.0 0.0 copy-start.2
  27.0 0.3 %collective-permute-start.11 = (bf16[128,256]{1,0:T(8,128)(2,1)S(1)}, bf16[128,256]{1,0:T(8,128)(2,1)S(1)}, u32[]{:S(2)}, u32[]{:S(2)}) collective-permute-start(bf16[128,256]{1,0:T(8,128)(2,1)S(1)} %get-tuple-element.40), channel_id=1, source_target_pairs={{0,1},{1,0},{2,3},{3,2},{4,5},{5,4},{6,7},{7,6},{8,9},{9,8},{10,11... | collective-permute-start | bytes 196616 | tf_op jit(solution)/shard_map/ppermute | solution.py:349
  27.3 0.0 copy-done
  27.3 0.0 copy-done.1
  27.3 0.3 %copy-done.3 = f32[3,768]{1,0:T(4,128)S(1)} copy-done((f32[3,768]{1,0:T(4,128)S(1)}, f32[3,768]{1,0:T(4,128)}, u32[]{:S(2)}) %copy-start.3) | copy-done | bytes 9240
  27.7 0.0 copy-done.4
  27.7 0.3 %shard_map.109.query_ref = f32[256,256]{1,0:T(8,128)S(1)} custom-call(bf16[256,256]{1,0:T(8,128)(2,1)S(1)} %copy-done.1, f32[1,256]{1,0:T(1,128)S(1)} %bitcast.3, bf16[256,768]{1,0:T(8,128)(2,1)S(1)} %copy-done, f32[3,768]{1,0:T(4,128)S(1)} %copy-done.3), custom_call_target="tpu_custom_call" | custom-call | flops 33554432 | bytes 800000 | tf_op jit(solution)/shard_map/pallas_call | solution.py:26
  28.0 0.3 %collective-permute-done.11.refs_1_ = bf16[128,256]{1,0:T(8,128)(2,1)S(1)} collective-permute-done((bf16[128,256]{1,0:T(8,128)(2,1)S(1)}, bf16[128,256]{1,0:T(8,128)(2,1)S(1)}, u32[]{:S(2)}, u32[]{:S(2)}) %collective-permute-start.11) | collective-permute-done | bytes 65568 | tf_op jit(solution)/shard_map/ppermute | solution.py:349
  28.3 0.0 copy-done.2
  28.3 0.9 %shard_map.116 = bf16[256,256]{1,0:T(8,128)(2,1)} custom-call(f32[256,256]{1,0:T(8,128)S(1)} %shard_map.109.query_ref, bf16[256,256]{1,0:T(8,128)(2,1)S(1)} %copy-done.2, bf16[128,256]{1,0:T(8,128)(2,1)S(1)} %get-tuple-element.39.refs_0_, bf16[128,256]{1,0:T(8,128)(2,1)S(1)} %collective-permute-done.11.refs_1_), custom_call_target="tpu_custom_call" | custom-call | flops 33554432 | bytes 600000 | tf_op jit(solution)/shard_map/pallas_call | solution.py:26
  (4 shorter events, 0.1 us)
Async XLA Ops:
  0.0 16.7 %copy-start.7 = (f32[32,256]{1,0:T(8,128)S(1)}, f32[32,256]{1,0:T(8,128)}, u32[]{:S(2)}) copy-start(f32[32,256]{1,0:T(8,128)} %constant.7.clone.twist_ref) | copy-start | bytes 98308
  1.8 3.1 %collective-permute-start = (bf16[3,136,128]{2,1,0:T(8,128)(2,1)S(1)}, bf16[3,136,128]{2,1,0:T(8,128)(2,1)S(1)}, u32[]{:S(2)}, u32[]{:S(2)}) collective-permute-start(bf16[3,136,128]{2,1,0:T(8,128)(2,1)S(1)} %get-tuple-element.24), channel_id=1, source_target_pairs={{0,1},{1,0},{2,3},{3,2},{4,5},{5,4},{6,7},{7,6},{8,9},{9,8},{10,11... | collective-permute-start | bytes 313352 | tf_op jit(solution)/shard_map/ppermute | solution.py:349
  2.3 7.1 %collective-permute-start.4 = (bf16[280,128]{1,0:T(8,128)(2,1)S(1)}, bf16[280,128]{1,0:T(8,128)(2,1)S(1)}, u32[]{:S(2)}, u32[]{:S(2)}) collective-permute-start(bf16[280,128]{1,0:T(8,128)(2,1)S(1)} %get-tuple-element.28), channel_id=1, source_target_pairs={{0,2},{1,3},{2,0},{3,1},{4,6},{5,7},{6,4},{7,5},{8,10},{9,11},{10,... | collective-permute-start | bytes 215048 | tf_op jit(solution)/shard_map/ppermute | solution.py:349
  4.9 11.8 %copy-start.5 = (bf16[512,256]{1,0:T(8,128)(2,1)S(1)}, bf16[512,256]{1,0:T(8,128)(2,1)}, u32[]{:S(2)}) copy-start(bf16[512,256]{1,0:T(8,128)(2,1)} %constant.6.clone.first_ref) | copy-start | bytes 786436
  4.9 11.8 %copy-start.6 = (bf16[256,512]{1,0:T(8,128)(2,1)S(1)}, bf16[256,512]{1,0:T(8,128)(2,1)}, u32[]{:S(2)}) copy-start(bf16[256,512]{1,0:T(8,128)(2,1)} %constant.8.clone.inner_ref) | copy-start | bytes 786436
  4.9 6.8 %collective-permute-start.1 = (bf16[264,128]{1,0:T(8,128)(2,1)S(1)}, bf16[264,128]{1,0:T(8,128)(2,1)S(1)}, u32[]{:S(2)}, u32[]{:S(2)}) collective-permute-start(bf16[264,128]{1,0:T(8,128)(2,1)S(1)} %get-tuple-element.25), channel_id=1, source_target_pairs={{0,12},{1,15},{2,14},{3,13},{4,8},{5,11},{6,10},{7,9},{8,4},{9,7},... | collective-permute-start | bytes 202760 | tf_op jit(solution)/shard_map/ppermute | solution.py:349
  8.6 6.6 %collective-permute-start.2 = (bf16[264,128]{1,0:T(8,128)(2,1)S(1)}, bf16[264,128]{1,0:T(8,128)(2,1)S(1)}, u32[]{:S(2)}, u32[]{:S(2)}) collective-permute-start(bf16[264,128]{1,0:T(8,128)(2,1)S(1)} %get-tuple-element.26), channel_id=1, source_target_pairs={{0,8},{1,11},{2,10},{3,9},{4,12},{5,15},{6,14},{7,13},{8,0},{9,3},... | collective-permute-start | bytes 202760 | tf_op jit(solution)/shard_map/ppermute | solution.py:349
  8.6 6.6 %collective-permute-start.3 = (bf16[264,128]{1,0:T(8,128)(2,1)S(1)}, bf16[264,128]{1,0:T(8,128)(2,1)S(1)}, u32[]{:S(2)}, u32[]{:S(2)}) collective-permute-start(bf16[264,128]{1,0:T(8,128)(2,1)S(1)} %get-tuple-element.27), channel_id=1, source_target_pairs={{0,4},{1,7},{2,6},{3,5},{4,0},{5,3},{6,2},{7,1},{8,12},{9,15},{10,... | collective-permute-start | bytes 202760 | tf_op jit(solution)/shard_map/ppermute | solution.py:349
  15.2 1.4 %collective-permute-start.5 = (bf16[544,128]{1,0:T(8,128)(2,1)S(1)}, bf16[544,128]{1,0:T(8,128)(2,1)S(1)}, u32[]{:S(2)}, u32[]{:S(2)}) collective-permute-start(bf16[544,128]{1,0:T(8,128)(2,1)S(1)} %get-tuple-element.31), channel_id=1, source_target_pairs={{0,1},{1,0},{2,3},{3,2},{4,5},{5,4},{6,7},{7,6},{8,9},{9,8},{10,11... | collective-permute-start | bytes 417800 | tf_op jit(solution)/shard_map/ppermute | solution.py:349
  16.7 10.7 %copy-start = (bf16[256,768]{1,0:T(8,128)(2,1)S(1)}, bf16[256,768]{1,0:T(8,128)(2,1)}, u32[]{:S(2)}) copy-start(bf16[256,768]{1,0:T(8,128)(2,1)} %refs_2_.1) | copy-start | bytes 1179652
  18.0 1.3 %collective-permute-start.6 = (bf16[3,32,256]{2,1,0:T(8,128)(2,1)S(1)}, bf16[3,32,256]{2,1,0:T(8,128)(2,1)S(1)}, u32[]{:S(2)}, u32[]{:S(2)}) collective-permute-start(bf16[3,32,256]{2,1,0:T(8,128)(2,1)S(1)} %get-tuple-element.33), channel_id=1, source_target_pairs={{0,1},{1,0},{2,3},{3,2},{4,5},{5,4},{6,7},{7,6},{8,9},{9,8},{10,11... | collective-permute-start | bytes 147464 | tf_op jit(solution)/shard_map/ppermute | solution.py:349
  18.2 5.6 %collective-permute-start.10 = (bf16[80,256]{1,0:T(8,128)(2,1)S(1)}, bf16[80,256]{1,0:T(8,128)(2,1)S(1)}, u32[]{:S(2)}, u32[]{:S(2)}) collective-permute-start(bf16[80,256]{1,0:T(8,128)(2,1)S(1)} %get-tuple-element.37), channel_id=1, source_target_pairs={{0,2},{1,3},{2,0},{3,1},{4,6},{5,7},{6,4},{7,5},{8,10},{9,11},{10,... | collective-permute-start | bytes 122888 | tf_op jit(solution)/shard_map/ppermute | solution.py:349
  19.3 8.0 %copy-start.1 = (bf16[256,256]{1,0:T(8,128)(2,1)S(1)}, bf16[256,256]{1,0:T(8,128)(2,1)}, u32[]{:S(2)}) copy-start(bf16[256,256]{1,0:T(8,128)(2,1)} %refs_0_.1) | copy-start | bytes 393220
  19.3 6.0 %collective-permute-start.7 = (bf16[64,256]{1,0:T(8,128)(2,1)S(1)}, bf16[64,256]{1,0:T(8,128)(2,1)S(1)}, u32[]{:S(2)}, u32[]{:S(2)}) collective-permute-start(bf16[64,256]{1,0:T(8,128)(2,1)S(1)} %get-tuple-element.34), channel_id=1, source_target_pairs={{0,12},{1,15},{2,14},{3,13},{4,8},{5,11},{6,10},{7,9},{8,4},{9,7},... | collective-permute-start | bytes 98312 | tf_op jit(solution)/shard_map/ppermute | solution.py:349
  21.9 5.1 %collective-permute-start.8 = (bf16[64,256]{1,0:T(8,128)(2,1)S(1)}, bf16[64,256]{1,0:T(8,128)(2,1)S(1)}, u32[]{:S(2)}, u32[]{:S(2)}) collective-permute-start(bf16[64,256]{1,0:T(8,128)(2,1)S(1)} %get-tuple-element.35), channel_id=1, source_target_pairs={{0,8},{1,11},{2,10},{3,9},{4,12},{5,15},{6,14},{7,13},{8,0},{9,3},... | collective-permute-start | bytes 98312 | tf_op jit(solution)/shard_map/ppermute | solution.py:349
  22.1 4.9 %collective-permute-start.9 = (bf16[64,256]{1,0:T(8,128)(2,1)S(1)}, bf16[64,256]{1,0:T(8,128)(2,1)S(1)}, u32[]{:S(2)}, u32[]{:S(2)}) collective-permute-start(bf16[64,256]{1,0:T(8,128)(2,1)S(1)} %get-tuple-element.36), channel_id=1, source_target_pairs={{0,4},{1,7},{2,6},{3,5},{4,0},{5,3},{6,2},{7,1},{8,12},{9,15},{10,... | collective-permute-start | bytes 98312 | tf_op jit(solution)/shard_map/ppermute | solution.py:349
  27.0 0.7 %copy-start.3 = (f32[3,768]{1,0:T(4,128)S(1)}, f32[3,768]{1,0:T(4,128)}, u32[]{:S(2)}) copy-start(f32[3,768]{1,0:T(4,128)} %refs_3_.1) | copy-start | bytes 27652
  27.0 0.7 %copy-start.4 = (f32[256]{0:T(256)S(1)}, f32[256]{0:T(256)}, u32[]{:S(2)}) copy-start(f32[256]{0:T(256)} %param.12) | copy-start | bytes 3076
  27.0 1.3 %copy-start.2 = (bf16[256,256]{1,0:T(8,128)(2,1)S(1)}, bf16[256,256]{1,0:T(8,128)(2,1)}, u32[]{:S(2)}) copy-start(bf16[256,256]{1,0:T(8,128)(2,1)} %w_ref.3) | copy-start | bytes 393220
  27.0 1.3 %collective-permute-start.11 = (bf16[128,256]{1,0:T(8,128)(2,1)S(1)}, bf16[128,256]{1,0:T(8,128)(2,1)S(1)}, u32[]{:S(2)}, u32[]{:S(2)}) collective-permute-start(bf16[128,256]{1,0:T(8,128)(2,1)S(1)} %get-tuple-element.40), channel_id=1, source_target_pairs={{0,1},{1,0},{2,3},{3,2},{4,5},{5,4},{6,7},{7,6},{8,9},{9,8},{10,11... | collective-permute-start | bytes 196616 | tf_op jit(solution)/shard_map/ppermute | solution.py:349

commit v22 on v21

--- a/solution.py
+++ b/solution.py
@@ -139,14 +139,14 @@
                 rim_ref[device, 0 : edge // 2, :] = rims[begin : begin + edge // 2]
 
 
-def normed_of(tokens_ref, gain_ref):
+def scaled_of(tokens_ref, gain_ref):
     inputs = tokens_ref[...].astype(jnp.float32)
     mean_sq = jnp.mean(inputs * inputs, axis=-1, keepdims=True)
-    return (inputs * lax.rsqrt(mean_sq + epsilon) * gain_ref[...]).astype(jnp.bfloat16)
-
-
-def projected_of(normed, weights):
-    projected = jnp.dot(normed, weights, preferred_element_type=jnp.float32)
+    return (inputs * gain_ref[...]).astype(jnp.bfloat16), lax.rsqrt(mean_sq + epsilon)
+
+
+def projected_of(scaled, factor, weights):
+    projected = jnp.dot(scaled, weights, preferred_element_type=jnp.float32) * factor
     projected = projected.astype(jnp.bfloat16).astype(jnp.float32)
     return jnp.concatenate([projected, jnp.zeros((edge, projected.shape[1]), jnp.float32)])
 
@@ -161,7 +161,8 @@
 def query_body(tokens_ref, gain_ref, w_ref, short_ref, query_ref):
     rows, width = tokens_ref.shape
     cols = slice(0, width)
-    query = short_mix(projected_of(normed_of(tokens_ref, gain_ref), w_ref[:, cols]), short_ref[:, cols])
+    projected = projected_of(*scaled_of(tokens_ref, gain_ref), w_ref[:, cols])
+    query = short_mix(projected, short_ref[:, cols])
     query_ref[...] = query[0:rows]
     row = lax.broadcasted_iota(jnp.int32, (edge, width), 0)
     query_ref[0:edge, :] = jnp.where(row < short_ref.shape[0] - 1, 1.0, query[0:edge])
@@ -178,16 +179,18 @@
         copy.start()
     copies[0].wait()
     copies[1].wait()
-    normed = normed_of(tokens_ref, gain_ref)
+    scaled, factor = scaled_of(tokens_ref, gain_ref)
     copies[2].wait()
     copies[3].wait()
     query_cols, cols = slice(0, width), slice(width, 3 * width)
-    mixed = short_mix(projected_of(normed, w_ref[:, cols]), short_ref[:, cols])
+    mixed = short_mix(projected_of(scaled, factor, w_ref[:, cols]), short_ref[:, cols])
     key, value = mixed[:, 0:width], mixed[:, width:]
     put_columns(packed_ref, 0, (key[0:rows] * value[0:rows]).astype(jnp.bfloat16).T)
     rims = [(key[0:edge], key[rows:]), (value[0:edge], value[rows:])]
-    some = jnp.concatenate([normed[0 : 2 * edge], normed[rows - 2 * edge :]])
-    some = short_mix(projected_of(some, w_ref[:, query_cols]), short_ref[:, query_cols])
+    some, some_factor = (
+        jnp.concatenate([part[0 : 2 * edge], part[rows - 2 * edge :]]) for part in (scaled, factor)
+    )
+    some = short_mix(projected_of(some, some_factor, w_ref[:, query_cols]), short_ref[:, query_cols])
     put_rim(packed_ref, rim_ref, [*rims, (some[0:edge], some[4 * edge :])])
     for copy in copies[4:]:
         copy.wait()

time: 29.4 us -> 29.4 us (level)
  no operation moved by 1% of the time
where the time goes in v22:
time: 29.4 us; the launch traced here: 29.2 us
  starting transfers between devices  13.7 us (47%)
  waiting for transfers between devices  10.7 us (36%)
  Pallas kernels  4.37 us (15%)
  local copies, waits for them, and re-layouts  0.36 us (1%)
    ppermute x12, starting transfers between devices, permute(): lax.ppermute(array, seq, [(i, partner(i)) for i in range(lax.axis_size(se...  13.7 us
    ppermute x12, waiting for transfers between devices, permute(): lax.ppermute(array, seq, [(i, partner(i)) for i in range(lax.axis_size(se...  10.7 us
    pallas_call x8, Pallas kernels, call(): pl.pallas_call(body, out_shape=outs, in_specs=[whole(space) for space in...  4.37 us
  transfers between devices with their start and end apart: 12, of which 7 were waited for; matrix products, arithmetic and copies ran while one was open for 0% of the time, Pallas kernels for 1%

profile of v22, /device:TPU:0, one launch (start us, length us, event | category | flops | bytes accessed | tf_op | source)
XLA Modules:
  0.0 29.2 jit_solution(12922669784999888068)
XLA Ops:
  0.0 0.0 copy-start.7
  0.0 1.8 %shard_map.110 = (bf16[3,136,128]{2,1,0:T(8,128)(2,1)S(1)}, bf16[3,136,128]{2,1,0:T(8,128)(2,1)S(1)}, bf16[280,128]{1,0:T(8,128)(2,1)S(1)}, bf16[136,128]{1,0:T(8,128)(2,1)S(1)}) custom-call(bf16[256,256]{1,0:T(8,128)(2,1)} %refs_0_.1, f32[1,256]{1,0:T(1,128)} %bitcast.2, bf16[256,768]{1,0:T(8,128)(2,1)} %refs_2_.1, f32[3,768]{1,0:T(4,128)} %refs_3_.1, ...), custom_call_target="tpu_custom_call" | custom-call | flops 100663296 | bytes 1500000 | tf_op jit(solution)/shard_map/pallas_call | solution.py:26
  1.8 0.5 %collective-permute-start = (bf16[3,136,128]{2,1,0:T(8,128)(2,1)S(1)}, bf16[3,136,128]{2,1,0:T(8,128)(2,1)S(1)}, u32[]{:S(2)}, u32[]{:S(2)}) collective-permute-start(bf16[3,136,128]{2,1,0:T(8,128)(2,1)S(1)} %get-tuple-element.24), channel_id=1, source_target_pairs={{0,1},{1,0},{2,3},{3,2},{4,5},{5,4},{6,7},{7,6},{8,9},{9,8},{10,11... | collective-permute-start | bytes 313352 | tf_op jit(solution)/shard_map/ppermute | solution.py:352
  2.3 2.6 %collective-permute-start.4 = (bf16[280,128]{1,0:T(8,128)(2,1)S(1)}, bf16[280,128]{1,0:T(8,128)(2,1)S(1)}, u32[]{:S(2)}, u32[]{:S(2)}) collective-permute-start(bf16[280,128]{1,0:T(8,128)(2,1)S(1)} %get-tuple-element.28), channel_id=1, source_target_pairs={{0,2},{1,3},{2,0},{3,1},{4,6},{5,7},{6,4},{7,5},{8,10},{9,11},{10,... | collective-permute-start | bytes 215048 | tf_op jit(solution)/shard_map/ppermute | solution.py:352
  4.9 0.0 collective-permute-done.got_ref
  4.9 0.0 copy-start.5
  4.9 0.0 copy-start.6
  4.9 3.7 %collective-permute-start.1 = (bf16[264,128]{1,0:T(8,128)(2,1)S(1)}, bf16[264,128]{1,0:T(8,128)(2,1)S(1)}, u32[]{:S(2)}, u32[]{:S(2)}) collective-permute-start(bf16[264,128]{1,0:T(8,128)(2,1)S(1)} %get-tuple-element.25), channel_id=1, source_target_pairs={{0,12},{1,15},{2,14},{3,13},{4,8},{5,11},{6,10},{7,9},{8,4},{9,7},... | collective-permute-start | bytes 202760 | tf_op jit(solution)/shard_map/ppermute | solution.py:352
  8.6 0.0 collective-permute-start.2
  8.6 0.8 %collective-permute-start.3 = (bf16[264,128]{1,0:T(8,128)(2,1)S(1)}, bf16[264,128]{1,0:T(8,128)(2,1)S(1)}, u32[]{:S(2)}, u32[]{:S(2)}) collective-permute-start(bf16[264,128]{1,0:T(8,128)(2,1)S(1)} %get-tuple-element.27), channel_id=1, source_target_pairs={{0,4},{1,7},{2,6},{3,5},{4,0},{5,3},{6,2},{7,1},{8,12},{9,15},{10,... | collective-permute-start | bytes 202760 | tf_op jit(solution)/shard_map/ppermute | solution.py:352
  9.4 0.0 collective-permute-done.4.refs_3_
  9.4 2.4 %collective-permute-done.1.refs_0_ = bf16[264,128]{1,0:T(8,128)(2,1)S(1)} collective-permute-done((bf16[264,128]{1,0:T(8,128)(2,1)S(1)}, bf16[264,128]{1,0:T(8,128)(2,1)S(1)}, u32[]{:S(2)}, u32[]{:S(2)}) %collective-permute-start.1) | collective-permute-done | bytes 67616 | tf_op jit(solution)/shard_map/ppermute | solution.py:352
  11.8 3.5 %collective-permute-done.2.refs_1_ = bf16[264,128]{1,0:T(8,128)(2,1)S(1)} collective-permute-done((bf16[264,128]{1,0:T(8,128)(2,1)S(1)}, bf16[264,128]{1,0:T(8,128)(2,1)S(1)}, u32[]{:S(2)}, u32[]{:S(2)}) %collective-permute-start.2) | collective-permute-done | bytes 67616 | tf_op jit(solution)/shard_map/ppermute | solution.py:352
  15.2 0.0 collective-permute-done.3.refs_2_
  15.2 0.2 collective-permute-start.5
  15.4 1.2 %collective-permute-done.5.refs_1_ = bf16[544,128]{1,0:T(8,128)(2,1)S(1)} collective-permute-done((bf16[544,128]{1,0:T(8,128)(2,1)S(1)}, bf16[544,128]{1,0:T(8,128)(2,1)S(1)}, u32[]{:S(2)}, u32[]{:S(2)}) %collective-permute-start.5) | collective-permute-done | bytes 139296 | tf_op jit(solution)/shard_map/ppermute | solution.py:352
  16.7 0.0 copy-done.7
  16.7 0.0 copy-done.5
  16.7 0.0 copy-done.6
  16.7 0.0 copy-start
  16.7 1.3 %shard_map.113 = (bf16[3,32,256]{2,1,0:T(8,128)(2,1)S(1)}, bf16[3,32,256]{2,1,0:T(8,128)(2,1)S(1)}, bf16[80,256]{1,0:T(8,128)(2,1)S(1)}, bf16[32,256]{1,0:T(8,128)(2,1)S(1)}) custom-call(bf16[512,256]{1,0:T(8,128)(2,1)S(1)} %copy-done.5, f32[32,256]{1,0:T(8,128)S(1)} %copy-done.7, bf16[256,512]{1,0:T(8,128)(2,1)S(1)} %copy-done.6, ...), custom_call_target="tpu_custom_call" | custom-call | flops 603979776 | bytes 2000000 | tf_op jit(solution)/shard_map/pallas_call | solution.py:26
  18.0 0.2 collective-permute-start.6
  18.3 1.0 %collective-permute-start.10 = (bf16[80,256]{1,0:T(8,128)(2,1)S(1)}, bf16[80,256]{1,0:T(8,128)(2,1)S(1)}, u32[]{:S(2)}, u32[]{:S(2)}) collective-permute-start(bf16[80,256]{1,0:T(8,128)(2,1)S(1)} %get-tuple-element.37), channel_id=1, source_target_pairs={{0,2},{1,3},{2,0},{3,1},{4,6},{5,7},{6,4},{7,5},{8,10},{9,11},{10,... | collective-permute-start | bytes 122888 | tf_op jit(solution)/shard_map/ppermute | solution.py:352
  19.2 0.1 collective-permute-done.6.got_ref
  19.3 0.0 copy-start.1
  19.4 2.5 %collective-permute-start.7 = (bf16[64,256]{1,0:T(8,128)(2,1)S(1)}, bf16[64,256]{1,0:T(8,128)(2,1)S(1)}, u32[]{:S(2)}, u32[]{:S(2)}) collective-permute-start(bf16[64,256]{1,0:T(8,128)(2,1)S(1)} %get-tuple-element.34), channel_id=1, source_target_pairs={{0,12},{1,15},{2,14},{3,13},{4,8},{5,11},{6,10},{7,9},{8,4},{9,7},... | collective-permute-start | bytes 98312 | tf_op jit(solution)/shard_map/ppermute | solution.py:352
  21.9 0.2 collective-permute-start.8
  22.1 1.7 %collective-permute-start.9 = (bf16[64,256]{1,0:T(8,128)(2,1)S(1)}, bf16[64,256]{1,0:T(8,128)(2,1)S(1)}, u32[]{:S(2)}, u32[]{:S(2)}) collective-permute-start(bf16[64,256]{1,0:T(8,128)(2,1)S(1)} %get-tuple-element.36), channel_id=1, source_target_pairs={{0,4},{1,7},{2,6},{3,5},{4,0},{5,3},{6,2},{7,1},{8,12},{9,15},{10,... | collective-permute-start | bytes 98312 | tf_op jit(solution)/shard_map/ppermute | solution.py:352
  23.8 0.0 collective-permute-done.10.refs_3_
  23.8 1.6 %collective-permute-done.7.refs_0_ = bf16[64,256]{1,0:T(8,128)(2,1)S(1)} collective-permute-done((bf16[64,256]{1,0:T(8,128)(2,1)S(1)}, bf16[64,256]{1,0:T(8,128)(2,1)S(1)}, u32[]{:S(2)}, u32[]{:S(2)}) %collective-permute-start.7) | collective-permute-done | bytes 32800 | tf_op jit(solution)/shard_map/ppermute | solution.py:352
  25.4 1.6 %collective-permute-done.8.refs_1_ = bf16[64,256]{1,0:T(8,128)(2,1)S(1)} collective-permute-done((bf16[64,256]{1,0:T(8,128)(2,1)S(1)}, bf16[64,256]{1,0:T(8,128)(2,1)S(1)}, u32[]{:S(2)}, u32[]{:S(2)}) %collective-permute-start.8) | collective-permute-done | bytes 32800 | tf_op jit(solution)/shard_map/ppermute | solution.py:352
  27.0 0.0 collective-permute-done.9.refs_2_
  27.0 0.0 copy-start.3
  27.0 0.0 copy-start.4
  27.0 0.0 copy-start.2
  27.0 0.3 %collective-permute-start.11 = (bf16[128,256]{1,0:T(8,128)(2,1)S(1)}, bf16[128,256]{1,0:T(8,128)(2,1)S(1)}, u32[]{:S(2)}, u32[]{:S(2)}) collective-permute-start(bf16[128,256]{1,0:T(8,128)(2,1)S(1)} %get-tuple-element.40), channel_id=1, source_target_pairs={{0,1},{1,0},{2,3},{3,2},{4,5},{5,4},{6,7},{7,6},{8,9},{9,8},{10,11... | collective-permute-start | bytes 196616 | tf_op jit(solution)/shard_map/ppermute | solution.py:352
  27.3 0.0 copy-done
  27.3 0.0 copy-done.1
  27.3 0.3 %copy-done.3 = f32[3,768]{1,0:T(4,128)S(1)} copy-done((f32[3,768]{1,0:T(4,128)S(1)}, f32[3,768]{1,0:T(4,128)}, u32[]{:S(2)}) %copy-start.3) | copy-done | bytes 9240
  27.7 0.0 copy-done.4
  27.7 0.3 shard_map.109.query_ref
  27.9 0.4 %collective-permute-done.11.refs_1_ = bf16[128,256]{1,0:T(8,128)(2,1)S(1)} collective-permute-done((bf16[128,256]{1,0:T(8,128)(2,1)S(1)}, bf16[128,256]{1,0:T(8,128)(2,1)S(1)}, u32[]{:S(2)}, u32[]{:S(2)}) %collective-permute-start.11) | collective-permute-done | bytes 65568 | tf_op jit(solution)/shard_map/ppermute | solution.py:352
  28.3 0.0 copy-done.2
  28.3 0.9 %shard_map.116 = bf16[256,256]{1,0:T(8,128)(2,1)} custom-call(f32[256,256]{1,0:T(8,128)S(1)} %shard_map.109.query_ref, bf16[256,256]{1,0:T(8,128)(2,1)S(1)} %copy-done.2, bf16[128,256]{1,0:T(8,128)(2,1)S(1)} %get-tuple-element.39.refs_0_, bf16[128,256]{1,0:T(8,128)(2,1)S(1)} %collective-permute-done.11.refs_1_), custom_call_target="tpu_custom_call" | custom-call | flops 33554432 | bytes 600000 | tf_op jit(solution)/shard_map/pallas_call | solution.py:26
  (4 shorter events, 0.1 us)
Async XLA Ops:
  0.0 16.7 %copy-start.7 = (f32[32,256]{1,0:T(8,128)S(1)}, f32[32,256]{1,0:T(8,128)}, u32[]{:S(2)}) copy-start(f32[32,256]{1,0:T(8,128)} %constant.7.clone.twist_ref) | copy-start | bytes 98308
  1.8 3.1 %collective-permute-start = (bf16[3,136,128]{2,1,0:T(8,128)(2,1)S(1)}, bf16[3,136,128]{2,1,0:T(8,128)(2,1)S(1)}, u32[]{:S(2)}, u32[]{:S(2)}) collective-permute-start(bf16[3,136,128]{2,1,0:T(8,128)(2,1)S(1)} %get-tuple-element.24), channel_id=1, source_target_pairs={{0,1},{1,0},{2,3},{3,2},{4,5},{5,4},{6,7},{7,6},{8,9},{9,8},{10,11... | collective-permute-start | bytes 313352 | tf_op jit(solution)/shard_map/ppermute | solution.py:352
  2.3 7.1 %collective-permute-start.4 = (bf16[280,128]{1,0:T(8,128)(2,1)S(1)}, bf16[280,128]{1,0:T(8,128)(2,1)S(1)}, u32[]{:S(2)}, u32[]{:S(2)}) collective-permute-start(bf16[280,128]{1,0:T(8,128)(2,1)S(1)} %get-tuple-element.28), channel_id=1, source_target_pairs={{0,2},{1,3},{2,0},{3,1},{4,6},{5,7},{6,4},{7,5},{8,10},{9,11},{10,... | collective-permute-start | bytes 215048 | tf_op jit(solution)/shard_map/ppermute | solution.py:352
  4.9 11.8 %copy-start.5 = (bf16[512,256]{1,0:T(8,128)(2,1)S(1)}, bf16[512,256]{1,0:T(8,128)(2,1)}, u32[]{:S(2)}) copy-start(bf16[512,256]{1,0:T(8,128)(2,1)} %constant.6.clone.first_ref) | copy-start | bytes 786436
  4.9 11.8 %copy-start.6 = (bf16[256,512]{1,0:T(8,128)(2,1)S(1)}, bf16[256,512]{1,0:T(8,128)(2,1)}, u32[]{:S(2)}) copy-start(bf16[256,512]{1,0:T(8,128)(2,1)} %constant.8.clone.inner_ref) | copy-start | bytes 786436
  4.9 6.8 %collective-permute-start.1 = (bf16[264,128]{1,0:T(8,128)(2,1)S(1)}, bf16[264,128]{1,0:T(8,128)(2,1)S(1)}, u32[]{:S(2)}, u32[]{:S(2)}) collective-permute-start(bf16[264,128]{1,0:T(8,128)(2,1)S(1)} %get-tuple-element.25), channel_id=1, source_target_pairs={{0,12},{1,15},{2,14},{3,13},{4,8},{5,11},{6,10},{7,9},{8,4},{9,7},... | collective-permute-start | bytes 202760 | tf_op jit(solution)/shard_map/ppermute | solution.py:352
  8.6 6.6 %collective-permute-start.2 = (bf16[264,128]{1,0:T(8,128)(2,1)S(1)}, bf16[264,128]{1,0:T(8,128)(2,1)S(1)}, u32[]{:S(2)}, u32[]{:S(2)}) collective-permute-start(bf16[264,128]{1,0:T(8,128)(2,1)S(1)} %get-tuple-element.26), channel_id=1, source_target_pairs={{0,8},{1,11},{2,10},{3,9},{4,12},{5,15},{6,14},{7,13},{8,0},{9,3},... | collective-permute-start | bytes 202760 | tf_op jit(solution)/shard_map/ppermute | solution.py:352
  8.6 6.6 %collective-permute-start.3 = (bf16[264,128]{1,0:T(8,128)(2,1)S(1)}, bf16[264,128]{1,0:T(8,128)(2,1)S(1)}, u32[]{:S(2)}, u32[]{:S(2)}) collective-permute-start(bf16[264,128]{1,0:T(8,128)(2,1)S(1)} %get-tuple-element.27), channel_id=1, source_target_pairs={{0,4},{1,7},{2,6},{3,5},{4,0},{5,3},{6,2},{7,1},{8,12},{9,15},{10,... | collective-permute-start | bytes 202760 | tf_op jit(solution)/shard_map/ppermute | solution.py:352
  15.2 1.4 %collective-permute-start.5 = (bf16[544,128]{1,0:T(8,128)(2,1)S(1)}, bf16[544,128]{1,0:T(8,128)(2,1)S(1)}, u32[]{:S(2)}, u32[]{:S(2)}) collective-permute-start(bf16[544,128]{1,0:T(8,128)(2,1)S(1)} %get-tuple-element.31), channel_id=1, source_target_pairs={{0,1},{1,0},{2,3},{3,2},{4,5},{5,4},{6,7},{7,6},{8,9},{9,8},{10,11... | collective-permute-start | bytes 417800 | tf_op jit(solution)/shard_map/ppermute | solution.py:352
  16.7 10.7 %copy-start = (bf16[256,768]{1,0:T(8,128)(2,1)S(1)}, bf16[256,768]{1,0:T(8,128)(2,1)}, u32[]{:S(2)}) copy-start(bf16[256,768]{1,0:T(8,128)(2,1)} %refs_2_.1) | copy-start | bytes 1179652
  18.0 1.3 %collective-permute-start.6 = (bf16[3,32,256]{2,1,0:T(8,128)(2,1)S(1)}, bf16[3,32,256]{2,1,0:T(8,128)(2,1)S(1)}, u32[]{:S(2)}, u32[]{:S(2)}) collective-permute-start(bf16[3,32,256]{2,1,0:T(8,128)(2,1)S(1)} %get-tuple-element.33), channel_id=1, source_target_pairs={{0,1},{1,0},{2,3},{3,2},{4,5},{5,4},{6,7},{7,6},{8,9},{9,8},{10,11... | collective-permute-start | bytes 147464 | tf_op jit(solution)/shard_map/ppermute | solution.py:352
  18.3 5.6 %collective-permute-start.10 = (bf16[80,256]{1,0:T(8,128)(2,1)S(1)}, bf16[80,256]{1,0:T(8,128)(2,1)S(1)}, u32[]{:S(2)}, u32[]{:S(2)}) collective-permute-start(bf16[80,256]{1,0:T(8,128)(2,1)S(1)} %get-tuple-element.37), channel_id=1, source_target_pairs={{0,2},{1,3},{2,0},{3,1},{4,6},{5,7},{6,4},{7,5},{8,10},{9,11},{10,... | collective-permute-start | bytes 122888 | tf_op jit(solution)/shard_map/ppermute | solution.py:352
  19.3 8.0 %copy-start.1 = (bf16[256,256]{1,0:T(8,128)(2,1)S(1)}, bf16[256,256]{1,0:T(8,128)(2,1)}, u32[]{:S(2)}) copy-start(bf16[256,256]{1,0:T(8,128)(2,1)} %refs_0_.1) | copy-start | bytes 393220
  19.4 6.0 %collective-permute-start.7 = (bf16[64,256]{1,0:T(8,128)(2,1)S(1)}, bf16[64,256]{1,0:T(8,128)(2,1)S(1)}, u32[]{:S(2)}, u32[]{:S(2)}) collective-permute-start(bf16[64,256]{1,0:T(8,128)(2,1)S(1)} %get-tuple-element.34), channel_id=1, source_target_pairs={{0,12},{1,15},{2,14},{3,13},{4,8},{5,11},{6,10},{7,9},{8,4},{9,7},... | collective-permute-start | bytes 98312 | tf_op jit(solution)/shard_map/ppermute | solution.py:352
  21.9 5.1 %collective-permute-start.8 = (bf16[64,256]{1,0:T(8,128)(2,1)S(1)}, bf16[64,256]{1,0:T(8,128)(2,1)S(1)}, u32[]{:S(2)}, u32[]{:S(2)}) collective-permute-start(bf16[64,256]{1,0:T(8,128)(2,1)S(1)} %get-tuple-element.35), channel_id=1, source_target_pairs={{0,8},{1,11},{2,10},{3,9},{4,12},{5,15},{6,14},{7,13},{8,0},{9,3},... | collective-permute-start | bytes 98312 | tf_op jit(solution)/shard_map/ppermute | solution.py:352
  22.1 4.9 %collective-permute-start.9 = (bf16[64,256]{1,0:T(8,128)(2,1)S(1)}, bf16[64,256]{1,0:T(8,128)(2,1)S(1)}, u32[]{:S(2)}, u32[]{:S(2)}) collective-permute-start(bf16[64,256]{1,0:T(8,128)(2,1)S(1)} %get-tuple-element.36), channel_id=1, source_target_pairs={{0,4},{1,7},{2,6},{3,5},{4,0},{5,3},{6,2},{7,1},{8,12},{9,15},{10,... | collective-permute-start | bytes 98312 | tf_op jit(solution)/shard_map/ppermute | solution.py:352
  27.0 0.7 %copy-start.3 = (f32[3,768]{1,0:T(4,128)S(1)}, f32[3,768]{1,0:T(4,128)}, u32[]{:S(2)}) copy-start(f32[3,768]{1,0:T(4,128)} %refs_3_.1) | copy-start | bytes 27652
  27.0 0.7 %copy-start.4 = (f32[256]{0:T(256)S(1)}, f32[256]{0:T(256)}, u32[]{:S(2)}) copy-start(f32[256]{0:T(256)} %param.12) | copy-start | bytes 3076
  27.0 1.3 %copy-start.2 = (bf16[256,256]{1,0:T(8,128)(2,1)S(1)}, bf16[256,256]{1,0:T(8,128)(2,1)}, u32[]{:S(2)}) copy-start(bf16[256,256]{1,0:T(8,128)(2,1)} %w_ref.3) | copy-start | bytes 393220
  27.0 1.3 %collective-permute-start.11 = (bf16[128,256]{1,0:T(8,128)(2,1)S(1)}, bf16[128,256]{1,0:T(8,128)(2,1)S(1)}, u32[]{:S(2)}, u32[]{:S(2)}) collective-permute-start(bf16[128,256]{1,0:T(8,128)(2,1)S(1)} %get-tuple-element.40), channel_id=1, source_target_pairs={{0,1},{1,0},{2,3},{3,2},{4,5},{5,4},{6,7},{7,6},{8,9},{9,8},{10,11... | collective-permute-start | bytes 196616 | tf_op jit(solution)/shard_map/ppermute | solution.py:352

commit v23 on v21

--- a/solution.py
+++ b/solution.py
@@ -55,8 +55,11 @@
     )
 
 
-def routes_of(chips):
-    return [(d, d + 1) for d in range(chips - 2, 1, -2)]
+def routes_of(chips, forward):
+    far = list(range(chips - 2, 1, -2))
+    if forward:
+        far = far[:1] + far[:0:-1]
+    return [(d, d + 1) for d in far]
 
 
 def carried(route, core):
@@ -75,7 +78,7 @@
         if extra:
             out_ref[2 * size : 2 * size + extra, :] = rim_ref[chip ^ distance]
 
-    for turn, route in enumerate(routes_of(lax.axis_size("chip"))):
+    for turn, route in enumerate(routes_of(lax.axis_size("chip"), extra > 0)):
         own, other = carried(route, core)
         put(keep_ref.at[turn], own)
         put(give_ref.at[turn], other)
@@ -123,7 +126,7 @@
 
 def take_routes(keep_ref, got_ref, target_ref, rim_ref=None):
     chip, core = lax.axis_index("chip"), lax.axis_index("core")
-    routes = routes_of(lax.axis_size("chip"))
+    routes = routes_of(lax.axis_size("chip"), rim_ref is not None)
     count = 2 * len(routes) + 2
     size = target_ref.shape[0] // (2 * lax.axis_size("chip"))
     places = [(*carried(route, core), sender) for route in routes for sender in range(2)]
@@ -365,7 +368,7 @@
         [pltpu.VMEM] * 2,
         moved=4 * keep.size,
     )
-    routes = routes_of(lax.axis_size("chip"))
+    routes = routes_of(lax.axis_size("chip"), extra > 0)
     far = [permute(part, lambda i: i ^ 2 * route[i % 2]) for part, route in zip(far, routes)]
     count = 2 * turns + 2
     half = bf16(count * size + count // 2 * extra, lanes)

time: 29.4 us -> 29.6 us (level)
  transfers between devices with their start and end apart: 12 -> 12, of which waited for: 7 -> 6; matrix products, arithmetic and copies ran while one was open for 0% -> 0% of each run, Pallas kernels for 1% -> 1%
where the time goes in v23:
time: 29.6 us; the launch traced here: 29.5 us
  starting transfers between devices  13.9 us (47%)
  waiting for transfers between devices  10.5 us (35%)
  Pallas kernels  4.41 us (15%)
  local copies, waits for them, and re-layouts  0.6 us (2%)
    ppermute x12, starting transfers between devices, permute(): lax.ppermute(array, seq, [(i, partner(i)) for i in range(lax.axis_size(se...  13.9 us
    ppermute x12, waiting for transfers between devices, permute(): lax.ppermute(array, seq, [(i, partner(i)) for i in range(lax.axis_size(se...  10.5 us
    pallas_call x8, Pallas kernels, call(): pl.pallas_call(body, out_shape=outs, in_specs=[whole(space) for space in...  4.41 us
    unnamed x16, local copies, waits for them, and re-layouts  0.6 us
  transfers between devices with their start and end apart: 12, of which 6 were waited for; matrix products, arithmetic and copies ran while one was open for 0% of the time, Pallas kernels for 1%

profile of v23, /device:TPU:0, one launch (start us, length us, event | category | flops | bytes accessed | tf_op | source)
XLA Modules:
  0.0 29.5 jit_solution(17183031558384293763)
XLA Ops:
  0.0 0.0 copy-start.7
  0.0 1.8 %shard_map.110 = (bf16[3,136,128]{2,1,0:T(8,128)(2,1)S(1)}, bf16[3,136,128]{2,1,0:T(8,128)(2,1)S(1)}, bf16[280,128]{1,0:T(8,128)(2,1)S(1)}, bf16[136,128]{1,0:T(8,128)(2,1)S(1)}) custom-call(bf16[256,256]{1,0:T(8,128)(2,1)} %refs_0_.1, f32[1,256]{1,0:T(1,128)} %bitcast.2, bf16[256,768]{1,0:T(8,128)(2,1)} %refs_2_.1, f32[3,768]{1,0:T(4,128)} %refs_3_.1, ...), custom_call_target="tpu_custom_call" | custom-call | flops 100663296 | bytes 1500000 | tf_op jit(solution)/shard_map/pallas_call | solution.py:26
  1.8 0.5 %collective-permute-start = (bf16[3,136,128]{2,1,0:T(8,128)(2,1)S(1)}, bf16[3,136,128]{2,1,0:T(8,128)(2,1)S(1)}, u32[]{:S(2)}, u32[]{:S(2)}) collective-permute-start(bf16[3,136,128]{2,1,0:T(8,128)(2,1)S(1)} %get-tuple-element.24), channel_id=1, source_target_pairs={{0,1},{1,0},{2,3},{3,2},{4,5},{5,4},{6,7},{7,6},{8,9},{9,8},{10,11... | collective-permute-start | bytes 313352 | tf_op jit(solution)/shard_map/ppermute | solution.py:352
  2.3 2.6 %collective-permute-start.4 = (bf16[280,128]{1,0:T(8,128)(2,1)S(1)}, bf16[280,128]{1,0:T(8,128)(2,1)S(1)}, u32[]{:S(2)}, u32[]{:S(2)}) collective-permute-start(bf16[280,128]{1,0:T(8,128)(2,1)S(1)} %get-tuple-element.28), channel_id=1, source_target_pairs={{0,2},{1,3},{2,0},{3,1},{4,6},{5,7},{6,4},{7,5},{8,10},{9,11},{10,... | collective-permute-start | bytes 215048 | tf_op jit(solution)/shard_map/ppermute | solution.py:352
  4.9 0.0 collective-permute-done.got_ref
  4.9 0.0 copy-start.5
  4.9 0.0 copy-start.6
  4.9 3.7 %collective-permute-start.1 = (bf16[264,128]{1,0:T(8,128)(2,1)S(1)}, bf16[264,128]{1,0:T(8,128)(2,1)S(1)}, u32[]{:S(2)}, u32[]{:S(2)}) collective-permute-start(bf16[264,128]{1,0:T(8,128)(2,1)S(1)} %get-tuple-element.25), channel_id=1, source_target_pairs={{0,12},{1,15},{2,14},{3,13},{4,8},{5,11},{6,10},{7,9},{8,4},{9,7},... | collective-permute-start | bytes 202760 | tf_op jit(solution)/shard_map/ppermute | solution.py:352
  8.6 0.0 collective-permute-start.2
  8.6 0.8 %collective-permute-start.3 = (bf16[264,128]{1,0:T(8,128)(2,1)S(1)}, bf16[264,128]{1,0:T(8,128)(2,1)S(1)}, u32[]{:S(2)}, u32[]{:S(2)}) collective-permute-start(bf16[264,128]{1,0:T(8,128)(2,1)S(1)} %get-tuple-element.27), channel_id=1, source_target_pairs={{0,8},{1,11},{2,10},{3,9},{4,12},{5,15},{6,14},{7,13},{8,0},{9,3},... | collective-permute-start | bytes 202760 | tf_op jit(solution)/shard_map/ppermute | solution.py:352
  9.4 0.0 collective-permute-done.4.refs_3_
  9.4 2.5 %collective-permute-done.1.refs_0_ = bf16[264,128]{1,0:T(8,128)(2,1)S(1)} collective-permute-done((bf16[264,128]{1,0:T(8,128)(2,1)S(1)}, bf16[264,128]{1,0:T(8,128)(2,1)S(1)}, u32[]{:S(2)}, u32[]{:S(2)}) %collective-permute-start.1) | collective-permute-done | bytes 67616 | tf_op jit(solution)/shard_map/ppermute | solution.py:352
  11.9 3.0 %collective-permute-done.2.refs_1_ = bf16[264,128]{1,0:T(8,128)(2,1)S(1)} collective-permute-done((bf16[264,128]{1,0:T(8,128)(2,1)S(1)}, bf16[264,128]{1,0:T(8,128)(2,1)S(1)}, u32[]{:S(2)}, u32[]{:S(2)}) %collective-permute-start.2) | collective-permute-done | bytes 67616 | tf_op jit(solution)/shard_map/ppermute | solution.py:352
  14.9 0.0 collective-permute-done.3.refs_2_
  14.9 0.3 %collective-permute-start.5 = (bf16[544,128]{1,0:T(8,128)(2,1)S(1)}, bf16[544,128]{1,0:T(8,128)(2,1)S(1)}, u32[]{:S(2)}, u32[]{:S(2)}) collective-permute-start(bf16[544,128]{1,0:T(8,128)(2,1)S(1)} %get-tuple-element.31), channel_id=1, source_target_pairs={{0,1},{1,0},{2,3},{3,2},{4,5},{5,4},{6,7},{7,6},{8,9},{9,8},{10,11... | collective-permute-start | bytes 417800 | tf_op jit(solution)/shard_map/ppermute | solution.py:352
  15.2 1.1 %collective-permute-done.5.refs_1_ = bf16[544,128]{1,0:T(8,128)(2,1)S(1)} collective-permute-done((bf16[544,128]{1,0:T(8,128)(2,1)S(1)}, bf16[544,128]{1,0:T(8,128)(2,1)S(1)}, u32[]{:S(2)}, u32[]{:S(2)}) %collective-permute-start.5) | collective-permute-done | bytes 139296 | tf_op jit(solution)/shard_map/ppermute | solution.py:352
  16.3 0.0 copy-done.7
  16.3 0.0 copy-done.5
  16.3 0.0 copy-done.6
  16.3 0.0 copy-start
  16.4 1.3 %shard_map.113 = (bf16[3,32,256]{2,1,0:T(8,128)(2,1)S(1)}, bf16[3,32,256]{2,1,0:T(8,128)(2,1)S(1)}, bf16[80,256]{1,0:T(8,128)(2,1)S(1)}, bf16[32,256]{1,0:T(8,128)(2,1)S(1)}) custom-call(bf16[512,256]{1,0:T(8,128)(2,1)S(1)} %copy-done.5, f32[32,256]{1,0:T(8,128)S(1)} %copy-done.7, bf16[256,512]{1,0:T(8,128)(2,1)S(1)} %copy-done.6, ...), custom_call_target="tpu_custom_call" | custom-call | flops 603979776 | bytes 2000000 | tf_op jit(solution)/shard_map/pallas_call | solution.py:26
  17.7 0.3 %collective-permute-start.6 = (bf16[3,32,256]{2,1,0:T(8,128)(2,1)S(1)}, bf16[3,32,256]{2,1,0:T(8,128)(2,1)S(1)}, u32[]{:S(2)}, u32[]{:S(2)}) collective-permute-start(bf16[3,32,256]{2,1,0:T(8,128)(2,1)S(1)} %get-tuple-element.33), channel_id=1, source_target_pairs={{0,1},{1,0},{2,3},{3,2},{4,5},{5,4},{6,7},{7,6},{8,9},{9,8},{10,11... | collective-permute-start | bytes 147464 | tf_op jit(solution)/shard_map/ppermute | solution.py:352
  18.0 1.1 %collective-permute-start.10 = (bf16[80,256]{1,0:T(8,128)(2,1)S(1)}, bf16[80,256]{1,0:T(8,128)(2,1)S(1)}, u32[]{:S(2)}, u32[]{:S(2)}) collective-permute-start(bf16[80,256]{1,0:T(8,128)(2,1)S(1)} %get-tuple-element.37), channel_id=1, source_target_pairs={{0,2},{1,3},{2,0},{3,1},{4,6},{5,7},{6,4},{7,5},{8,10},{9,11},{10,... | collective-permute-start | bytes 122888 | tf_op jit(solution)/shard_map/ppermute | solution.py:352
  19.1 0.0 collective-permute-done.6.got_ref
  19.1 0.0 copy-start.1
  19.1 3.0 %collective-permute-start.7 = (bf16[64,256]{1,0:T(8,128)(2,1)S(1)}, bf16[64,256]{1,0:T(8,128)(2,1)S(1)}, u32[]{:S(2)}, u32[]{:S(2)}) collective-permute-start(bf16[64,256]{1,0:T(8,128)(2,1)S(1)} %get-tuple-element.34), channel_id=1, source_target_pairs={{0,12},{1,15},{2,14},{3,13},{4,8},{5,11},{6,10},{7,9},{8,4},{9,7},... | collective-permute-start | bytes 98312 | tf_op jit(solution)/shard_map/ppermute | solution.py:352
  22.1 0.1 collective-permute-start.8
  22.3 1.4 %collective-permute-start.9 = (bf16[64,256]{1,0:T(8,128)(2,1)S(1)}, bf16[64,256]{1,0:T(8,128)(2,1)S(1)}, u32[]{:S(2)}, u32[]{:S(2)}) collective-permute-start(bf16[64,256]{1,0:T(8,128)(2,1)S(1)} %get-tuple-element.36), channel_id=1, source_target_pairs={{0,4},{1,7},{2,6},{3,5},{4,0},{5,3},{6,2},{7,1},{8,12},{9,15},{10,... | collective-permute-start | bytes 98312 | tf_op jit(solution)/shard_map/ppermute | solution.py:352
  23.6 0.0 collective-permute-done.10.refs_3_
  23.6 1.4 %collective-permute-done.7.refs_0_ = bf16[64,256]{1,0:T(8,128)(2,1)S(1)} collective-permute-done((bf16[64,256]{1,0:T(8,128)(2,1)S(1)}, bf16[64,256]{1,0:T(8,128)(2,1)S(1)}, u32[]{:S(2)}, u32[]{:S(2)}) %collective-permute-start.7) | collective-permute-done | bytes 32800 | tf_op jit(solution)/shard_map/ppermute | solution.py:352
  25.0 2.2 %collective-permute-done.8.refs_1_ = bf16[64,256]{1,0:T(8,128)(2,1)S(1)} collective-permute-done((bf16[64,256]{1,0:T(8,128)(2,1)S(1)}, bf16[64,256]{1,0:T(8,128)(2,1)S(1)}, u32[]{:S(2)}, u32[]{:S(2)}) %collective-permute-start.8) | collective-permute-done | bytes 32800 | tf_op jit(solution)/shard_map/ppermute | solution.py:352
  27.2 0.0 collective-permute-done.9.refs_2_
  27.2 0.0 copy-start.3
  27.2 0.0 copy-start.4
  27.3 0.0 copy-start.2
  27.3 0.1 collective-permute-start.11
  27.3 0.0 copy-done
  27.4 0.0 copy-done.1
  27.4 0.6 %copy-done.3 = f32[3,768]{1,0:T(4,128)S(1)} copy-done((f32[3,768]{1,0:T(4,128)S(1)}, f32[3,768]{1,0:T(4,128)}, u32[]{:S(2)}) %copy-start.3) | copy-done | bytes 9240
  27.9 0.0 copy-done.4
  27.9 0.3 %shard_map.109.query_ref = f32[256,256]{1,0:T(8,128)S(1)} custom-call(bf16[256,256]{1,0:T(8,128)(2,1)S(1)} %copy-done.1, f32[1,256]{1,0:T(1,128)S(1)} %bitcast.3, bf16[256,768]{1,0:T(8,128)(2,1)S(1)} %copy-done, f32[3,768]{1,0:T(4,128)S(1)} %copy-done.3), custom_call_target="tpu_custom_call" | custom-call | flops 33554432 | bytes 800000 | tf_op jit(solution)/shard_map/pallas_call | solution.py:26
  28.3 0.3 %collective-permute-done.11.refs_1_ = bf16[128,256]{1,0:T(8,128)(2,1)S(1)} collective-permute-done((bf16[128,256]{1,0:T(8,128)(2,1)S(1)}, bf16[128,256]{1,0:T(8,128)(2,1)S(1)}, u32[]{:S(2)}, u32[]{:S(2)}) %collective-permute-start.11) | collective-permute-done | bytes 65568 | tf_op jit(solution)/shard_map/ppermute | solution.py:352
  28.6 0.0 copy-done.2
  28.6 0.9 %shard_map.116 = bf16[256,256]{1,0:T(8,128)(2,1)} custom-call(f32[256,256]{1,0:T(8,128)S(1)} %shard_map.109.query_ref, bf16[256,256]{1,0:T(8,128)(2,1)S(1)} %copy-done.2, bf16[128,256]{1,0:T(8,128)(2,1)S(1)} %get-tuple-element.39.refs_0_, bf16[128,256]{1,0:T(8,128)(2,1)S(1)} %collective-permute-done.11.refs_1_), custom_call_target="tpu_custom_call" | custom-call | flops 33554432 | bytes 600000 | tf_op jit(solution)/shard_map/pallas_call | solution.py:26
  (4 shorter events, 0.1 us)
Async XLA Ops:
  0.0 16.3 %copy-start.7 = (f32[32,256]{1,0:T(8,128)S(1)}, f32[32,256]{1,0:T(8,128)}, u32[]{:S(2)}) copy-start(f32[32,256]{1,0:T(8,128)} %constant.7.clone.twist_ref) | copy-start | bytes 98308
  1.8 3.1 %collective-permute-start = (bf16[3,136,128]{2,1,0:T(8,128)(2,1)S(1)}, bf16[3,136,128]{2,1,0:T(8,128)(2,1)S(1)}, u32[]{:S(2)}, u32[]{:S(2)}) collective-permute-start(bf16[3,136,128]{2,1,0:T(8,128)(2,1)S(1)} %get-tuple-element.24), channel_id=1, source_target_pairs={{0,1},{1,0},{2,3},{3,2},{4,5},{5,4},{6,7},{7,6},{8,9},{9,8},{10,11... | collective-permute-start | bytes 313352 | tf_op jit(solution)/shard_map/ppermute | solution.py:352
  2.3 7.1 %collective-permute-start.4 = (bf16[280,128]{1,0:T(8,128)(2,1)S(1)}, bf16[280,128]{1,0:T(8,128)(2,1)S(1)}, u32[]{:S(2)}, u32[]{:S(2)}) collective-permute-start(bf16[280,128]{1,0:T(8,128)(2,1)S(1)} %get-tuple-element.28), channel_id=1, source_target_pairs={{0,2},{1,3},{2,0},{3,1},{4,6},{5,7},{6,4},{7,5},{8,10},{9,11},{10,... | collective-permute-start | bytes 215048 | tf_op jit(solution)/shard_map/ppermute | solution.py:352
  4.9 11.4 %copy-start.5 = (bf16[512,256]{1,0:T(8,128)(2,1)S(1)}, bf16[512,256]{1,0:T(8,128)(2,1)}, u32[]{:S(2)}) copy-start(bf16[512,256]{1,0:T(8,128)(2,1)} %constant.6.clone.first_ref) | copy-start | bytes 786436
  4.9 11.4 %copy-start.6 = (bf16[256,512]{1,0:T(8,128)(2,1)S(1)}, bf16[256,512]{1,0:T(8,128)(2,1)}, u32[]{:S(2)}) copy-start(bf16[256,512]{1,0:T(8,128)(2,1)} %constant.8.clone.inner_ref) | copy-start | bytes 786436
  4.9 6.9 %collective-permute-start.1 = (bf16[264,128]{1,0:T(8,128)(2,1)S(1)}, bf16[264,128]{1,0:T(8,128)(2,1)S(1)}, u32[]{:S(2)}, u32[]{:S(2)}) collective-permute-start(bf16[264,128]{1,0:T(8,128)(2,1)S(1)} %get-tuple-element.25), channel_id=1, source_target_pairs={{0,12},{1,15},{2,14},{3,13},{4,8},{5,11},{6,10},{7,9},{8,4},{9,7},... | collective-permute-start | bytes 202760 | tf_op jit(solution)/shard_map/ppermute | solution.py:352
  8.6 6.3 %collective-permute-start.2 = (bf16[264,128]{1,0:T(8,128)(2,1)S(1)}, bf16[264,128]{1,0:T(8,128)(2,1)S(1)}, u32[]{:S(2)}, u32[]{:S(2)}) collective-permute-start(bf16[264,128]{1,0:T(8,128)(2,1)S(1)} %get-tuple-element.26), channel_id=1, source_target_pairs={{0,4},{1,7},{2,6},{3,5},{4,0},{5,3},{6,2},{7,1},{8,12},{9,15},{10,... | collective-permute-start | bytes 202760 | tf_op jit(solution)/shard_map/ppermute | solution.py:352
  8.6 6.3 %collective-permute-start.3 = (bf16[264,128]{1,0:T(8,128)(2,1)S(1)}, bf16[264,128]{1,0:T(8,128)(2,1)S(1)}, u32[]{:S(2)}, u32[]{:S(2)}) collective-permute-start(bf16[264,128]{1,0:T(8,128)(2,1)S(1)} %get-tuple-element.27), channel_id=1, source_target_pairs={{0,8},{1,11},{2,10},{3,9},{4,12},{5,15},{6,14},{7,13},{8,0},{9,3},... | collective-permute-start | bytes 202760 | tf_op jit(solution)/shard_map/ppermute | solution.py:352
  14.9 1.4 %collective-permute-start.5 = (bf16[544,128]{1,0:T(8,128)(2,1)S(1)}, bf16[544,128]{1,0:T(8,128)(2,1)S(1)}, u32[]{:S(2)}, u32[]{:S(2)}) collective-permute-start(bf16[544,128]{1,0:T(8,128)(2,1)S(1)} %get-tuple-element.31), channel_id=1, source_target_pairs={{0,1},{1,0},{2,3},{3,2},{4,5},{5,4},{6,7},{7,6},{8,9},{9,8},{10,11... | collective-permute-start | bytes 417800 | tf_op jit(solution)/shard_map/ppermute | solution.py:352
  16.3 11.0 %copy-start = (bf16[256,768]{1,0:T(8,128)(2,1)S(1)}, bf16[256,768]{1,0:T(8,128)(2,1)}, u32[]{:S(2)}) copy-start(bf16[256,768]{1,0:T(8,128)(2,1)} %refs_2_.1) | copy-start | bytes 1179652
  17.7 1.4 %collective-permute-start.6 = (bf16[3,32,256]{2,1,0:T(8,128)(2,1)S(1)}, bf16[3,32,256]{2,1,0:T(8,128)(2,1)S(1)}, u32[]{:S(2)}, u32[]{:S(2)}) collective-permute-start(bf16[3,32,256]{2,1,0:T(8,128)(2,1)S(1)} %get-tuple-element.33), channel_id=1, source_target_pairs={{0,1},{1,0},{2,3},{3,2},{4,5},{5,4},{6,7},{7,6},{8,9},{9,8},{10,11... | collective-permute-start | bytes 147464 | tf_op jit(solution)/shard_map/ppermute | solution.py:352
  18.0 5.6 %collective-permute-start.10 = (bf16[80,256]{1,0:T(8,128)(2,1)S(1)}, bf16[80,256]{1,0:T(8,128)(2,1)S(1)}, u32[]{:S(2)}, u32[]{:S(2)}) collective-permute-start(bf16[80,256]{1,0:T(8,128)(2,1)S(1)} %get-tuple-element.37), channel_id=1, source_target_pairs={{0,2},{1,3},{2,0},{3,1},{4,6},{5,7},{6,4},{7,5},{8,10},{9,11},{10,... | collective-permute-start | bytes 122888 | tf_op jit(solution)/shard_map/ppermute | solution.py:352
  19.1 8.2 %copy-start.1 = (bf16[256,256]{1,0:T(8,128)(2,1)S(1)}, bf16[256,256]{1,0:T(8,128)(2,1)}, u32[]{:S(2)}) copy-start(bf16[256,256]{1,0:T(8,128)(2,1)} %refs_0_.1) | copy-start | bytes 393220
  19.1 5.8 %collective-permute-start.7 = (bf16[64,256]{1,0:T(8,128)(2,1)S(1)}, bf16[64,256]{1,0:T(8,128)(2,1)S(1)}, u32[]{:S(2)}, u32[]{:S(2)}) collective-permute-start(bf16[64,256]{1,0:T(8,128)(2,1)S(1)} %get-tuple-element.34), channel_id=1, source_target_pairs={{0,12},{1,15},{2,14},{3,13},{4,8},{5,11},{6,10},{7,9},{8,4},{9,7},... | collective-permute-start | bytes 98312 | tf_op jit(solution)/shard_map/ppermute | solution.py:352
  22.1 5.1 %collective-permute-start.8 = (bf16[64,256]{1,0:T(8,128)(2,1)S(1)}, bf16[64,256]{1,0:T(8,128)(2,1)S(1)}, u32[]{:S(2)}, u32[]{:S(2)}) collective-permute-start(bf16[64,256]{1,0:T(8,128)(2,1)S(1)} %get-tuple-element.35), channel_id=1, source_target_pairs={{0,8},{1,11},{2,10},{3,9},{4,12},{5,15},{6,14},{7,13},{8,0},{9,3},... | collective-permute-start | bytes 98312 | tf_op jit(solution)/shard_map/ppermute | solution.py:352
  22.3 5.0 %collective-permute-start.9 = (bf16[64,256]{1,0:T(8,128)(2,1)S(1)}, bf16[64,256]{1,0:T(8,128)(2,1)S(1)}, u32[]{:S(2)}, u32[]{:S(2)}) collective-permute-start(bf16[64,256]{1,0:T(8,128)(2,1)S(1)} %get-tuple-element.36), channel_id=1, source_target_pairs={{0,4},{1,7},{2,6},{3,5},{4,0},{5,3},{6,2},{7,1},{8,12},{9,15},{10,... | collective-permute-start | bytes 98312 | tf_op jit(solution)/shard_map/ppermute | solution.py:352
  27.2 0.7 %copy-start.3 = (f32[3,768]{1,0:T(4,128)S(1)}, f32[3,768]{1,0:T(4,128)}, u32[]{:S(2)}) copy-start(f32[3,768]{1,0:T(4,128)} %refs_3_.1) | copy-start | bytes 27652
  27.2 0.7 %copy-start.4 = (f32[256]{0:T(256)S(1)}, f32[256]{0:T(256)}, u32[]{:S(2)}) copy-start(f32[256]{0:T(256)} %param.12) | copy-start | bytes 3076
  27.3 1.3 %copy-start.2 = (bf16[256,256]{1,0:T(8,128)(2,1)S(1)}, bf16[256,256]{1,0:T(8,128)(2,1)}, u32[]{:S(2)}) copy-start(bf16[256,256]{1,0:T(8,128)(2,1)} %w_ref.3) | copy-start | bytes 393220
  27.3 1.3 %collective-permute-start.11 = (bf16[128,256]{1,0:T(8,128)(2,1)S(1)}, bf16[128,256]{1,0:T(8,128)(2,1)S(1)}, u32[]{:S(2)}, u32[]{:S(2)}) collective-permute-start(bf16[128,256]{1,0:T(8,128)(2,1)S(1)} %get-tuple-element.40), channel_id=1, source_target_pairs={{0,1},{1,0},{2,3},{3,2},{4,5},{5,4},{6,7},{7,6},{8,9},{9,8},{10,11... | collective-permute-start | bytes 196616 | tf_op jit(solution)/shard_map/ppermute | solution.py:352

commit v24 on v21

--- a/solution.py
+++ b/solution.py
@@ -56,7 +56,9 @@
 
 
 def routes_of(chips):
-    return [(d, d + 1) for d in range(chips - 2, 1, -2)]
+    far = list(range(chips - 2, 1, -2))
+    others = far[1::-1] + far[2:]
+    return [(mine, other + 1) for mine, other in zip(far, others)]
 
 
 def carried(route, core):

time: 29.4 us -> 29.8 us (1.014)
  starting transfers between devices: 13.7 us -> 14 us
where the time goes in v24:
time: 29.8 us; the launch traced here: 29.6 us
  starting transfers between devices  14 us (47%)
  waiting for transfers between devices  10.7 us (36%)
  Pallas kernels  4.41 us (15%)
  local copies, waits for them, and re-layouts  0.42 us (1%)
    ppermute x12, starting transfers between devices, permute(): lax.ppermute(array, seq, [(i, partner(i)) for i in range(lax.axis_size(se...  14 us
    ppermute x12, waiting for transfers between devices, permute(): lax.ppermute(array, seq, [(i, partner(i)) for i in range(lax.axis_size(se...  10.7 us
    pallas_call x8, Pallas kernels, call(): pl.pallas_call(body, out_shape=outs, in_specs=[whole(space) for space in...  4.41 us
  transfers between devices with their start and end apart: 12, of which 7 were waited for; matrix products, arithmetic and copies ran while one was open for 0% of the time, Pallas kernels for 1%

profile of v24, /device:TPU:0, one launch (start us, length us, event | category | flops | bytes accessed | tf_op | source)
XLA Modules:
  0.0 29.6 jit_solution(16882100017327644143)
XLA Ops:
  0.0 0.0 copy-start.7
  0.0 1.8 %shard_map.110 = (bf16[3,136,128]{2,1,0:T(8,128)(2,1)S(1)}, bf16[3,136,128]{2,1,0:T(8,128)(2,1)S(1)}, bf16[280,128]{1,0:T(8,128)(2,1)S(1)}, bf16[136,128]{1,0:T(8,128)(2,1)S(1)}) custom-call(bf16[256,256]{1,0:T(8,128)(2,1)} %refs_0_.1, f32[1,256]{1,0:T(1,128)} %bitcast.2, bf16[256,768]{1,0:T(8,128)(2,1)} %refs_2_.1, f32[3,768]{1,0:T(4,128)} %refs_3_.1, ...), custom_call_target="tpu_custom_call" | custom-call | flops 100663296 | bytes 1500000 | tf_op jit(solution)/shard_map/pallas_call | solution.py:26
  1.8 0.5 %collective-permute-start = (bf16[3,136,128]{2,1,0:T(8,128)(2,1)S(1)}, bf16[3,136,128]{2,1,0:T(8,128)(2,1)S(1)}, u32[]{:S(2)}, u32[]{:S(2)}) collective-permute-start(bf16[3,136,128]{2,1,0:T(8,128)(2,1)S(1)} %get-tuple-element.24), channel_id=1, source_target_pairs={{0,1},{1,0},{2,3},{3,2},{4,5},{5,4},{6,7},{7,6},{8,9},{9,8},{10,11... | collective-permute-start | bytes 313352 | tf_op jit(solution)/shard_map/ppermute | solution.py:351
  2.3 2.6 %collective-permute-start.4 = (bf16[280,128]{1,0:T(8,128)(2,1)S(1)}, bf16[280,128]{1,0:T(8,128)(2,1)S(1)}, u32[]{:S(2)}, u32[]{:S(2)}) collective-permute-start(bf16[280,128]{1,0:T(8,128)(2,1)S(1)} %get-tuple-element.28), channel_id=1, source_target_pairs={{0,2},{1,3},{2,0},{3,1},{4,6},{5,7},{6,4},{7,5},{8,10},{9,11},{10,... | collective-permute-start | bytes 215048 | tf_op jit(solution)/shard_map/ppermute | solution.py:351
  4.9 0.0 collective-permute-done.got_ref
  4.9 0.0 copy-start.5
  4.9 0.0 copy-start.6
  4.9 3.7 %collective-permute-start.1 = (bf16[264,128]{1,0:T(8,128)(2,1)S(1)}, bf16[264,128]{1,0:T(8,128)(2,1)S(1)}, u32[]{:S(2)}, u32[]{:S(2)}) collective-permute-start(bf16[264,128]{1,0:T(8,128)(2,1)S(1)} %get-tuple-element.25), channel_id=1, source_target_pairs={{0,12},{1,11},{2,14},{3,9},{4,8},{5,15},{6,10},{7,13},{8,4},{9,3},... | collective-permute-start | bytes 202760 | tf_op jit(solution)/shard_map/ppermute | solution.py:351
  8.6 0.0 collective-permute-start.2
  8.6 0.8 %collective-permute-start.3 = (bf16[264,128]{1,0:T(8,128)(2,1)S(1)}, bf16[264,128]{1,0:T(8,128)(2,1)S(1)}, u32[]{:S(2)}, u32[]{:S(2)}) collective-permute-start(bf16[264,128]{1,0:T(8,128)(2,1)S(1)} %get-tuple-element.27), channel_id=1, source_target_pairs={{0,4},{1,7},{2,6},{3,5},{4,0},{5,3},{6,2},{7,1},{8,12},{9,15},{10,... | collective-permute-start | bytes 202760 | tf_op jit(solution)/shard_map/ppermute | solution.py:351
  9.4 0.0 collective-permute-done.4.refs_3_
  9.4 2.5 %collective-permute-done.1.refs_0_ = bf16[264,128]{1,0:T(8,128)(2,1)S(1)} collective-permute-done((bf16[264,128]{1,0:T(8,128)(2,1)S(1)}, bf16[264,128]{1,0:T(8,128)(2,1)S(1)}, u32[]{:S(2)}, u32[]{:S(2)}) %collective-permute-start.1) | collective-permute-done | bytes 67616 | tf_op jit(solution)/shard_map/ppermute | solution.py:351
  11.9 3.2 %collective-permute-done.2.refs_1_ = bf16[264,128]{1,0:T(8,128)(2,1)S(1)} collective-permute-done((bf16[264,128]{1,0:T(8,128)(2,1)S(1)}, bf16[264,128]{1,0:T(8,128)(2,1)S(1)}, u32[]{:S(2)}, u32[]{:S(2)}) %collective-permute-start.2) | collective-permute-done | bytes 67616 | tf_op jit(solution)/shard_map/ppermute | solution.py:351
  15.1 0.0 collective-permute-done.3.refs_2_
  15.1 0.5 %collective-permute-start.5 = (bf16[544,128]{1,0:T(8,128)(2,1)S(1)}, bf16[544,128]{1,0:T(8,128)(2,1)S(1)}, u32[]{:S(2)}, u32[]{:S(2)}) collective-permute-start(bf16[544,128]{1,0:T(8,128)(2,1)S(1)} %get-tuple-element.31), channel_id=1, source_target_pairs={{0,1},{1,0},{2,3},{3,2},{4,5},{5,4},{6,7},{7,6},{8,9},{9,8},{10,11... | collective-permute-start | bytes 417800 | tf_op jit(solution)/shard_map/ppermute | solution.py:351
  15.6 1.0 %collective-permute-done.5.refs_1_ = bf16[544,128]{1,0:T(8,128)(2,1)S(1)} collective-permute-done((bf16[544,128]{1,0:T(8,128)(2,1)S(1)}, bf16[544,128]{1,0:T(8,128)(2,1)S(1)}, u32[]{:S(2)}, u32[]{:S(2)}) %collective-permute-start.5) | collective-permute-done | bytes 139296 | tf_op jit(solution)/shard_map/ppermute | solution.py:351
  16.6 0.0 copy-done.7
  16.6 0.0 copy-done.5
  16.6 0.0 copy-done.6
  16.6 0.0 copy-start
  16.6 1.3 %shard_map.113 = (bf16[3,32,256]{2,1,0:T(8,128)(2,1)S(1)}, bf16[3,32,256]{2,1,0:T(8,128)(2,1)S(1)}, bf16[80,256]{1,0:T(8,128)(2,1)S(1)}, bf16[32,256]{1,0:T(8,128)(2,1)S(1)}) custom-call(bf16[512,256]{1,0:T(8,128)(2,1)S(1)} %copy-done.5, f32[32,256]{1,0:T(8,128)S(1)} %copy-done.7, bf16[256,512]{1,0:T(8,128)(2,1)S(1)} %copy-done.6, ...), custom_call_target="tpu_custom_call" | custom-call | flops 603979776 | bytes 2000000 | tf_op jit(solution)/shard_map/pallas_call | solution.py:26
  18.0 0.4 %collective-permute-start.6 = (bf16[3,32,256]{2,1,0:T(8,128)(2,1)S(1)}, bf16[3,32,256]{2,1,0:T(8,128)(2,1)S(1)}, u32[]{:S(2)}, u32[]{:S(2)}) collective-permute-start(bf16[3,32,256]{2,1,0:T(8,128)(2,1)S(1)} %get-tuple-element.33), channel_id=1, source_target_pairs={{0,1},{1,0},{2,3},{3,2},{4,5},{5,4},{6,7},{7,6},{8,9},{9,8},{10,11... | collective-permute-start | bytes 147464 | tf_op jit(solution)/shard_map/ppermute | solution.py:351
  18.4 0.8 %collective-permute-start.10 = (bf16[80,256]{1,0:T(8,128)(2,1)S(1)}, bf16[80,256]{1,0:T(8,128)(2,1)S(1)}, u32[]{:S(2)}, u32[]{:S(2)}) collective-permute-start(bf16[80,256]{1,0:T(8,128)(2,1)S(1)} %get-tuple-element.37), channel_id=1, source_target_pairs={{0,2},{1,3},{2,0},{3,1},{4,6},{5,7},{6,4},{7,5},{8,10},{9,11},{10,... | collective-permute-start | bytes 122888 | tf_op jit(solution)/shard_map/ppermute | solution.py:351
  19.2 0.1 collective-permute-done.6.got_ref
  19.3 0.0 copy-start.1
  19.3 2.9 %collective-permute-start.7 = (bf16[64,256]{1,0:T(8,128)(2,1)S(1)}, bf16[64,256]{1,0:T(8,128)(2,1)S(1)}, u32[]{:S(2)}, u32[]{:S(2)}) collective-permute-start(bf16[64,256]{1,0:T(8,128)(2,1)S(1)} %get-tuple-element.34), channel_id=1, source_target_pairs={{0,12},{1,11},{2,14},{3,9},{4,8},{5,15},{6,10},{7,13},{8,4},{9,3},... | collective-permute-start | bytes 98312 | tf_op jit(solution)/shard_map/ppermute | solution.py:351
  22.2 0.0 collective-permute-start.8
  22.2 1.6 %collective-permute-start.9 = (bf16[64,256]{1,0:T(8,128)(2,1)S(1)}, bf16[64,256]{1,0:T(8,128)(2,1)S(1)}, u32[]{:S(2)}, u32[]{:S(2)}) collective-permute-start(bf16[64,256]{1,0:T(8,128)(2,1)S(1)} %get-tuple-element.36), channel_id=1, source_target_pairs={{0,4},{1,7},{2,6},{3,5},{4,0},{5,3},{6,2},{7,1},{8,12},{9,15},{10,... | collective-permute-start | bytes 98312 | tf_op jit(solution)/shard_map/ppermute | solution.py:351
  23.8 0.0 collective-permute-done.10.refs_3_
  23.8 1.3 %collective-permute-done.7.refs_0_ = bf16[64,256]{1,0:T(8,128)(2,1)S(1)} collective-permute-done((bf16[64,256]{1,0:T(8,128)(2,1)S(1)}, bf16[64,256]{1,0:T(8,128)(2,1)S(1)}, u32[]{:S(2)}, u32[]{:S(2)}) %collective-permute-start.7) | collective-permute-done | bytes 32800 | tf_op jit(solution)/shard_map/ppermute | solution.py:351
  25.1 2.2 %collective-permute-done.8.refs_1_ = bf16[64,256]{1,0:T(8,128)(2,1)S(1)} collective-permute-done((bf16[64,256]{1,0:T(8,128)(2,1)S(1)}, bf16[64,256]{1,0:T(8,128)(2,1)S(1)}, u32[]{:S(2)}, u32[]{:S(2)}) %collective-permute-start.8) | collective-permute-done | bytes 32800 | tf_op jit(solution)/shard_map/ppermute | solution.py:351
  27.3 0.0 collective-permute-done.9.refs_2_
  27.3 0.0 copy-start.3
  27.4 0.0 copy-start.4
  27.4 0.0 copy-start.2
  27.4 0.3 collective-permute-start.11
  27.7 0.0 copy-done
  27.7 0.0 copy-done.1
  27.7 0.4 %copy-done.3 = f32[3,768]{1,0:T(4,128)S(1)} copy-done((f32[3,768]{1,0:T(4,128)S(1)}, f32[3,768]{1,0:T(4,128)}, u32[]{:S(2)}) %copy-start.3) | copy-done | bytes 9240
  28.1 0.0 copy-done.4
  28.1 0.3 %shard_map.109.query_ref = f32[256,256]{1,0:T(8,128)S(1)} custom-call(bf16[256,256]{1,0:T(8,128)(2,1)S(1)} %copy-done.1, f32[1,256]{1,0:T(1,128)S(1)} %bitcast.3, bf16[256,768]{1,0:T(8,128)(2,1)S(1)} %copy-done, f32[3,768]{1,0:T(4,128)S(1)} %copy-done.3), custom_call_target="tpu_custom_call" | custom-call | flops 33554432 | bytes 800000 | tf_op jit(solution)/shard_map/pallas_call | solution.py:26
  28.4 0.3 %collective-permute-done.11.refs_1_ = bf16[128,256]{1,0:T(8,128)(2,1)S(1)} collective-permute-done((bf16[128,256]{1,0:T(8,128)(2,1)S(1)}, bf16[128,256]{1,0:T(8,128)(2,1)S(1)}, u32[]{:S(2)}, u32[]{:S(2)}) %collective-permute-start.11) | collective-permute-done | bytes 65568 | tf_op jit(solution)/shard_map/ppermute | solution.py:351
  28.7 0.0 copy-done.2
  28.7 0.9 %shard_map.116 = bf16[256,256]{1,0:T(8,128)(2,1)} custom-call(f32[256,256]{1,0:T(8,128)S(1)} %shard_map.109.query_ref, bf16[256,256]{1,0:T(8,128)(2,1)S(1)} %copy-done.2, bf16[128,256]{1,0:T(8,128)(2,1)S(1)} %get-tuple-element.39.refs_0_, bf16[128,256]{1,0:T(8,128)(2,1)S(1)} %collective-permute-done.11.refs_1_), custom_call_target="tpu_custom_call" | custom-call | flops 33554432 | bytes 600000 | tf_op jit(solution)/shard_map/pallas_call | solution.py:26
  (4 shorter events, 0.1 us)
Async XLA Ops:
  0.0 16.6 %copy-start.7 = (f32[32,256]{1,0:T(8,128)S(1)}, f32[32,256]{1,0:T(8,128)}, u32[]{:S(2)}) copy-start(f32[32,256]{1,0:T(8,128)} %constant.7.clone.twist_ref) | copy-start | bytes 98308
  1.8 3.1 %collective-permute-start = (bf16[3,136,128]{2,1,0:T(8,128)(2,1)S(1)}, bf16[3,136,128]{2,1,0:T(8,128)(2,1)S(1)}, u32[]{:S(2)}, u32[]{:S(2)}) collective-permute-start(bf16[3,136,128]{2,1,0:T(8,128)(2,1)S(1)} %get-tuple-element.24), channel_id=1, source_target_pairs={{0,1},{1,0},{2,3},{3,2},{4,5},{5,4},{6,7},{7,6},{8,9},{9,8},{10,11... | collective-permute-start | bytes 313352 | tf_op jit(solution)/shard_map/ppermute | solution.py:351
  2.3 7.1 %collective-permute-start.4 = (bf16[280,128]{1,0:T(8,128)(2,1)S(1)}, bf16[280,128]{1,0:T(8,128)(2,1)S(1)}, u32[]{:S(2)}, u32[]{:S(2)}) collective-permute-start(bf16[280,128]{1,0:T(8,128)(2,1)S(1)} %get-tuple-element.28), channel_id=1, source_target_pairs={{0,2},{1,3},{2,0},{3,1},{4,6},{5,7},{6,4},{7,5},{8,10},{9,11},{10,... | collective-permute-start | bytes 215048 | tf_op jit(solution)/shard_map/ppermute | solution.py:351
  4.9 11.7 %copy-start.5 = (bf16[512,256]{1,0:T(8,128)(2,1)S(1)}, bf16[512,256]{1,0:T(8,128)(2,1)}, u32[]{:S(2)}) copy-start(bf16[512,256]{1,0:T(8,128)(2,1)} %constant.6.clone.first_ref) | copy-start | bytes 786436
  4.9 11.7 %copy-start.6 = (bf16[256,512]{1,0:T(8,128)(2,1)S(1)}, bf16[256,512]{1,0:T(8,128)(2,1)}, u32[]{:S(2)}) copy-start(bf16[256,512]{1,0:T(8,128)(2,1)} %constant.8.clone.inner_ref) | copy-start | bytes 786436
  4.9 6.9 %collective-permute-start.1 = (bf16[264,128]{1,0:T(8,128)(2,1)S(1)}, bf16[264,128]{1,0:T(8,128)(2,1)S(1)}, u32[]{:S(2)}, u32[]{:S(2)}) collective-permute-start(bf16[264,128]{1,0:T(8,128)(2,1)S(1)} %get-tuple-element.25), channel_id=1, source_target_pairs={{0,12},{1,11},{2,14},{3,9},{4,8},{5,15},{6,10},{7,13},{8,4},{9,3},... | collective-permute-start | bytes 202760 | tf_op jit(solution)/shard_map/ppermute | solution.py:351
  8.6 6.5 %collective-permute-start.2 = (bf16[264,128]{1,0:T(8,128)(2,1)S(1)}, bf16[264,128]{1,0:T(8,128)(2,1)S(1)}, u32[]{:S(2)}, u32[]{:S(2)}) collective-permute-start(bf16[264,128]{1,0:T(8,128)(2,1)S(1)} %get-tuple-element.26), channel_id=1, source_target_pairs={{0,8},{1,15},{2,10},{3,13},{4,12},{5,11},{6,14},{7,9},{8,0},{9,7},... | collective-permute-start | bytes 202760 | tf_op jit(solution)/shard_map/ppermute | solution.py:351
  8.6 6.5 %collective-permute-start.3 = (bf16[264,128]{1,0:T(8,128)(2,1)S(1)}, bf16[264,128]{1,0:T(8,128)(2,1)S(1)}, u32[]{:S(2)}, u32[]{:S(2)}) collective-permute-start(bf16[264,128]{1,0:T(8,128)(2,1)S(1)} %get-tuple-element.27), channel_id=1, source_target_pairs={{0,4},{1,7},{2,6},{3,5},{4,0},{5,3},{6,2},{7,1},{8,12},{9,15},{10,... | collective-permute-start | bytes 202760 | tf_op jit(solution)/shard_map/ppermute | solution.py:351
  15.1 1.5 %collective-permute-start.5 = (bf16[544,128]{1,0:T(8,128)(2,1)S(1)}, bf16[544,128]{1,0:T(8,128)(2,1)S(1)}, u32[]{:S(2)}, u32[]{:S(2)}) collective-permute-start(bf16[544,128]{1,0:T(8,128)(2,1)S(1)} %get-tuple-element.31), channel_id=1, source_target_pairs={{0,1},{1,0},{2,3},{3,2},{4,5},{5,4},{6,7},{7,6},{8,9},{9,8},{10,11... | collective-permute-start | bytes 417800 | tf_op jit(solution)/shard_map/ppermute | solution.py:351
  16.6 11.0 %copy-start = (bf16[256,768]{1,0:T(8,128)(2,1)S(1)}, bf16[256,768]{1,0:T(8,128)(2,1)}, u32[]{:S(2)}) copy-start(bf16[256,768]{1,0:T(8,128)(2,1)} %refs_2_.1) | copy-start | bytes 1179652
  18.0 1.3 %collective-permute-start.6 = (bf16[3,32,256]{2,1,0:T(8,128)(2,1)S(1)}, bf16[3,32,256]{2,1,0:T(8,128)(2,1)S(1)}, u32[]{:S(2)}, u32[]{:S(2)}) collective-permute-start(bf16[3,32,256]{2,1,0:T(8,128)(2,1)S(1)} %get-tuple-element.33), channel_id=1, source_target_pairs={{0,1},{1,0},{2,3},{3,2},{4,5},{5,4},{6,7},{7,6},{8,9},{9,8},{10,11... | collective-permute-start | bytes 147464 | tf_op jit(solution)/shard_map/ppermute | solution.py:351
  18.4 5.4 %collective-permute-start.10 = (bf16[80,256]{1,0:T(8,128)(2,1)S(1)}, bf16[80,256]{1,0:T(8,128)(2,1)S(1)}, u32[]{:S(2)}, u32[]{:S(2)}) collective-permute-start(bf16[80,256]{1,0:T(8,128)(2,1)S(1)} %get-tuple-element.37), channel_id=1, source_target_pairs={{0,2},{1,3},{2,0},{3,1},{4,6},{5,7},{6,4},{7,5},{8,10},{9,11},{10,... | collective-permute-start | bytes 122888 | tf_op jit(solution)/shard_map/ppermute | solution.py:351
  19.3 8.4 %copy-start.1 = (bf16[256,256]{1,0:T(8,128)(2,1)S(1)}, bf16[256,256]{1,0:T(8,128)(2,1)}, u32[]{:S(2)}) copy-start(bf16[256,256]{1,0:T(8,128)(2,1)} %refs_0_.1) | copy-start | bytes 393220
  19.3 5.8 %collective-permute-start.7 = (bf16[64,256]{1,0:T(8,128)(2,1)S(1)}, bf16[64,256]{1,0:T(8,128)(2,1)S(1)}, u32[]{:S(2)}, u32[]{:S(2)}) collective-permute-start(bf16[64,256]{1,0:T(8,128)(2,1)S(1)} %get-tuple-element.34), channel_id=1, source_target_pairs={{0,12},{1,11},{2,14},{3,9},{4,8},{5,15},{6,10},{7,13},{8,4},{9,3},... | collective-permute-start | bytes 98312 | tf_op jit(solution)/shard_map/ppermute | solution.py:351
  22.2 5.2 %collective-permute-start.8 = (bf16[64,256]{1,0:T(8,128)(2,1)S(1)}, bf16[64,256]{1,0:T(8,128)(2,1)S(1)}, u32[]{:S(2)}, u32[]{:S(2)}) collective-permute-start(bf16[64,256]{1,0:T(8,128)(2,1)S(1)} %get-tuple-element.35), channel_id=1, source_target_pairs={{0,8},{1,15},{2,10},{3,13},{4,12},{5,11},{6,14},{7,9},{8,0},{9,7},... | collective-permute-start | bytes 98312 | tf_op jit(solution)/shard_map/ppermute | solution.py:351
  22.2 5.2 %collective-permute-start.9 = (bf16[64,256]{1,0:T(8,128)(2,1)S(1)}, bf16[64,256]{1,0:T(8,128)(2,1)S(1)}, u32[]{:S(2)}, u32[]{:S(2)}) collective-permute-start(bf16[64,256]{1,0:T(8,128)(2,1)S(1)} %get-tuple-element.36), channel_id=1, source_target_pairs={{0,4},{1,7},{2,6},{3,5},{4,0},{5,3},{6,2},{7,1},{8,12},{9,15},{10,... | collective-permute-start | bytes 98312 | tf_op jit(solution)/shard_map/ppermute | solution.py:351
  27.3 0.7 %copy-start.3 = (f32[3,768]{1,0:T(4,128)S(1)}, f32[3,768]{1,0:T(4,128)}, u32[]{:S(2)}) copy-start(f32[3,768]{1,0:T(4,128)} %refs_3_.1) | copy-start | bytes 27652
  27.4 0.7 %copy-start.4 = (f32[256]{0:T(256)S(1)}, f32[256]{0:T(256)}, u32[]{:S(2)}) copy-start(f32[256]{0:T(256)} %param.12) | copy-start | bytes 3076
  27.4 1.3 %copy-start.2 = (bf16[256,256]{1,0:T(8,128)(2,1)S(1)}, bf16[256,256]{1,0:T(8,128)(2,1)}, u32[]{:S(2)}) copy-start(bf16[256,256]{1,0:T(8,128)(2,1)} %w_ref.3) | copy-start | bytes 393220
  27.4 1.3 %collective-permute-start.11 = (bf16[128,256]{1,0:T(8,128)(2,1)S(1)}, bf16[128,256]{1,0:T(8,128)(2,1)S(1)}, u32[]{:S(2)}, u32[]{:S(2)}) collective-permute-start(bf16[128,256]{1,0:T(8,128)(2,1)S(1)} %get-tuple-element.40), channel_id=1, source_target_pairs={{0,1},{1,0},{2,3},{3,2},{4,5},{5,4},{6,7},{7,6},{8,9},{9,8},{10,11... | collective-permute-start | bytes 196616 | tf_op jit(solution)/shard_map/ppermute | solution.py:351

commit v25 on v21

--- a/solution.py
+++ b/solution.py
@@ -174,8 +174,8 @@
     tokens_ref, gain_ref, w_ref, short_ref, long_ref, medium_ref, skip_ref = held
     rows, width = tokens_ref.shape
     copies = [pltpu.make_async_copy(h, v, sems.at[i]) for i, (h, v) in enumerate(zip(hbm, held))]
-    for copy in copies:
-        copy.start()
+    for index in (2, 0, 1, 3, 4, 5, 6):
+        copies[index].start()
     copies[0].wait()
     copies[1].wait()
     normed = normed_of(tokens_ref, gain_ref)

time: 29.4 us -> 29.4 us (level)
  no operation moved by 1% of the time
where the time goes in v25:
time: 29.4 us; the launch traced here: 29.3 us
  starting transfers between devices  13.7 us (47%)
  waiting for transfers between devices  10.7 us (36%)
  Pallas kernels  4.48 us (15%)
  local copies, waits for them, and re-layouts  0.36 us (1%)
    ppermute x12, starting transfers between devices, permute(): lax.ppermute(array, seq, [(i, partner(i)) for i in range(lax.axis_size(se...  13.7 us
    ppermute x12, waiting for transfers between devices, permute(): lax.ppermute(array, seq, [(i, partner(i)) for i in range(lax.axis_size(se...  10.7 us
    pallas_call x8, Pallas kernels, call(): pl.pallas_call(body, out_shape=outs, in_specs=[whole(space) for space in...  4.48 us
  transfers between devices with their start and end apart: 12, of which 7 were waited for; matrix products, arithmetic and copies ran while one was open for 0% of the time, Pallas kernels for 1%

profile of v25, /device:TPU:0, one launch (start us, length us, event | category | flops | bytes accessed | tf_op | source)
XLA Modules:
  0.0 29.3 jit_solution(7238280091498237728)
XLA Ops:
  0.0 0.0 copy-start.7
  0.0 1.8 %shard_map.110 = (bf16[3,136,128]{2,1,0:T(8,128)(2,1)S(1)}, bf16[3,136,128]{2,1,0:T(8,128)(2,1)S(1)}, bf16[280,128]{1,0:T(8,128)(2,1)S(1)}, bf16[136,128]{1,0:T(8,128)(2,1)S(1)}) custom-call(bf16[256,256]{1,0:T(8,128)(2,1)} %refs_0_.1, f32[1,256]{1,0:T(1,128)} %bitcast.2, bf16[256,768]{1,0:T(8,128)(2,1)} %refs_2_.1, f32[3,768]{1,0:T(4,128)} %refs_3_.1, ...), custom_call_target="tpu_custom_call" | custom-call | flops 100663296 | bytes 1500000 | tf_op jit(solution)/shard_map/pallas_call | solution.py:26
  1.9 0.5 %collective-permute-start = (bf16[3,136,128]{2,1,0:T(8,128)(2,1)S(1)}, bf16[3,136,128]{2,1,0:T(8,128)(2,1)S(1)}, u32[]{:S(2)}, u32[]{:S(2)}) collective-permute-start(bf16[3,136,128]{2,1,0:T(8,128)(2,1)S(1)} %get-tuple-element.24), channel_id=1, source_target_pairs={{0,1},{1,0},{2,3},{3,2},{4,5},{5,4},{6,7},{7,6},{8,9},{9,8},{10,11... | collective-permute-start | bytes 313352 | tf_op jit(solution)/shard_map/ppermute | solution.py:349
  2.4 2.6 %collective-permute-start.4 = (bf16[280,128]{1,0:T(8,128)(2,1)S(1)}, bf16[280,128]{1,0:T(8,128)(2,1)S(1)}, u32[]{:S(2)}, u32[]{:S(2)}) collective-permute-start(bf16[280,128]{1,0:T(8,128)(2,1)S(1)} %get-tuple-element.28), channel_id=1, source_target_pairs={{0,2},{1,3},{2,0},{3,1},{4,6},{5,7},{6,4},{7,5},{8,10},{9,11},{10,... | collective-permute-start | bytes 215048 | tf_op jit(solution)/shard_map/ppermute | solution.py:349
  5.0 0.0 collective-permute-done.got_ref
  5.0 0.0 copy-start.5
  5.0 0.0 copy-start.6
  5.0 3.7 %collective-permute-start.1 = (bf16[264,128]{1,0:T(8,128)(2,1)S(1)}, bf16[264,128]{1,0:T(8,128)(2,1)S(1)}, u32[]{:S(2)}, u32[]{:S(2)}) collective-permute-start(bf16[264,128]{1,0:T(8,128)(2,1)S(1)} %get-tuple-element.25), channel_id=1, source_target_pairs={{0,12},{1,15},{2,14},{3,13},{4,8},{5,11},{6,10},{7,9},{8,4},{9,7},... | collective-permute-start | bytes 202760 | tf_op jit(solution)/shard_map/ppermute | solution.py:349
  8.7 0.0 collective-permute-start.2
  8.7 0.8 %collective-permute-start.3 = (bf16[264,128]{1,0:T(8,128)(2,1)S(1)}, bf16[264,128]{1,0:T(8,128)(2,1)S(1)}, u32[]{:S(2)}, u32[]{:S(2)}) collective-permute-start(bf16[264,128]{1,0:T(8,128)(2,1)S(1)} %get-tuple-element.27), channel_id=1, source_target_pairs={{0,4},{1,7},{2,6},{3,5},{4,0},{5,3},{6,2},{7,1},{8,12},{9,15},{10,... | collective-permute-start | bytes 202760 | tf_op jit(solution)/shard_map/ppermute | solution.py:349
  9.5 0.0 collective-permute-done.4.refs_3_
  9.5 2.4 %collective-permute-done.1.refs_0_ = bf16[264,128]{1,0:T(8,128)(2,1)S(1)} collective-permute-done((bf16[264,128]{1,0:T(8,128)(2,1)S(1)}, bf16[264,128]{1,0:T(8,128)(2,1)S(1)}, u32[]{:S(2)}, u32[]{:S(2)}) %collective-permute-start.1) | collective-permute-done | bytes 67616 | tf_op jit(solution)/shard_map/ppermute | solution.py:349
  11.8 3.5 %collective-permute-done.2.refs_1_ = bf16[264,128]{1,0:T(8,128)(2,1)S(1)} collective-permute-done((bf16[264,128]{1,0:T(8,128)(2,1)S(1)}, bf16[264,128]{1,0:T(8,128)(2,1)S(1)}, u32[]{:S(2)}, u32[]{:S(2)}) %collective-permute-start.2) | collective-permute-done | bytes 67616 | tf_op jit(solution)/shard_map/ppermute | solution.py:349
  15.3 0.0 collective-permute-done.3.refs_2_
  15.3 0.2 collective-permute-start.5
  15.5 1.2 %collective-permute-done.5.refs_1_ = bf16[544,128]{1,0:T(8,128)(2,1)S(1)} collective-permute-done((bf16[544,128]{1,0:T(8,128)(2,1)S(1)}, bf16[544,128]{1,0:T(8,128)(2,1)S(1)}, u32[]{:S(2)}, u32[]{:S(2)}) %collective-permute-start.5) | collective-permute-done | bytes 139296 | tf_op jit(solution)/shard_map/ppermute | solution.py:349
  16.7 0.0 copy-done.7
  16.7 0.0 copy-done.5
  16.7 0.0 copy-done.6
  16.7 0.0 copy-start
  16.8 1.3 %shard_map.113 = (bf16[3,32,256]{2,1,0:T(8,128)(2,1)S(1)}, bf16[3,32,256]{2,1,0:T(8,128)(2,1)S(1)}, bf16[80,256]{1,0:T(8,128)(2,1)S(1)}, bf16[32,256]{1,0:T(8,128)(2,1)S(1)}) custom-call(bf16[512,256]{1,0:T(8,128)(2,1)S(1)} %copy-done.5, f32[32,256]{1,0:T(8,128)S(1)} %copy-done.7, bf16[256,512]{1,0:T(8,128)(2,1)S(1)} %copy-done.6, ...), custom_call_target="tpu_custom_call" | custom-call | flops 603979776 | bytes 2000000 | tf_op jit(solution)/shard_map/pallas_call | solution.py:26
  18.1 0.2 collective-permute-start.6
  18.3 1.0 %collective-permute-start.10 = (bf16[80,256]{1,0:T(8,128)(2,1)S(1)}, bf16[80,256]{1,0:T(8,128)(2,1)S(1)}, u32[]{:S(2)}, u32[]{:S(2)}) collective-permute-start(bf16[80,256]{1,0:T(8,128)(2,1)S(1)} %get-tuple-element.37), channel_id=1, source_target_pairs={{0,2},{1,3},{2,0},{3,1},{4,6},{5,7},{6,4},{7,5},{8,10},{9,11},{10,... | collective-permute-start | bytes 122888 | tf_op jit(solution)/shard_map/ppermute | solution.py:349
  19.3 0.1 collective-permute-done.6.got_ref
  19.4 0.0 copy-start.1
  19.4 2.5 %collective-permute-start.7 = (bf16[64,256]{1,0:T(8,128)(2,1)S(1)}, bf16[64,256]{1,0:T(8,128)(2,1)S(1)}, u32[]{:S(2)}, u32[]{:S(2)}) collective-permute-start(bf16[64,256]{1,0:T(8,128)(2,1)S(1)} %get-tuple-element.34), channel_id=1, source_target_pairs={{0,12},{1,15},{2,14},{3,13},{4,8},{5,11},{6,10},{7,9},{8,4},{9,7},... | collective-permute-start | bytes 98312 | tf_op jit(solution)/shard_map/ppermute | solution.py:349
  22.0 0.2 collective-permute-start.8
  22.1 1.8 %collective-permute-start.9 = (bf16[64,256]{1,0:T(8,128)(2,1)S(1)}, bf16[64,256]{1,0:T(8,128)(2,1)S(1)}, u32[]{:S(2)}, u32[]{:S(2)}) collective-permute-start(bf16[64,256]{1,0:T(8,128)(2,1)S(1)} %get-tuple-element.36), channel_id=1, source_target_pairs={{0,4},{1,7},{2,6},{3,5},{4,0},{5,3},{6,2},{7,1},{8,12},{9,15},{10,... | collective-permute-start | bytes 98312 | tf_op jit(solution)/shard_map/ppermute | solution.py:349
  23.9 0.0 collective-permute-done.10.refs_3_
  23.9 1.6 %collective-permute-done.7.refs_0_ = bf16[64,256]{1,0:T(8,128)(2,1)S(1)} collective-permute-done((bf16[64,256]{1,0:T(8,128)(2,1)S(1)}, bf16[64,256]{1,0:T(8,128)(2,1)S(1)}, u32[]{:S(2)}, u32[]{:S(2)}) %collective-permute-start.7) | collective-permute-done | bytes 32800 | tf_op jit(solution)/shard_map/ppermute | solution.py:349
  25.5 1.6 %collective-permute-done.8.refs_1_ = bf16[64,256]{1,0:T(8,128)(2,1)S(1)} collective-permute-done((bf16[64,256]{1,0:T(8,128)(2,1)S(1)}, bf16[64,256]{1,0:T(8,128)(2,1)S(1)}, u32[]{:S(2)}, u32[]{:S(2)}) %collective-permute-start.8) | collective-permute-done | bytes 32800 | tf_op jit(solution)/shard_map/ppermute | solution.py:349
  27.0 0.0 collective-permute-done.9.refs_2_
  27.0 0.0 copy-start.3
  27.0 0.0 copy-start.4
  27.0 0.0 copy-start.2
  27.1 0.3 %collective-permute-start.11 = (bf16[128,256]{1,0:T(8,128)(2,1)S(1)}, bf16[128,256]{1,0:T(8,128)(2,1)S(1)}, u32[]{:S(2)}, u32[]{:S(2)}) collective-permute-start(bf16[128,256]{1,0:T(8,128)(2,1)S(1)} %get-tuple-element.40), channel_id=1, source_target_pairs={{0,1},{1,0},{2,3},{3,2},{4,5},{5,4},{6,7},{7,6},{8,9},{9,8},{10,11... | collective-permute-start | bytes 196616 | tf_op jit(solution)/shard_map/ppermute | solution.py:349
  27.4 0.0 copy-done
  27.4 0.0 copy-done.1
  27.4 0.3 %copy-done.3 = f32[3,768]{1,0:T(4,128)S(1)} copy-done((f32[3,768]{1,0:T(4,128)S(1)}, f32[3,768]{1,0:T(4,128)}, u32[]{:S(2)}) %copy-start.3) | copy-done | bytes 9240
  27.7 0.0 copy-done.4
  27.7 0.3 %shard_map.109.query_ref = f32[256,256]{1,0:T(8,128)S(1)} custom-call(bf16[256,256]{1,0:T(8,128)(2,1)S(1)} %copy-done.1, f32[1,256]{1,0:T(1,128)S(1)} %bitcast.3, bf16[256,768]{1,0:T(8,128)(2,1)S(1)} %copy-done, f32[3,768]{1,0:T(4,128)S(1)} %copy-done.3), custom_call_target="tpu_custom_call" | custom-call | flops 33554432 | bytes 800000 | tf_op jit(solution)/shard_map/pallas_call | solution.py:26
  28.1 0.3 %collective-permute-done.11.refs_1_ = bf16[128,256]{1,0:T(8,128)(2,1)S(1)} collective-permute-done((bf16[128,256]{1,0:T(8,128)(2,1)S(1)}, bf16[128,256]{1,0:T(8,128)(2,1)S(1)}, u32[]{:S(2)}, u32[]{:S(2)}) %collective-permute-start.11) | collective-permute-done | bytes 65568 | tf_op jit(solution)/shard_map/ppermute | solution.py:349
  28.4 0.0 copy-done.2
  28.4 0.9 %shard_map.116 = bf16[256,256]{1,0:T(8,128)(2,1)} custom-call(f32[256,256]{1,0:T(8,128)S(1)} %shard_map.109.query_ref, bf16[256,256]{1,0:T(8,128)(2,1)S(1)} %copy-done.2, bf16[128,256]{1,0:T(8,128)(2,1)S(1)} %get-tuple-element.39.refs_0_, bf16[128,256]{1,0:T(8,128)(2,1)S(1)} %collective-permute-done.11.refs_1_), custom_call_target="tpu_custom_call" | custom-call | flops 33554432 | bytes 600000 | tf_op jit(solution)/shard_map/pallas_call | solution.py:26
  (4 shorter events, 0.1 us)
Async XLA Ops:
  0.0 16.7 %copy-start.7 = (f32[32,256]{1,0:T(8,128)S(1)}, f32[32,256]{1,0:T(8,128)}, u32[]{:S(2)}) copy-start(f32[32,256]{1,0:T(8,128)} %constant.7.clone.twist_ref) | copy-start | bytes 98308
  1.9 3.1 %collective-permute-start = (bf16[3,136,128]{2,1,0:T(8,128)(2,1)S(1)}, bf16[3,136,128]{2,1,0:T(8,128)(2,1)S(1)}, u32[]{:S(2)}, u32[]{:S(2)}) collective-permute-start(bf16[3,136,128]{2,1,0:T(8,128)(2,1)S(1)} %get-tuple-element.24), channel_id=1, source_target_pairs={{0,1},{1,0},{2,3},{3,2},{4,5},{5,4},{6,7},{7,6},{8,9},{9,8},{10,11... | collective-permute-start | bytes 313352 | tf_op jit(solution)/shard_map/ppermute | solution.py:349
  2.4 7.1 %collective-permute-start.4 = (bf16[280,128]{1,0:T(8,128)(2,1)S(1)}, bf16[280,128]{1,0:T(8,128)(2,1)S(1)}, u32[]{:S(2)}, u32[]{:S(2)}) collective-permute-start(bf16[280,128]{1,0:T(8,128)(2,1)S(1)} %get-tuple-element.28), channel_id=1, source_target_pairs={{0,2},{1,3},{2,0},{3,1},{4,6},{5,7},{6,4},{7,5},{8,10},{9,11},{10,... | collective-permute-start | bytes 215048 | tf_op jit(solution)/shard_map/ppermute | solution.py:349
  5.0 11.8 %copy-start.5 = (bf16[512,256]{1,0:T(8,128)(2,1)S(1)}, bf16[512,256]{1,0:T(8,128)(2,1)}, u32[]{:S(2)}) copy-start(bf16[512,256]{1,0:T(8,128)(2,1)} %constant.6.clone.first_ref) | copy-start | bytes 786436
  5.0 11.8 %copy-start.6 = (bf16[256,512]{1,0:T(8,128)(2,1)S(1)}, bf16[256,512]{1,0:T(8,128)(2,1)}, u32[]{:S(2)}) copy-start(bf16[256,512]{1,0:T(8,128)(2,1)} %constant.8.clone.inner_ref) | copy-start | bytes 786436
  5.0 6.8 %collective-permute-start.1 = (bf16[264,128]{1,0:T(8,128)(2,1)S(1)}, bf16[264,128]{1,0:T(8,128)(2,1)S(1)}, u32[]{:S(2)}, u32[]{:S(2)}) collective-permute-start(bf16[264,128]{1,0:T(8,128)(2,1)S(1)} %get-tuple-element.25), channel_id=1, source_target_pairs={{0,12},{1,15},{2,14},{3,13},{4,8},{5,11},{6,10},{7,9},{8,4},{9,7},... | collective-permute-start | bytes 202760 | tf_op jit(solution)/shard_map/ppermute | solution.py:349
  8.7 6.6 %collective-permute-start.2 = (bf16[264,128]{1,0:T(8,128)(2,1)S(1)}, bf16[264,128]{1,0:T(8,128)(2,1)S(1)}, u32[]{:S(2)}, u32[]{:S(2)}) collective-permute-start(bf16[264,128]{1,0:T(8,128)(2,1)S(1)} %get-tuple-element.26), channel_id=1, source_target_pairs={{0,8},{1,11},{2,10},{3,9},{4,12},{5,15},{6,14},{7,13},{8,0},{9,3},... | collective-permute-start | bytes 202760 | tf_op jit(solution)/shard_map/ppermute | solution.py:349
  8.7 6.6 %collective-permute-start.3 = (bf16[264,128]{1,0:T(8,128)(2,1)S(1)}, bf16[264,128]{1,0:T(8,128)(2,1)S(1)}, u32[]{:S(2)}, u32[]{:S(2)}) collective-permute-start(bf16[264,128]{1,0:T(8,128)(2,1)S(1)} %get-tuple-element.27), channel_id=1, source_target_pairs={{0,4},{1,7},{2,6},{3,5},{4,0},{5,3},{6,2},{7,1},{8,12},{9,15},{10,... | collective-permute-start | bytes 202760 | tf_op jit(solution)/shard_map/ppermute | solution.py:349
  15.3 1.4 %collective-permute-start.5 = (bf16[544,128]{1,0:T(8,128)(2,1)S(1)}, bf16[544,128]{1,0:T(8,128)(2,1)S(1)}, u32[]{:S(2)}, u32[]{:S(2)}) collective-permute-start(bf16[544,128]{1,0:T(8,128)(2,1)S(1)} %get-tuple-element.31), channel_id=1, source_target_pairs={{0,1},{1,0},{2,3},{3,2},{4,5},{5,4},{6,7},{7,6},{8,9},{9,8},{10,11... | collective-permute-start | bytes 417800 | tf_op jit(solution)/shard_map/ppermute | solution.py:349
  16.7 10.7 %copy-start = (bf16[256,768]{1,0:T(8,128)(2,1)S(1)}, bf16[256,768]{1,0:T(8,128)(2,1)}, u32[]{:S(2)}) copy-start(bf16[256,768]{1,0:T(8,128)(2,1)} %refs_2_.1) | copy-start | bytes 1179652
  18.1 1.3 %collective-permute-start.6 = (bf16[3,32,256]{2,1,0:T(8,128)(2,1)S(1)}, bf16[3,32,256]{2,1,0:T(8,128)(2,1)S(1)}, u32[]{:S(2)}, u32[]{:S(2)}) collective-permute-start(bf16[3,32,256]{2,1,0:T(8,128)(2,1)S(1)} %get-tuple-element.33), channel_id=1, source_target_pairs={{0,1},{1,0},{2,3},{3,2},{4,5},{5,4},{6,7},{7,6},{8,9},{9,8},{10,11... | collective-permute-start | bytes 147464 | tf_op jit(solution)/shard_map/ppermute | solution.py:349
  18.3 5.6 %collective-permute-start.10 = (bf16[80,256]{1,0:T(8,128)(2,1)S(1)}, bf16[80,256]{1,0:T(8,128)(2,1)S(1)}, u32[]{:S(2)}, u32[]{:S(2)}) collective-permute-start(bf16[80,256]{1,0:T(8,128)(2,1)S(1)} %get-tuple-element.37), channel_id=1, source_target_pairs={{0,2},{1,3},{2,0},{3,1},{4,6},{5,7},{6,4},{7,5},{8,10},{9,11},{10,... | collective-permute-start | bytes 122888 | tf_op jit(solution)/shard_map/ppermute | solution.py:349
  19.4 8.0 %copy-start.1 = (bf16[256,256]{1,0:T(8,128)(2,1)S(1)}, bf16[256,256]{1,0:T(8,128)(2,1)}, u32[]{:S(2)}) copy-start(bf16[256,256]{1,0:T(8,128)(2,1)} %refs_0_.1) | copy-start | bytes 393220
  19.4 6.0 %collective-permute-start.7 = (bf16[64,256]{1,0:T(8,128)(2,1)S(1)}, bf16[64,256]{1,0:T(8,128)(2,1)S(1)}, u32[]{:S(2)}, u32[]{:S(2)}) collective-permute-start(bf16[64,256]{1,0:T(8,128)(2,1)S(1)} %get-tuple-element.34), channel_id=1, source_target_pairs={{0,12},{1,15},{2,14},{3,13},{4,8},{5,11},{6,10},{7,9},{8,4},{9,7},... | collective-permute-start | bytes 98312 | tf_op jit(solution)/shard_map/ppermute | solution.py:349
  22.0 5.1 %collective-permute-start.8 = (bf16[64,256]{1,0:T(8,128)(2,1)S(1)}, bf16[64,256]{1,0:T(8,128)(2,1)S(1)}, u32[]{:S(2)}, u32[]{:S(2)}) collective-permute-start(bf16[64,256]{1,0:T(8,128)(2,1)S(1)} %get-tuple-element.35), channel_id=1, source_target_pairs={{0,8},{1,11},{2,10},{3,9},{4,12},{5,15},{6,14},{7,13},{8,0},{9,3},... | collective-permute-start | bytes 98312 | tf_op jit(solution)/shard_map/ppermute | solution.py:349
  22.1 4.9 %collective-permute-start.9 = (bf16[64,256]{1,0:T(8,128)(2,1)S(1)}, bf16[64,256]{1,0:T(8,128)(2,1)S(1)}, u32[]{:S(2)}, u32[]{:S(2)}) collective-permute-start(bf16[64,256]{1,0:T(8,128)(2,1)S(1)} %get-tuple-element.36), channel_id=1, source_target_pairs={{0,4},{1,7},{2,6},{3,5},{4,0},{5,3},{6,2},{7,1},{8,12},{9,15},{10,... | collective-permute-start | bytes 98312 | tf_op jit(solution)/shard_map/ppermute | solution.py:349
  27.0 0.7 %copy-start.3 = (f32[3,768]{1,0:T(4,128)S(1)}, f32[3,768]{1,0:T(4,128)}, u32[]{:S(2)}) copy-start(f32[3,768]{1,0:T(4,128)} %refs_3_.1) | copy-start | bytes 27652
  27.0 0.7 %copy-start.4 = (f32[256]{0:T(256)S(1)}, f32[256]{0:T(256)}, u32[]{:S(2)}) copy-start(f32[256]{0:T(256)} %param.12) | copy-start | bytes 3076
  27.0 1.3 %copy-start.2 = (bf16[256,256]{1,0:T(8,128)(2,1)S(1)}, bf16[256,256]{1,0:T(8,128)(2,1)}, u32[]{:S(2)}) copy-start(bf16[256,256]{1,0:T(8,128)(2,1)} %w_ref.3) | copy-start | bytes 393220
  27.1 1.3 %collective-permute-start.11 = (bf16[128,256]{1,0:T(8,128)(2,1)S(1)}, bf16[128,256]{1,0:T(8,128)(2,1)S(1)}, u32[]{:S(2)}, u32[]{:S(2)}) collective-permute-start(bf16[128,256]{1,0:T(8,128)(2,1)S(1)} %get-tuple-element.40), channel_id=1, source_target_pairs={{0,1},{1,0},{2,3},{3,2},{4,5},{5,4},{6,7},{7,6},{8,9},{9,8},{10,11... | collective-permute-start | bytes 196616 | tf_op jit(solution)/shard_map/ppermute | solution.py:349

commit v26 on v21

--- a/solution.py
+++ b/solution.py
@@ -430,7 +430,7 @@
         moved=1_500_000,
     )
     conv = ((width, rows), jnp.bfloat16)
-    parts = swap(parts)
+    parts, query = lax.optimization_barrier((swap(parts), query))
     parts = call(
         functools.partial(convolve_body, chans, short_filter.shape[0] - 1),
         pieces((width, rows), 0),

time: 29.4 us -> 29.4 us (level)
  local copies, waits for them, and re-layouts: 0.36 us -> 0.67 us
  waiting for transfers between devices: 10.7 us -> 10.4 us
    unnamed x16, local copies, waits for them, and re-layouts: 0.36 us -> 0.67 us
    ppermute x12, waiting for transfers between devices: 10.7 us -> 10.4 us  [permute(): lax.ppermute(array, seq, [(i, partner(i)) for i in range(lax.axis_size(se...]
where the time goes in v26:
time: 29.4 us; the launch traced here: 29.3 us
  starting transfers between devices  13.7 us (47%)
  waiting for transfers between devices  10.4 us (35%)
  Pallas kernels  4.44 us (15%)
  local copies, waits for them, and re-layouts  0.67 us (2%)
    ppermute x12, starting transfers between devices, permute(): lax.ppermute(array, seq, [(i, partner(i)) for i in range(lax.axis_size(se...  13.7 us
    ppermute x12, waiting for transfers between devices, permute(): lax.ppermute(array, seq, [(i, partner(i)) for i in range(lax.axis_size(se...  10.4 us
    pallas_call x8, Pallas kernels, call(): pl.pallas_call(body, out_shape=outs, in_specs=[whole(space) for space in...  4.44 us
    unnamed x16, local copies, waits for them, and re-layouts  0.67 us
  transfers between devices with their start and end apart: 12, of which 7 were waited for; matrix products, arithmetic and copies ran while one was open for 0% of the time, Pallas kernels for 1%

profile of v26, /device:TPU:0, one launch (start us, length us, event | category | flops | bytes accessed | tf_op | source)
XLA Modules:
  0.0 29.3 jit_solution(11163238839736359425)
XLA Ops:
  0.0 0.0 copy-start.3
  0.0 1.8 %shard_map.109 = (bf16[3,136,128]{2,1,0:T(8,128)(2,1)S(1)}, bf16[3,136,128]{2,1,0:T(8,128)(2,1)S(1)}, bf16[280,128]{1,0:T(8,128)(2,1)S(1)}, bf16[136,128]{1,0:T(8,128)(2,1)S(1)}) custom-call(bf16[256,256]{1,0:T(8,128)(2,1)} %tokens_ref.1, f32[1,256]{1,0:T(1,128)} %bitcast.2, bf16[256,768]{1,0:T(8,128)(2,1)} %w_ref.2, f32[3,768]{1,0:T(4,128)} %short_ref.1, ...), custom_call_target="tpu_custom_call" | custom-call | flops 100663296 | bytes 1500000 | tf_op jit(solution)/shard_map/pallas_call | solution.py:26
  1.8 0.0 copy-start
  1.8 0.5 %collective-permute-start = (bf16[3,136,128]{2,1,0:T(8,128)(2,1)S(1)}, bf16[3,136,128]{2,1,0:T(8,128)(2,1)S(1)}, u32[]{:S(2)}, u32[]{:S(2)}) collective-permute-start(bf16[3,136,128]{2,1,0:T(8,128)(2,1)S(1)} %get-tuple-element.27), channel_id=1, source_target_pairs={{0,1},{1,0},{2,3},{3,2},{4,5},{5,4},{6,7},{7,6},{8,9},{9,8},{10,11... | collective-permute-start | bytes 313352 | tf_op jit(solution)/shard_map/ppermute | solution.py:349
  2.3 2.6 %collective-permute-start.4 = (bf16[280,128]{1,0:T(8,128)(2,1)S(1)}, bf16[280,128]{1,0:T(8,128)(2,1)S(1)}, u32[]{:S(2)}, u32[]{:S(2)}) collective-permute-start(bf16[280,128]{1,0:T(8,128)(2,1)S(1)} %get-tuple-element.31), channel_id=1, source_target_pairs={{0,2},{1,3},{2,0},{3,1},{4,6},{5,7},{6,4},{7,5},{8,10},{9,11},{10,... | collective-permute-start | bytes 215048 | tf_op jit(solution)/shard_map/ppermute | solution.py:349
  4.9 0.0 collective-permute-done.got_ref
  4.9 3.7 %collective-permute-start.1 = (bf16[264,128]{1,0:T(8,128)(2,1)S(1)}, bf16[264,128]{1,0:T(8,128)(2,1)S(1)}, u32[]{:S(2)}, u32[]{:S(2)}) collective-permute-start(bf16[264,128]{1,0:T(8,128)(2,1)S(1)} %get-tuple-element.28), channel_id=1, source_target_pairs={{0,12},{1,15},{2,14},{3,13},{4,8},{5,11},{6,10},{7,9},{8,4},{9,7},... | collective-permute-start | bytes 202760 | tf_op jit(solution)/shard_map/ppermute | solution.py:349
  8.6 0.0 collective-permute-start.2
  8.6 0.8 %collective-permute-start.3 = (bf16[264,128]{1,0:T(8,128)(2,1)S(1)}, bf16[264,128]{1,0:T(8,128)(2,1)S(1)}, u32[]{:S(2)}, u32[]{:S(2)}) collective-permute-start(bf16[264,128]{1,0:T(8,128)(2,1)S(1)} %get-tuple-element.30), channel_id=1, source_target_pairs={{0,4},{1,7},{2,6},{3,5},{4,0},{5,3},{6,2},{7,1},{8,12},{9,15},{10,... | collective-permute-start | bytes 202760 | tf_op jit(solution)/shard_map/ppermute | solution.py:349
  9.4 0.0 collective-permute-done.4.refs_3_
  9.4 2.4 %collective-permute-done.1.refs_0_ = bf16[264,128]{1,0:T(8,128)(2,1)S(1)} collective-permute-done((bf16[264,128]{1,0:T(8,128)(2,1)S(1)}, bf16[264,128]{1,0:T(8,128)(2,1)S(1)}, u32[]{:S(2)}, u32[]{:S(2)}) %collective-permute-start.1) | collective-permute-done | bytes 67616 | tf_op jit(solution)/shard_map/ppermute | solution.py:349
  11.8 3.5 %collective-permute-done.2.refs_1_ = bf16[264,128]{1,0:T(8,128)(2,1)S(1)} collective-permute-done((bf16[264,128]{1,0:T(8,128)(2,1)S(1)}, bf16[264,128]{1,0:T(8,128)(2,1)S(1)}, u32[]{:S(2)}, u32[]{:S(2)}) %collective-permute-start.2) | collective-permute-done | bytes 67616 | tf_op jit(solution)/shard_map/ppermute | solution.py:349
  15.2 0.0 collective-permute-done.3.refs_2_
  15.2 0.0 copy-start.1
  15.3 0.0 copy-start.4
  15.3 0.0 copy-start.5
  15.3 0.0 copy-start.6
  15.3 0.0 copy-start.7
  15.3 0.2 collective-permute-start.5
  15.5 0.0 copy-done.3
  15.5 0.0 copy-done
  15.5 0.6 %copy-done.1 = bf16[256,256]{1,0:T(8,128)(2,1)S(1)} copy-done((bf16[256,256]{1,0:T(8,128)(2,1)S(1)}, bf16[256,256]{1,0:T(8,128)(2,1)}, u32[]{:S(2)}) %copy-start.1) | copy-done | bytes 131096
  16.1 0.0 copy-done.4
  16.1 0.3 %shard_map.112.query_ref = f32[256,256]{1,0:T(8,128)S(1)} custom-call(bf16[256,256]{1,0:T(8,128)(2,1)S(1)} %copy-done.1, f32[1,256]{1,0:T(1,128)S(1)} %bitcast.3, bf16[256,768]{1,0:T(8,128)(2,1)S(1)} %copy-done, f32[3,768]{1,0:T(4,128)S(1)} %copy-done.3), custom_call_target="tpu_custom_call" | custom-call | flops 33554432 | bytes 800000 | tf_op jit(solution)/shard_map/pallas_call | solution.py:26
  16.5 0.3 collective-permute-done.5.refs_1_
  16.7 0.0 copy-done.5
  16.7 0.0 copy-done.6
  16.7 0.0 copy-done.7
  16.7 1.4 %shard_map.113 = (bf16[3,32,256]{2,1,0:T(8,128)(2,1)S(1)}, bf16[3,32,256]{2,1,0:T(8,128)(2,1)S(1)}, bf16[80,256]{1,0:T(8,128)(2,1)S(1)}, bf16[32,256]{1,0:T(8,128)(2,1)S(1)}) custom-call(bf16[512,256]{1,0:T(8,128)(2,1)S(1)} %copy-done.5, f32[32,256]{1,0:T(8,128)S(1)} %copy-done.7, bf16[256,512]{1,0:T(8,128)(2,1)S(1)} %copy-done.6, ...), custom_call_target="tpu_custom_call" | custom-call | flops 603979776 | bytes 2000000 | tf_op jit(solution)/shard_map/pallas_call | solution.py:26
  18.1 0.2 collective-permute-start.6
  18.3 1.0 %collective-permute-start.10 = (bf16[80,256]{1,0:T(8,128)(2,1)S(1)}, bf16[80,256]{1,0:T(8,128)(2,1)S(1)}, u32[]{:S(2)}, u32[]{:S(2)}) collective-permute-start(bf16[80,256]{1,0:T(8,128)(2,1)S(1)} %get-tuple-element.43), channel_id=1, source_target_pairs={{0,2},{1,3},{2,0},{3,1},{4,6},{5,7},{6,4},{7,5},{8,10},{9,11},{10,... | collective-permute-start | bytes 122888 | tf_op jit(solution)/shard_map/ppermute | solution.py:349
  19.3 0.1 collective-permute-done.6.got_ref
  19.4 0.0 copy-start.2
  19.4 2.5 %collective-permute-start.7 = (bf16[64,256]{1,0:T(8,128)(2,1)S(1)}, bf16[64,256]{1,0:T(8,128)(2,1)S(1)}, u32[]{:S(2)}, u32[]{:S(2)}) collective-permute-start(bf16[64,256]{1,0:T(8,128)(2,1)S(1)} %get-tuple-element.40), channel_id=1, source_target_pairs={{0,12},{1,15},{2,14},{3,13},{4,8},{5,11},{6,10},{7,9},{8,4},{9,7},... | collective-permute-start | bytes 98312 | tf_op jit(solution)/shard_map/ppermute | solution.py:349
  22.0 0.2 collective-permute-start.8
  22.1 1.8 %collective-permute-start.9 = (bf16[64,256]{1,0:T(8,128)(2,1)S(1)}, bf16[64,256]{1,0:T(8,128)(2,1)S(1)}, u32[]{:S(2)}, u32[]{:S(2)}) collective-permute-start(bf16[64,256]{1,0:T(8,128)(2,1)S(1)} %get-tuple-element.42), channel_id=1, source_target_pairs={{0,4},{1,7},{2,6},{3,5},{4,0},{5,3},{6,2},{7,1},{8,12},{9,15},{10,... | collective-permute-start | bytes 98312 | tf_op jit(solution)/shard_map/ppermute | solution.py:349
  23.9 0.0 collective-permute-done.10.refs_3_
  23.9 1.6 %collective-permute-done.7.refs_0_ = bf16[64,256]{1,0:T(8,128)(2,1)S(1)} collective-permute-done((bf16[64,256]{1,0:T(8,128)(2,1)S(1)}, bf16[64,256]{1,0:T(8,128)(2,1)S(1)}, u32[]{:S(2)}, u32[]{:S(2)}) %collective-permute-start.7) | collective-permute-done | bytes 32800 | tf_op jit(solution)/shard_map/ppermute | solution.py:349
  25.5 1.6 %collective-permute-done.8.refs_1_ = bf16[64,256]{1,0:T(8,128)(2,1)S(1)} collective-permute-done((bf16[64,256]{1,0:T(8,128)(2,1)S(1)}, bf16[64,256]{1,0:T(8,128)(2,1)S(1)}, u32[]{:S(2)}, u32[]{:S(2)}) %collective-permute-start.8) | collective-permute-done | bytes 32800 | tf_op jit(solution)/shard_map/ppermute | solution.py:349
  27.0 0.0 collective-permute-done.9.refs_2_
  27.1 0.3 %collective-permute-start.11 = (bf16[128,256]{1,0:T(8,128)(2,1)S(1)}, bf16[128,256]{1,0:T(8,128)(2,1)S(1)}, u32[]{:S(2)}, u32[]{:S(2)}) collective-permute-start(bf16[128,256]{1,0:T(8,128)(2,1)S(1)} %get-tuple-element.46), channel_id=1, source_target_pairs={{0,1},{1,0},{2,3},{3,2},{4,5},{5,4},{6,7},{7,6},{8,9},{9,8},{10,11... | collective-permute-start | bytes 196616 | tf_op jit(solution)/shard_map/ppermute | solution.py:349
  27.4 1.0 %collective-permute-done.11.refs_1_ = bf16[128,256]{1,0:T(8,128)(2,1)S(1)} collective-permute-done((bf16[128,256]{1,0:T(8,128)(2,1)S(1)}, bf16[128,256]{1,0:T(8,128)(2,1)S(1)}, u32[]{:S(2)}, u32[]{:S(2)}) %collective-permute-start.11) | collective-permute-done | bytes 65568 | tf_op jit(solution)/shard_map/ppermute | solution.py:349
  28.4 0.0 copy-done.2
  28.4 0.9 %shard_map.116 = bf16[256,256]{1,0:T(8,128)(2,1)} custom-call(f32[256,256]{1,0:T(8,128)S(1)} %shard_map.112.query_ref, bf16[256,256]{1,0:T(8,128)(2,1)S(1)} %copy-done.2, bf16[128,256]{1,0:T(8,128)(2,1)S(1)} %get-tuple-element.45.refs_0_, bf16[128,256]{1,0:T(8,128)(2,1)S(1)} %collective-permute-done.11.refs_1_), custom_call_target="tpu_custom_call" | custom-call | flops 33554432 | bytes 600000 | tf_op jit(solution)/shard_map/pallas_call | solution.py:26
  (4 shorter events, 0.1 us)
Async XLA Ops:
  0.0 15.5 %copy-start.3 = (f32[3,768]{1,0:T(4,128)S(1)}, f32[3,768]{1,0:T(4,128)}, u32[]{:S(2)}) copy-start(f32[3,768]{1,0:T(4,128)} %short_ref.1) | copy-start | bytes 27652
  1.8 13.7 %copy-start = (bf16[256,768]{1,0:T(8,128)(2,1)S(1)}, bf16[256,768]{1,0:T(8,128)(2,1)}, u32[]{:S(2)}) copy-start(bf16[256,768]{1,0:T(8,128)(2,1)} %w_ref.2) | copy-start | bytes 1179652
  1.8 3.1 %collective-permute-start = (bf16[3,136,128]{2,1,0:T(8,128)(2,1)S(1)}, bf16[3,136,128]{2,1,0:T(8,128)(2,1)S(1)}, u32[]{:S(2)}, u32[]{:S(2)}) collective-permute-start(bf16[3,136,128]{2,1,0:T(8,128)(2,1)S(1)} %get-tuple-element.27), channel_id=1, source_target_pairs={{0,1},{1,0},{2,3},{3,2},{4,5},{5,4},{6,7},{7,6},{8,9},{9,8},{10,11... | collective-permute-start | bytes 313352 | tf_op jit(solution)/shard_map/ppermute | solution.py:349
  2.3 7.1 %collective-permute-start.4 = (bf16[280,128]{1,0:T(8,128)(2,1)S(1)}, bf16[280,128]{1,0:T(8,128)(2,1)S(1)}, u32[]{:S(2)}, u32[]{:S(2)}) collective-permute-start(bf16[280,128]{1,0:T(8,128)(2,1)S(1)} %get-tuple-element.31), channel_id=1, source_target_pairs={{0,2},{1,3},{2,0},{3,1},{4,6},{5,7},{6,4},{7,5},{8,10},{9,11},{10,... | collective-permute-start | bytes 215048 | tf_op jit(solution)/shard_map/ppermute | solution.py:349
  4.9 6.8 %collective-permute-start.1 = (bf16[264,128]{1,0:T(8,128)(2,1)S(1)}, bf16[264,128]{1,0:T(8,128)(2,1)S(1)}, u32[]{:S(2)}, u32[]{:S(2)}) collective-permute-start(bf16[264,128]{1,0:T(8,128)(2,1)S(1)} %get-tuple-element.28), channel_id=1, source_target_pairs={{0,12},{1,15},{2,14},{3,13},{4,8},{5,11},{6,10},{7,9},{8,4},{9,7},... | collective-permute-start | bytes 202760 | tf_op jit(solution)/shard_map/ppermute | solution.py:349
  8.6 6.6 %collective-permute-start.2 = (bf16[264,128]{1,0:T(8,128)(2,1)S(1)}, bf16[264,128]{1,0:T(8,128)(2,1)S(1)}, u32[]{:S(2)}, u32[]{:S(2)}) collective-permute-start(bf16[264,128]{1,0:T(8,128)(2,1)S(1)} %get-tuple-element.29), channel_id=1, source_target_pairs={{0,8},{1,11},{2,10},{3,9},{4,12},{5,15},{6,14},{7,13},{8,0},{9,3},... | collective-permute-start | bytes 202760 | tf_op jit(solution)/shard_map/ppermute | solution.py:349
  8.6 6.6 %collective-permute-start.3 = (bf16[264,128]{1,0:T(8,128)(2,1)S(1)}, bf16[264,128]{1,0:T(8,128)(2,1)S(1)}, u32[]{:S(2)}, u32[]{:S(2)}) collective-permute-start(bf16[264,128]{1,0:T(8,128)(2,1)S(1)} %get-tuple-element.30), channel_id=1, source_target_pairs={{0,4},{1,7},{2,6},{3,5},{4,0},{5,3},{6,2},{7,1},{8,12},{9,15},{10,... | collective-permute-start | bytes 202760 | tf_op jit(solution)/shard_map/ppermute | solution.py:349
  15.2 0.9 %copy-start.1 = (bf16[256,256]{1,0:T(8,128)(2,1)S(1)}, bf16[256,256]{1,0:T(8,128)(2,1)}, u32[]{:S(2)}) copy-start(bf16[256,256]{1,0:T(8,128)(2,1)} %tokens_ref.1) | copy-start | bytes 393220
  15.3 0.9 %copy-start.4 = (f32[256]{0:T(256)S(1)}, f32[256]{0:T(256)}, u32[]{:S(2)}) copy-start(f32[256]{0:T(256)} %param.12) | copy-start | bytes 3076
  15.3 1.5 %copy-start.5 = (bf16[512,256]{1,0:T(8,128)(2,1)S(1)}, bf16[512,256]{1,0:T(8,128)(2,1)}, u32[]{:S(2)}) copy-start(bf16[512,256]{1,0:T(8,128)(2,1)} %constant.6.clone.first_ref) | copy-start | bytes 786436
  15.3 1.5 %copy-start.6 = (bf16[256,512]{1,0:T(8,128)(2,1)S(1)}, bf16[256,512]{1,0:T(8,128)(2,1)}, u32[]{:S(2)}) copy-start(bf16[256,512]{1,0:T(8,128)(2,1)} %constant.8.clone.inner_ref) | copy-start | bytes 786436
  15.3 1.4 %copy-start.7 = (f32[32,256]{1,0:T(8,128)S(1)}, f32[32,256]{1,0:T(8,128)}, u32[]{:S(2)}) copy-start(f32[32,256]{1,0:T(8,128)} %constant.7.clone.twist_ref) | copy-start | bytes 98308
  15.3 1.4 %collective-permute-start.5 = (bf16[544,128]{1,0:T(8,128)(2,1)S(1)}, bf16[544,128]{1,0:T(8,128)(2,1)S(1)}, u32[]{:S(2)}, u32[]{:S(2)}) collective-permute-start(bf16[544,128]{1,0:T(8,128)(2,1)S(1)} %get-tuple-element.34), channel_id=1, source_target_pairs={{0,1},{1,0},{2,3},{3,2},{4,5},{5,4},{6,7},{7,6},{8,9},{9,8},{10,11... | collective-permute-start | bytes 417800 | tf_op jit(solution)/shard_map/ppermute | solution.py:349
  18.1 1.3 %collective-permute-start.6 = (bf16[3,32,256]{2,1,0:T(8,128)(2,1)S(1)}, bf16[3,32,256]{2,1,0:T(8,128)(2,1)S(1)}, u32[]{:S(2)}, u32[]{:S(2)}) collective-permute-start(bf16[3,32,256]{2,1,0:T(8,128)(2,1)S(1)} %get-tuple-element.39), channel_id=1, source_target_pairs={{0,1},{1,0},{2,3},{3,2},{4,5},{5,4},{6,7},{7,6},{8,9},{9,8},{10,11... | collective-permute-start | bytes 147464 | tf_op jit(solution)/shard_map/ppermute | solution.py:349
  18.3 5.6 %collective-permute-start.10 = (bf16[80,256]{1,0:T(8,128)(2,1)S(1)}, bf16[80,256]{1,0:T(8,128)(2,1)S(1)}, u32[]{:S(2)}, u32[]{:S(2)}) collective-permute-start(bf16[80,256]{1,0:T(8,128)(2,1)S(1)} %get-tuple-element.43), channel_id=1, source_target_pairs={{0,2},{1,3},{2,0},{3,1},{4,6},{5,7},{6,4},{7,5},{8,10},{9,11},{10,... | collective-permute-start | bytes 122888 | tf_op jit(solution)/shard_map/ppermute | solution.py:349
  19.4 9.0 %copy-start.2 = (bf16[256,256]{1,0:T(8,128)(2,1)S(1)}, bf16[256,256]{1,0:T(8,128)(2,1)}, u32[]{:S(2)}) copy-start(bf16[256,256]{1,0:T(8,128)(2,1)} %w_ref.3) | copy-start | bytes 393220
  19.4 6.0 %collective-permute-start.7 = (bf16[64,256]{1,0:T(8,128)(2,1)S(1)}, bf16[64,256]{1,0:T(8,128)(2,1)S(1)}, u32[]{:S(2)}, u32[]{:S(2)}) collective-permute-start(bf16[64,256]{1,0:T(8,128)(2,1)S(1)} %get-tuple-element.40), channel_id=1, source_target_pairs={{0,12},{1,15},{2,14},{3,13},{4,8},{5,11},{6,10},{7,9},{8,4},{9,7},... | collective-permute-start | bytes 98312 | tf_op jit(solution)/shard_map/ppermute | solution.py:349
  22.0 5.1 %collective-permute-start.8 = (bf16[64,256]{1,0:T(8,128)(2,1)S(1)}, bf16[64,256]{1,0:T(8,128)(2,1)S(1)}, u32[]{:S(2)}, u32[]{:S(2)}) collective-permute-start(bf16[64,256]{1,0:T(8,128)(2,1)S(1)} %get-tuple-element.41), channel_id=1, source_target_pairs={{0,8},{1,11},{2,10},{3,9},{4,12},{5,15},{6,14},{7,13},{8,0},{9,3},... | collective-permute-start | bytes 98312 | tf_op jit(solution)/shard_map/ppermute | solution.py:349
  22.1 4.9 %collective-permute-start.9 = (bf16[64,256]{1,0:T(8,128)(2,1)S(1)}, bf16[64,256]{1,0:T(8,128)(2,1)S(1)}, u32[]{:S(2)}, u32[]{:S(2)}) collective-permute-start(bf16[64,256]{1,0:T(8,128)(2,1)S(1)} %get-tuple-element.42), channel_id=1, source_target_pairs={{0,4},{1,7},{2,6},{3,5},{4,0},{5,3},{6,2},{7,1},{8,12},{9,15},{10,... | collective-permute-start | bytes 98312 | tf_op jit(solution)/shard_map/ppermute | solution.py:349
  27.1 1.3 %collective-permute-start.11 = (bf16[128,256]{1,0:T(8,128)(2,1)S(1)}, bf16[128,256]{1,0:T(8,128)(2,1)S(1)}, u32[]{:S(2)}, u32[]{:S(2)}) collective-permute-start(bf16[128,256]{1,0:T(8,128)(2,1)S(1)} %get-tuple-element.46), channel_id=1, source_target_pairs={{0,1},{1,0},{2,3},{3,2},{4,5},{5,4},{6,7},{7,6},{8,9},{9,8},{10,11... | collective-permute-start | bytes 196616 | tf_op jit(solution)/shard_map/ppermute | solution.py:349

commit v27 on v21

--- a/solution.py
+++ b/solution.py
@@ -56,7 +56,7 @@
 
 
 def routes_of(chips):
-    return [(d, d + 1) for d in range(chips - 2, 1, -2)]
+    return [(d, d + 1) for d in range(chips - 2, 2, -2)] + [(3, 2)]
 
 
 def carried(route, core):

time: 29.4 us -> 30 us (1.020)
  starting transfers between devices: 13.7 us -> 14.5 us
  waiting for transfers between devices: 10.7 us -> 10.3 us
    ppermute x12, starting transfers between devices: 13.7 us -> 14.5 us  [permute(): lax.ppermute(array, seq, [(i, partner(i)) for i in range(lax.axis_size(se...]
    ppermute x12, waiting for transfers between devices: 10.7 us -> 10.3 us  [permute(): lax.ppermute(array, seq, [(i, partner(i)) for i in range(lax.axis_size(se...]
  transfers between devices with their start and end apart: 12 -> 12, of which waited for: 7 -> 8; matrix products, arithmetic and copies ran while one was open for 0% -> 0% of each run, Pallas kernels for 1% -> 1%
where the time goes in v27:
time: 30 us; the launch traced here: 29.9 us
  starting transfers between devices  14.5 us (48%)
  waiting for transfers between devices  10.3 us (34%)
  Pallas kernels  4.41 us (15%)
  local copies, waits for them, and re-layouts  0.6 us (2%)
    ppermute x12, starting transfers between devices, permute(): lax.ppermute(array, seq, [(i, partner(i)) for i in range(lax.axis_size(se...  14.5 us
    ppermute x12, waiting for transfers between devices, permute(): lax.ppermute(array, seq, [(i, partner(i)) for i in range(lax.axis_size(se...  10.3 us
    pallas_call x8, Pallas kernels, call(): pl.pallas_call(body, out_shape=outs, in_specs=[whole(space) for space in...  4.41 us
    unnamed x16, local copies, waits for them, and re-layouts  0.6 us
  transfers between devices with their start and end apart: 12, of which 8 were waited for; matrix products, arithmetic and copies ran while one was open for 0% of the time, Pallas kernels for 1%

profile of v27, /device:TPU:0, one launch (start us, length us, event | category | flops | bytes accessed | tf_op | source)
XLA Modules:
  0.0 29.9 jit_solution(1741074814423007800)
XLA Ops:
  0.0 0.0 copy-start.7
  0.0 1.8 %shard_map.110 = (bf16[3,136,128]{2,1,0:T(8,128)(2,1)S(1)}, bf16[3,136,128]{2,1,0:T(8,128)(2,1)S(1)}, bf16[280,128]{1,0:T(8,128)(2,1)S(1)}, bf16[136,128]{1,0:T(8,128)(2,1)S(1)}) custom-call(bf16[256,256]{1,0:T(8,128)(2,1)} %refs_0_.1, f32[1,256]{1,0:T(1,128)} %bitcast.2, bf16[256,768]{1,0:T(8,128)(2,1)} %refs_2_.1, f32[3,768]{1,0:T(4,128)} %refs_3_.1, ...), custom_call_target="tpu_custom_call" | custom-call | flops 100663296 | bytes 1500000 | tf_op jit(solution)/shard_map/pallas_call | solution.py:26
  1.8 0.5 %collective-permute-start = (bf16[3,136,128]{2,1,0:T(8,128)(2,1)S(1)}, bf16[3,136,128]{2,1,0:T(8,128)(2,1)S(1)}, u32[]{:S(2)}, u32[]{:S(2)}) collective-permute-start(bf16[3,136,128]{2,1,0:T(8,128)(2,1)S(1)} %get-tuple-element.24), channel_id=1, source_target_pairs={{0,1},{1,0},{2,3},{3,2},{4,5},{5,4},{6,7},{7,6},{8,9},{9,8},{10,11... | collective-permute-start | bytes 313352 | tf_op jit(solution)/shard_map/ppermute | solution.py:349
  2.3 2.6 %collective-permute-start.4 = (bf16[280,128]{1,0:T(8,128)(2,1)S(1)}, bf16[280,128]{1,0:T(8,128)(2,1)S(1)}, u32[]{:S(2)}, u32[]{:S(2)}) collective-permute-start(bf16[280,128]{1,0:T(8,128)(2,1)S(1)} %get-tuple-element.28), channel_id=1, source_target_pairs={{0,2},{1,3},{2,0},{3,1},{4,6},{5,7},{6,4},{7,5},{8,10},{9,11},{10,... | collective-permute-start | bytes 215048 | tf_op jit(solution)/shard_map/ppermute | solution.py:349
  4.9 0.0 collective-permute-done.got_ref
  4.9 0.0 copy-start.5
  4.9 0.0 copy-start.6
  4.9 3.7 %collective-permute-start.1 = (bf16[264,128]{1,0:T(8,128)(2,1)S(1)}, bf16[264,128]{1,0:T(8,128)(2,1)S(1)}, u32[]{:S(2)}, u32[]{:S(2)}) collective-permute-start(bf16[264,128]{1,0:T(8,128)(2,1)S(1)} %get-tuple-element.25), channel_id=1, source_target_pairs={{0,12},{1,15},{2,14},{3,13},{4,8},{5,11},{6,10},{7,9},{8,4},{9,7},... | collective-permute-start | bytes 202760 | tf_op jit(solution)/shard_map/ppermute | solution.py:349
  8.6 0.0 collective-permute-start.2
  8.6 1.5 %collective-permute-start.3 = (bf16[264,128]{1,0:T(8,128)(2,1)S(1)}, bf16[264,128]{1,0:T(8,128)(2,1)S(1)}, u32[]{:S(2)}, u32[]{:S(2)}) collective-permute-start(bf16[264,128]{1,0:T(8,128)(2,1)S(1)} %get-tuple-element.27), channel_id=1, source_target_pairs={{0,6},{1,5},{2,4},{3,7},{4,2},{5,1},{6,0},{7,3},{8,14},{9,13},{10,... | collective-permute-start | bytes 202760 | tf_op jit(solution)/shard_map/ppermute | solution.py:349
  10.0 0.0 collective-permute-done.4.refs_3_
  10.1 1.7 %collective-permute-done.1.refs_0_ = bf16[264,128]{1,0:T(8,128)(2,1)S(1)} collective-permute-done((bf16[264,128]{1,0:T(8,128)(2,1)S(1)}, bf16[264,128]{1,0:T(8,128)(2,1)S(1)}, u32[]{:S(2)}, u32[]{:S(2)}) %collective-permute-start.1) | collective-permute-done | bytes 67616 | tf_op jit(solution)/shard_map/ppermute | solution.py:349
  11.8 3.5 %collective-permute-done.2.refs_1_ = bf16[264,128]{1,0:T(8,128)(2,1)S(1)} collective-permute-done((bf16[264,128]{1,0:T(8,128)(2,1)S(1)}, bf16[264,128]{1,0:T(8,128)(2,1)S(1)}, u32[]{:S(2)}, u32[]{:S(2)}) %collective-permute-start.2) | collective-permute-done | bytes 67616 | tf_op jit(solution)/shard_map/ppermute | solution.py:349
  15.2 0.0 collective-permute-done.3.refs_2_
  15.2 0.1 collective-permute-start.5
  15.4 1.3 %collective-permute-done.5.refs_1_ = bf16[544,128]{1,0:T(8,128)(2,1)S(1)} collective-permute-done((bf16[544,128]{1,0:T(8,128)(2,1)S(1)}, bf16[544,128]{1,0:T(8,128)(2,1)S(1)}, u32[]{:S(2)}, u32[]{:S(2)}) %collective-permute-start.5) | collective-permute-done | bytes 139296 | tf_op jit(solution)/shard_map/ppermute | solution.py:349
  16.7 0.0 copy-done.7
  16.7 0.0 copy-done.5
  16.7 0.0 copy-done.6
  16.7 0.0 copy-start
  16.7 1.3 %shard_map.113 = (bf16[3,32,256]{2,1,0:T(8,128)(2,1)S(1)}, bf16[3,32,256]{2,1,0:T(8,128)(2,1)S(1)}, bf16[80,256]{1,0:T(8,128)(2,1)S(1)}, bf16[32,256]{1,0:T(8,128)(2,1)S(1)}) custom-call(bf16[512,256]{1,0:T(8,128)(2,1)S(1)} %copy-done.5, f32[32,256]{1,0:T(8,128)S(1)} %copy-done.7, bf16[256,512]{1,0:T(8,128)(2,1)S(1)} %copy-done.6, ...), custom_call_target="tpu_custom_call" | custom-call | flops 603979776 | bytes 2000000 | tf_op jit(solution)/shard_map/pallas_call | solution.py:26
  18.0 0.2 collective-permute-start.6
  18.2 1.0 %collective-permute-start.10 = (bf16[80,256]{1,0:T(8,128)(2,1)S(1)}, bf16[80,256]{1,0:T(8,128)(2,1)S(1)}, u32[]{:S(2)}, u32[]{:S(2)}) collective-permute-start(bf16[80,256]{1,0:T(8,128)(2,1)S(1)} %get-tuple-element.37), channel_id=1, source_target_pairs={{0,2},{1,3},{2,0},{3,1},{4,6},{5,7},{6,4},{7,5},{8,10},{9,11},{10,... | collective-permute-start | bytes 122888 | tf_op jit(solution)/shard_map/ppermute | solution.py:349
  19.2 0.1 collective-permute-done.6.got_ref
  19.3 0.0 copy-start.1
  19.3 2.5 %collective-permute-start.7 = (bf16[64,256]{1,0:T(8,128)(2,1)S(1)}, bf16[64,256]{1,0:T(8,128)(2,1)S(1)}, u32[]{:S(2)}, u32[]{:S(2)}) collective-permute-start(bf16[64,256]{1,0:T(8,128)(2,1)S(1)} %get-tuple-element.34), channel_id=1, source_target_pairs={{0,12},{1,15},{2,14},{3,13},{4,8},{5,11},{6,10},{7,9},{8,4},{9,7},... | collective-permute-start | bytes 98312 | tf_op jit(solution)/shard_map/ppermute | solution.py:349
  21.9 0.6 %collective-permute-start.8 = (bf16[64,256]{1,0:T(8,128)(2,1)S(1)}, bf16[64,256]{1,0:T(8,128)(2,1)S(1)}, u32[]{:S(2)}, u32[]{:S(2)}) collective-permute-start(bf16[64,256]{1,0:T(8,128)(2,1)S(1)} %get-tuple-element.35), channel_id=1, source_target_pairs={{0,8},{1,11},{2,10},{3,9},{4,12},{5,15},{6,14},{7,13},{8,0},{9,3},... | collective-permute-start | bytes 98312 | tf_op jit(solution)/shard_map/ppermute | solution.py:349
  22.4 1.8 %collective-permute-start.9 = (bf16[64,256]{1,0:T(8,128)(2,1)S(1)}, bf16[64,256]{1,0:T(8,128)(2,1)S(1)}, u32[]{:S(2)}, u32[]{:S(2)}) collective-permute-start(bf16[64,256]{1,0:T(8,128)(2,1)S(1)} %get-tuple-element.36), channel_id=1, source_target_pairs={{0,6},{1,5},{2,4},{3,7},{4,2},{5,1},{6,0},{7,3},{8,14},{9,13},{10,... | collective-permute-start | bytes 98312 | tf_op jit(solution)/shard_map/ppermute | solution.py:349
  24.2 0.0 collective-permute-done.10.refs_3_
  24.2 0.9 %collective-permute-done.7.refs_0_ = bf16[64,256]{1,0:T(8,128)(2,1)S(1)} collective-permute-done((bf16[64,256]{1,0:T(8,128)(2,1)S(1)}, bf16[64,256]{1,0:T(8,128)(2,1)S(1)}, u32[]{:S(2)}, u32[]{:S(2)}) %collective-permute-start.7) | collective-permute-done | bytes 32800 | tf_op jit(solution)/shard_map/ppermute | solution.py:349
  25.1 1.8 %collective-permute-done.8.refs_1_ = bf16[64,256]{1,0:T(8,128)(2,1)S(1)} collective-permute-done((bf16[64,256]{1,0:T(8,128)(2,1)S(1)}, bf16[64,256]{1,0:T(8,128)(2,1)S(1)}, u32[]{:S(2)}, u32[]{:S(2)}) %collective-permute-start.8) | collective-permute-done | bytes 32800 | tf_op jit(solution)/shard_map/ppermute | solution.py:349
  26.9 0.7 %collective-permute-done.9.refs_2_ = bf16[64,256]{1,0:T(8,128)(2,1)S(1)} collective-permute-done((bf16[64,256]{1,0:T(8,128)(2,1)S(1)}, bf16[64,256]{1,0:T(8,128)(2,1)S(1)}, u32[]{:S(2)}, u32[]{:S(2)}) %collective-permute-start.9) | collective-permute-done | bytes 32800 | tf_op jit(solution)/shard_map/ppermute | solution.py:349
  27.6 0.0 copy-start.3
  27.6 0.0 copy-start.4
  27.6 0.0 copy-start.2
  27.7 0.1 collective-permute-start.11
  27.7 0.0 copy-done
  27.7 0.0 copy-done.1
  27.8 0.6 %copy-done.3 = f32[3,768]{1,0:T(4,128)S(1)} copy-done((f32[3,768]{1,0:T(4,128)S(1)}, f32[3,768]{1,0:T(4,128)}, u32[]{:S(2)}) %copy-start.3) | copy-done | bytes 9240
  28.3 0.0 copy-done.4
  28.3 0.3 %shard_map.109.query_ref = f32[256,256]{1,0:T(8,128)S(1)} custom-call(bf16[256,256]{1,0:T(8,128)(2,1)S(1)} %copy-done.1, f32[1,256]{1,0:T(1,128)S(1)} %bitcast.3, bf16[256,768]{1,0:T(8,128)(2,1)S(1)} %copy-done, f32[3,768]{1,0:T(4,128)S(1)} %copy-done.3), custom_call_target="tpu_custom_call" | custom-call | flops 33554432 | bytes 800000 | tf_op jit(solution)/shard_map/pallas_call | solution.py:26
  28.6 0.3 %collective-permute-done.11.refs_1_ = bf16[128,256]{1,0:T(8,128)(2,1)S(1)} collective-permute-done((bf16[128,256]{1,0:T(8,128)(2,1)S(1)}, bf16[128,256]{1,0:T(8,128)(2,1)S(1)}, u32[]{:S(2)}, u32[]{:S(2)}) %collective-permute-start.11) | collective-permute-done | bytes 65568 | tf_op jit(solution)/shard_map/ppermute | solution.py:349
  29.0 0.0 copy-done.2
  29.0 0.9 %shard_map.116 = bf16[256,256]{1,0:T(8,128)(2,1)} custom-call(f32[256,256]{1,0:T(8,128)S(1)} %shard_map.109.query_ref, bf16[256,256]{1,0:T(8,128)(2,1)S(1)} %copy-done.2, bf16[128,256]{1,0:T(8,128)(2,1)S(1)} %get-tuple-element.39.refs_0_, bf16[128,256]{1,0:T(8,128)(2,1)S(1)} %collective-permute-done.11.refs_1_), custom_call_target="tpu_custom_call" | custom-call | flops 33554432 | bytes 600000 | tf_op jit(solution)/shard_map/pallas_call | solution.py:26
  (4 shorter events, 0.1 us)
Async XLA Ops:
  0.0 16.7 %copy-start.7 = (f32[32,256]{1,0:T(8,128)S(1)}, f32[32,256]{1,0:T(8,128)}, u32[]{:S(2)}) copy-start(f32[32,256]{1,0:T(8,128)} %constant.7.clone.twist_ref) | copy-start | bytes 98308
  1.8 3.1 %collective-permute-start = (bf16[3,136,128]{2,1,0:T(8,128)(2,1)S(1)}, bf16[3,136,128]{2,1,0:T(8,128)(2,1)S(1)}, u32[]{:S(2)}, u32[]{:S(2)}) collective-permute-start(bf16[3,136,128]{2,1,0:T(8,128)(2,1)S(1)} %get-tuple-element.24), channel_id=1, source_target_pairs={{0,1},{1,0},{2,3},{3,2},{4,5},{5,4},{6,7},{7,6},{8,9},{9,8},{10,11... | collective-permute-start | bytes 313352 | tf_op jit(solution)/shard_map/ppermute | solution.py:349
  2.3 7.7 %collective-permute-start.4 = (bf16[280,128]{1,0:T(8,128)(2,1)S(1)}, bf16[280,128]{1,0:T(8,128)(2,1)S(1)}, u32[]{:S(2)}, u32[]{:S(2)}) collective-permute-start(bf16[280,128]{1,0:T(8,128)(2,1)S(1)} %get-tuple-element.28), channel_id=1, source_target_pairs={{0,2},{1,3},{2,0},{3,1},{4,6},{5,7},{6,4},{7,5},{8,10},{9,11},{10,... | collective-permute-start | bytes 215048 | tf_op jit(solution)/shard_map/ppermute | solution.py:349
  4.9 11.8 %copy-start.5 = (bf16[512,256]{1,0:T(8,128)(2,1)S(1)}, bf16[512,256]{1,0:T(8,128)(2,1)}, u32[]{:S(2)}) copy-start(bf16[512,256]{1,0:T(8,128)(2,1)} %constant.6.clone.first_ref) | copy-start | bytes 786436
  4.9 11.8 %copy-start.6 = (bf16[256,512]{1,0:T(8,128)(2,1)S(1)}, bf16[256,512]{1,0:T(8,128)(2,1)}, u32[]{:S(2)}) copy-start(bf16[256,512]{1,0:T(8,128)(2,1)} %constant.8.clone.inner_ref) | copy-start | bytes 786436
  4.9 6.8 %collective-permute-start.1 = (bf16[264,128]{1,0:T(8,128)(2,1)S(1)}, bf16[264,128]{1,0:T(8,128)(2,1)S(1)}, u32[]{:S(2)}, u32[]{:S(2)}) collective-permute-start(bf16[264,128]{1,0:T(8,128)(2,1)S(1)} %get-tuple-element.25), channel_id=1, source_target_pairs={{0,12},{1,15},{2,14},{3,13},{4,8},{5,11},{6,10},{7,9},{8,4},{9,7},... | collective-permute-start | bytes 202760 | tf_op jit(solution)/shard_map/ppermute | solution.py:349
  8.6 6.6 %collective-permute-start.2 = (bf16[264,128]{1,0:T(8,128)(2,1)S(1)}, bf16[264,128]{1,0:T(8,128)(2,1)S(1)}, u32[]{:S(2)}, u32[]{:S(2)}) collective-permute-start(bf16[264,128]{1,0:T(8,128)(2,1)S(1)} %get-tuple-element.26), channel_id=1, source_target_pairs={{0,8},{1,11},{2,10},{3,9},{4,12},{5,15},{6,14},{7,13},{8,0},{9,3},... | collective-permute-start | bytes 202760 | tf_op jit(solution)/shard_map/ppermute | solution.py:349
  8.6 6.6 %collective-permute-start.3 = (bf16[264,128]{1,0:T(8,128)(2,1)S(1)}, bf16[264,128]{1,0:T(8,128)(2,1)S(1)}, u32[]{:S(2)}, u32[]{:S(2)}) collective-permute-start(bf16[264,128]{1,0:T(8,128)(2,1)S(1)} %get-tuple-element.27), channel_id=1, source_target_pairs={{0,6},{1,5},{2,4},{3,7},{4,2},{5,1},{6,0},{7,3},{8,14},{9,13},{10,... | collective-permute-start | bytes 202760 | tf_op jit(solution)/shard_map/ppermute | solution.py:349
  15.2 1.4 %collective-permute-start.5 = (bf16[544,128]{1,0:T(8,128)(2,1)S(1)}, bf16[544,128]{1,0:T(8,128)(2,1)S(1)}, u32[]{:S(2)}, u32[]{:S(2)}) collective-permute-start(bf16[544,128]{1,0:T(8,128)(2,1)S(1)} %get-tuple-element.31), channel_id=1, source_target_pairs={{0,1},{1,0},{2,3},{3,2},{4,5},{5,4},{6,7},{7,6},{8,9},{9,8},{10,11... | collective-permute-start | bytes 417800 | tf_op jit(solution)/shard_map/ppermute | solution.py:349
  16.7 11.1 %copy-start = (bf16[256,768]{1,0:T(8,128)(2,1)S(1)}, bf16[256,768]{1,0:T(8,128)(2,1)}, u32[]{:S(2)}) copy-start(bf16[256,768]{1,0:T(8,128)(2,1)} %refs_2_.1) | copy-start | bytes 1179652
  18.0 1.3 %collective-permute-start.6 = (bf16[3,32,256]{2,1,0:T(8,128)(2,1)S(1)}, bf16[3,32,256]{2,1,0:T(8,128)(2,1)S(1)}, u32[]{:S(2)}, u32[]{:S(2)}) collective-permute-start(bf16[3,32,256]{2,1,0:T(8,128)(2,1)S(1)} %get-tuple-element.33), channel_id=1, source_target_pairs={{0,1},{1,0},{2,3},{3,2},{4,5},{5,4},{6,7},{7,6},{8,9},{9,8},{10,11... | collective-permute-start | bytes 147464 | tf_op jit(solution)/shard_map/ppermute | solution.py:349
  18.2 6.0 %collective-permute-start.10 = (bf16[80,256]{1,0:T(8,128)(2,1)S(1)}, bf16[80,256]{1,0:T(8,128)(2,1)S(1)}, u32[]{:S(2)}, u32[]{:S(2)}) collective-permute-start(bf16[80,256]{1,0:T(8,128)(2,1)S(1)} %get-tuple-element.37), channel_id=1, source_target_pairs={{0,2},{1,3},{2,0},{3,1},{4,6},{5,7},{6,4},{7,5},{8,10},{9,11},{10,... | collective-permute-start | bytes 122888 | tf_op jit(solution)/shard_map/ppermute | solution.py:349
  19.3 8.4 %copy-start.1 = (bf16[256,256]{1,0:T(8,128)(2,1)S(1)}, bf16[256,256]{1,0:T(8,128)(2,1)}, u32[]{:S(2)}) copy-start(bf16[256,256]{1,0:T(8,128)(2,1)} %refs_0_.1) | copy-start | bytes 393220
  19.3 5.8 %collective-permute-start.7 = (bf16[64,256]{1,0:T(8,128)(2,1)S(1)}, bf16[64,256]{1,0:T(8,128)(2,1)S(1)}, u32[]{:S(2)}, u32[]{:S(2)}) collective-permute-start(bf16[64,256]{1,0:T(8,128)(2,1)S(1)} %get-tuple-element.34), channel_id=1, source_target_pairs={{0,12},{1,15},{2,14},{3,13},{4,8},{5,11},{6,10},{7,9},{8,4},{9,7},... | collective-permute-start | bytes 98312 | tf_op jit(solution)/shard_map/ppermute | solution.py:349
  21.9 5.0 %collective-permute-start.8 = (bf16[64,256]{1,0:T(8,128)(2,1)S(1)}, bf16[64,256]{1,0:T(8,128)(2,1)S(1)}, u32[]{:S(2)}, u32[]{:S(2)}) collective-permute-start(bf16[64,256]{1,0:T(8,128)(2,1)S(1)} %get-tuple-element.35), channel_id=1, source_target_pairs={{0,8},{1,11},{2,10},{3,9},{4,12},{5,15},{6,14},{7,13},{8,0},{9,3},... | collective-permute-start | bytes 98312 | tf_op jit(solution)/shard_map/ppermute | solution.py:349
  22.4 5.2 %collective-permute-start.9 = (bf16[64,256]{1,0:T(8,128)(2,1)S(1)}, bf16[64,256]{1,0:T(8,128)(2,1)S(1)}, u32[]{:S(2)}, u32[]{:S(2)}) collective-permute-start(bf16[64,256]{1,0:T(8,128)(2,1)S(1)} %get-tuple-element.36), channel_id=1, source_target_pairs={{0,6},{1,5},{2,4},{3,7},{4,2},{5,1},{6,0},{7,3},{8,14},{9,13},{10,... | collective-permute-start | bytes 98312 | tf_op jit(solution)/shard_map/ppermute | solution.py:349
  27.6 0.7 %copy-start.3 = (f32[3,768]{1,0:T(4,128)S(1)}, f32[3,768]{1,0:T(4,128)}, u32[]{:S(2)}) copy-start(f32[3,768]{1,0:T(4,128)} %refs_3_.1) | copy-start | bytes 27652
  27.6 0.7 %copy-start.4 = (f32[256]{0:T(256)S(1)}, f32[256]{0:T(256)}, u32[]{:S(2)}) copy-start(f32[256]{0:T(256)} %param.12) | copy-start | bytes 3076
  27.6 1.3 %copy-start.2 = (bf16[256,256]{1,0:T(8,128)(2,1)S(1)}, bf16[256,256]{1,0:T(8,128)(2,1)}, u32[]{:S(2)}) copy-start(bf16[256,256]{1,0:T(8,128)(2,1)} %w_ref.3) | copy-start | bytes 393220
  27.7 1.3 %collective-permute-start.11 = (bf16[128,256]{1,0:T(8,128)(2,1)S(1)}, bf16[128,256]{1,0:T(8,128)(2,1)S(1)}, u32[]{:S(2)}, u32[]{:S(2)}) collective-permute-start(bf16[128,256]{1,0:T(8,128)(2,1)S(1)} %get-tuple-element.40), channel_id=1, source_target_pairs={{0,1},{1,0},{2,3},{3,2},{4,5},{5,4},{6,7},{7,6},{8,9},{9,8},{10,11... | collective-permute-start | bytes 196616 | tf_op jit(solution)/shard_map/ppermute | solution.py:349
